TPU v7x, 256 devices: a whole 4x4x8 slice. The times are simulated.
256 devices in a mesh: shard: 64 (over z, y, core), rep: 4 (over x).
Axes of the slice: x: 4, y: 4, z: 8, core: 2. Of those that a mesh axis runs over, the one named last changes fastest.
Arguments:
- index_states: bfloat16 [65536, 768], P('shard'), may hold values from -6 to 6
- questions: bfloat16 [2048, 768], P(('shard', 'rep')), may hold values from -6 to 6
- reader_attention_scores: float32 [2048, 32], P(('shard', 'rep')), may hold values from -6 to 6
- owners: int32 [2048, 32, 1], P(('shard', 'rep')), may hold values from 0 to 63; in each aligned block of 256 rows (0 to 255, 256 to 511, ..., all dimensions but the last counted through in order) at most 8 rows name the same one
- passage_rows: int32 [2048, 32], P(('shard', 'rep')), may hold values from 0 to 1023
- w_up: bfloat16 [768, 3072], replicated, may hold values from -0.21875 to 0.21875
- final_lowering_matrix: bfloat16 [3072, 768], replicated, may hold values from -0.109375 to 0.109375
Outputs:
- ranking_logit_derivative: float32 [2048, 32], P(('shard', 'rep'))
- grad_up_t: float32 [3072, 768], P('shard')
- grad_down: float32 [3072, 768], P('shard')
Inputs may be any that keep to these rules, and one draw needn't show every extreme that they name: `owners`: among the 256 retrieved passages of one device's questions (aligned blocks of 8 questions), at most 8 have the same owner; some owner has exactly 8.
All inputs are finite; a program needn't handle non-finite values.
Results may differ from a plain program's by a relative error of at most 0.0053.
Values may be sent and summed in bfloat16 or wider, within the bound.
No kernel may reach another device: no remote copies, remote signals or barrier semaphores. Data moves between devices by JAX's collectives and lax.ppermute only.
A program may use at most 128 MiB of HBM per device.

v0:
```python
import jax
import jax.numpy as jnp
from jax import lax
from jax.sharding import PartitionSpec as P

K = 32


normalizer_heat = 0.1
loss_scale = 64.0
epsilon = 1e-06
gelu_coeff = 0.7978845608028654
cubic = 0.044715


def gelu_tanh(values):
    inner = gelu_coeff * (values + cubic * values * values * values)
    return 0.5 * values * (1.0 + jnp.tanh(inner))


def gelu_slope(values):
    inner = gelu_coeff * (values + cubic * values * values * values)
    tangent = jnp.tanh(inner)
    return 0.5 * (1.0 + tangent) + 0.5 * values * (1.0 - tangent * tangent) * gelu_coeff * (
        1.0 + 3.0 * cubic * values * values
    )


def normalize_questions(questions):
    wide = questions.astype(jnp.float32)
    return (wide / jnp.sqrt(jnp.sum(wide * wide, -1, keepdims=True) + epsilon)).astype(jnp.bfloat16)


def encode_rows(states, w_up, final_lowering_matrix):
    pre_act = jnp.dot(states, w_up, preferred_element_type=jnp.float32)
    hidden = gelu_tanh(pre_act).astype(jnp.bfloat16)
    embedded = states.astype(jnp.float32) + jnp.dot(
        hidden, final_lowering_matrix, preferred_element_type=jnp.float32
    )
    norms = jnp.sqrt(jnp.sum(embedded * embedded, -1, keepdims=True) + epsilon)
    return (pre_act, hidden, embedded / norms, norms)


def score_gradient(angular_match, reader_attention_scores):
    exponentiated_logits = jnp.exp(angular_match / normalizer_heat)
    probs = exponentiated_logits / jnp.sum(exponentiated_logits, -1, keepdims=True)
    target_raw = jnp.exp(reader_attention_scores)
    target = target_raw / jnp.sum(target_raw, -1, keepdims=True)
    return loss_scale * (probs - target)


def embed_gradient(mixing_weights, query_rows, unit_emb, norms, angular_match):
    return (
        mixing_weights[:, None]
        * (query_rows.astype(jnp.float32) - angular_match[:, None] * unit_emb)
        / norms
    ).astype(jnp.bfloat16)


def contract_rows(left, right):
    return lax.dot_general(
        left, right, (((0,), (0,)), ((), ())), preferred_element_type=jnp.float32
    )


def on_device(
    index_states,
    questions,
    reader_attention_scores,
    owners,
    passage_rows,
    w_up,
    final_lowering_matrix,
):
    shards = lax.axis_size("shard")
    quest_count = passage_rows.shape[0]
    slots_used = quest_count * K
    capacity = max(8, 2 * slots_used // shards)
    width = questions.shape[1]
    q_hat = normalize_questions(questions)
    owner_ids = owners.reshape(slots_used)
    row_ids = passage_rows.reshape(slots_used)
    onehot = (owner_ids[:, None] == jnp.arange(shards, dtype=jnp.int32)[None, :]).astype(jnp.int32)
    prior_state = jnp.cumsum(onehot, axis=0) - onehot
    position = owner_ids * capacity + jnp.sum(prior_state * onehot, axis=1)
    query_rows = jnp.repeat(q_hat, K, axis=0)
    send_rows = (
        jnp.zeros((shards * capacity,), jnp.int32)
        .at[position]
        .set(row_ids)
        .reshape(shards, capacity)
    )
    send_query = (
        jnp.zeros((shards * capacity, width), jnp.bfloat16)
        .at[position]
        .set(query_rows)
        .reshape(shards, capacity, width)
    )
    rows_in = lax.all_to_all(send_rows, "shard", split_axis=0, concat_axis=0, tiled=True)
    query_in = lax.all_to_all(send_query, "shard", split_axis=0, concat_axis=0, tiled=True)
    lead = (rows_in.shape[0], rows_in.shape[1])
    states_in = index_states[rows_in.reshape(-1)]
    pre_in, hidden_in, unit_in, norms_in = encode_rows(states_in, w_up, final_lowering_matrix)
    cosine_in = jnp.sum(unit_in * query_in.reshape(-1, width).astype(jnp.float32), -1)
    cosine_own, pre_act, hidden, unit_emb, norms, states, query_in = (
        cosine_in.reshape(lead),
        pre_in.reshape(lead + (-1,)),
        hidden_in.reshape(lead + (-1,)),
        unit_in.reshape(lead + (width,)),
        norms_in.reshape(lead + (1,)),
        states_in.reshape(lead + (width,)),
        query_in,
    )
    cosine_back = lax.all_to_all(cosine_own, "shard", split_axis=0, concat_axis=0, tiled=True)
    cosine_mine = cosine_back.reshape(-1)[position].reshape(quest_count, K)
    ranking_logit_derivative = score_gradient(cosine_mine, reader_attention_scores)
    coefs_send = (
        jnp.zeros((shards * capacity,), jnp.float32)
        .at[position]
        .set((ranking_logit_derivative / normalizer_heat).reshape(-1))
        .reshape(shards, capacity)
    )
    coefs_own = lax.all_to_all(coefs_send, "shard", split_axis=0, concat_axis=0, tiled=True)
    total_rows = shards * capacity
    pre_act = pre_act.reshape(total_rows, -1)
    hidden = hidden.reshape(total_rows, -1)
    states = states.reshape(total_rows, width)
    grad_emb = embed_gradient(
        coefs_own.reshape(-1),
        query_in.reshape(total_rows, width),
        unit_emb.reshape(total_rows, width),
        norms.reshape(total_rows, 1),
        cosine_own.reshape(-1),
    )
    grad_hidden = lax.dot_general(
        grad_emb,
        final_lowering_matrix,
        (((1,), (1,)), ((), ())),
        preferred_element_type=jnp.float32,
    )
    grad_pre = (grad_hidden * gelu_slope(pre_act)).astype(jnp.bfloat16)
    hidden_part = lax.slice_in_dim(
        hidden, 0, w_up.shape[1] // shards * lax.axis_size("shard"), axis=1
    )
    share = lax.psum_scatter(
        jnp.concatenate(
            [contract_rows(grad_pre, states), contract_rows(hidden_part, grad_emb)], axis=1
        ),
        "shard",
        scatter_dimension=0,
        tiled=True,
    )
    summed = lax.psum(share, "rep")
    return (ranking_logit_derivative, summed[:, :width], summed[:, width:])


def solution(mesh):
    placed = (
        P("shard", None),
        P(("shard", "rep"), None),
        P(("shard", "rep"), None),
        P(("shard", "rep"), None, None),
        P(("shard", "rep"), None),
        P(),
        P(),
    )
    return jax.shard_map(
        on_device,
        mesh=mesh,
        in_specs=placed,
        out_specs=(P(("shard", "rep"), None), P("shard", None), P("shard", None)),
        check_vma=False,
    )
```

profile of v0, /device:TPU:64, one launch (start us, length us, event | category | flops | bytes accessed | tf_op | source)
XLA Modules:
  0.0 396.4 jit_solution(7921035595909885217)
XLA Ops:
  7.2 0.9 reshape.165
  8.1 0.8 eq.29
  9.3 1.4 fusion.33
  11.8 1.4 scatter_custom_fusion
  13.9 11.3 %all-to-all-start = ((s32[64,1,8]{2,1,0:T(1,128)}), s32[64,1,8]{2,1,0:T(1,128)S(1)}, u32[]{:S(2)}, u32[]{:S(2)}) async-start(s32[64,1,8]{2,1,0:T(1,128)} %bitcast.3), calls=%async_computation | async-start | bytes 65536 | tf_op jit(solution)/shard_map/all_to_all | solution.py:99
  25.3 0.8 fusion.18
  26.1 0.8 fusion.19
  26.9 0.8 exponential_reduce_fusion
  27.7 2.6 scatter_custom_fusion.1
  30.3 2.7 all-to-all-done
  33.0 7.6 %all-to-all-start.1 = ((bf16[64,8,768]{2,1,0:T(8,128)(2,1)}), bf16[64,8,768]{2,1,0:T(8,128)(2,1)S(1)}, u32[]{:S(2)}, u32[]{:S(2)}) async-start(bf16[64,8,768]{2,1,0:T(8,128)(2,1)} %bitcast.6), calls=%async_computation.1 | async-start | bytes 1572864 | tf_op jit(solution)/shard_map/all_to_all | solution.py:100
  40.6 0.7 reduce.21
  41.5 2.0 gather_fusion
  43.5 4.5 %fusion.35 = f32[512,3072]{1,0:T(8,128)S(1)} fusion(bf16[512,768]{1,0:T(8,128)(2,1)S(1)} %gather_fusion, bf16[768,3072]{1,0:T(8,128)(2,1)} %param.12), kind=kOutput, calls=%fused_computation.65 | convolution fusion | flops 2415919104 | bytes 11796480 | tf_op jit(solution)/shard_map/dot_general | solution.py:35
  48.0 8.4 %multiply_reduce_fusion = (f32[512]{0:T(512)S(1)}, f32[512,768]{1,0:T(8,128)S(1)}) fusion(bf16[3072,768]{1,0:T(8,128)(2,1)} %param.13, f32[512,3072]{1,0:T(8,128)S(1)} %fusion.35, bf16[512,768]{1,0:T(8,128)(2,1)S(1)} %gather_fusion), kind=kOutput, calls=%fused_computation.23 | convolution fusion | flops 2431647232 | bytes 13371392 | tf_op jit(solution)/shard_map/dot_general | solution.py:37
  56.5 7.2 %all-to-all-done.1 = bf16[64,8,768]{2,1,0:T(8,128)(2,1)S(1)} async-done(((bf16[64,8,768]{2,1,0:T(8,128)(2,1)}), bf16[64,8,768]{2,1,0:T(8,128)(2,1)S(1)}, u32[]{:S(2)}, u32[]{:S(2)}) %all-to-all-start.1) | async-done | bytes 786464 | tf_op jit(solution)/shard_map/all_to_all | solution.py:100
  64.8 5.9 %all-to-all-start.2 = ((f32[64,1,8]{2,1,0:T(1,128)}), f32[64,1,8]{2,1,0:T(1,128)S(1)}, u32[]{:S(2)}, u32[]{:S(2)}) async-start(f32[64,1,8]{2,1,0:T(1,128)} %bitcast.8), calls=%async_computation.2 | async-start | bytes 65536 | tf_op jit(solution)/shard_map/all_to_all | solution.py:114
  70.9 7.5 %all-to-all-done.2 = f32[64,1,8]{2,1,0:T(1,128)S(1)} async-done(((f32[64,1,8]{2,1,0:T(1,128)}), f32[64,1,8]{2,1,0:T(1,128)S(1)}, u32[]{:S(2)}, u32[]{:S(2)}) %all-to-all-start.2) | async-done | bytes 2080 | tf_op jit(solution)/shard_map/all_to_all | solution.py:114
  78.9 0.7 reduce.22
  79.7 1.9 gather_fusion.1
  82.1 1.4 scatter_custom_fusion.2
  83.6 13.4 %all_to_all.32 = f32[64,1,8]{2,1,0:T(1,128)S(1)} all-to-all(f32[64,1,8]{2,1,0:T(1,128)S(1)} %bitcast.46), channel_id=1, replica_groups=mesh['shard'=64,'rep'=4] {'shard'}, dimensions={0} | all-to-all | bytes 4096 | tf_op jit(solution)/shard_map/all_to_all | solution.py:123
  97.8 13.2 %fusion.7 = f32[3072,768]{0,1:T(8,128)} fusion(bf16[512,768]{1,0:T(8,128)(2,1)S(1)} %gather_fusion, f32[512,3072]{1,0:T(8,128)} %copy-done.3, bf16[3072,768]{1,0:T(8,128)(2,1)} %param.13, bf16[64,8,768]{2,1,0:T(8,128)(2,1)S(1)} %all-to-all-done.1, f32[512]{0:T(512)S(1)} %fusion.8, f32[512]{0:T(512)S(1)} %mul.117, f32[512]{0:T(512)S(1)} %add_sqrt_fusion, ...), kind=kOutput, calls=%fused_computation.16 | convolution fusion | flops 4864475136 | bytes 23599104 | tf_op jit(solution)/shard_map/dot_general | solution.py:61
  110.9 6.2 %fusion.29 = f32[3072,768]{0,1:T(8,128)S(1)} fusion(f32[512,3072]{1,0:T(8,128)} %copy-done.3, bf16[64,8,768]{2,1,0:T(8,128)(2,1)S(1)} %all-to-all-done.1, f32[512]{0:T(512)S(1)} %fusion.8, f32[512]{0:T(512)S(1)} %mul.117, f32[512]{0:T(512)S(1)} %add_sqrt_fusion, f32[512,768]{1,0:T(8,128)S(1)} %copy-done.5), kind=kOutput, calls=%fused_computation.62 | convolution fusion | flops 2432827392 | bytes 18094080 | tf_op jit(solution)/shard_map/dot_general | solution.py:61
  117.2 7.1 %pad_maximum_fusion = f32[3072,1536]{0,1:T(8,128)} fusion(f32[3072,768]{0,1:T(8,128)S(1)} %fusion.29, f32[3072,768]{0,1:T(8,128)S(1)} %copy-done.2), kind=kLoop, calls=%fused_computation.5 | loop fusion | flops 4718592 | bytes 37748736 | tf_op jit(solution)/shard_map/concatenate | solution.py:146
  124.3 18.7 %copy.21 = f32[3072,1536]{1,0:T(8,128)} copy(f32[3072,1536]{0,1:T(8,128)} %pad_maximum_fusion) | data formatting | bytes 37748736
  143.1 192.9 %reduce-scatter.4.cloned.1.call-done = f32[48,1536]{1,0:T(8,128)} async-done(((f32[3072,1536]{1,0:T(8,128)}), f32[48,1536]{1,0:T(8,128)}) %reduce-scatter.4.cloned.1.call-update) | async-done | bytes 294928
  336.0 2.1 copy.22
  338.8 48.0 %all-reduce.2.cloned.1.call-done = f32[48,1536]{0,1:T(8,128)} async-done(((f32[48,1536]{0,1:T(8,128)}), f32[48,1536]{0,1:T(8,128)}) %all-reduce.2.cloned.1.call-update) | async-done | bytes 294928 | tf_op jit(solution)/shard_map/psum | solution.py:153
  386.8 1.2 fusion.34
  388.0 0.8 copy.20
  388.8 0.8 copy.19
  (49 shorter events, 6.4 us)
Async XLA Ops:
  7.2 34.3 %copy-start = (bf16[1024,768]{1,0:T(8,128)(2,1)S(1)}, bf16[1024,768]{1,0:T(8,128)(2,1)}, u32[]{:S(2)}) copy-start(bf16[1024,768]{1,0:T(8,128)(2,1)} %param.7) | copy-start | bytes 4718596
  13.9 19.0 %all-to-all-start = ((s32[64,1,8]{2,1,0:T(1,128)}), s32[64,1,8]{2,1,0:T(1,128)S(1)}, u32[]{:S(2)}, u32[]{:S(2)}) async-start(s32[64,1,8]{2,1,0:T(1,128)} %bitcast.3), calls=%async_computation | async-start | bytes 65536 | tf_op jit(solution)/shard_map/all_to_all | solution.py:99
  33.0 30.7 %all-to-all-start.1 = ((bf16[64,8,768]{2,1,0:T(8,128)(2,1)}), bf16[64,8,768]{2,1,0:T(8,128)(2,1)S(1)}, u32[]{:S(2)}, u32[]{:S(2)}) async-start(bf16[64,8,768]{2,1,0:T(8,128)(2,1)} %bitcast.6), calls=%async_computation.1 | async-start | bytes 1572864 | tf_op jit(solution)/shard_map/all_to_all | solution.py:100
  48.0 8.5 %copy-start.3 = (f32[512,3072]{1,0:T(8,128)}, f32[512,3072]{1,0:T(8,128)S(1)}, u32[]{:S(2)}) copy-start(f32[512,3072]{1,0:T(8,128)S(1)} %fusion.35) | copy-start | bytes 18874372
  48.0 33.9 %copy-start.6 = (f32[8,32]{1,0:T(8,128)S(1)}, f32[8,32]{1,0:T(8,128)}, u32[]{:S(2)}) copy-start(f32[8,32]{1,0:T(8,128)} %param.9) | copy-start | bytes 3076
  56.5 22.4 %copy-start.4 = (f32[512,768]{1,0:T(8,128)}, f32[512,768]{1,0:T(8,128)S(1)}, u32[]{:S(2)}) copy-start(f32[512,768]{1,0:T(8,128)S(1)} %get-tuple-element.19) | copy-start | bytes 4718596
  64.8 13.6 %all-to-all-start.2 = ((f32[64,1,8]{2,1,0:T(1,128)}), f32[64,1,8]{2,1,0:T(1,128)S(1)}, u32[]{:S(2)}, u32[]{:S(2)}) async-start(f32[64,1,8]{2,1,0:T(1,128)} %bitcast.8), calls=%async_computation.2 | async-start | bytes 65536 | tf_op jit(solution)/shard_map/all_to_all | solution.py:114
  70.7 265.4 %reduce-scatter.4.cloned.1.call-start = ((), (), s32[]{:S(2)}) async-start(), calls=%async_computation.6 | async-start | bytes 19169280
  97.8 13.2 %copy-start.5 = (f32[512,768]{1,0:T(8,128)S(1)}, f32[512,768]{1,0:T(8,128)}, u32[]{:S(2)}) copy-start(f32[512,768]{1,0:T(8,128)} %copy-done.4) | copy-start | bytes 4718596
  110.9 6.2 %copy-start.2 = (f32[3072,768]{0,1:T(8,128)S(1)}, f32[3072,768]{0,1:T(8,128)}, u32[]{:S(2)}) copy-start(f32[3072,768]{0,1:T(8,128)} %fusion.7) | copy-start | bytes 28311556
  143.0 246.6 %copy-start.1 = (bf16[1024,768]{1,0:T(8,128)(2,1)S(1)}, bf16[1024,768]{1,0:T(8,128)(2,1)}, u32[]{:S(2)}) copy-start(bf16[1024,768]{1,0:T(8,128)(2,1)} %param.7) | copy-start | bytes 4718596
  143.0 243.8 %all-reduce.2.cloned.1.call-start = ((), (), s32[]{:S(2)}) async-start(), calls=%async_computation.5 | async-start | bytes 1572864 | tf_op jit(solution)/shard_map/psum | solution.py:153
Sparse Core Ops, SparseCore 0:
  143.2 192.8 reduce-scatter.3
  338.5 48.2 all-reduce.1
where the time goes:
time: 398 us; the launch traced here: 396 us
  waiting for transfers between devices  258 us (65%)
  local copies, waits for them, and re-layouts  37.9 us (10%)
  matrix products  32.3 us (8%)
  starting transfers between devices  25.1 us (6%)
  other arithmetic  15.1 us (4%)
  between operations  14.3 us (4%)
  blocking collectives  13.4 us (3%)
    unnamed x3, waiting for transfers between devices  193 us
    psum x1, waiting for transfers between devices, on_device(): summed = lax.psum(share, 'rep')  48 us
    unnamed x19, local copies, waits for them, and re-layouts  22.9 us
    dot_general x2, matrix products, contract_rows(): lax.dot_general(left, right, (((0,), (0,)), ((), ())), preferred_element_...  19.4 us
    all_to_all x1, blocking collectives, on_device(): lax.all_to_all(coefs_send, 'shard', split_axis=0, concat_axis=0, tiled=True)  13.4 us
    all_to_all x1, starting transfers between devices, on_device(): lax.all_to_all(send_rows, 'shard', split_axis=0, concat_axis=0, tiled=True)  11.3 us
    dot_general x1, matrix products, encode_rows(): jnp.dot(hidden, final_lowering_matrix, preferred_element_type=jnp.float32)  8.45 us
  transfers between devices with their start and end apart: 5, of which 5 were waited for; matrix products, arithmetic and copies ran while one was open for 5% of the time, Pallas kernels for 0%

commit v1 on v0

v1 whole, which is shorter than its diff:
```python
import itertools

import jax
import jax.numpy as jnp
from jax import lax
from jax.experimental import pallas as pl
from jax.experimental.pallas import tpu as pltpu
from jax.sharding import PartitionSpec as P

K = 32
Q = 8
CAP = 8
NZ, NY, NC, NX = 8, 4, 2, 4
OWN = 48
CHUNK = NY * NC * OWN
HALF_R, HALF_C = 24, 384

normalizer_heat = 0.1
loss_scale = 64.0
epsilon = 1e-06
gelu_coeff = 0.7978845608028654
cubic = 0.044715

bf16, f32, i32 = jnp.bfloat16, jnp.float32, jnp.int32
AXES = ("shard", "rep")


def gray(v):
    return v ^ (v >> 1)


def low_bit(v):
    return gray(v) & 1


def high_bit(v):
    return v >> 1


def label4(v, core):
    low, high = low_bit(v), high_bit(v)
    return (low * (1 - core) + high * core) * 2 + (high * (1 - core) + low * core)


def label8(v, core):
    g = gray((v - core) & 7)
    return ((g & 1) << 2) | (g & 2) | (g >> 2)


def partner(step):
    def meet(z, y, c, x):
        if step == "c":
            return (z, y, 1 - c, x)
        axis, turn = step[0], int(step[1]) - 1
        if axis == "z":
            mine = label8(z, c)
            other = [v for v in range(NZ) if label8(v, c) == mine ^ (4 >> turn)][0]
            return (other, y, c, x)
        at = x if axis == "x" else y
        mine = label4(at, c)
        other = [v for v in range(4) if label4(v, c) == mine ^ (2 >> turn)][0]
        return (z, y, c, other) if axis == "x" else (z, other, c, x)

    pairs = []
    for at, place in enumerate(itertools.product(range(NZ), range(NY), range(NC), range(NX))):
        z, y, c, x = meet(*place)
        pairs.append((at, ((z * NY + y) * NC + c) * NX + x))
    return pairs


def swap(array, step):
    return lax.ppermute(array, AXES, partner(step))


def column(values):
    count, width = values.shape
    spread = jnp.broadcast_to(values[:, None, :], (count, width, width))
    mask = lax.broadcasted_iota(i32, spread.shape, 1) == lax.broadcasted_iota(i32, spread.shape, 2)
    return jnp.sum(jnp.where(mask, spread, 0.0).reshape(count * width, width), -1, keepdims=True)


def uncolumn(values, width):
    spread = jnp.broadcast_to(values, (values.shape[0], width)).reshape(-1, width, width)
    mask = lax.broadcasted_iota(i32, spread.shape, 1) == lax.broadcasted_iota(i32, spread.shape, 2)
    return jnp.sum(jnp.where(mask, spread, 0.0), 1)


def dot(left, right, dims):
    return lax.dot_general(left, right, ((dims[0], dims[1]), ((), ())), preferred_element_type=f32)


def route_kernel(owner_ref, row_ref, send_ref, slot_ref):
    rows = Q * K
    shards = send_ref.shape[0]
    owner = column(owner_ref[...].astype(f32))
    row = column(row_ref[...].astype(f32))
    lanes = lax.broadcasted_iota(i32, (rows, shards), 1).astype(f32)
    onehot = (lanes == owner).astype(f32)
    earlier = (
        lax.broadcasted_iota(i32, (rows, rows), 1) < lax.broadcasted_iota(i32, (rows, rows), 0)
    ).astype(bf16)
    hot = onehot.astype(bf16)
    prior = dot(earlier, hot, ((1,), (0,)))
    rank = jnp.sum(prior * onehot, -1, keepdims=True)
    high = jnp.floor(row * (1.0 / 32.0))
    low = row - 32.0 * high
    at = lax.broadcasted_iota(i32, (rows, 128), 1).astype(f32) == rank
    send_high = dot(hot, jnp.where(at, high, 0.0).astype(bf16), ((0,), (0,)))
    send_low = dot(hot, jnp.where(at, low, 0.0).astype(bf16), ((0,), (0,)))
    send_ref[:, 0, :] = (32.0 * send_high + send_low).astype(i32)
    slot_ref[...] = jnp.broadcast_to(owner * CAP + rank, slot_ref.shape).astype(i32)


def fetch_kernel(rows_ref, index_ref, out_ref):
    shards, cap, width = out_ref.shape
    want = rows_ref[...].astype(f32)
    spread = jnp.broadcast_to(want, (shards, cap, want.shape[2]))
    mask = lax.broadcasted_iota(i32, spread.shape, 1) == lax.broadcasted_iota(i32, spread.shape, 2)
    at = jnp.sum(jnp.where(mask, spread, 0.0).reshape(shards * cap, -1), -1, keepdims=True)
    here = lax.broadcasted_iota(i32, (shards * cap, index_ref.shape[0]), 1).astype(f32) == at
    got = dot(here.astype(f32).astype(bf16), index_ref[...], ((1,), (0,)))
    out_ref[...] = got.reshape(shards, cap, width).astype(bf16)


def place_pieces(place_ref, value_ref, outs, x_first):
    y, c, x = place_ref[1], place_ref[2], place_ref[3]
    for other, out_ref in enumerate(outs):
        core = c ^ other
        mine_x, mine_y = label4(x, core), label4(y, core)
        for j in range(NY):
            at_y = label4(j, core) ^ mine_y
            for piece in range(4):
                at_x = piece ^ mine_x
                at = at_x * NY + at_y if x_first else at_y * NX + at_x
                start = pl.multiple_of(j * NC * OWN + core * OWN + (piece & 1) * HALF_R, 8)
                columns = (piece >> 1) * HALF_C
                out_ref[at, 0] = value_ref[pl.ds(start, HALF_R), columns : columns + HALF_C].astype(bf16)


def forward_kernel(
    place_ref, got_ref, slot_ref, question_ref, reader_ref, up_ref, down_ref,
    derivative_ref, states_out_ref, grad_emb_ref, slope_ref, keep_ref, send_ref,
    states_ref, embedded_ref, hidden_ref, value_ref,
):
    step = pl.program_id(0)
    width = question_ref.shape[1]

    @pl.when(step == 0)
    def _():
        lanes = lax.broadcasted_iota(i32, (Q * K, got_ref.shape[0]), 1)
        onehot = (lanes == slot_ref[:, :1]).astype(f32).astype(bf16)
        states = dot(onehot, got_ref[...], ((1,), (0,)))
        embedded_ref[...] = states
        states_ref[...] = states.astype(bf16)
        states_out_ref[...] = states.astype(bf16)

    @pl.when(step < NZ)
    def _():
        pre = dot(states_ref[...], up_ref[...], ((1,), (0,)))
        square = pre * pre
        tangent = jnp.tanh(gelu_coeff * (pre + cubic * square * pre))
        gate = 0.5 * (1.0 + tangent)
        hidden = (pre * gate).astype(bf16)
        slope_ref[...] = gate + 0.5 * pre * (1.0 - tangent * tangent) * gelu_coeff * (
            1.0 + 3.0 * cubic * square
        )
        hidden_ref[step] = hidden
        embedded_ref[...] += dot(hidden, down_ref[...], ((1,), (0,)))

    @pl.when(step == NZ)
    def _():
        embedded = embedded_ref[...]
        norms = jnp.sqrt(jnp.sum(embedded * embedded, -1, keepdims=True) + epsilon)
        unit = embedded / norms
        wide = question_ref[...].astype(f32)
        q_hat = (wide / jnp.sqrt(jnp.sum(wide * wide, -1, keepdims=True) + epsilon)).astype(bf16)
        query = jnp.broadcast_to(q_hat.astype(f32)[:, None, :], (Q, K, width)).reshape(Q * K, width)
        cosine = jnp.sum(unit * query, -1, keepdims=True)

        def share(scores):
            raised = jnp.exp(scores).reshape(Q, K, 1)
            return (raised / jnp.sum(raised, 1, keepdims=True)).reshape(Q * K, 1)

        derivative = loss_scale * (share(cosine / normalizer_heat) - share(column(reader_ref[...])))
        derivative_ref[...] = uncolumn(derivative, K)
        grad_emb_ref[...] = (
            (derivative / normalizer_heat) * (query - cosine * unit) / norms
        ).astype(bf16)

    @pl.when(step >= NZ)
    def _():
        value_ref[...] = dot(hidden_ref[step - NZ], grad_emb_ref[...], ((0,), (0,)))
        place_pieces(place_ref, value_ref, (keep_ref, send_ref), True)


def backward_kernel(
    place_ref, grad_emb_ref, states_ref, slope_ref, down_ref, keep_ref, send_ref, value_ref
):
    grad_hidden = dot(grad_emb_ref[...], down_ref[...], ((1,), (1,)))
    grad_pre = (grad_hidden * slope_ref[...]).astype(bf16)
    value_ref[...] = dot(grad_pre, states_ref[...], ((0,), (0,)))
    place_pieces(place_ref, value_ref, (keep_ref, send_ref), False)


def whole(shape):
    return pl.BlockSpec(shape, lambda *_: (0,) * len(shape))


def z_block(place_ref, block, other):
    core = place_ref[2] ^ other
    return (0, label8(block, core) ^ label8(place_ref[0], core), 0, 0)


def route(owners, passage_rows, shards):
    return pl.pallas_call(
        route_kernel,
        out_shape=(
            jax.ShapeDtypeStruct((shards, 1, 128), i32),
            jax.ShapeDtypeStruct((Q * K, 128), i32),
        ),
        name="route",
    )(owners, passage_rows)


def fetch(rows_in, index_states):
    shards, width = rows_in.shape[0], index_states.shape[1]
    return pl.pallas_call(
        fetch_kernel,
        out_shape=jax.ShapeDtypeStruct((shards, CAP, width), bf16),
        compiler_params=pltpu.CompilerParams(vmem_limit_bytes=32 << 20),
        name="fetch",
    )(rows_in, index_states)


def forward(place, got, slot, questions, reader, w_up, w_down):
    width, hidden = w_up.shape
    rows = Q * K
    piece = (NX * NY, NZ, HALF_R, HALF_C)
    last = NZ - 1

    def part(other):
        return pl.BlockSpec(
            (NX * NY, 1, HALF_R, HALF_C),
            lambda t, place_ref: z_block(place_ref, jnp.maximum(t - NZ, 0), other),
        )

    return pl.pallas_call(
        forward_kernel,
        grid_spec=pltpu.PrefetchScalarGridSpec(
            num_scalar_prefetch=1,
            grid=(2 * NZ,),
            in_specs=[
                whole(got.shape),
                whole(slot.shape),
                whole(questions.shape),
                whole(reader.shape),
                pl.BlockSpec((width, CHUNK), lambda t, _: (0, jnp.minimum(t, last))),
                pl.BlockSpec((CHUNK, width), lambda t, _: (jnp.minimum(t, last), 0)),
            ],
            out_specs=[
                whole((Q, K)),
                whole((rows, width)),
                whole((rows, width)),
                pl.BlockSpec((rows, CHUNK), lambda t, _: (0, jnp.minimum(t, last))),
                part(0),
                part(1),
            ],
            scratch_shapes=[
                pltpu.VMEM((rows, width), bf16),
                pltpu.VMEM((rows, width), f32),
                pltpu.VMEM((NZ, rows, CHUNK), bf16),
                pltpu.VMEM((CHUNK, width), f32),
            ],
        ),
        out_shape=(
            jax.ShapeDtypeStruct((Q, K), f32),
            jax.ShapeDtypeStruct((rows, width), bf16),
            jax.ShapeDtypeStruct((rows, width), bf16),
            jax.ShapeDtypeStruct((rows, hidden), f32),
            jax.ShapeDtypeStruct(piece, bf16),
            jax.ShapeDtypeStruct(piece, bf16),
        ),
        compiler_params=pltpu.CompilerParams(vmem_limit_bytes=40 << 20),
        cost_estimate=pl.CostEstimate(
            flops=6 * rows * width * hidden, bytes_accessed=24 << 20, transcendentals=rows * hidden
        ),
        name="forward",
    )(place, got, slot, questions, reader, w_up, w_down)


def backward(place, grad_emb, states, slope, w_down):
    hidden, width = w_down.shape
    rows = Q * K
    piece = (NX * NY, NZ, HALF_R, HALF_C)

    def part(other):
        return pl.BlockSpec(
            (NX * NY, 1, HALF_R, HALF_C), lambda t, place_ref: z_block(place_ref, t, other)
        )

    return pl.pallas_call(
        backward_kernel,
        grid_spec=pltpu.PrefetchScalarGridSpec(
            num_scalar_prefetch=1,
            grid=(NZ,),
            in_specs=[
                whole((rows, width)),
                whole((rows, width)),
                pl.BlockSpec((rows, CHUNK), lambda t, _: (0, t)),
                pl.BlockSpec((CHUNK, width), lambda t, _: (t, 0)),
            ],
            out_specs=[part(0), part(1)],
            scratch_shapes=[pltpu.VMEM((CHUNK, width), f32)],
        ),
        out_shape=(jax.ShapeDtypeStruct(piece, bf16), jax.ShapeDtypeStruct(piece, bf16)),
        compiler_params=pltpu.CompilerParams(vmem_limit_bytes=40 << 20),
        cost_estimate=pl.CostEstimate(
            flops=4 * rows * width * hidden, bytes_accessed=16 << 20, transcendentals=0
        ),
        name="backward",
    )(place, grad_emb, states, slope, w_down)


def halves(array):
    half = array.shape[0] // 2
    return array[:half], array[half:]


def meet(keep, send, step):
    came = swap(send, step)
    keep_own, keep_next = halves(keep)
    came_own, came_next = halves(came)
    return (
        keep_own.astype(f32) + came_own.astype(f32),
        (keep_next.astype(f32) + came_next.astype(f32)).astype(bf16),
    )


def total(keep, send, step):
    return keep.astype(f32) + swap(send, step).astype(f32)


def on_device(index_states, questions, reader, owners, passage_rows, w_up, w_down):
    shards = lax.axis_size("shard")
    width = questions.shape[1]
    shard, x = lax.axis_index("shard"), lax.axis_index("rep")
    z, y, c = shard >> 3, (shard >> 1) & 3, shard & 1
    place = jnp.stack([z, y, c, x]).astype(i32)

    send_rows, slot = route(owners.reshape(Q, K), passage_rows, shards)
    rows_in = lax.all_to_all(send_rows, "shard", split_axis=0, concat_axis=0, tiled=True)
    states_out = fetch(rows_in, index_states)
    got = lax.all_to_all(states_out, "shard", split_axis=0, concat_axis=0, tiled=True)
    derivative, states, grad_emb, slope, keep_down, send_down = forward(
        place, got.reshape(shards * CAP, width), slot, questions, reader, w_up, w_down
    )
    keep_up, send_up = backward(place, grad_emb, states, slope, w_down)

    down, up = (keep_down, send_down), (keep_up, send_up)
    for step in ("c", "x1", "x2", "y1"):
        down = meet(*down, step)
    for step in ("c", "y1", "y2", "x1"):
        up = meet(*up, step)
    both = jnp.concatenate([total(*down, "y2"), total(*up, "x2")])
    both = both.reshape(2, NZ, HALF_R, HALF_C).swapaxes(0, 1)
    keep, send = halves(both)
    send = send.astype(bf16)
    for step in ("z1", "z2"):
        keep, send = meet(keep, send, step)
    mine = total(keep, send, "z3")[0]

    label = label4(x, c)
    came = swap(mine, "x2")
    first = (label & 1) == 0
    mine = jnp.concatenate([jnp.where(first, mine, came), jnp.where(first, came, mine)], 1)
    came = swap(mine, "x1")
    first = (label >> 1) == 0
    mine = jnp.concatenate([jnp.where(first, mine, came), jnp.where(first, came, mine)], 2)
    return derivative, mine[1], mine[0]


def solution(mesh):
    placed = (
        P("shard", None),
        P(("shard", "rep"), None),
        P(("shard", "rep"), None),
        P(("shard", "rep"), None, None),
        P(("shard", "rep"), None),
        P(),
        P(),
    )
    return jax.shard_map(
        on_device,
        mesh=mesh,
        in_specs=placed,
        out_specs=(P(("shard", "rep"), None), P("shard", None), P("shard", None)),
        check_vma=False,
    )
```

time: 398 us -> 167 us (0.42)
  waiting for transfers between devices: 258 us -> 80.7 us
  matrix products: 32.3 us -> 0 us
  local copies, waits for them, and re-layouts: 37.9 us -> 9.63 us
  Pallas kernels: 0 us -> 27.9 us
  between operations: 14.3 us -> 0.8 us
  other arithmetic: 15.1 us -> 3.01 us
  blocking collectives: 13.4 us -> 19 us
    unnamed x3 -> x0, waiting for transfers between devices: 193 us -> none
    ppermute x0 -> x15, waiting for transfers between devices: none -> 57.4 us  [swap(): return lax.ppermute(array, AXES, partner(step))]
    psum x1 -> x0, waiting for transfers between devices: 48 us -> none  [on_device(): summed = lax.psum(share, 'rep')]
    dot_general x4 -> x0, matrix products: 32.3 us -> none  [the longest x2 19.4 us: contract_rows(): lax.dot_general(left, right, (((0,), (0,)), ((), ())), preferred_element_...]
    pallas_call x0 -> x4, Pallas kernels: none -> 27.9 us  [the longest x1 15.7 us: forward(): pl.pallas_call(forward_kernel, grid_spec=pltpu.PrefetchScalarGridSpec(num...]
    ppermute x0 -> x15, starting transfers between devices: none -> 18.5 us  [swap(): return lax.ppermute(array, AXES, partner(step))]
    all_to_all x3 -> x1, starting transfers between devices: 24.9 us -> 6.57 us  [on_device(): lax.all_to_all(states_out, 'shard', split_axis=0, concat_axis=0, tiled=True)]
    unnamed x19 -> x16, local copies, waits for them, and re-layouts: 22.9 us -> 9.61 us
  transfers between devices with their start and end apart: 5 -> 16, of which waited for: 5 -> 13; matrix products, arithmetic and copies ran while one was open for 5% -> 1% of each run, Pallas kernels for 0% -> 5%
where the time goes in v1:
time: 167 us; the launch traced here: 166 us
  waiting for transfers between devices  80.7 us (48%)
  Pallas kernels  27.9 us (17%)
  starting transfers between devices  25.1 us (15%)
  blocking collectives  19 us (11%)
  local copies, waits for them, and re-layouts  9.63 us (6%)
  other arithmetic  3.01 us (2%)
    ppermute x15, waiting for transfers between devices, swap(): return lax.ppermute(array, AXES, partner(step))  57.4 us
    all_to_all x1, waiting for transfers between devices, on_device(): lax.all_to_all(states_out, 'shard', split_axis=0, concat_axis=0, tiled=True)  23.2 us
    all_to_all x1, blocking collectives, on_device(): lax.all_to_all(send_rows, 'shard', split_axis=0, concat_axis=0, tiled=True)  19 us
    ppermute x15, starting transfers between devices, swap(): return lax.ppermute(array, AXES, partner(step))  18.5 us
    pallas_call x1, Pallas kernels, forward(): pl.pallas_call(forward_kernel, grid_spec=pltpu.PrefetchScalarGridSpec(num...  15.7 us
    unnamed x16, local copies, waits for them, and re-layouts  9.61 us
    pallas_call x1, Pallas kernels, backward(): pl.pallas_call(backward_kernel, grid_spec=pltpu.PrefetchScalarGridSpec(nu...  8.41 us
    all_to_all x1, starting transfers between devices, on_device(): lax.all_to_all(states_out, 'shard', split_axis=0, concat_axis=0, tiled=True)  6.57 us
  transfers between devices with their start and end apart: 16, of which 13 were waited for; matrix products, arithmetic and copies ran while one was open for 1% of the time, Pallas kernels for 5%

profile of v1, /device:TPU:64, one launch (start us, length us, event | category | flops | bytes accessed | tf_op | source)
XLA Modules:
  0.0 166.1 jit_solution(10461081707252787782)
XLA Ops:
  0.6 1.9 %route.1 = (s32[64,1,128]{2,1,0:T(1,128)}, s32[256,128]{1,0:T(8,128)}) custom-call(s32[8,32]{1,0:T(8,128)} %bitcast.15, s32[8,32]{1,0:T(8,128)} %row_ref.1), custom_call_target="tpu_custom_call" | custom-call | tf_op jit(solution)/shard_map/route/pallas_call | solution.py:215
  2.5 19.0 %all_to_all.10.rows_ref = s32[64,1,128]{2,1,0:T(1,128)S(1)} all-to-all(s32[64,1,128]{2,1,0:T(1,128)} %get-tuple-element.13), channel_id=1, replica_groups=mesh['shard'=64,'rep'=4] {'shard'}, dimensions={0} | all-to-all | bytes 65536 | tf_op jit(solution)/shard_map/all_to_all | solution.py:351
  21.5 1.4 copy-done
  22.9 1.9 %fetch.1 = bf16[64,8,768]{2,1,0:T(8,128)(2,1)} custom-call(s32[64,1,128]{2,1,0:T(1,128)S(1)} %all_to_all.10.rows_ref, bf16[1024,768]{1,0:T(8,128)(2,1)S(1)} %copy-done), custom_call_target="tpu_custom_call" | custom-call | tf_op jit(solution)/shard_map/fetch/pallas_call | solution.py:227
  24.9 6.6 %all-to-all-start.1 = ((bf16[64,8,768]{2,1,0:T(8,128)(2,1)}), bf16[64,8,768]{2,1,0:T(8,128)(2,1)S(1)}, u32[]{:S(2)}, u32[]{:S(2)}) async-start(bf16[64,8,768]{2,1,0:T(8,128)(2,1)} %fetch.1), calls=%async_computation.1 | async-start | bytes 1572864 | tf_op jit(solution)/shard_map/all_to_all | solution.py:353
  31.5 23.2 %all-to-all-done.1 = bf16[64,8,768]{2,1,0:T(8,128)(2,1)S(1)} async-done(((bf16[64,8,768]{2,1,0:T(8,128)(2,1)}), bf16[64,8,768]{2,1,0:T(8,128)(2,1)S(1)}, u32[]{:S(2)}, u32[]{:S(2)}) %all-to-all-start.1) | async-done | bytes 786464 | tf_op jit(solution)/shard_map/all_to_all | solution.py:353
  54.8 2.3 %copy-done.1 = bf16[768,3072]{1,0:T(8,128)(2,1)S(1)} copy-done((bf16[768,3072]{1,0:T(8,128)(2,1)S(1)}, bf16[768,3072]{1,0:T(8,128)(2,1)}, u32[]{:S(2)}) %copy-start.1) | copy-done | bytes 4718616
  57.1 15.7 %forward.1 = (f32[8,32]{1,0:T(8,128)}, bf16[256,768]{1,0:T(8,128)(2,1)S(1)}, bf16[256,768]{1,0:T(8,128)(2,1)S(1)}, f32[256,3072]{1,0:T(8,128)S(1)}, bf16[16,8,24...) custom-call(s32[4]{0:T(128)S(1)} %pad_add_fusion.place_ref, bf16[512,768]{1,0:T(8,128)(2,1)S(1)} %bitcast.14, ...), custom_call_target="tpu_custom_call" | custom-call | flops 3623878656 | bytes 25165824 | tf_op jit(solution)/shard_map/forward/pallas_call | solution.py:247
  72.8 1.6 copy-done.6
  74.4 2.3 %copy-done.2 = bf16[3072,768]{1,0:T(8,128)(2,1)S(1)} copy-done((bf16[3072,768]{1,0:T(8,128)(2,1)S(1)}, bf16[3072,768]{1,0:T(8,128)(2,1)}, u32[]{:S(2)}) %copy-start.2) | copy-done | bytes 4718616
  76.8 1.9 %copy-done.7 = f32[256,3072]{1,0:T(8,128)S(1)} copy-done((f32[256,3072]{1,0:T(8,128)S(1)}, f32[256,3072]{1,0:T(8,128)}, u32[]{:S(2)}) %copy-start.7) | copy-done | bytes 3145752
  78.7 8.4 %backward.1 = (bf16[16,8,24,384]{3,2,1,0:T(8,128)(2,1)S(1)}, bf16[16,8,24,384]{3,2,1,0:T(8,128)(2,1)S(1)}) custom-call(s32[4]{0:T(128)S(1)} %pad_add_fusion.place_ref, bf16[256,768]{1,0:T(8,128)(2,1)S(1)} %get-tuple-element.18.grad_emb_ref, bf16[256,768]{1,0:T(8,128)(2,1)S(1)} %get-tuple-element.19.states_ref, f32[256,3072]{1,0:T(8,128)S(1)} %copy-done.7, ...), custom_call_target="tpu_custom_call" | custom-call | flops 2415919104 | bytes 16777216 | tf_op jit(solution)/shard_map/backward/pallas_call | solution.py:301
  88.3 1.5 collective-permute-start.1
  89.8 2.1 %collective-permute-done.5 = bf16[16,8,24,384]{3,2,1,0:T(8,128)(2,1)S(1)} collective-permute-done((bf16[16,8,24,384]{3,2,1,0:T(8,128)(2,1)S(1)}, bf16[16,8,24,384]{3,2,1,0:T(8,128)(2,1)S(1)}, u32[]{:S(2)}, u32[]{:S(2)}) %collective-permute-start.5) | collective-permute-done | bytes 2359328 | tf_op jit(solution)/shard_map/ppermute | solution.py:72
  92.9 11.6 %collective-permute-done.1 = bf16[8,8,24,384]{3,2,1,0:T(8,128)(2,1)S(1)} collective-permute-done((bf16[8,8,24,384]{3,2,1,0:T(8,128)(2,1)S(1)}, bf16[8,8,24,384]{3,2,1,0:T(8,128)(2,1)S(1)}, u32[]{:S(2)}, u32[]{:S(2)}) %collective-permute-start.1) | collective-permute-done | bytes 1179680 | tf_op jit(solution)/shard_map/ppermute | solution.py:72
  104.8 2.8 %collective-permute-start.2 = (bf16[4,8,24,384]{3,2,1,0:T(8,128)(2,1)S(1)}, bf16[4,8,24,384]{3,2,1,0:T(8,128)(2,1)S(1)}, u32[]{:S(2)}, u32[]{:S(2)}) collective-permute-start(bf16[4,8,24,384]{3,2,1,0:T(8,128)(2,1)S(1)} %get-tuple-element.27), channel_id=1, source_target_pairs={{0,3},{1,2},{2,1},{3,0},{4,5},{5,4},{6,7},{7,6},{8,11},{9,10},{10,... | collective-permute-start | bytes 1769480 | tf_op jit(solution)/shard_map/ppermute | solution.py:72
  107.7 1.1 collective-permute-done.6
  109.0 1.5 collective-permute-start.7
  110.5 5.5 %collective-permute-done.2 = bf16[4,8,24,384]{3,2,1,0:T(8,128)(2,1)S(1)} collective-permute-done((bf16[4,8,24,384]{3,2,1,0:T(8,128)(2,1)S(1)}, bf16[4,8,24,384]{3,2,1,0:T(8,128)(2,1)S(1)}, u32[]{:S(2)}, u32[]{:S(2)}) %collective-permute-start.2) | collective-permute-done | bytes 589856 | tf_op jit(solution)/shard_map/ppermute | solution.py:72
  116.6 5.7 %collective-permute-done.7 = bf16[4,8,24,384]{3,2,1,0:T(8,128)(2,1)S(1)} collective-permute-done((bf16[4,8,24,384]{3,2,1,0:T(8,128)(2,1)S(1)}, bf16[4,8,24,384]{3,2,1,0:T(8,128)(2,1)S(1)}, u32[]{:S(2)}, u32[]{:S(2)}) %collective-permute-start.7) | collective-permute-done | bytes 589856 | tf_op jit(solution)/shard_map/ppermute | solution.py:72
  122.4 2.6 %collective-permute-start.8 = (bf16[2,8,24,384]{3,2,1,0:T(8,128)(2,1)S(1)}, bf16[2,8,24,384]{3,2,1,0:T(8,128)(2,1)S(1)}, u32[]{:S(2)}, u32[]{:S(2)}) collective-permute-start(bf16[2,8,24,384]{3,2,1,0:T(8,128)(2,1)S(1)} %get-tuple-element.33), channel_id=1, source_target_pairs={{0,1},{1,0},{2,3},{3,2},{4,7},{5,6},{6,5},{7,4},{8,9},{9,8},{10,11... | collective-permute-start | bytes 884744 | tf_op jit(solution)/shard_map/ppermute | solution.py:72
  125.1 1.6 collective-permute-start.4
  126.6 4.3 %collective-permute-done.8 = bf16[2,8,24,384]{3,2,1,0:T(8,128)(2,1)S(1)} collective-permute-done((bf16[2,8,24,384]{3,2,1,0:T(8,128)(2,1)S(1)}, bf16[2,8,24,384]{3,2,1,0:T(8,128)(2,1)S(1)}, u32[]{:S(2)}, u32[]{:S(2)}) %collective-permute-start.8) | collective-permute-done | bytes 294944 | tf_op jit(solution)/shard_map/ppermute | solution.py:72
  131.0 2.2 %collective-permute-start.9 = (bf16[1,8,24,384]{3,2,1,0:T(8,128)(2,1)S(1)}, bf16[1,8,24,384]{3,2,1,0:T(8,128)(2,1)S(1)}, u32[]{:S(2)}, u32[]{:S(2)}) collective-permute-start(bf16[1,8,24,384]{3,2,1,0:T(8,128)(2,1)S(1)} %fusion.4), channel_id=1, source_target_pairs={{0,3},{1,2},{2,1},{3,0},{4,5},{5,4},{6,7},{7,6},{8,11},{9,10},{10,... | collective-permute-start | bytes 442376 | tf_op jit(solution)/shard_map/ppermute | solution.py:72
  133.2 4.2 %collective-permute-done.9 = bf16[1,8,24,384]{3,2,1,0:T(8,128)(2,1)S(1)} collective-permute-done((bf16[1,8,24,384]{3,2,1,0:T(8,128)(2,1)S(1)}, bf16[1,8,24,384]{3,2,1,0:T(8,128)(2,1)S(1)}, u32[]{:S(2)}, u32[]{:S(2)}) %collective-permute-start.9) | collective-permute-done | bytes 147488 | tf_op jit(solution)/shard_map/ppermute | solution.py:72
  138.5 4.3 %collective-permute-done.10 = bf16[4,2,24,384]{3,2,0,1:T(8,128)(2,1)S(1)} collective-permute-done((bf16[4,2,24,384]{3,2,0,1:T(8,128)(2,1)S(1)}, bf16[4,2,24,384]{3,2,0,1:T(8,128)(2,1)S(1)}, u32[]{:S(2)}, u32[]{:S(2)}) %collective-permute-start.10) | collective-permute-done | bytes 147488 | tf_op jit(solution)/shard_map/ppermute | solution.py:72
  143.0 4.3 %collective-permute-done.11 = bf16[2,2,24,384]{3,2,0,1:T(8,128)(2,1)S(1)} collective-permute-done((bf16[2,2,24,384]{3,2,0,1:T(8,128)(2,1)S(1)}, bf16[2,2,24,384]{3,2,0,1:T(8,128)(2,1)S(1)}, u32[]{:S(2)}, u32[]{:S(2)}) %collective-permute-start.11) | collective-permute-done | bytes 73760 | tf_op jit(solution)/shard_map/ppermute | solution.py:72
  147.3 1.3 collective-permute-start.12
  148.6 5.7 %collective-permute-done.12 = bf16[1,2,24,384]{3,2,0,1:T(8,128)(2,1)S(1)} collective-permute-done((bf16[1,2,24,384]{3,2,0,1:T(8,128)(2,1)S(1)}, bf16[1,2,24,384]{3,2,0,1:T(8,128)(2,1)S(1)}, u32[]{:S(2)}, u32[]{:S(2)}) %collective-permute-start.12) | collective-permute-done | bytes 36896 | tf_op jit(solution)/shard_map/ppermute | solution.py:72
  154.4 2.2 %collective-permute-start.13 = (f32[2,24,384]{2,1,0:T(8,128)S(1)}, f32[2,24,384]{2,1,0:T(8,128)S(1)}, u32[]{:S(2)}, u32[]{:S(2)}) collective-permute-start(f32[2,24,384]{2,1,0:T(8,128)S(1)} %fusion.14), channel_id=1, source_target_pairs={{0,3},{1,2},{2,1},{3,0},{4,5},{5,4},{6,7},{7,6},{8,11},{9,10},{10,... | collective-permute-start | bytes 221192 | tf_op jit(solution)/shard_map/ppermute | solution.py:72
  156.6 3.4 %collective-permute-done.13 = f32[2,24,384]{2,1,0:T(8,128)S(1)} collective-permute-done((f32[2,24,384]{2,1,0:T(8,128)S(1)}, f32[2,24,384]{2,1,0:T(8,128)S(1)}, u32[]{:S(2)}, u32[]{:S(2)}) %collective-permute-start.13) | collective-permute-done | bytes 73760 | tf_op jit(solution)/shard_map/ppermute | solution.py:72
  160.2 5.1 %collective-permute-done.14 = f32[2,48,384]{2,1,0:T(8,128)S(1)} collective-permute-done((f32[2,48,384]{2,1,0:T(8,128)S(1)}, f32[2,48,384]{2,1,0:T(8,128)S(1)}, u32[]{:S(2)}, u32[]{:S(2)}) %collective-permute-start.14) | collective-permute-done | bytes 147488 | tf_op jit(solution)/shard_map/ppermute | solution.py:72
  (41 shorter events, 5.8 us)
Async XLA Ops:
  21.5 1.4 copy-start
  24.9 29.9 %copy-start.3 = (s32[256,128]{1,0:T(8,128)S(1)}, s32[256,128]{1,0:T(8,128)}, u32[]{:S(2)}) copy-start(s32[256,128]{1,0:T(8,128)} %get-tuple-element.14.slot_ref) | copy-start | bytes 393220
  24.9 29.9 %copy-start.4 = (bf16[8,768]{1,0:T(8,128)(2,1)S(1)}, bf16[8,768]{1,0:T(8,128)(2,1)}, u32[]{:S(2)}) copy-start(bf16[8,768]{1,0:T(8,128)(2,1)} %question_ref.1) | copy-start | bytes 36868
  24.9 29.9 %copy-start.5 = (f32[8,32]{1,0:T(8,128)S(1)}, f32[8,32]{1,0:T(8,128)}, u32[]{:S(2)}) copy-start(f32[8,32]{1,0:T(8,128)} %reader_ref.1) | copy-start | bytes 3076
  24.9 29.9 %all-to-all-start.1 = ((bf16[64,8,768]{2,1,0:T(8,128)(2,1)}), bf16[64,8,768]{2,1,0:T(8,128)(2,1)S(1)}, u32[]{:S(2)}, u32[]{:S(2)}) async-start(bf16[64,8,768]{2,1,0:T(8,128)(2,1)} %fetch.1), calls=%async_computation.1 | async-start | bytes 1572864 | tf_op jit(solution)/shard_map/all_to_all | solution.py:353
  54.8 2.3 %copy-start.1 = (bf16[768,3072]{1,0:T(8,128)(2,1)S(1)}, bf16[768,3072]{1,0:T(8,128)(2,1)}, u32[]{:S(2)}) copy-start(bf16[768,3072]{1,0:T(8,128)(2,1)} %up_ref.1) | copy-start | bytes 14155780
  72.8 1.6 copy-start.6
  74.4 13.2 %collective-permute-start = (bf16[16,8,24,384]{3,2,1,0:T(8,128)(2,1)S(1)}, bf16[16,8,24,384]{3,2,1,0:T(8,128)(2,1)S(1)}, u32[]{:S(2)}, u32[]{:S(2)}) collective-permute-start(bf16[16,8,24,384]{3,2,1,0:T(8,128)(2,1)S(1)} %get-tuple-element.17), channel_id=1, source_target_pairs={{0,4},{1,5},{2,6},{3,7},{4,0},{5,1},{6,2},{7,3},{8,12},{9,13},{10,... | collective-permute-start | bytes 7077896 | tf_op jit(solution)/shard_map/ppermute | solution.py:72
  74.4 2.3 %copy-start.2 = (bf16[3072,768]{1,0:T(8,128)(2,1)S(1)}, bf16[3072,768]{1,0:T(8,128)(2,1)}, u32[]{:S(2)}) copy-start(bf16[3072,768]{1,0:T(8,128)(2,1)} %down_ref.3) | copy-start | bytes 14155780
  76.8 1.9 %copy-start.7 = (f32[256,3072]{1,0:T(8,128)S(1)}, f32[256,3072]{1,0:T(8,128)}, u32[]{:S(2)}) copy-start(f32[256,3072]{1,0:T(8,128)} %copy-done.6) | copy-start | bytes 9437188
  87.1 4.8 %collective-permute-start.5 = (bf16[16,8,24,384]{3,2,1,0:T(8,128)(2,1)S(1)}, bf16[16,8,24,384]{3,2,1,0:T(8,128)(2,1)S(1)}, u32[]{:S(2)}, u32[]{:S(2)}) collective-permute-start(bf16[16,8,24,384]{3,2,1,0:T(8,128)(2,1)S(1)} %get-tuple-element.22), channel_id=1, source_target_pairs={{0,4},{1,5},{2,6},{3,7},{4,0},{5,1},{6,2},{7,3},{8,12},{9,13},{10,... | collective-permute-start | bytes 7077896 | tf_op jit(solution)/shard_map/ppermute | solution.py:72
  88.3 16.3 %collective-permute-start.1 = (bf16[8,8,24,384]{3,2,1,0:T(8,128)(2,1)S(1)}, bf16[8,8,24,384]{3,2,1,0:T(8,128)(2,1)S(1)}, u32[]{:S(2)}, u32[]{:S(2)}) collective-permute-start(bf16[8,8,24,384]{3,2,1,0:T(8,128)(2,1)S(1)} %get-tuple-element.23), channel_id=1, source_target_pairs={{0,1},{1,0},{2,3},{3,2},{4,7},{5,6},{6,5},{7,4},{8,9},{9,8},{10,11... | collective-permute-start | bytes 3538952 | tf_op jit(solution)/shard_map/ppermute | solution.py:72
  92.5 16.3 %collective-permute-start.6 = (bf16[8,8,24,384]{3,2,1,0:T(8,128)(2,1)S(1)}, bf16[8,8,24,384]{3,2,1,0:T(8,128)(2,1)S(1)}, u32[]{:S(2)}, u32[]{:S(2)}) collective-permute-start(bf16[8,8,24,384]{3,2,1,0:T(8,128)(2,1)S(1)} %get-tuple-element.25), channel_id=1, source_target_pairs={{0,8},{1,9},{2,10},{3,11},{4,28},{5,29},{6,30},{7,31},{8,0},{9,1},... | collective-permute-start | bytes 3538952 | tf_op jit(solution)/shard_map/ppermute | solution.py:72
  104.8 11.2 %collective-permute-start.2 = (bf16[4,8,24,384]{3,2,1,0:T(8,128)(2,1)S(1)}, bf16[4,8,24,384]{3,2,1,0:T(8,128)(2,1)S(1)}, u32[]{:S(2)}, u32[]{:S(2)}) collective-permute-start(bf16[4,8,24,384]{3,2,1,0:T(8,128)(2,1)S(1)} %get-tuple-element.27), channel_id=1, source_target_pairs={{0,3},{1,2},{2,1},{3,0},{4,5},{5,4},{6,7},{7,6},{8,11},{9,10},{10,... | collective-permute-start | bytes 1769480 | tf_op jit(solution)/shard_map/ppermute | solution.py:72
  109.0 13.3 %collective-permute-start.7 = (bf16[4,8,24,384]{3,2,1,0:T(8,128)(2,1)S(1)}, bf16[4,8,24,384]{3,2,1,0:T(8,128)(2,1)S(1)}, u32[]{:S(2)}, u32[]{:S(2)}) collective-permute-start(bf16[4,8,24,384]{3,2,1,0:T(8,128)(2,1)S(1)} %get-tuple-element.29), channel_id=1, source_target_pairs={{0,24},{1,25},{2,26},{3,27},{4,12},{5,13},{6,14},{7,15},{8,16},{9,... | collective-permute-start | bytes 1769480 | tf_op jit(solution)/shard_map/ppermute | solution.py:72
  116.1 8.9 %collective-permute-start.3 = (bf16[2,8,24,384]{3,2,1,0:T(8,128)(2,1)S(1)}, bf16[2,8,24,384]{3,2,1,0:T(8,128)(2,1)S(1)}, u32[]{:S(2)}, u32[]{:S(2)}) collective-permute-start(bf16[2,8,24,384]{3,2,1,0:T(8,128)(2,1)S(1)} %get-tuple-element.31), channel_id=1, source_target_pairs={{0,8},{1,9},{2,10},{3,11},{4,28},{5,29},{6,30},{7,31},{8,0},{9,1},... | collective-permute-start | bytes 884744 | tf_op jit(solution)/shard_map/ppermute | solution.py:72
  122.4 8.5 %collective-permute-start.8 = (bf16[2,8,24,384]{3,2,1,0:T(8,128)(2,1)S(1)}, bf16[2,8,24,384]{3,2,1,0:T(8,128)(2,1)S(1)}, u32[]{:S(2)}, u32[]{:S(2)}) collective-permute-start(bf16[2,8,24,384]{3,2,1,0:T(8,128)(2,1)S(1)} %get-tuple-element.33), channel_id=1, source_target_pairs={{0,1},{1,0},{2,3},{3,2},{4,7},{5,6},{6,5},{7,4},{8,9},{9,8},{10,11... | collective-permute-start | bytes 884744 | tf_op jit(solution)/shard_map/ppermute | solution.py:72
  125.1 8.1 %collective-permute-start.4 = (bf16[1,8,24,384]{3,2,1,0:T(8,128)(2,1)S(1)}, bf16[1,8,24,384]{3,2,1,0:T(8,128)(2,1)S(1)}, u32[]{:S(2)}, u32[]{:S(2)}) collective-permute-start(bf16[1,8,24,384]{3,2,1,0:T(8,128)(2,1)S(1)} %fusion.6), channel_id=1, source_target_pairs={{0,24},{1,25},{2,26},{3,27},{4,12},{5,13},{6,14},{7,15},{8,16},{9,... | collective-permute-start | bytes 442376 | tf_op jit(solution)/shard_map/ppermute | solution.py:72
  131.0 6.4 %collective-permute-start.9 = (bf16[1,8,24,384]{3,2,1,0:T(8,128)(2,1)S(1)}, bf16[1,8,24,384]{3,2,1,0:T(8,128)(2,1)S(1)}, u32[]{:S(2)}, u32[]{:S(2)}) collective-permute-start(bf16[1,8,24,384]{3,2,1,0:T(8,128)(2,1)S(1)} %fusion.4), channel_id=1, source_target_pairs={{0,3},{1,2},{2,1},{3,0},{4,5},{5,4},{6,7},{7,6},{8,11},{9,10},{10,... | collective-permute-start | bytes 442376 | tf_op jit(solution)/shard_map/ppermute | solution.py:72
  137.5 5.3 %collective-permute-start.10 = (bf16[4,2,24,384]{3,2,0,1:T(8,128)(2,1)S(1)}, bf16[4,2,24,384]{3,2,0,1:T(8,128)(2,1)S(1)}, u32[]{:S(2)}, u32[]{:S(2)}) collective-permute-start(bf16[4,2,24,384]{3,2,0,1:T(8,128)(2,1)S(1)} %slice.288), channel_id=1, source_target_pairs={{0,32},{1,33},{2,34},{3,35},{4,228},{5,229},{6,230},{7,231},{8,40}... | collective-permute-start | bytes 442376 | tf_op jit(solution)/shard_map/ppermute | solution.py:72
  142.9 4.4 %collective-permute-start.11 = (bf16[2,2,24,384]{3,2,0,1:T(8,128)(2,1)S(1)}, bf16[2,2,24,384]{3,2,0,1:T(8,128)(2,1)S(1)}, u32[]{:S(2)}, u32[]{:S(2)}) collective-permute-start(bf16[2,2,24,384]{3,2,0,1:T(8,128)(2,1)S(1)} %get-tuple-element.35), channel_id=1, source_target_pairs={{0,96},{1,97},{2,98},{3,99},{4,164},{5,165},{6,166},{7,167},{8,104... | collective-permute-start | bytes 221192 | tf_op jit(solution)/shard_map/ppermute | solution.py:72
  147.3 7.1 %collective-permute-start.12 = (bf16[1,2,24,384]{3,2,0,1:T(8,128)(2,1)S(1)}, bf16[1,2,24,384]{3,2,0,1:T(8,128)(2,1)S(1)}, u32[]{:S(2)}, u32[]{:S(2)}) collective-permute-start(bf16[1,2,24,384]{3,2,0,1:T(8,128)(2,1)S(1)} %fusion.12), channel_id=1, source_target_pairs={{0,224},{1,225},{2,226},{3,227},{4,36},{5,37},{6,38},{7,39},{8,232... | collective-permute-start | bytes 110600 | tf_op jit(solution)/shard_map/ppermute | solution.py:72
  154.4 5.7 %collective-permute-start.13 = (f32[2,24,384]{2,1,0:T(8,128)S(1)}, f32[2,24,384]{2,1,0:T(8,128)S(1)}, u32[]{:S(2)}, u32[]{:S(2)}) collective-permute-start(f32[2,24,384]{2,1,0:T(8,128)S(1)} %fusion.14), channel_id=1, source_target_pairs={{0,3},{1,2},{2,1},{3,0},{4,5},{5,4},{6,7},{7,6},{8,11},{9,10},{10,... | collective-permute-start | bytes 221192 | tf_op jit(solution)/shard_map/ppermute | solution.py:72
  160.1 5.2 %collective-permute-start.14 = (f32[2,48,384]{2,1,0:T(8,128)S(1)}, f32[2,48,384]{2,1,0:T(8,128)S(1)}, u32[]{:S(2)}, u32[]{:S(2)}) collective-permute-start(f32[2,48,384]{2,1,0:T(8,128)S(1)} %pad_maximum_fusion.1), channel_id=1, source_target_pairs={{0,1},{1,0},{2,3},{3,2},{4,7},{5,6},{6,5},{7,4},{8,9},{9,8},{10,11... | collective-permute-start | bytes 442376 | tf_op jit(solution)/shard_map/ppermute | solution.py:72

commit v2 on v1

v2 whole, which is shorter than its diff:
```python
import itertools

import jax
import jax.numpy as jnp
from jax import lax
from jax.experimental import pallas as pl
from jax.experimental.pallas import tpu as pltpu
from jax.sharding import PartitionSpec as P

K = 32
Q = 8
CAP = 8
NZ, NY, NC, NX = 8, 4, 2, 4
OWN = 48
CHUNK = NY * NC * OWN
HALF_R, HALF_C = 24, 384
WIDE = 512

normalizer_heat = 0.1
loss_scale = 64.0
epsilon = 1e-06
gelu_coeff = 0.7978845608028654
cubic = 0.044715

bf16, f32, i32 = jnp.bfloat16, jnp.float32, jnp.int32
AXES = ("shard", "rep")


def gray(v):
    return v ^ (v >> 1)


def low_bit(v):
    return gray(v) & 1


def high_bit(v):
    return v >> 1


def label4(v, core):
    low, high = low_bit(v), high_bit(v)
    return (low * (1 - core) + high * core) * 2 + (high * (1 - core) + low * core)


def label8(v, core):
    g = gray((v - core) & 7)
    return ((g & 1) << 2) | (g & 2) | (g >> 2)


def partner(step):
    def meet(z, y, c, x):
        if step == "c":
            return (z, y, 1 - c, x)
        axis, turn = step[0], int(step[1]) - 1
        if axis == "z":
            mine = label8(z, c)
            other = [v for v in range(NZ) if label8(v, c) == mine ^ (4 >> turn)][0]
            return (other, y, c, x)
        at = x if axis == "x" else y
        mine = label4(at, c)
        other = [v for v in range(4) if label4(v, c) == mine ^ (2 >> turn)][0]
        return (z, y, c, other) if axis == "x" else (z, other, c, x)

    pairs = []
    for at, place in enumerate(itertools.product(range(NZ), range(NY), range(NC), range(NX))):
        z, y, c, x = meet(*place)
        pairs.append((at, ((z * NY + y) * NC + c) * NX + x))
    return pairs


def swap(array, step):
    return lax.ppermute(array, AXES, partner(step))


def column(values):
    count, width = values.shape
    spread = jnp.broadcast_to(values[:, None, :], (count, width, width))
    mask = lax.broadcasted_iota(i32, spread.shape, 1) == lax.broadcasted_iota(i32, spread.shape, 2)
    return jnp.sum(jnp.where(mask, spread, 0.0).reshape(count * width, width), -1, keepdims=True)


def uncolumn(values, width):
    spread = jnp.broadcast_to(values, (values.shape[0], width)).reshape(-1, width, width)
    mask = lax.broadcasted_iota(i32, spread.shape, 1) == lax.broadcasted_iota(i32, spread.shape, 2)
    return jnp.sum(jnp.where(mask, spread, 0.0), 1)


def dot(left, right, dims):
    return lax.dot_general(left, right, ((dims[0], dims[1]), ((), ())), preferred_element_type=f32)


def route_kernel(owner_ref, row_ref, index_hbm, send_ref, slot_ref, index_ref, sem):
    load = pltpu.make_async_copy(index_hbm, index_ref, sem)
    load.start()
    rows = Q * K
    shards = send_ref.shape[0]
    owner = column(owner_ref[...].astype(f32))
    row = column(row_ref[...].astype(f32))
    lanes = lax.broadcasted_iota(i32, (rows, shards), 1).astype(f32)
    onehot = (lanes == owner).astype(f32)
    earlier = (
        lax.broadcasted_iota(i32, (rows, rows), 1) < lax.broadcasted_iota(i32, (rows, rows), 0)
    ).astype(bf16)
    hot = onehot.astype(bf16)
    prior = dot(earlier, hot, ((1,), (0,)))
    rank = jnp.sum(prior * onehot, -1, keepdims=True)
    high = jnp.floor(row * (1.0 / 32.0))
    low = row - 32.0 * high
    at = lax.broadcasted_iota(i32, (rows, 128), 1).astype(f32) == rank
    send_high = dot(hot, jnp.where(at, high, 0.0).astype(bf16), ((0,), (0,)))
    send_low = dot(hot, jnp.where(at, low, 0.0).astype(bf16), ((0,), (0,)))
    send_ref[:, 0, :] = (32.0 * send_high + send_low).astype(i32)
    slot_ref[...] = jnp.broadcast_to(owner * CAP + rank, slot_ref.shape).astype(i32)
    load.wait()


def fetch_kernel(rows_ref, index_ref, out_ref):
    shards, cap, width = out_ref.shape
    want = rows_ref[...].astype(f32)
    spread = jnp.broadcast_to(want, (shards, cap, want.shape[2]))
    mask = lax.broadcasted_iota(i32, spread.shape, 1) == lax.broadcasted_iota(i32, spread.shape, 2)
    at = jnp.sum(jnp.where(mask, spread, 0.0).reshape(shards * cap, -1), -1, keepdims=True)
    lanes = lax.broadcasted_iota(i32, (shards * cap, index_ref.shape[0]), 1).astype(f32)
    here = (lanes == at).astype(f32).astype(bf16)
    got = dot(here, index_ref[...], ((1,), (0,)))
    out_ref[...] = got.reshape(shards, cap, width).astype(bf16)


def place_gradient(place_ref, value_ref, outs, z, x_first):
    y, c, x = place_ref[1], place_ref[2], place_ref[3]
    for other, out_ref in enumerate(outs):
        core = c ^ other
        mine_x, mine_y = label4(x, core), label4(y, core)
        at_z = label8(z, core) ^ label8(place_ref[0], core)
        for j in range(NY):
            at_y = label4(j, core) ^ mine_y
            for piece in range(4):
                at_x = piece ^ mine_x
                at = at_x * NY + at_y if x_first else at_y * NX + at_x
                start = pl.multiple_of(j * NC * OWN + core * OWN + (piece & 1) * HALF_R, 8)
                columns = (piece >> 1) * HALF_C
                out_ref[at, at_z] = value_ref[pl.ds(start, HALF_R), columns : columns + HALF_C].astype(bf16)


def forward_kernel(
    place_ref, got_ref, slot_ref, question_ref, reader_ref, up_hbm, down_hbm,
    derivative_ref, states_ref, grad_emb_ref, slope_ref, keep_ref, send_ref,
    up_ref, down_ref, hidden_ref, value_ref, sems,
):
    width = question_ref.shape[1]
    parts = up_ref.shape[1] // WIDE
    ups, downs = [], []
    for t in range(parts):
        cut = pl.ds(t * WIDE, WIDE)
        ups.append(pltpu.make_async_copy(up_hbm.at[:, cut], up_ref.at[:, cut], sems.at[0, t]))
        downs.append(pltpu.make_async_copy(down_hbm.at[cut, :], down_ref.at[cut, :], sems.at[1, t]))
        ups[t].start()
        downs[t].start()

    lanes = lax.broadcasted_iota(i32, (Q * K, got_ref.shape[0]), 1)
    onehot = (lanes == slot_ref[:, :1]).astype(f32).astype(bf16)
    states = dot(onehot, got_ref[...], ((1,), (0,))).astype(bf16)
    states_ref[...] = states
    for t in range(parts):
        cut = slice(t * WIDE, (t + 1) * WIDE)
        ups[t].wait()
        pre = dot(states, up_ref[:, cut], ((1,), (0,)))
        square = pre * pre
        tangent = jnp.tanh(pre * (gelu_coeff + (gelu_coeff * cubic) * square))
        gate = 0.5 + 0.5 * tangent
        hidden = (pre * gate).astype(bf16)
        slope_ref[:, cut] = gate + pre * (1.0 - tangent * tangent) * (
            0.5 * gelu_coeff + (1.5 * gelu_coeff * cubic) * square
        )
        hidden_ref[:, cut] = hidden
    for copy in downs:
        copy.wait()
    embedded = states.astype(f32) + dot(hidden_ref[...], down_ref[...], ((1,), (0,)))
    norms = jnp.sqrt(jnp.sum(embedded * embedded, -1, keepdims=True) + epsilon)
    unit = embedded / norms
    wide = question_ref[...].astype(f32)
    q_hat = (wide / jnp.sqrt(jnp.sum(wide * wide, -1, keepdims=True) + epsilon)).astype(bf16)
    query = jnp.broadcast_to(q_hat.astype(f32)[:, None, :], (Q, K, width)).reshape(Q * K, width)
    cosine = jnp.sum(unit * query, -1, keepdims=True)

    def share(scores):
        raised = jnp.exp(scores).reshape(Q, K, 1)
        return (raised / jnp.sum(raised, 1, keepdims=True)).reshape(Q * K, 1)

    derivative = loss_scale * (share(cosine / normalizer_heat) - share(column(reader_ref[...])))
    derivative_ref[...] = uncolumn(derivative, K)
    grad_emb = ((derivative / normalizer_heat) * (query - cosine * unit) / norms).astype(bf16)
    grad_emb_ref[...] = grad_emb
    for z in range(NZ):
        value_ref[z % 2] = dot(hidden_ref[:, z * CHUNK : (z + 1) * CHUNK], grad_emb, ((0,), (0,)))
        place_gradient(place_ref, value_ref.at[z % 2], (keep_ref, send_ref), z, True)


def backward_kernel(
    place_ref, grad_emb_ref, states_ref, slope_ref, down_hbm,
    keep_ref, send_ref,
    down_ref, grad_pre_ref, value_ref, sems,
):
    parts = down_ref.shape[0] // WIDE
    downs = []
    for t in range(parts):
        cut = pl.ds(t * WIDE, WIDE)
        downs.append(pltpu.make_async_copy(down_hbm.at[cut, :], down_ref.at[cut, :], sems.at[t]))
        downs[t].start()
    grad_emb, states = grad_emb_ref[...], states_ref[...]
    for t in range(parts):
        cut = slice(t * WIDE, (t + 1) * WIDE)
        downs[t].wait()
        grad_hidden = dot(grad_emb, down_ref[cut, :], ((1,), (1,)))
        grad_pre_ref[:, cut] = (grad_hidden * slope_ref[:, cut]).astype(bf16)
    for z in range(NZ):
        value_ref[z % 2] = dot(grad_pre_ref[:, z * CHUNK : (z + 1) * CHUNK], states, ((0,), (0,)))
        place_gradient(place_ref, value_ref.at[z % 2], (keep_ref, send_ref), z, False)


def far(array):
    return pltpu.with_memory_space_constraint(array, pltpu.HBM)


SMEM, VMEM, HBM = (
    pl.BlockSpec(memory_space=pltpu.SMEM),
    pl.BlockSpec(memory_space=pltpu.VMEM),
    pl.BlockSpec(memory_space=pltpu.HBM),
)


def route(owners, passage_rows, index_states, shards):
    return pl.pallas_call(
        route_kernel,
        in_specs=[VMEM, VMEM, HBM],
        out_specs=[VMEM] * 3,
        out_shape=(
            jax.ShapeDtypeStruct((shards, 1, 128), i32),
            jax.ShapeDtypeStruct((Q * K, 128), i32),
            jax.ShapeDtypeStruct(index_states.shape, index_states.dtype),
        ),
        scratch_shapes=[pltpu.SemaphoreType.DMA],
        name="route",
    )(owners, passage_rows, far(index_states))


def fetch(rows_in, index_states):
    shards, width = rows_in.shape[0], index_states.shape[1]
    return pl.pallas_call(
        fetch_kernel,
        out_shape=jax.ShapeDtypeStruct((shards, CAP, width), bf16),
        compiler_params=pltpu.CompilerParams(vmem_limit_bytes=32 << 20),
        name="fetch",
    )(rows_in, index_states)


def forward(place, got, slot, questions, reader, w_up, w_down):
    width, hidden = w_up.shape
    rows = Q * K
    piece = (NX * NY, NZ, HALF_R, HALF_C)
    return pl.pallas_call(
        forward_kernel,
        in_specs=[SMEM, VMEM, VMEM, VMEM, VMEM, HBM, HBM],
        out_specs=[VMEM] * 6,
        scratch_shapes=[
            pltpu.VMEM((width, hidden), bf16),
            pltpu.VMEM((hidden, width), bf16),
            pltpu.VMEM((rows, hidden), bf16),
            pltpu.VMEM((2, CHUNK, width), f32),
            pltpu.SemaphoreType.DMA((2, hidden // WIDE)),
        ],
        out_shape=(
            jax.ShapeDtypeStruct((Q, K), f32),
            jax.ShapeDtypeStruct((rows, width), bf16),
            jax.ShapeDtypeStruct((rows, width), bf16),
            jax.ShapeDtypeStruct((rows, hidden), f32),
            jax.ShapeDtypeStruct(piece, bf16),
            jax.ShapeDtypeStruct(piece, bf16),
        ),
        compiler_params=pltpu.CompilerParams(vmem_limit_bytes=32 << 20),
        cost_estimate=pl.CostEstimate(
            flops=6 * rows * width * hidden, bytes_accessed=24 << 20, transcendentals=rows * hidden
        ),
        name="forward",
    )(place, got, slot, questions, reader, far(w_up), far(w_down))


def backward(place, grad_emb, states, slope, w_down):
    hidden, width = w_down.shape
    rows = Q * K
    piece = (NX * NY, NZ, HALF_R, HALF_C)
    return pl.pallas_call(
        backward_kernel,
        in_specs=[SMEM, VMEM, VMEM, VMEM, HBM],
        out_specs=[VMEM] * 2,
        scratch_shapes=[
            pltpu.VMEM((hidden, width), bf16),
            pltpu.VMEM((rows, hidden), bf16),
            pltpu.VMEM((2, CHUNK, width), f32),
            pltpu.SemaphoreType.DMA((hidden // WIDE,)),
        ],
        out_shape=(jax.ShapeDtypeStruct(piece, bf16), jax.ShapeDtypeStruct(piece, bf16)),
        compiler_params=pltpu.CompilerParams(vmem_limit_bytes=24 << 20),
        cost_estimate=pl.CostEstimate(
            flops=4 * rows * width * hidden, bytes_accessed=16 << 20, transcendentals=0
        ),
        name="backward",
    )(place, grad_emb, states, slope, far(w_down))


def halves(array):
    half = array.shape[0] // 2
    return array[:half], array[half:]


def meet(keep, send, step):
    came = swap(send, step)
    keep_own, keep_next = halves(keep)
    came_own, came_next = halves(came)
    return (
        keep_own.astype(f32) + came_own.astype(f32),
        (keep_next.astype(f32) + came_next.astype(f32)).astype(bf16),
    )


def total(keep, send, step):
    return keep.astype(f32) + swap(send, step).astype(f32)


def on_device(index_states, questions, reader, owners, passage_rows, w_up, w_down):
    shards = lax.axis_size("shard")
    width = questions.shape[1]
    shard, x = lax.axis_index("shard"), lax.axis_index("rep")
    z, y, c = shard >> 3, (shard >> 1) & 3, shard & 1
    place = jnp.stack([z, y, c, x]).astype(i32)

    send_rows, slot, index_near = route(owners.reshape(Q, K), passage_rows, index_states, shards)
    rows_in = lax.all_to_all(send_rows, "shard", split_axis=0, concat_axis=0, tiled=True)
    states_out = fetch(rows_in, index_near)
    got = lax.all_to_all(states_out, "shard", split_axis=0, concat_axis=0, tiled=True)
    derivative, states, grad_emb, slope, keep_down, send_down = forward(
        place, got.reshape(shards * CAP, width), slot, questions, reader, w_up, w_down
    )
    keep_up, send_up = backward(place, grad_emb, states, slope, w_down)

    down, up = (keep_down, send_down), (keep_up, send_up)
    for step in ("c", "x1", "x2", "y1"):
        down = meet(*down, step)
    for step in ("c", "y1", "y2", "x1"):
        up = meet(*up, step)
    both = jnp.concatenate([total(*down, "y2"), total(*up, "x2")])
    both = both.reshape(2, NZ, HALF_R, HALF_C).swapaxes(0, 1)
    keep, send = halves(both)
    send = send.astype(bf16)
    for step in ("z1", "z2"):
        keep, send = meet(keep, send, step)
    mine = total(keep, send, "z3")[0]

    label = label4(x, c)
    came = swap(mine, "x2")
    first = (label & 1) == 0
    mine = jnp.concatenate([jnp.where(first, mine, came), jnp.where(first, came, mine)], 1)
    came = swap(mine, "x1")
    first = (label >> 1) == 0
    mine = jnp.concatenate([jnp.where(first, mine, came), jnp.where(first, came, mine)], 2)
    return derivative, mine[1], mine[0]


def solution(mesh):
    placed = (
        P("shard", None),
        P(("shard", "rep"), None),
        P(("shard", "rep"), None),
        P(("shard", "rep"), None, None),
        P(("shard", "rep"), None),
        P(),
        P(),
    )
    return jax.shard_map(
        on_device,
        mesh=mesh,
        in_specs=placed,
        out_specs=(P(("shard", "rep"), None), P("shard", None), P("shard", None)),
        check_vma=False,
    )
```

time: 167 us -> 153 us (0.916)
  local copies, waits for them, and re-layouts: 9.63 us -> 1.44 us
  Pallas kernels: 27.9 us -> 21.8 us
    unnamed x16 -> x8, local copies, waits for them, and re-layouts: 9.61 us -> 1.42 us
    pallas_call x3, Pallas kernels: 25.9 us -> 19.8 us  [the longest x1 10.3 us: forward(): pl.pallas_call(forward_kernel, in_specs=[SMEM, VMEM, VMEM, VMEM, VMEM, HB...]
  transfers between devices with their start and end apart: 16 -> 16, of which waited for: 13 -> 13; matrix products, arithmetic and copies ran while one was open for 1% -> 1% of each run, Pallas kernels for 5% -> 4%
where the time goes in v2:
time: 153 us; the launch traced here: 152 us
  waiting for transfers between devices  80.6 us (53%)
  starting transfers between devices  25.1 us (16%)
  Pallas kernels  21.8 us (14%)
  blocking collectives  19 us (12%)
  other arithmetic  3.14 us (2%)
    ppermute x15, waiting for transfers between devices, swap(): return lax.ppermute(array, AXES, partner(step))  57.3 us
    all_to_all x1, waiting for transfers between devices, on_device(): lax.all_to_all(states_out, 'shard', split_axis=0, concat_axis=0, tiled=True)  23.2 us
    all_to_all x1, blocking collectives, on_device(): lax.all_to_all(send_rows, 'shard', split_axis=0, concat_axis=0, tiled=True)  19 us
    ppermute x15, starting transfers between devices, swap(): return lax.ppermute(array, AXES, partner(step))  18.6 us
    pallas_call x1, Pallas kernels, forward(): pl.pallas_call(forward_kernel, in_specs=[SMEM, VMEM, VMEM, VMEM, VMEM, HB...  10.3 us
    all_to_all x1, starting transfers between devices, on_device(): lax.all_to_all(states_out, 'shard', split_axis=0, concat_axis=0, tiled=True)  6.57 us
    pallas_call x1, Pallas kernels, backward(): pl.pallas_call(backward_kernel, in_specs=[SMEM, VMEM, VMEM, VMEM, HBM], o...  6.1 us
    pallas_call x1, Pallas kernels, route(): pl.pallas_call(route_kernel, in_specs=[VMEM, VMEM, HBM], out_specs=[VMEM]...  3.36 us
  transfers between devices with their start and end apart: 16, of which 13 were waited for; matrix products, arithmetic and copies ran while one was open for 1% of the time, Pallas kernels for 4%

profile of v2, /device:TPU:64, one launch (start us, length us, event | category | flops | bytes accessed | tf_op | source)
XLA Modules:
  0.0 151.9 jit_solution(3795625021320394015)
XLA Ops:
  0.6 3.4 %route.1 = (s32[64,1,128]{2,1,0:T(1,128)}, s32[256,128]{1,0:T(8,128)}, bf16[1024,768]{1,0:T(8,128)(2,1)}) custom-call(s32[8,32]{1,0:T(8,128)} %bitcast.15, s32[8,32]{1,0:T(8,128)} %row_ref.1, bf16[1024,768]{1,0:T(8,128)(2,1)} %index_hbm.1), custom_call_target="tpu_custom_call" | custom-call | tf_op jit(solution)/shard_map/route/pallas_call | solution.py:234
  4.0 19.0 %all_to_all.10.rows_ref = s32[64,1,128]{2,1,0:T(1,128)S(1)} all-to-all(s32[64,1,128]{2,1,0:T(1,128)} %get-tuple-element.14), channel_id=1, replica_groups=mesh['shard'=64,'rep'=4] {'shard'}, dimensions={0} | all-to-all | bytes 65536 | tf_op jit(solution)/shard_map/all_to_all | solution.py:339
  23.0 1.4 copy-done
  24.4 2.0 %fetch.1 = bf16[64,8,768]{2,1,0:T(8,128)(2,1)} custom-call(s32[64,1,128]{2,1,0:T(1,128)S(1)} %all_to_all.10.rows_ref, bf16[1024,768]{1,0:T(8,128)(2,1)S(1)} %copy-done), custom_call_target="tpu_custom_call" | custom-call | tf_op jit(solution)/shard_map/fetch/pallas_call | solution.py:250
  26.4 6.6 %all-to-all-start.1 = ((bf16[64,8,768]{2,1,0:T(8,128)(2,1)}), bf16[64,8,768]{2,1,0:T(8,128)(2,1)S(1)}, u32[]{:S(2)}, u32[]{:S(2)}) async-start(bf16[64,8,768]{2,1,0:T(8,128)(2,1)} %fetch.1), calls=%async_computation.1 | async-start | bytes 1572864 | tf_op jit(solution)/shard_map/all_to_all | solution.py:341
  33.1 23.2 %all-to-all-done.1 = bf16[64,8,768]{2,1,0:T(8,128)(2,1)S(1)} async-done(((bf16[64,8,768]{2,1,0:T(8,128)(2,1)}), bf16[64,8,768]{2,1,0:T(8,128)(2,1)S(1)}, u32[]{:S(2)}, u32[]{:S(2)}) %all-to-all-start.1) | async-done | bytes 786464 | tf_op jit(solution)/shard_map/all_to_all | solution.py:341
  56.3 10.3 %forward.1 = (f32[8,32]{1,0:T(8,128)}, bf16[256,768]{1,0:T(8,128)(2,1)S(1)}, bf16[256,768]{1,0:T(8,128)(2,1)S(1)}, f32[256,3072]{1,0:T(8,128)S(1)}, bf16[16,8,24...) custom-call(s32[4]{0:T(128)S(1)} %pad_add_fusion.place_ref, bf16[512,768]{1,0:T(8,128)(2,1)S(1)} %bitcast.14, ...), custom_call_target="tpu_custom_call" | custom-call | flops 3623878656 | bytes 25165824 | tf_op jit(solution)/shard_map/forward/pallas_call | solution.py:262
  67.0 6.1 %backward.1 = (bf16[16,8,24,384]{3,2,1,0:T(8,128)(2,1)S(1)}, bf16[16,8,24,384]{3,2,1,0:T(8,128)(2,1)S(1)}) custom-call(s32[4]{0:T(128)S(1)} %pad_add_fusion.place_ref, bf16[256,768]{1,0:T(8,128)(2,1)S(1)} %get-tuple-element.20.grad_emb_ref, bf16[256,768]{1,0:T(8,128)(2,1)S(1)} %get-tuple-element.21.states_ref, f32[256,3072]{1,0:T(8,128)S(1)} %get-tuple-element.22.slope_ref, ...), custom_call_target="tpu_custom_call" | custom-call | flops 2415919104 | bytes 16777216 | tf_op jit(solution)/shard_map/backward/pallas_call | solution.py:293
  73.1 0.6 collective-permute-start.5
  73.7 0.6 add_convert_fusion.1
  74.2 1.6 %collective-permute-start.1 = (bf16[8,8,24,384]{3,2,1,0:T(8,128)(2,1)S(1)}, bf16[8,8,24,384]{3,2,1,0:T(8,128)(2,1)S(1)}, u32[]{:S(2)}, u32[]{:S(2)}) collective-permute-start(bf16[8,8,24,384]{3,2,1,0:T(8,128)(2,1)S(1)} %get-tuple-element.25), channel_id=1, source_target_pairs={{0,1},{1,0},{2,3},{3,2},{4,7},{5,6},{6,5},{7,4},{8,9},{9,8},{10,11... | collective-permute-start | bytes 3538952 | tf_op jit(solution)/shard_map/ppermute | solution.py:73
  75.8 2.0 %collective-permute-done.5 = bf16[16,8,24,384]{3,2,1,0:T(8,128)(2,1)S(1)} collective-permute-done((bf16[16,8,24,384]{3,2,1,0:T(8,128)(2,1)S(1)}, bf16[16,8,24,384]{3,2,1,0:T(8,128)(2,1)S(1)}, u32[]{:S(2)}, u32[]{:S(2)}) %collective-permute-start.5) | collective-permute-done | bytes 2359328 | tf_op jit(solution)/shard_map/ppermute | solution.py:73
  78.9 11.6 %collective-permute-done.1 = bf16[8,8,24,384]{3,2,1,0:T(8,128)(2,1)S(1)} collective-permute-done((bf16[8,8,24,384]{3,2,1,0:T(8,128)(2,1)S(1)}, bf16[8,8,24,384]{3,2,1,0:T(8,128)(2,1)S(1)}, u32[]{:S(2)}, u32[]{:S(2)}) %collective-permute-start.1) | collective-permute-done | bytes 1179680 | tf_op jit(solution)/shard_map/ppermute | solution.py:73
  90.8 2.8 %collective-permute-start.2 = (bf16[4,8,24,384]{3,2,1,0:T(8,128)(2,1)S(1)}, bf16[4,8,24,384]{3,2,1,0:T(8,128)(2,1)S(1)}, u32[]{:S(2)}, u32[]{:S(2)}) collective-permute-start(bf16[4,8,24,384]{3,2,1,0:T(8,128)(2,1)S(1)} %get-tuple-element.29), channel_id=1, source_target_pairs={{0,3},{1,2},{2,1},{3,0},{4,5},{5,4},{6,7},{7,6},{8,11},{9,10},{10,... | collective-permute-start | bytes 1769480 | tf_op jit(solution)/shard_map/ppermute | solution.py:73
  93.7 1.0 collective-permute-done.6
  95.0 1.5 %collective-permute-start.7 = (bf16[4,8,24,384]{3,2,1,0:T(8,128)(2,1)S(1)}, bf16[4,8,24,384]{3,2,1,0:T(8,128)(2,1)S(1)}, u32[]{:S(2)}, u32[]{:S(2)}) collective-permute-start(bf16[4,8,24,384]{3,2,1,0:T(8,128)(2,1)S(1)} %get-tuple-element.31), channel_id=1, source_target_pairs={{0,24},{1,25},{2,26},{3,27},{4,12},{5,13},{6,14},{7,15},{8,16},{9,... | collective-permute-start | bytes 1769480 | tf_op jit(solution)/shard_map/ppermute | solution.py:73
  96.5 5.5 %collective-permute-done.2 = bf16[4,8,24,384]{3,2,1,0:T(8,128)(2,1)S(1)} collective-permute-done((bf16[4,8,24,384]{3,2,1,0:T(8,128)(2,1)S(1)}, bf16[4,8,24,384]{3,2,1,0:T(8,128)(2,1)S(1)}, u32[]{:S(2)}, u32[]{:S(2)}) %collective-permute-start.2) | collective-permute-done | bytes 589856 | tf_op jit(solution)/shard_map/ppermute | solution.py:73
  102.7 5.5 %collective-permute-done.7 = bf16[4,8,24,384]{3,2,1,0:T(8,128)(2,1)S(1)} collective-permute-done((bf16[4,8,24,384]{3,2,1,0:T(8,128)(2,1)S(1)}, bf16[4,8,24,384]{3,2,1,0:T(8,128)(2,1)S(1)}, u32[]{:S(2)}, u32[]{:S(2)}) %collective-permute-start.7) | collective-permute-done | bytes 589856 | tf_op jit(solution)/shard_map/ppermute | solution.py:73
  108.3 2.5 %collective-permute-start.8 = (bf16[2,8,24,384]{3,2,1,0:T(8,128)(2,1)S(1)}, bf16[2,8,24,384]{3,2,1,0:T(8,128)(2,1)S(1)}, u32[]{:S(2)}, u32[]{:S(2)}) collective-permute-start(bf16[2,8,24,384]{3,2,1,0:T(8,128)(2,1)S(1)} %get-tuple-element.35), channel_id=1, source_target_pairs={{0,1},{1,0},{2,3},{3,2},{4,7},{5,6},{6,5},{7,4},{8,9},{9,8},{10,11... | collective-permute-start | bytes 884744 | tf_op jit(solution)/shard_map/ppermute | solution.py:73
  110.9 1.6 %collective-permute-start.4 = (bf16[1,8,24,384]{3,2,1,0:T(8,128)(2,1)S(1)}, bf16[1,8,24,384]{3,2,1,0:T(8,128)(2,1)S(1)}, u32[]{:S(2)}, u32[]{:S(2)}) collective-permute-start(bf16[1,8,24,384]{3,2,1,0:T(8,128)(2,1)S(1)} %fusion.6), channel_id=1, source_target_pairs={{0,24},{1,25},{2,26},{3,27},{4,12},{5,13},{6,14},{7,15},{8,16},{9,... | collective-permute-start | bytes 442376 | tf_op jit(solution)/shard_map/ppermute | solution.py:73
  112.4 4.3 %collective-permute-done.8 = bf16[2,8,24,384]{3,2,1,0:T(8,128)(2,1)S(1)} collective-permute-done((bf16[2,8,24,384]{3,2,1,0:T(8,128)(2,1)S(1)}, bf16[2,8,24,384]{3,2,1,0:T(8,128)(2,1)S(1)}, u32[]{:S(2)}, u32[]{:S(2)}) %collective-permute-start.8) | collective-permute-done | bytes 294944 | tf_op jit(solution)/shard_map/ppermute | solution.py:73
  116.8 2.1 %collective-permute-start.9 = (bf16[1,8,24,384]{3,2,1,0:T(8,128)(2,1)S(1)}, bf16[1,8,24,384]{3,2,1,0:T(8,128)(2,1)S(1)}, u32[]{:S(2)}, u32[]{:S(2)}) collective-permute-start(bf16[1,8,24,384]{3,2,1,0:T(8,128)(2,1)S(1)} %fusion.4), channel_id=1, source_target_pairs={{0,3},{1,2},{2,1},{3,0},{4,5},{5,4},{6,7},{7,6},{8,11},{9,10},{10,... | collective-permute-start | bytes 442376 | tf_op jit(solution)/shard_map/ppermute | solution.py:73
  118.9 4.3 %collective-permute-done.9 = bf16[1,8,24,384]{3,2,1,0:T(8,128)(2,1)S(1)} collective-permute-done((bf16[1,8,24,384]{3,2,1,0:T(8,128)(2,1)S(1)}, bf16[1,8,24,384]{3,2,1,0:T(8,128)(2,1)S(1)}, u32[]{:S(2)}, u32[]{:S(2)}) %collective-permute-start.9) | collective-permute-done | bytes 147488 | tf_op jit(solution)/shard_map/ppermute | solution.py:73
  123.3 0.9 collective-permute-start.10
  124.3 4.4 %collective-permute-done.10 = bf16[4,2,24,384]{3,2,0,1:T(8,128)(2,1)S(1)} collective-permute-done((bf16[4,2,24,384]{3,2,0,1:T(8,128)(2,1)S(1)}, bf16[4,2,24,384]{3,2,0,1:T(8,128)(2,1)S(1)}, u32[]{:S(2)}, u32[]{:S(2)}) %collective-permute-start.10) | collective-permute-done | bytes 147488 | tf_op jit(solution)/shard_map/ppermute | solution.py:73
  128.8 4.3 %collective-permute-done.11 = bf16[2,2,24,384]{3,2,0,1:T(8,128)(2,1)S(1)} collective-permute-done((bf16[2,2,24,384]{3,2,0,1:T(8,128)(2,1)S(1)}, bf16[2,2,24,384]{3,2,0,1:T(8,128)(2,1)S(1)}, u32[]{:S(2)}, u32[]{:S(2)}) %collective-permute-start.11) | collective-permute-done | bytes 73760 | tf_op jit(solution)/shard_map/ppermute | solution.py:73
  133.1 1.3 collective-permute-start.12
  134.4 5.7 %collective-permute-done.12 = bf16[1,2,24,384]{3,2,0,1:T(8,128)(2,1)S(1)} collective-permute-done((bf16[1,2,24,384]{3,2,0,1:T(8,128)(2,1)S(1)}, bf16[1,2,24,384]{3,2,0,1:T(8,128)(2,1)S(1)}, u32[]{:S(2)}, u32[]{:S(2)}) %collective-permute-start.12) | collective-permute-done | bytes 36896 | tf_op jit(solution)/shard_map/ppermute | solution.py:73
  140.2 2.2 %collective-permute-start.13 = (f32[2,24,384]{2,1,0:T(8,128)S(1)}, f32[2,24,384]{2,1,0:T(8,128)S(1)}, u32[]{:S(2)}, u32[]{:S(2)}) collective-permute-start(f32[2,24,384]{2,1,0:T(8,128)S(1)} %fusion.14), channel_id=1, source_target_pairs={{0,3},{1,2},{2,1},{3,0},{4,5},{5,4},{6,7},{7,6},{8,11},{9,10},{10,... | collective-permute-start | bytes 221192 | tf_op jit(solution)/shard_map/ppermute | solution.py:73
  142.4 3.5 %collective-permute-done.13 = f32[2,24,384]{2,1,0:T(8,128)S(1)} collective-permute-done((f32[2,24,384]{2,1,0:T(8,128)S(1)}, f32[2,24,384]{2,1,0:T(8,128)S(1)}, u32[]{:S(2)}, u32[]{:S(2)}) %collective-permute-start.13) | collective-permute-done | bytes 73760 | tf_op jit(solution)/shard_map/ppermute | solution.py:73
  146.0 5.1 %collective-permute-done.14 = f32[2,48,384]{2,1,0:T(8,128)S(1)} collective-permute-done((f32[2,48,384]{2,1,0:T(8,128)S(1)}, f32[2,48,384]{2,1,0:T(8,128)S(1)}, u32[]{:S(2)}, u32[]{:S(2)}) %collective-permute-start.14) | collective-permute-done | bytes 147488 | tf_op jit(solution)/shard_map/ppermute | solution.py:73
  151.1 0.7 fusion.10
  (33 shorter events, 3.4 us)
Async XLA Ops:
  23.0 1.4 copy-start
  26.4 29.9 %copy-start.1 = (s32[256,128]{1,0:T(8,128)S(1)}, s32[256,128]{1,0:T(8,128)}, u32[]{:S(2)}) copy-start(s32[256,128]{1,0:T(8,128)} %get-tuple-element.16.slot_ref) | copy-start | bytes 393220
  26.4 29.9 %copy-start.2 = (bf16[8,768]{1,0:T(8,128)(2,1)S(1)}, bf16[8,768]{1,0:T(8,128)(2,1)}, u32[]{:S(2)}) copy-start(bf16[8,768]{1,0:T(8,128)(2,1)} %question_ref.1) | copy-start | bytes 36868
  26.4 29.9 %copy-start.3 = (f32[8,32]{1,0:T(8,128)S(1)}, f32[8,32]{1,0:T(8,128)}, u32[]{:S(2)}) copy-start(f32[8,32]{1,0:T(8,128)} %reader_ref.1) | copy-start | bytes 3076
  26.4 29.9 %all-to-all-start.1 = ((bf16[64,8,768]{2,1,0:T(8,128)(2,1)}), bf16[64,8,768]{2,1,0:T(8,128)(2,1)S(1)}, u32[]{:S(2)}, u32[]{:S(2)}) async-start(bf16[64,8,768]{2,1,0:T(8,128)(2,1)} %fetch.1), calls=%async_computation.1 | async-start | bytes 1572864 | tf_op jit(solution)/shard_map/all_to_all | solution.py:341
  66.7 7.0 %collective-permute-start = (bf16[16,8,24,384]{3,2,1,0:T(8,128)(2,1)S(1)}, bf16[16,8,24,384]{3,2,1,0:T(8,128)(2,1)S(1)}, u32[]{:S(2)}, u32[]{:S(2)}) collective-permute-start(bf16[16,8,24,384]{3,2,1,0:T(8,128)(2,1)S(1)} %get-tuple-element.19), channel_id=1, source_target_pairs={{0,4},{1,5},{2,6},{3,7},{4,0},{5,1},{6,2},{7,3},{8,12},{9,13},{10,... | collective-permute-start | bytes 7077896 | tf_op jit(solution)/shard_map/ppermute | solution.py:73
  73.1 4.7 %collective-permute-start.5 = (bf16[16,8,24,384]{3,2,1,0:T(8,128)(2,1)S(1)}, bf16[16,8,24,384]{3,2,1,0:T(8,128)(2,1)S(1)}, u32[]{:S(2)}, u32[]{:S(2)}) collective-permute-start(bf16[16,8,24,384]{3,2,1,0:T(8,128)(2,1)S(1)} %get-tuple-element.24), channel_id=1, source_target_pairs={{0,4},{1,5},{2,6},{3,7},{4,0},{5,1},{6,2},{7,3},{8,12},{9,13},{10,... | collective-permute-start | bytes 7077896 | tf_op jit(solution)/shard_map/ppermute | solution.py:73
  74.2 16.3 %collective-permute-start.1 = (bf16[8,8,24,384]{3,2,1,0:T(8,128)(2,1)S(1)}, bf16[8,8,24,384]{3,2,1,0:T(8,128)(2,1)S(1)}, u32[]{:S(2)}, u32[]{:S(2)}) collective-permute-start(bf16[8,8,24,384]{3,2,1,0:T(8,128)(2,1)S(1)} %get-tuple-element.25), channel_id=1, source_target_pairs={{0,1},{1,0},{2,3},{3,2},{4,7},{5,6},{6,5},{7,4},{8,9},{9,8},{10,11... | collective-permute-start | bytes 3538952 | tf_op jit(solution)/shard_map/ppermute | solution.py:73
  78.4 16.3 %collective-permute-start.6 = (bf16[8,8,24,384]{3,2,1,0:T(8,128)(2,1)S(1)}, bf16[8,8,24,384]{3,2,1,0:T(8,128)(2,1)S(1)}, u32[]{:S(2)}, u32[]{:S(2)}) collective-permute-start(bf16[8,8,24,384]{3,2,1,0:T(8,128)(2,1)S(1)} %get-tuple-element.27), channel_id=1, source_target_pairs={{0,8},{1,9},{2,10},{3,11},{4,28},{5,29},{6,30},{7,31},{8,0},{9,1},... | collective-permute-start | bytes 3538952 | tf_op jit(solution)/shard_map/ppermute | solution.py:73
  90.8 11.2 %collective-permute-start.2 = (bf16[4,8,24,384]{3,2,1,0:T(8,128)(2,1)S(1)}, bf16[4,8,24,384]{3,2,1,0:T(8,128)(2,1)S(1)}, u32[]{:S(2)}, u32[]{:S(2)}) collective-permute-start(bf16[4,8,24,384]{3,2,1,0:T(8,128)(2,1)S(1)} %get-tuple-element.29), channel_id=1, source_target_pairs={{0,3},{1,2},{2,1},{3,0},{4,5},{5,4},{6,7},{7,6},{8,11},{9,10},{10,... | collective-permute-start | bytes 1769480 | tf_op jit(solution)/shard_map/ppermute | solution.py:73
  95.0 13.2 %collective-permute-start.7 = (bf16[4,8,24,384]{3,2,1,0:T(8,128)(2,1)S(1)}, bf16[4,8,24,384]{3,2,1,0:T(8,128)(2,1)S(1)}, u32[]{:S(2)}, u32[]{:S(2)}) collective-permute-start(bf16[4,8,24,384]{3,2,1,0:T(8,128)(2,1)S(1)} %get-tuple-element.31), channel_id=1, source_target_pairs={{0,24},{1,25},{2,26},{3,27},{4,12},{5,13},{6,14},{7,15},{8,16},{9,... | collective-permute-start | bytes 1769480 | tf_op jit(solution)/shard_map/ppermute | solution.py:73
  102.2 8.7 %collective-permute-start.3 = (bf16[2,8,24,384]{3,2,1,0:T(8,128)(2,1)S(1)}, bf16[2,8,24,384]{3,2,1,0:T(8,128)(2,1)S(1)}, u32[]{:S(2)}, u32[]{:S(2)}) collective-permute-start(bf16[2,8,24,384]{3,2,1,0:T(8,128)(2,1)S(1)} %get-tuple-element.33), channel_id=1, source_target_pairs={{0,8},{1,9},{2,10},{3,11},{4,28},{5,29},{6,30},{7,31},{8,0},{9,1},... | collective-permute-start | bytes 884744 | tf_op jit(solution)/shard_map/ppermute | solution.py:73
  108.3 8.4 %collective-permute-start.8 = (bf16[2,8,24,384]{3,2,1,0:T(8,128)(2,1)S(1)}, bf16[2,8,24,384]{3,2,1,0:T(8,128)(2,1)S(1)}, u32[]{:S(2)}, u32[]{:S(2)}) collective-permute-start(bf16[2,8,24,384]{3,2,1,0:T(8,128)(2,1)S(1)} %get-tuple-element.35), channel_id=1, source_target_pairs={{0,1},{1,0},{2,3},{3,2},{4,7},{5,6},{6,5},{7,4},{8,9},{9,8},{10,11... | collective-permute-start | bytes 884744 | tf_op jit(solution)/shard_map/ppermute | solution.py:73
  110.9 8.0 %collective-permute-start.4 = (bf16[1,8,24,384]{3,2,1,0:T(8,128)(2,1)S(1)}, bf16[1,8,24,384]{3,2,1,0:T(8,128)(2,1)S(1)}, u32[]{:S(2)}, u32[]{:S(2)}) collective-permute-start(bf16[1,8,24,384]{3,2,1,0:T(8,128)(2,1)S(1)} %fusion.6), channel_id=1, source_target_pairs={{0,24},{1,25},{2,26},{3,27},{4,12},{5,13},{6,14},{7,15},{8,16},{9,... | collective-permute-start | bytes 442376 | tf_op jit(solution)/shard_map/ppermute | solution.py:73
  116.8 6.4 %collective-permute-start.9 = (bf16[1,8,24,384]{3,2,1,0:T(8,128)(2,1)S(1)}, bf16[1,8,24,384]{3,2,1,0:T(8,128)(2,1)S(1)}, u32[]{:S(2)}, u32[]{:S(2)}) collective-permute-start(bf16[1,8,24,384]{3,2,1,0:T(8,128)(2,1)S(1)} %fusion.4), channel_id=1, source_target_pairs={{0,3},{1,2},{2,1},{3,0},{4,5},{5,4},{6,7},{7,6},{8,11},{9,10},{10,... | collective-permute-start | bytes 442376 | tf_op jit(solution)/shard_map/ppermute | solution.py:73
  123.3 5.3 %collective-permute-start.10 = (bf16[4,2,24,384]{3,2,0,1:T(8,128)(2,1)S(1)}, bf16[4,2,24,384]{3,2,0,1:T(8,128)(2,1)S(1)}, u32[]{:S(2)}, u32[]{:S(2)}) collective-permute-start(bf16[4,2,24,384]{3,2,0,1:T(8,128)(2,1)S(1)} %slice.288), channel_id=1, source_target_pairs={{0,32},{1,33},{2,34},{3,35},{4,228},{5,229},{6,230},{7,231},{8,40}... | collective-permute-start | bytes 442376 | tf_op jit(solution)/shard_map/ppermute | solution.py:73
  128.7 4.4 %collective-permute-start.11 = (bf16[2,2,24,384]{3,2,0,1:T(8,128)(2,1)S(1)}, bf16[2,2,24,384]{3,2,0,1:T(8,128)(2,1)S(1)}, u32[]{:S(2)}, u32[]{:S(2)}) collective-permute-start(bf16[2,2,24,384]{3,2,0,1:T(8,128)(2,1)S(1)} %get-tuple-element.37), channel_id=1, source_target_pairs={{0,96},{1,97},{2,98},{3,99},{4,164},{5,165},{6,166},{7,167},{8,104... | collective-permute-start | bytes 221192 | tf_op jit(solution)/shard_map/ppermute | solution.py:73
  133.1 7.1 %collective-permute-start.12 = (bf16[1,2,24,384]{3,2,0,1:T(8,128)(2,1)S(1)}, bf16[1,2,24,384]{3,2,0,1:T(8,128)(2,1)S(1)}, u32[]{:S(2)}, u32[]{:S(2)}) collective-permute-start(bf16[1,2,24,384]{3,2,0,1:T(8,128)(2,1)S(1)} %fusion.12), channel_id=1, source_target_pairs={{0,224},{1,225},{2,226},{3,227},{4,36},{5,37},{6,38},{7,39},{8,232... | collective-permute-start | bytes 110600 | tf_op jit(solution)/shard_map/ppermute | solution.py:73
  140.2 5.7 %collective-permute-start.13 = (f32[2,24,384]{2,1,0:T(8,128)S(1)}, f32[2,24,384]{2,1,0:T(8,128)S(1)}, u32[]{:S(2)}, u32[]{:S(2)}) collective-permute-start(f32[2,24,384]{2,1,0:T(8,128)S(1)} %fusion.14), channel_id=1, source_target_pairs={{0,3},{1,2},{2,1},{3,0},{4,5},{5,4},{6,7},{7,6},{8,11},{9,10},{10,... | collective-permute-start | bytes 221192 | tf_op jit(solution)/shard_map/ppermute | solution.py:73
  145.9 5.2 %collective-permute-start.14 = (f32[2,48,384]{2,1,0:T(8,128)S(1)}, f32[2,48,384]{2,1,0:T(8,128)S(1)}, u32[]{:S(2)}, u32[]{:S(2)}) collective-permute-start(f32[2,48,384]{2,1,0:T(8,128)S(1)} %pad_maximum_fusion.1), channel_id=1, source_target_pairs={{0,1},{1,0},{2,3},{3,2},{4,7},{5,6},{6,5},{7,4},{8,9},{9,8},{10,11... | collective-permute-start | bytes 442376 | tf_op jit(solution)/shard_map/ppermute | solution.py:73

commit v3 on v2

--- a/solution.py
+++ b/solution.py
@@ -44,8 +44,9 @@
 
 
 def label8(v, core):
-    g = gray((v - core) & 7)
-    return ((g & 1) << 2) | (g & 2) | (g >> 2)
+    v = (v - core) & 7
+    top = v >> 2
+    return (((v & 1) ^ top) << 2) | ((((v >> 1) & 1) ^ top) << 1) | top
 
 
 def partner(step):
@@ -238,7 +239,7 @@
         out_shape=(
             jax.ShapeDtypeStruct((shards, 1, 128), i32),
             jax.ShapeDtypeStruct((Q * K, 128), i32),
-            jax.ShapeDtypeStruct(index_states.shape, index_states.dtype),
+            pltpu.VMEM(index_states.shape, index_states.dtype),
         ),
         scratch_shapes=[pltpu.SemaphoreType.DMA],
         name="route",
@@ -252,7 +253,7 @@
         out_shape=jax.ShapeDtypeStruct((shards, CAP, width), bf16),
         compiler_params=pltpu.CompilerParams(vmem_limit_bytes=32 << 20),
         name="fetch",
-    )(rows_in, index_states)
+    )(rows_in, pltpu.with_memory_space_constraint(index_states, pltpu.VMEM))
 
 
 def forward(place, got, slot, questions, reader, w_up, w_down):
@@ -328,6 +329,16 @@
     return keep.astype(f32) + swap(send, step).astype(f32)
 
 
+def sum_plane(keep, send, steps):
+    ahead, rest = swap(send[4:], steps[0]), swap(send[:4], steps[0])
+    send = (keep[4:].astype(f32) + ahead.astype(f32)).astype(bf16)
+    keep = keep[:4].astype(f32) + rest.astype(f32)
+    ahead, rest = swap(send[2:], steps[1]), swap(send[:2], steps[1])
+    came = swap((keep[2:] + ahead.astype(f32)).astype(bf16), steps[2])
+    keep = keep[:2] + rest.astype(f32) + came.astype(f32)
+    return keep[:1] + swap(keep[1:].astype(bf16), steps[3]).astype(f32)
+
+
 def on_device(index_states, questions, reader, owners, passage_rows, w_up, w_down):
     shards = lax.axis_size("shard")
     width = questions.shape[1]
@@ -344,12 +355,9 @@
     )
     keep_up, send_up = backward(place, grad_emb, states, slope, w_down)
 
-    down, up = (keep_down, send_down), (keep_up, send_up)
-    for step in ("c", "x1", "x2", "y1"):
-        down = meet(*down, step)
-    for step in ("c", "y1", "y2", "x1"):
-        up = meet(*up, step)
-    both = jnp.concatenate([total(*down, "y2"), total(*up, "x2")])
+    down = sum_plane(*meet(keep_down, send_down, "c"), ("x1", "x2", "y1", "y2"))
+    up = sum_plane(*meet(keep_up, send_up, "c"), ("y1", "y2", "x1", "x2"))
+    both = jnp.concatenate([down, up])
     both = both.reshape(2, NZ, HALF_R, HALF_C).swapaxes(0, 1)
     keep, send = halves(both)
     send = send.astype(bf16)

time: 153 us -> 148 us (0.967)
  waiting for transfers between devices: 80.6 us -> 70.7 us
  starting transfers between devices: 25.1 us -> 32.7 us
    ppermute x15 -> x19, waiting for transfers between devices: 57.3 us -> 47.4 us  [swap(): return lax.ppermute(array, AXES, partner(step))]
    ppermute x15 -> x19, starting transfers between devices: 18.6 us -> 26.1 us  [swap(): return lax.ppermute(array, AXES, partner(step))]
  transfers between devices with their start and end apart: 16 -> 20, of which waited for: 13 -> 13; matrix products, arithmetic and copies ran while one was open for 1% -> 2% of each run, Pallas kernels for 4% -> 4%
where the time goes in v3:
time: 148 us
  waiting for transfers between devices  70.7 us (48%)
  starting transfers between devices  32.7 us (22%)
  Pallas kernels  21.2 us (14%)
  blocking collectives  19 us (13%)
  other arithmetic  3.08 us (2%)
    ppermute x19, waiting for transfers between devices, swap(): return lax.ppermute(array, AXES, partner(step))  47.4 us
    ppermute x19, starting transfers between devices, swap(): return lax.ppermute(array, AXES, partner(step))  26.1 us
    all_to_all x1, waiting for transfers between devices, on_device(): lax.all_to_all(states_out, 'shard', split_axis=0, concat_axis=0, tiled=True)  23.2 us
    all_to_all x1, blocking collectives, on_device(): lax.all_to_all(send_rows, 'shard', split_axis=0, concat_axis=0, tiled=True)  19 us
    pallas_call x1, Pallas kernels, forward(): pl.pallas_call(forward_kernel, in_specs=[SMEM, VMEM, VMEM, VMEM, VMEM, HB...  10.3 us
    all_to_all x1, starting transfers between devices, on_device(): lax.all_to_all(states_out, 'shard', split_axis=0, concat_axis=0, tiled=True)  6.57 us
    pallas_call x1, Pallas kernels, backward(): pl.pallas_call(backward_kernel, in_specs=[SMEM, VMEM, VMEM, VMEM, HBM], o...  6.1 us
  transfers between devices with their start and end apart: 20, of which 13 were waited for; matrix products, arithmetic and copies ran while one was open for 2% of the time, Pallas kernels for 4%

profile of v3, /device:TPU:64, one launch (start us, length us, event | category | flops | bytes accessed | tf_op | source)
XLA Modules:
  0.0 147.9 jit_solution(14634955559674727211)
XLA Ops:
  0.6 2.8 %route.1 = (s32[64,1,128]{2,1,0:T(1,128)}, s32[256,128]{1,0:T(8,128)}, bf16[1024,768]{1,0:T(8,128)(2,1)S(1)}) custom-call(s32[8,32]{1,0:T(8,128)} %bitcast.15, s32[8,32]{1,0:T(8,128)} %row_ref.1, bf16[1024,768]{1,0:T(8,128)(2,1)} %index_hbm.1), custom_call_target="tpu_custom_call" | custom-call | tf_op jit(solution)/shard_map/route/pallas_call | solution.py:235
  3.4 19.0 %all_to_all.10.rows_ref = s32[64,1,128]{2,1,0:T(1,128)S(1)} all-to-all(s32[64,1,128]{2,1,0:T(1,128)} %get-tuple-element.14), channel_id=1, replica_groups=mesh['shard'=64,'rep'=4] {'shard'}, dimensions={0} | all-to-all | bytes 65536 | tf_op jit(solution)/shard_map/all_to_all | solution.py:350
  22.5 1.9 %fetch.1 = bf16[64,8,768]{2,1,0:T(8,128)(2,1)} custom-call(s32[64,1,128]{2,1,0:T(1,128)S(1)} %all_to_all.10.rows_ref, bf16[1024,768]{1,0:T(8,128)(2,1)S(1)} %get-tuple-element.15.index_ref), custom_call_target="tpu_custom_call" | custom-call | tf_op jit(solution)/shard_map/fetch/pallas_call | solution.py:251
  24.4 6.6 %all-to-all-start.1 = ((bf16[64,8,768]{2,1,0:T(8,128)(2,1)}), bf16[64,8,768]{2,1,0:T(8,128)(2,1)S(1)}, u32[]{:S(2)}, u32[]{:S(2)}) async-start(bf16[64,8,768]{2,1,0:T(8,128)(2,1)} %fetch.1), calls=%async_computation.1 | async-start | bytes 1572864 | tf_op jit(solution)/shard_map/all_to_all | solution.py:352
  31.1 23.2 %all-to-all-done.1 = bf16[64,8,768]{2,1,0:T(8,128)(2,1)S(1)} async-done(((bf16[64,8,768]{2,1,0:T(8,128)(2,1)}), bf16[64,8,768]{2,1,0:T(8,128)(2,1)S(1)}, u32[]{:S(2)}, u32[]{:S(2)}) %all-to-all-start.1) | async-done | bytes 786464 | tf_op jit(solution)/shard_map/all_to_all | solution.py:352
  54.3 10.3 %forward.1 = (f32[8,32]{1,0:T(8,128)}, bf16[256,768]{1,0:T(8,128)(2,1)S(1)}, bf16[256,768]{1,0:T(8,128)(2,1)S(1)}, f32[256,3072]{1,0:T(8,128)S(1)}, bf16[16,8,24...) custom-call(s32[4]{0:T(128)S(1)} %pad_add_fusion.place_ref, bf16[512,768]{1,0:T(8,128)(2,1)S(1)} %bitcast.14, ...), custom_call_target="tpu_custom_call" | custom-call | flops 3623878656 | bytes 25165824 | tf_op jit(solution)/shard_map/forward/pallas_call | solution.py:263
  64.9 6.1 %backward.1 = (bf16[16,8,24,384]{3,2,1,0:T(8,128)(2,1)S(1)}, bf16[16,8,24,384]{3,2,1,0:T(8,128)(2,1)S(1)}) custom-call(s32[4]{0:T(128)S(1)} %pad_add_fusion.place_ref, bf16[256,768]{1,0:T(8,128)(2,1)S(1)} %get-tuple-element.20.grad_emb_ref, bf16[256,768]{1,0:T(8,128)(2,1)S(1)} %get-tuple-element.21.states_ref, f32[256,3072]{1,0:T(8,128)S(1)} %get-tuple-element.22.slope_ref, ...), custom_call_target="tpu_custom_call" | custom-call | flops 2415919104 | bytes 16777216 | tf_op jit(solution)/shard_map/backward/pallas_call | solution.py:294
  72.4 1.6 %collective-permute-start.2 = (bf16[4,8,24,384]{3,2,1,0:T(8,128)(2,1)S(1)}, bf16[4,8,24,384]{3,2,1,0:T(8,128)(2,1)S(1)}, u32[]{:S(2)}, u32[]{:S(2)}) collective-permute-start(bf16[4,8,24,384]{3,2,1,0:T(8,128)(2,1)S(1)} %get-tuple-element.33), channel_id=1, source_target_pairs={{0,1},{1,0},{2,3},{3,2},{4,7},{5,6},{6,5},{7,4},{8,9},{9,8},{10,11... | collective-permute-start | bytes 1769480 | tf_op jit(solution)/shard_map/ppermute | solution.py:74
  74.5 1.3 collective-permute-done.7
  77.1 1.6 %collective-permute-start.8 = (bf16[4,8,24,384]{3,2,1,0:T(8,128)(2,1)S(1)}, bf16[4,8,24,384]{3,2,1,0:T(8,128)(2,1)S(1)}, u32[]{:S(2)}, u32[]{:S(2)}) collective-permute-start(bf16[4,8,24,384]{3,2,1,0:T(8,128)(2,1)S(1)} %get-tuple-element.36), channel_id=1, source_target_pairs={{0,8},{1,9},{2,10},{3,11},{4,28},{5,29},{6,30},{7,31},{8,0},{9,1},... | collective-permute-start | bytes 1769480 | tf_op jit(solution)/shard_map/ppermute | solution.py:74
  78.6 3.7 %collective-permute-done.2 = bf16[4,8,24,384]{3,2,1,0:T(8,128)(2,1)S(1)} collective-permute-done((bf16[4,8,24,384]{3,2,1,0:T(8,128)(2,1)S(1)}, bf16[4,8,24,384]{3,2,1,0:T(8,128)(2,1)S(1)}, u32[]{:S(2)}, u32[]{:S(2)}) %collective-permute-start.2) | collective-permute-done | bytes 589856 | tf_op jit(solution)/shard_map/ppermute | solution.py:74
  82.3 6.3 %collective-permute-done.1 = bf16[4,8,24,384]{3,2,1,0:T(8,128)(2,1)S(1)} collective-permute-done((bf16[4,8,24,384]{3,2,1,0:T(8,128)(2,1)S(1)}, bf16[4,8,24,384]{3,2,1,0:T(8,128)(2,1)S(1)}, u32[]{:S(2)}, u32[]{:S(2)}) %collective-permute-start.1) | collective-permute-done | bytes 589856 | tf_op jit(solution)/shard_map/ppermute | solution.py:74
  89.0 2.9 %collective-permute-start.4 = (bf16[2,8,24,384]{3,2,1,0:T(8,128)(2,1)S(1)}, bf16[2,8,24,384]{3,2,1,0:T(8,128)(2,1)S(1)}, u32[]{:S(2)}, u32[]{:S(2)}) collective-permute-start(bf16[2,8,24,384]{3,2,1,0:T(8,128)(2,1)S(1)} %get-tuple-element.40), channel_id=1, source_target_pairs={{0,3},{1,2},{2,1},{3,0},{4,5},{5,4},{6,7},{7,6},{8,11},{9,10},{10,... | collective-permute-start | bytes 884744 | tf_op jit(solution)/shard_map/ppermute | solution.py:74
  91.9 1.0 collective-permute-done.8
  93.2 1.5 %collective-permute-start.11 = (bf16[2,8,24,384]{3,2,1,0:T(8,128)(2,1)S(1)}, bf16[2,8,24,384]{3,2,1,0:T(8,128)(2,1)S(1)}, u32[]{:S(2)}, u32[]{:S(2)}) collective-permute-start(bf16[2,8,24,384]{3,2,1,0:T(8,128)(2,1)S(1)} %get-tuple-element.42), channel_id=1, source_target_pairs={{0,24},{1,25},{2,26},{3,27},{4,12},{5,13},{6,14},{7,15},{8,16},{9,... | collective-permute-start | bytes 884744 | tf_op jit(solution)/shard_map/ppermute | solution.py:74
  94.7 2.8 %collective-permute-start.3 = (bf16[2,8,24,384]{3,2,1,0:T(8,128)(2,1)S(1)}, bf16[2,8,24,384]{3,2,1,0:T(8,128)(2,1)S(1)}, u32[]{:S(2)}, u32[]{:S(2)}) collective-permute-start(bf16[2,8,24,384]{3,2,1,0:T(8,128)(2,1)S(1)} %get-tuple-element.39), channel_id=1, source_target_pairs={{0,3},{1,2},{2,1},{3,0},{4,5},{5,4},{6,7},{7,6},{8,11},{9,10},{10,... | collective-permute-start | bytes 884744 | tf_op jit(solution)/shard_map/ppermute | solution.py:74
  97.7 1.9 %collective-permute-start.10 = (bf16[2,8,24,384]{3,2,1,0:T(8,128)(2,1)S(1)}, bf16[2,8,24,384]{3,2,1,0:T(8,128)(2,1)S(1)}, u32[]{:S(2)}, u32[]{:S(2)}) collective-permute-start(bf16[2,8,24,384]{3,2,1,0:T(8,128)(2,1)S(1)} %get-tuple-element.41), channel_id=1, source_target_pairs={{0,24},{1,25},{2,26},{3,27},{4,12},{5,13},{6,14},{7,15},{8,16},{9,... | collective-permute-start | bytes 884744 | tf_op jit(solution)/shard_map/ppermute | solution.py:74
  99.5 3.9 %collective-permute-done.11 = bf16[2,8,24,384]{3,2,1,0:T(8,128)(2,1)S(1)} collective-permute-done((bf16[2,8,24,384]{3,2,1,0:T(8,128)(2,1)S(1)}, bf16[2,8,24,384]{3,2,1,0:T(8,128)(2,1)S(1)}, u32[]{:S(2)}, u32[]{:S(2)}) %collective-permute-start.11) | collective-permute-done | bytes 294944 | tf_op jit(solution)/shard_map/ppermute | solution.py:74
  103.5 2.5 %collective-permute-start.12 = (bf16[2,8,24,384]{3,2,1,0:T(8,128)(2,1)S(1)}, bf16[2,8,24,384]{3,2,1,0:T(8,128)(2,1)S(1)}, u32[]{:S(2)}, u32[]{:S(2)}) collective-permute-start(bf16[2,8,24,384]{3,2,1,0:T(8,128)(2,1)S(1)} %fusion.2), channel_id=1, source_target_pairs={{0,1},{1,0},{2,3},{3,2},{4,7},{5,6},{6,5},{7,4},{8,9},{9,8},{10,11... | collective-permute-start | bytes 884744 | tf_op jit(solution)/shard_map/ppermute | solution.py:74
  106.1 1.8 %collective-permute-start.6 = (bf16[1,8,24,384]{3,2,1,0:T(8,128)(2,1)S(1)}, bf16[1,8,24,384]{3,2,1,0:T(8,128)(2,1)S(1)}, u32[]{:S(2)}, u32[]{:S(2)}) collective-permute-start(bf16[1,8,24,384]{3,2,1,0:T(8,128)(2,1)S(1)} %slice.256), channel_id=1, source_target_pairs={{0,24},{1,25},{2,26},{3,27},{4,12},{5,13},{6,14},{7,15},{8,16},{9,... | collective-permute-start | bytes 442376 | tf_op jit(solution)/shard_map/ppermute | solution.py:74
  107.9 3.9 %collective-permute-done.12 = bf16[2,8,24,384]{3,2,1,0:T(8,128)(2,1)S(1)} collective-permute-done((bf16[2,8,24,384]{3,2,1,0:T(8,128)(2,1)S(1)}, bf16[2,8,24,384]{3,2,1,0:T(8,128)(2,1)S(1)}, u32[]{:S(2)}, u32[]{:S(2)}) %collective-permute-start.12) | collective-permute-done | bytes 294944 | tf_op jit(solution)/shard_map/ppermute | solution.py:74
  111.9 2.0 %collective-permute-start.13 = (bf16[1,8,24,384]{3,2,1,0:T(8,128)(2,1)S(1)}, bf16[1,8,24,384]{3,2,1,0:T(8,128)(2,1)S(1)}, u32[]{:S(2)}, u32[]{:S(2)}) collective-permute-start(bf16[1,8,24,384]{3,2,1,0:T(8,128)(2,1)S(1)} %slice.255), channel_id=1, source_target_pairs={{0,3},{1,2},{2,1},{3,0},{4,5},{5,4},{6,7},{7,6},{8,11},{9,10},{10,... | collective-permute-start | bytes 442376 | tf_op jit(solution)/shard_map/ppermute | solution.py:74
  113.9 4.4 %collective-permute-done.13 = bf16[1,8,24,384]{3,2,1,0:T(8,128)(2,1)S(1)} collective-permute-done((bf16[1,8,24,384]{3,2,1,0:T(8,128)(2,1)S(1)}, bf16[1,8,24,384]{3,2,1,0:T(8,128)(2,1)S(1)}, u32[]{:S(2)}, u32[]{:S(2)}) %collective-permute-start.13) | collective-permute-done | bytes 147488 | tf_op jit(solution)/shard_map/ppermute | solution.py:74
  118.5 0.9 collective-permute-start.14
  119.4 4.3 %collective-permute-done.14 = bf16[4,2,24,384]{3,2,0,1:T(8,128)(2,1)S(1)} collective-permute-done((bf16[4,2,24,384]{3,2,0,1:T(8,128)(2,1)S(1)}, bf16[4,2,24,384]{3,2,0,1:T(8,128)(2,1)S(1)}, u32[]{:S(2)}, u32[]{:S(2)}) %collective-permute-start.14) | collective-permute-done | bytes 147488 | tf_op jit(solution)/shard_map/ppermute | solution.py:74
  124.1 5.0 %collective-permute-done.15 = bf16[2,2,24,384]{3,2,0,1:T(8,128)(2,1)S(1)} collective-permute-done((bf16[2,2,24,384]{3,2,0,1:T(8,128)(2,1)S(1)}, bf16[2,2,24,384]{3,2,0,1:T(8,128)(2,1)S(1)}, u32[]{:S(2)}, u32[]{:S(2)}) %collective-permute-start.15) | collective-permute-done | bytes 73760 | tf_op jit(solution)/shard_map/ppermute | solution.py:74
  129.1 1.5 %collective-permute-start.16 = (bf16[1,2,24,384]{3,2,0,1:T(8,128)(2,1)S(1)}, bf16[1,2,24,384]{3,2,0,1:T(8,128)(2,1)S(1)}, u32[]{:S(2)}, u32[]{:S(2)}) collective-permute-start(bf16[1,2,24,384]{3,2,0,1:T(8,128)(2,1)S(1)} %fusion.10), channel_id=1, source_target_pairs={{0,224},{1,225},{2,226},{3,227},{4,36},{5,37},{6,38},{7,39},{8,232... | collective-permute-start | bytes 110600 | tf_op jit(solution)/shard_map/ppermute | solution.py:74
  130.6 5.6 %collective-permute-done.16 = bf16[1,2,24,384]{3,2,0,1:T(8,128)(2,1)S(1)} collective-permute-done((bf16[1,2,24,384]{3,2,0,1:T(8,128)(2,1)S(1)}, bf16[1,2,24,384]{3,2,0,1:T(8,128)(2,1)S(1)}, u32[]{:S(2)}, u32[]{:S(2)}) %collective-permute-start.16) | collective-permute-done | bytes 36896 | tf_op jit(solution)/shard_map/ppermute | solution.py:74
  136.2 2.7 %collective-permute-start.17 = (f32[2,24,384]{2,1,0:T(8,128)S(1)}, f32[2,24,384]{2,1,0:T(8,128)S(1)}, u32[]{:S(2)}, u32[]{:S(2)}) collective-permute-start(f32[2,24,384]{2,1,0:T(8,128)S(1)} %fusion.12), channel_id=1, source_target_pairs={{0,3},{1,2},{2,1},{3,0},{4,5},{5,4},{6,7},{7,6},{8,11},{9,10},{10,... | collective-permute-start | bytes 221192 | tf_op jit(solution)/shard_map/ppermute | solution.py:74
  138.9 2.9 %collective-permute-done.17 = f32[2,24,384]{2,1,0:T(8,128)S(1)} collective-permute-done((f32[2,24,384]{2,1,0:T(8,128)S(1)}, f32[2,24,384]{2,1,0:T(8,128)S(1)}, u32[]{:S(2)}, u32[]{:S(2)}) %collective-permute-start.17) | collective-permute-done | bytes 73760 | tf_op jit(solution)/shard_map/ppermute | solution.py:74
  142.1 5.1 %collective-permute-done.18 = f32[2,48,384]{2,1,0:T(8,128)S(1)} collective-permute-done((f32[2,48,384]{2,1,0:T(8,128)S(1)}, f32[2,48,384]{2,1,0:T(8,128)S(1)}, u32[]{:S(2)}, u32[]{:S(2)}) %collective-permute-start.18) | collective-permute-done | bytes 147488 | tf_op jit(solution)/shard_map/ppermute | solution.py:74
  147.2 0.7 fusion.8
  (45 shorter events, 5.4 us)
Async XLA Ops:
  24.4 29.9 %copy-start = (s32[256,128]{1,0:T(8,128)S(1)}, s32[256,128]{1,0:T(8,128)}, u32[]{:S(2)}) copy-start(s32[256,128]{1,0:T(8,128)} %get-tuple-element.16.slot_ref) | copy-start | bytes 393220
  24.4 29.9 %copy-start.1 = (bf16[8,768]{1,0:T(8,128)(2,1)S(1)}, bf16[8,768]{1,0:T(8,128)(2,1)}, u32[]{:S(2)}) copy-start(bf16[8,768]{1,0:T(8,128)(2,1)} %question_ref.1) | copy-start | bytes 36868
  24.4 29.9 %copy-start.2 = (f32[8,32]{1,0:T(8,128)S(1)}, f32[8,32]{1,0:T(8,128)}, u32[]{:S(2)}) copy-start(f32[8,32]{1,0:T(8,128)} %reader_ref.1) | copy-start | bytes 3076
  24.4 29.9 %all-to-all-start.1 = ((bf16[64,8,768]{2,1,0:T(8,128)(2,1)}), bf16[64,8,768]{2,1,0:T(8,128)(2,1)S(1)}, u32[]{:S(2)}, u32[]{:S(2)}) async-start(bf16[64,8,768]{2,1,0:T(8,128)(2,1)} %fetch.1), calls=%async_computation.1 | async-start | bytes 1572864 | tf_op jit(solution)/shard_map/all_to_all | solution.py:352
  64.7 7.0 %collective-permute-start = (bf16[16,8,24,384]{3,2,1,0:T(8,128)(2,1)S(1)}, bf16[16,8,24,384]{3,2,1,0:T(8,128)(2,1)S(1)}, u32[]{:S(2)}, u32[]{:S(2)}) collective-permute-start(bf16[16,8,24,384]{3,2,1,0:T(8,128)(2,1)S(1)} %get-tuple-element.19), channel_id=1, source_target_pairs={{0,4},{1,5},{2,6},{3,7},{4,0},{5,1},{6,2},{7,3},{8,12},{9,13},{10,... | collective-permute-start | bytes 7077896 | tf_op jit(solution)/shard_map/ppermute | solution.py:74
  71.1 4.7 %collective-permute-start.7 = (bf16[16,8,24,384]{3,2,1,0:T(8,128)(2,1)S(1)}, bf16[16,8,24,384]{3,2,1,0:T(8,128)(2,1)S(1)}, u32[]{:S(2)}, u32[]{:S(2)}) collective-permute-start(bf16[16,8,24,384]{3,2,1,0:T(8,128)(2,1)S(1)} %get-tuple-element.24), channel_id=1, source_target_pairs={{0,4},{1,5},{2,6},{3,7},{4,0},{5,1},{6,2},{7,3},{8,12},{9,13},{10,... | collective-permute-start | bytes 7077896 | tf_op jit(solution)/shard_map/ppermute | solution.py:74
  72.4 10.0 %collective-permute-start.2 = (bf16[4,8,24,384]{3,2,1,0:T(8,128)(2,1)S(1)}, bf16[4,8,24,384]{3,2,1,0:T(8,128)(2,1)S(1)}, u32[]{:S(2)}, u32[]{:S(2)}) collective-permute-start(bf16[4,8,24,384]{3,2,1,0:T(8,128)(2,1)S(1)} %get-tuple-element.33), channel_id=1, source_target_pairs={{0,1},{1,0},{2,3},{3,2},{4,7},{5,6},{6,5},{7,4},{8,9},{9,8},{10,11... | collective-permute-start | bytes 1769480 | tf_op jit(solution)/shard_map/ppermute | solution.py:74
  73.9 14.7 %collective-permute-start.1 = (bf16[4,8,24,384]{3,2,1,0:T(8,128)(2,1)S(1)}, bf16[4,8,24,384]{3,2,1,0:T(8,128)(2,1)S(1)}, u32[]{:S(2)}, u32[]{:S(2)}) collective-permute-start(bf16[4,8,24,384]{3,2,1,0:T(8,128)(2,1)S(1)} %get-tuple-element.34), channel_id=1, source_target_pairs={{0,1},{1,0},{2,3},{3,2},{4,7},{5,6},{6,5},{7,4},{8,9},{9,8},{10,11... | collective-permute-start | bytes 1769480 | tf_op jit(solution)/shard_map/ppermute | solution.py:74
  76.5 15.3 %collective-permute-start.9 = (bf16[4,8,24,384]{3,2,1,0:T(8,128)(2,1)S(1)}, bf16[4,8,24,384]{3,2,1,0:T(8,128)(2,1)S(1)}, u32[]{:S(2)}, u32[]{:S(2)}) collective-permute-start(bf16[4,8,24,384]{3,2,1,0:T(8,128)(2,1)S(1)} %get-tuple-element.35), channel_id=1, source_target_pairs={{0,8},{1,9},{2,10},{3,11},{4,28},{5,29},{6,30},{7,31},{8,0},{9,1},... | collective-permute-start | bytes 1769480 | tf_op jit(solution)/shard_map/ppermute | solution.py:74
  77.1 15.7 %collective-permute-start.8 = (bf16[4,8,24,384]{3,2,1,0:T(8,128)(2,1)S(1)}, bf16[4,8,24,384]{3,2,1,0:T(8,128)(2,1)S(1)}, u32[]{:S(2)}, u32[]{:S(2)}) collective-permute-start(bf16[4,8,24,384]{3,2,1,0:T(8,128)(2,1)S(1)} %get-tuple-element.36), channel_id=1, source_target_pairs={{0,8},{1,9},{2,10},{3,11},{4,28},{5,29},{6,30},{7,31},{8,0},{9,1},... | collective-permute-start | bytes 1769480 | tf_op jit(solution)/shard_map/ppermute | solution.py:74
  89.0 8.5 %collective-permute-start.4 = (bf16[2,8,24,384]{3,2,1,0:T(8,128)(2,1)S(1)}, bf16[2,8,24,384]{3,2,1,0:T(8,128)(2,1)S(1)}, u32[]{:S(2)}, u32[]{:S(2)}) collective-permute-start(bf16[2,8,24,384]{3,2,1,0:T(8,128)(2,1)S(1)} %get-tuple-element.40), channel_id=1, source_target_pairs={{0,3},{1,2},{2,1},{3,0},{4,5},{5,4},{6,7},{7,6},{8,11},{9,10},{10,... | collective-permute-start | bytes 884744 | tf_op jit(solution)/shard_map/ppermute | solution.py:74
  93.2 10.2 %collective-permute-start.11 = (bf16[2,8,24,384]{3,2,1,0:T(8,128)(2,1)S(1)}, bf16[2,8,24,384]{3,2,1,0:T(8,128)(2,1)S(1)}, u32[]{:S(2)}, u32[]{:S(2)}) collective-permute-start(bf16[2,8,24,384]{3,2,1,0:T(8,128)(2,1)S(1)} %get-tuple-element.42), channel_id=1, source_target_pairs={{0,24},{1,25},{2,26},{3,27},{4,12},{5,13},{6,14},{7,15},{8,16},{9,... | collective-permute-start | bytes 884744 | tf_op jit(solution)/shard_map/ppermute | solution.py:74
  94.7 11.2 %collective-permute-start.3 = (bf16[2,8,24,384]{3,2,1,0:T(8,128)(2,1)S(1)}, bf16[2,8,24,384]{3,2,1,0:T(8,128)(2,1)S(1)}, u32[]{:S(2)}, u32[]{:S(2)}) collective-permute-start(bf16[2,8,24,384]{3,2,1,0:T(8,128)(2,1)S(1)} %get-tuple-element.39), channel_id=1, source_target_pairs={{0,3},{1,2},{2,1},{3,0},{4,5},{5,4},{6,7},{7,6},{8,11},{9,10},{10,... | collective-permute-start | bytes 884744 | tf_op jit(solution)/shard_map/ppermute | solution.py:74
  97.6 8.4 %collective-permute-start.5 = (bf16[2,8,24,384]{3,2,1,0:T(8,128)(2,1)S(1)}, bf16[2,8,24,384]{3,2,1,0:T(8,128)(2,1)S(1)}, u32[]{:S(2)}, u32[]{:S(2)}) collective-permute-start(bf16[2,8,24,384]{3,2,1,0:T(8,128)(2,1)S(1)} %fusion.4), channel_id=1, source_target_pairs={{0,8},{1,9},{2,10},{3,11},{4,28},{5,29},{6,30},{7,31},{8,0},{9,1},... | collective-permute-start | bytes 884744 | tf_op jit(solution)/shard_map/ppermute | solution.py:74
  97.7 10.2 %collective-permute-start.10 = (bf16[2,8,24,384]{3,2,1,0:T(8,128)(2,1)S(1)}, bf16[2,8,24,384]{3,2,1,0:T(8,128)(2,1)S(1)}, u32[]{:S(2)}, u32[]{:S(2)}) collective-permute-start(bf16[2,8,24,384]{3,2,1,0:T(8,128)(2,1)S(1)} %get-tuple-element.41), channel_id=1, source_target_pairs={{0,24},{1,25},{2,26},{3,27},{4,12},{5,13},{6,14},{7,15},{8,16},{9,... | collective-permute-start | bytes 884744 | tf_op jit(solution)/shard_map/ppermute | solution.py:74
  103.5 8.3 %collective-permute-start.12 = (bf16[2,8,24,384]{3,2,1,0:T(8,128)(2,1)S(1)}, bf16[2,8,24,384]{3,2,1,0:T(8,128)(2,1)S(1)}, u32[]{:S(2)}, u32[]{:S(2)}) collective-permute-start(bf16[2,8,24,384]{3,2,1,0:T(8,128)(2,1)S(1)} %fusion.2), channel_id=1, source_target_pairs={{0,1},{1,0},{2,3},{3,2},{4,7},{5,6},{6,5},{7,4},{8,9},{9,8},{10,11... | collective-permute-start | bytes 884744 | tf_op jit(solution)/shard_map/ppermute | solution.py:74
  106.1 7.8 %collective-permute-start.6 = (bf16[1,8,24,384]{3,2,1,0:T(8,128)(2,1)S(1)}, bf16[1,8,24,384]{3,2,1,0:T(8,128)(2,1)S(1)}, u32[]{:S(2)}, u32[]{:S(2)}) collective-permute-start(bf16[1,8,24,384]{3,2,1,0:T(8,128)(2,1)S(1)} %slice.256), channel_id=1, source_target_pairs={{0,24},{1,25},{2,26},{3,27},{4,12},{5,13},{6,14},{7,15},{8,16},{9,... | collective-permute-start | bytes 442376 | tf_op jit(solution)/shard_map/ppermute | solution.py:74
  111.9 6.4 %collective-permute-start.13 = (bf16[1,8,24,384]{3,2,1,0:T(8,128)(2,1)S(1)}, bf16[1,8,24,384]{3,2,1,0:T(8,128)(2,1)S(1)}, u32[]{:S(2)}, u32[]{:S(2)}) collective-permute-start(bf16[1,8,24,384]{3,2,1,0:T(8,128)(2,1)S(1)} %slice.255), channel_id=1, source_target_pairs={{0,3},{1,2},{2,1},{3,0},{4,5},{5,4},{6,7},{7,6},{8,11},{9,10},{10,... | collective-permute-start | bytes 442376 | tf_op jit(solution)/shard_map/ppermute | solution.py:74
  118.5 5.3 %collective-permute-start.14 = (bf16[4,2,24,384]{3,2,0,1:T(8,128)(2,1)S(1)}, bf16[4,2,24,384]{3,2,0,1:T(8,128)(2,1)S(1)}, u32[]{:S(2)}, u32[]{:S(2)}) collective-permute-start(bf16[4,2,24,384]{3,2,0,1:T(8,128)(2,1)S(1)} %slice.254), channel_id=1, source_target_pairs={{0,32},{1,33},{2,34},{3,35},{4,228},{5,229},{6,230},{7,231},{8,40}... | collective-permute-start | bytes 442376 | tf_op jit(solution)/shard_map/ppermute | solution.py:74
  123.8 5.3 %collective-permute-start.15 = (bf16[2,2,24,384]{3,2,0,1:T(8,128)(2,1)S(1)}, bf16[2,2,24,384]{3,2,0,1:T(8,128)(2,1)S(1)}, u32[]{:S(2)}, u32[]{:S(2)}) collective-permute-start(bf16[2,2,24,384]{3,2,0,1:T(8,128)(2,1)S(1)} %get-tuple-element.37), channel_id=1, source_target_pairs={{0,64},{1,65},{2,66},{3,67},{4,196},{5,197},{6,198},{7,199},{8,72}... | collective-permute-start | bytes 221192 | tf_op jit(solution)/shard_map/ppermute | solution.py:74
  129.1 7.1 %collective-permute-start.16 = (bf16[1,2,24,384]{3,2,0,1:T(8,128)(2,1)S(1)}, bf16[1,2,24,384]{3,2,0,1:T(8,128)(2,1)S(1)}, u32[]{:S(2)}, u32[]{:S(2)}) collective-permute-start(bf16[1,2,24,384]{3,2,0,1:T(8,128)(2,1)S(1)} %fusion.10), channel_id=1, source_target_pairs={{0,224},{1,225},{2,226},{3,227},{4,36},{5,37},{6,38},{7,39},{8,232... | collective-permute-start | bytes 110600 | tf_op jit(solution)/shard_map/ppermute | solution.py:74
  136.2 5.7 %collective-permute-start.17 = (f32[2,24,384]{2,1,0:T(8,128)S(1)}, f32[2,24,384]{2,1,0:T(8,128)S(1)}, u32[]{:S(2)}, u32[]{:S(2)}) collective-permute-start(f32[2,24,384]{2,1,0:T(8,128)S(1)} %fusion.12), channel_id=1, source_target_pairs={{0,3},{1,2},{2,1},{3,0},{4,5},{5,4},{6,7},{7,6},{8,11},{9,10},{10,... | collective-permute-start | bytes 221192 | tf_op jit(solution)/shard_map/ppermute | solution.py:74
  141.9 5.2 %collective-permute-start.18 = (f32[2,48,384]{2,1,0:T(8,128)S(1)}, f32[2,48,384]{2,1,0:T(8,128)S(1)}, u32[]{:S(2)}, u32[]{:S(2)}) collective-permute-start(f32[2,48,384]{2,1,0:T(8,128)S(1)} %pad_maximum_fusion.1), channel_id=1, source_target_pairs={{0,1},{1,0},{2,3},{3,2},{4,7},{5,6},{6,5},{7,4},{8,9},{9,8},{10,11... | collective-permute-start | bytes 442376 | tf_op jit(solution)/shard_map/ppermute | solution.py:74

commit v4 on v3

--- a/solution.py
+++ b/solution.py
@@ -329,14 +329,21 @@
     return keep.astype(f32) + swap(send, step).astype(f32)
 
 
+def apart(array):
+    half = array.shape[0] // 2
+    return array[half:], array[:half]
+
+
 def sum_plane(keep, send, steps):
-    ahead, rest = swap(send[4:], steps[0]), swap(send[:4], steps[0])
-    send = (keep[4:].astype(f32) + ahead.astype(f32)).astype(bf16)
-    keep = keep[:4].astype(f32) + rest.astype(f32)
-    ahead, rest = swap(send[2:], steps[1]), swap(send[:2], steps[1])
-    came = swap((keep[2:] + ahead.astype(f32)).astype(bf16), steps[2])
-    keep = keep[:2] + rest.astype(f32) + came.astype(f32)
-    return keep[:1] + swap(keep[1:].astype(bf16), steps[3]).astype(f32)
+    next_keep, keep, next_send, send = lax.optimization_barrier((*apart(keep), *apart(send)))
+    ahead, rest = swap(next_send, steps[0]), swap(send, steps[0])
+    next_send, send = apart((ahead.astype(f32) + next_keep).astype(bf16))
+    next_send, send = lax.optimization_barrier((next_send, send))
+    ahead, rest_two = swap(next_send, steps[1]), swap(send, steps[1])
+    next_keep, keep = lax.optimization_barrier(apart(keep + rest.astype(f32)))
+    came = swap((ahead.astype(f32) + next_keep).astype(bf16), steps[2])
+    keep = came.astype(f32) + (keep + rest_two.astype(f32))
+    return swap(keep[1:].astype(bf16), steps[3]).astype(f32) + keep[:1]
 
 
 def on_device(index_states, questions, reader, owners, passage_rows, w_up, w_down):

time: 148 us -> 148 us (level)
  transfers between devices with their start and end apart: 20 -> 20, of which waited for: 13 -> 12; matrix products, arithmetic and copies ran while one was open for 2% -> 2% of each run, Pallas kernels for 4% -> 4%
where the time goes in v4:
time: 148 us
  waiting for transfers between devices  71.7 us (48%)
  starting transfers between devices  31.3 us (21%)
  Pallas kernels  21.1 us (14%)
  blocking collectives  19 us (13%)
  other arithmetic  2.98 us (2%)
    ppermute x19, waiting for transfers between devices, swap(): return lax.ppermute(array, AXES, partner(step))  48.5 us
    ppermute x19, starting transfers between devices, swap(): return lax.ppermute(array, AXES, partner(step))  24.8 us
    all_to_all x1, waiting for transfers between devices, on_device(): lax.all_to_all(states_out, 'shard', split_axis=0, concat_axis=0, tiled=True)  23.2 us
    all_to_all x1, blocking collectives, on_device(): lax.all_to_all(send_rows, 'shard', split_axis=0, concat_axis=0, tiled=True)  19 us
    pallas_call x1, Pallas kernels, forward(): pl.pallas_call(forward_kernel, in_specs=[SMEM, VMEM, VMEM, VMEM, VMEM, HB...  10.3 us
    all_to_all x1, starting transfers between devices, on_device(): lax.all_to_all(states_out, 'shard', split_axis=0, concat_axis=0, tiled=True)  6.57 us
    pallas_call x1, Pallas kernels, backward(): pl.pallas_call(backward_kernel, in_specs=[SMEM, VMEM, VMEM, VMEM, HBM], o...  6.1 us
  transfers between devices with their start and end apart: 20, of which 12 were waited for; matrix products, arithmetic and copies ran while one was open for 2% of the time, Pallas kernels for 4%

profile of v4, /device:TPU:64, one launch (start us, length us, event | category | flops | bytes accessed | tf_op | source)
XLA Modules:
  0.0 148.0 jit_solution(1585180749920198071)
XLA Ops:
  0.6 2.8 %route.1 = (s32[64,1,128]{2,1,0:T(1,128)}, s32[256,128]{1,0:T(8,128)}, bf16[1024,768]{1,0:T(8,128)(2,1)S(1)}) custom-call(s32[8,32]{1,0:T(8,128)} %bitcast.15, s32[8,32]{1,0:T(8,128)} %row_ref.1, bf16[1024,768]{1,0:T(8,128)(2,1)} %index_hbm.1), custom_call_target="tpu_custom_call" | custom-call | tf_op jit(solution)/shard_map/route/pallas_call | solution.py:235
  3.4 19.0 %all_to_all.10.rows_ref = s32[64,1,128]{2,1,0:T(1,128)S(1)} all-to-all(s32[64,1,128]{2,1,0:T(1,128)} %get-tuple-element.30), channel_id=1, replica_groups=mesh['shard'=64,'rep'=4] {'shard'}, dimensions={0} | all-to-all | bytes 65536 | tf_op jit(solution)/shard_map/all_to_all | solution.py:357
  22.5 1.9 %fetch.1 = bf16[64,8,768]{2,1,0:T(8,128)(2,1)} custom-call(s32[64,1,128]{2,1,0:T(1,128)S(1)} %all_to_all.10.rows_ref, bf16[1024,768]{1,0:T(8,128)(2,1)S(1)} %get-tuple-element.31.index_ref), custom_call_target="tpu_custom_call" | custom-call | tf_op jit(solution)/shard_map/fetch/pallas_call | solution.py:251
  24.4 6.6 %all-to-all-start.1 = ((bf16[64,8,768]{2,1,0:T(8,128)(2,1)}), bf16[64,8,768]{2,1,0:T(8,128)(2,1)S(1)}, u32[]{:S(2)}, u32[]{:S(2)}) async-start(bf16[64,8,768]{2,1,0:T(8,128)(2,1)} %fetch.1), calls=%async_computation.1 | async-start | bytes 1572864 | tf_op jit(solution)/shard_map/all_to_all | solution.py:359
  31.1 23.2 %all-to-all-done.1 = bf16[64,8,768]{2,1,0:T(8,128)(2,1)S(1)} async-done(((bf16[64,8,768]{2,1,0:T(8,128)(2,1)}), bf16[64,8,768]{2,1,0:T(8,128)(2,1)S(1)}, u32[]{:S(2)}, u32[]{:S(2)}) %all-to-all-start.1) | async-done | bytes 786464 | tf_op jit(solution)/shard_map/all_to_all | solution.py:359
  54.3 10.3 %forward.1 = (f32[8,32]{1,0:T(8,128)}, bf16[256,768]{1,0:T(8,128)(2,1)S(1)}, bf16[256,768]{1,0:T(8,128)(2,1)S(1)}, f32[256,3072]{1,0:T(8,128)S(1)}, bf16[16,8,24...) custom-call(s32[4]{0:T(128)S(1)} %pad_add_fusion.place_ref, bf16[512,768]{1,0:T(8,128)(2,1)S(1)} %bitcast.14, ...), custom_call_target="tpu_custom_call" | custom-call | flops 3623878656 | bytes 25165824 | tf_op jit(solution)/shard_map/forward/pallas_call | solution.py:263
  64.9 6.1 %backward.1 = (bf16[16,8,24,384]{3,2,1,0:T(8,128)(2,1)S(1)}, bf16[16,8,24,384]{3,2,1,0:T(8,128)(2,1)S(1)}) custom-call(s32[4]{0:T(128)S(1)} %pad_add_fusion.place_ref, bf16[256,768]{1,0:T(8,128)(2,1)S(1)} %get-tuple-element.44.grad_emb_ref, bf16[256,768]{1,0:T(8,128)(2,1)S(1)} %get-tuple-element.45.states_ref, f32[256,3072]{1,0:T(8,128)S(1)} %get-tuple-element.46.slope_ref, ...), custom_call_target="tpu_custom_call" | custom-call | flops 2415919104 | bytes 16777216 | tf_op jit(solution)/shard_map/backward/pallas_call | solution.py:294
  71.0 0.6 collective-permute-start.7
  71.6 0.6 add_convert_fusion.1
  72.5 1.6 %collective-permute-start.1 = (bf16[4,8,24,384]{3,2,1,0:T(8,128)(2,1)S(1)}, bf16[4,8,24,384]{3,2,1,0:T(8,128)(2,1)S(1)}, u32[]{:S(2)}, u32[]{:S(2)}) collective-permute-start(bf16[4,8,24,384]{3,2,1,0:T(8,128)(2,1)S(1)} %get-tuple-element.36), channel_id=1, source_target_pairs={{0,1},{1,0},{2,3},{3,2},{4,7},{5,6},{6,5},{7,4},{8,9},{9,8},{10,11... | collective-permute-start | bytes 1769480 | tf_op jit(solution)/shard_map/ppermute | solution.py:74
  74.6 1.2 collective-permute-done.7
  77.2 1.6 %collective-permute-start.10 = (bf16[4,8,24,384]{3,2,1,0:T(8,128)(2,1)S(1)}, bf16[4,8,24,384]{3,2,1,0:T(8,128)(2,1)S(1)}, u32[]{:S(2)}, u32[]{:S(2)}) collective-permute-start(bf16[4,8,24,384]{3,2,1,0:T(8,128)(2,1)S(1)} %get-tuple-element.53), channel_id=1, source_target_pairs={{0,8},{1,9},{2,10},{3,11},{4,28},{5,29},{6,30},{7,31},{8,0},{9,1},... | collective-permute-start | bytes 1769480 | tf_op jit(solution)/shard_map/ppermute | solution.py:74
  78.8 3.7 %collective-permute-done.1 = bf16[4,8,24,384]{3,2,1,0:T(8,128)(2,1)S(1)} collective-permute-done((bf16[4,8,24,384]{3,2,1,0:T(8,128)(2,1)S(1)}, bf16[4,8,24,384]{3,2,1,0:T(8,128)(2,1)S(1)}, u32[]{:S(2)}, u32[]{:S(2)}) %collective-permute-start.1) | collective-permute-done | bytes 589856 | tf_op jit(solution)/shard_map/ppermute | solution.py:74
  82.7 2.9 %collective-permute-start.2 = (bf16[2,8,24,384]{3,2,1,0:T(8,128)(2,1)S(1)}, bf16[2,8,24,384]{3,2,1,0:T(8,128)(2,1)S(1)}, u32[]{:S(2)}, u32[]{:S(2)}) collective-permute-start(bf16[2,8,24,384]{3,2,1,0:T(8,128)(2,1)S(1)} %get-tuple-element.38), channel_id=1, source_target_pairs={{0,3},{1,2},{2,1},{3,0},{4,5},{5,4},{6,7},{7,6},{8,11},{9,10},{10,... | collective-permute-start | bytes 884744 | tf_op jit(solution)/shard_map/ppermute | solution.py:74
  86.0 6.0 %collective-permute-done.3 = bf16[4,8,24,384]{3,2,1,0:T(8,128)(2,1)S(1)} collective-permute-done((bf16[4,8,24,384]{3,2,1,0:T(8,128)(2,1)S(1)}, bf16[4,8,24,384]{3,2,1,0:T(8,128)(2,1)S(1)}, u32[]{:S(2)}, u32[]{:S(2)}) %collective-permute-start.3) | collective-permute-done | bytes 589856 | tf_op jit(solution)/shard_map/ppermute | solution.py:74
  92.5 1.6 %collective-permute-start.9 = (bf16[2,8,24,384]{3,2,1,0:T(8,128)(2,1)S(1)}, bf16[2,8,24,384]{3,2,1,0:T(8,128)(2,1)S(1)}, u32[]{:S(2)}, u32[]{:S(2)}) collective-permute-start(bf16[2,8,24,384]{3,2,1,0:T(8,128)(2,1)S(1)} %get-tuple-element.51), channel_id=1, source_target_pairs={{0,24},{1,25},{2,26},{3,27},{4,12},{5,13},{6,14},{7,15},{8,16},{9,... | collective-permute-start | bytes 884744 | tf_op jit(solution)/shard_map/ppermute | solution.py:74
  94.1 1.8 %collective-permute-start.12 = (bf16[2,8,24,384]{3,2,1,0:T(8,128)(2,1)S(1)}, bf16[2,8,24,384]{3,2,1,0:T(8,128)(2,1)S(1)}, u32[]{:S(2)}, u32[]{:S(2)}) collective-permute-start(bf16[2,8,24,384]{3,2,1,0:T(8,128)(2,1)S(1)} %get-tuple-element.56), channel_id=1, source_target_pairs={{0,24},{1,25},{2,26},{3,27},{4,12},{5,13},{6,14},{7,15},{8,16},{9,... | collective-permute-start | bytes 884744 | tf_op jit(solution)/shard_map/ppermute | solution.py:74
  96.2 7.1 %collective-permute-done.9 = bf16[2,8,24,384]{3,2,1,0:T(8,128)(2,1)S(1)} collective-permute-done((bf16[2,8,24,384]{3,2,1,0:T(8,128)(2,1)S(1)}, bf16[2,8,24,384]{3,2,1,0:T(8,128)(2,1)S(1)}, u32[]{:S(2)}, u32[]{:S(2)}) %collective-permute-start.9) | collective-permute-done | bytes 294944 | tf_op jit(solution)/shard_map/ppermute | solution.py:74
  103.4 2.3 %collective-permute-start.11 = (bf16[2,8,24,384]{3,2,1,0:T(8,128)(2,1)S(1)}, bf16[2,8,24,384]{3,2,1,0:T(8,128)(2,1)S(1)}, u32[]{:S(2)}, u32[]{:S(2)}) collective-permute-start(bf16[2,8,24,384]{3,2,1,0:T(8,128)(2,1)S(1)} %add_convert_fusion.4), channel_id=1, source_target_pairs={{0,1},{1,0},{2,3},{3,2},{4,7},{5,6},{6,5},{7,4},{8,9},{9,8},{10,11... | collective-permute-start | bytes 884744 | tf_op jit(solution)/shard_map/ppermute | solution.py:74
  105.8 1.5 %collective-permute-start.6 = (bf16[1,8,24,384]{3,2,1,0:T(8,128)(2,1)S(1)}, bf16[1,8,24,384]{3,2,1,0:T(8,128)(2,1)S(1)}, u32[]{:S(2)}, u32[]{:S(2)}) collective-permute-start(bf16[1,8,24,384]{3,2,1,0:T(8,128)(2,1)S(1)} %slice.236), channel_id=1, source_target_pairs={{0,24},{1,25},{2,26},{3,27},{4,12},{5,13},{6,14},{7,15},{8,16},{9,... | collective-permute-start | bytes 442376 | tf_op jit(solution)/shard_map/ppermute | solution.py:74
  107.4 4.6 %collective-permute-done.11 = bf16[2,8,24,384]{3,2,1,0:T(8,128)(2,1)S(1)} collective-permute-done((bf16[2,8,24,384]{3,2,1,0:T(8,128)(2,1)S(1)}, bf16[2,8,24,384]{3,2,1,0:T(8,128)(2,1)S(1)}, u32[]{:S(2)}, u32[]{:S(2)}) %collective-permute-start.11) | collective-permute-done | bytes 294944 | tf_op jit(solution)/shard_map/ppermute | solution.py:74
  112.0 2.9 %collective-permute-start.13 = (bf16[1,8,24,384]{3,2,1,0:T(8,128)(2,1)S(1)}, bf16[1,8,24,384]{3,2,1,0:T(8,128)(2,1)S(1)}, u32[]{:S(2)}, u32[]{:S(2)}) collective-permute-start(bf16[1,8,24,384]{3,2,1,0:T(8,128)(2,1)S(1)} %slice.235), channel_id=1, source_target_pairs={{0,3},{1,2},{2,1},{3,0},{4,5},{5,4},{6,7},{7,6},{8,11},{9,10},{10,... | collective-permute-start | bytes 442376 | tf_op jit(solution)/shard_map/ppermute | solution.py:74
  114.9 3.6 %collective-permute-done.13 = bf16[1,8,24,384]{3,2,1,0:T(8,128)(2,1)S(1)} collective-permute-done((bf16[1,8,24,384]{3,2,1,0:T(8,128)(2,1)S(1)}, bf16[1,8,24,384]{3,2,1,0:T(8,128)(2,1)S(1)}, u32[]{:S(2)}, u32[]{:S(2)}) %collective-permute-start.13) | collective-permute-done | bytes 147488 | tf_op jit(solution)/shard_map/ppermute | solution.py:74
  118.6 1.0 collective-permute-start.14
  119.5 4.3 %collective-permute-done.14 = bf16[4,2,24,384]{3,2,0,1:T(8,128)(2,1)S(1)} collective-permute-done((bf16[4,2,24,384]{3,2,0,1:T(8,128)(2,1)S(1)}, bf16[4,2,24,384]{3,2,0,1:T(8,128)(2,1)S(1)}, u32[]{:S(2)}, u32[]{:S(2)}) %collective-permute-start.14) | collective-permute-done | bytes 147488 | tf_op jit(solution)/shard_map/ppermute | solution.py:74
  124.3 5.0 %collective-permute-done.15 = bf16[2,2,24,384]{3,2,0,1:T(8,128)(2,1)S(1)} collective-permute-done((bf16[2,2,24,384]{3,2,0,1:T(8,128)(2,1)S(1)}, bf16[2,2,24,384]{3,2,0,1:T(8,128)(2,1)S(1)}, u32[]{:S(2)}, u32[]{:S(2)}) %collective-permute-start.15) | collective-permute-done | bytes 73760 | tf_op jit(solution)/shard_map/ppermute | solution.py:74
  129.3 1.8 %collective-permute-start.16 = (bf16[1,2,24,384]{3,2,0,1:T(8,128)(2,1)S(1)}, bf16[1,2,24,384]{3,2,0,1:T(8,128)(2,1)S(1)}, u32[]{:S(2)}, u32[]{:S(2)}) collective-permute-start(bf16[1,2,24,384]{3,2,0,1:T(8,128)(2,1)S(1)} %fusion.4), channel_id=1, source_target_pairs={{0,224},{1,225},{2,226},{3,227},{4,36},{5,37},{6,38},{7,39},{8,232... | collective-permute-start | bytes 110600 | tf_op jit(solution)/shard_map/ppermute | solution.py:74
  131.1 5.2 %collective-permute-done.16 = bf16[1,2,24,384]{3,2,0,1:T(8,128)(2,1)S(1)} collective-permute-done((bf16[1,2,24,384]{3,2,0,1:T(8,128)(2,1)S(1)}, bf16[1,2,24,384]{3,2,0,1:T(8,128)(2,1)S(1)}, u32[]{:S(2)}, u32[]{:S(2)}) %collective-permute-start.16) | collective-permute-done | bytes 36896 | tf_op jit(solution)/shard_map/ppermute | solution.py:74
  136.4 2.9 %collective-permute-start.17 = (f32[2,24,384]{2,1,0:T(8,128)S(1)}, f32[2,24,384]{2,1,0:T(8,128)S(1)}, u32[]{:S(2)}, u32[]{:S(2)}) collective-permute-start(f32[2,24,384]{2,1,0:T(8,128)S(1)} %fusion.6), channel_id=1, source_target_pairs={{0,3},{1,2},{2,1},{3,0},{4,5},{5,4},{6,7},{7,6},{8,11},{9,10},{10,... | collective-permute-start | bytes 221192 | tf_op jit(solution)/shard_map/ppermute | solution.py:74
  139.2 2.8 %collective-permute-done.17 = f32[2,24,384]{2,1,0:T(8,128)S(1)} collective-permute-done((f32[2,24,384]{2,1,0:T(8,128)S(1)}, f32[2,24,384]{2,1,0:T(8,128)S(1)}, u32[]{:S(2)}, u32[]{:S(2)}) %collective-permute-start.17) | collective-permute-done | bytes 73760 | tf_op jit(solution)/shard_map/ppermute | solution.py:74
  142.2 5.1 %collective-permute-done.18 = f32[2,48,384]{2,1,0:T(8,128)S(1)} collective-permute-done((f32[2,48,384]{2,1,0:T(8,128)S(1)}, f32[2,48,384]{2,1,0:T(8,128)S(1)}, u32[]{:S(2)}, u32[]{:S(2)}) %collective-permute-start.18) | collective-permute-done | bytes 147488 | tf_op jit(solution)/shard_map/ppermute | solution.py:74
  147.3 0.7 fusion.2
  (51 shorter events, 5.1 us)
Async XLA Ops:
  24.4 29.9 %copy-start = (s32[256,128]{1,0:T(8,128)S(1)}, s32[256,128]{1,0:T(8,128)}, u32[]{:S(2)}) copy-start(s32[256,128]{1,0:T(8,128)} %get-tuple-element.32.slot_ref) | copy-start | bytes 393220
  24.4 29.9 %copy-start.1 = (bf16[8,768]{1,0:T(8,128)(2,1)S(1)}, bf16[8,768]{1,0:T(8,128)(2,1)}, u32[]{:S(2)}) copy-start(bf16[8,768]{1,0:T(8,128)(2,1)} %question_ref.1) | copy-start | bytes 36868
  24.4 29.9 %copy-start.2 = (f32[8,32]{1,0:T(8,128)S(1)}, f32[8,32]{1,0:T(8,128)}, u32[]{:S(2)}) copy-start(f32[8,32]{1,0:T(8,128)} %reader_ref.1) | copy-start | bytes 3076
  24.4 29.9 %all-to-all-start.1 = ((bf16[64,8,768]{2,1,0:T(8,128)(2,1)}), bf16[64,8,768]{2,1,0:T(8,128)(2,1)S(1)}, u32[]{:S(2)}, u32[]{:S(2)}) async-start(bf16[64,8,768]{2,1,0:T(8,128)(2,1)} %fetch.1), calls=%async_computation.1 | async-start | bytes 1572864 | tf_op jit(solution)/shard_map/all_to_all | solution.py:359
  64.7 7.0 %collective-permute-start = (bf16[16,8,24,384]{3,2,1,0:T(8,128)(2,1)S(1)}, bf16[16,8,24,384]{3,2,1,0:T(8,128)(2,1)S(1)}, u32[]{:S(2)}, u32[]{:S(2)}) collective-permute-start(bf16[16,8,24,384]{3,2,1,0:T(8,128)(2,1)S(1)} %get-tuple-element.35), channel_id=1, source_target_pairs={{0,4},{1,5},{2,6},{3,7},{4,0},{5,1},{6,2},{7,3},{8,12},{9,13},{10,... | collective-permute-start | bytes 7077896 | tf_op jit(solution)/shard_map/ppermute | solution.py:74
  71.0 4.8 %collective-permute-start.7 = (bf16[16,8,24,384]{3,2,1,0:T(8,128)(2,1)S(1)}, bf16[16,8,24,384]{3,2,1,0:T(8,128)(2,1)S(1)}, u32[]{:S(2)}, u32[]{:S(2)}) collective-permute-start(bf16[16,8,24,384]{3,2,1,0:T(8,128)(2,1)S(1)} %get-tuple-element.48), channel_id=1, source_target_pairs={{0,4},{1,5},{2,6},{3,7},{4,0},{5,1},{6,2},{7,3},{8,12},{9,13},{10,... | collective-permute-start | bytes 7077896 | tf_op jit(solution)/shard_map/ppermute | solution.py:74
  72.5 10.0 %collective-permute-start.1 = (bf16[4,8,24,384]{3,2,1,0:T(8,128)(2,1)S(1)}, bf16[4,8,24,384]{3,2,1,0:T(8,128)(2,1)S(1)}, u32[]{:S(2)}, u32[]{:S(2)}) collective-permute-start(bf16[4,8,24,384]{3,2,1,0:T(8,128)(2,1)S(1)} %get-tuple-element.36), channel_id=1, source_target_pairs={{0,1},{1,0},{2,3},{3,2},{4,7},{5,6},{6,5},{7,4},{8,9},{9,8},{10,11... | collective-permute-start | bytes 1769480 | tf_op jit(solution)/shard_map/ppermute | solution.py:74
  74.1 18.0 %collective-permute-start.3 = (bf16[4,8,24,384]{3,2,1,0:T(8,128)(2,1)S(1)}, bf16[4,8,24,384]{3,2,1,0:T(8,128)(2,1)S(1)}, u32[]{:S(2)}, u32[]{:S(2)}) collective-permute-start(bf16[4,8,24,384]{3,2,1,0:T(8,128)(2,1)S(1)} %get-tuple-element.40), channel_id=1, source_target_pairs={{0,1},{1,0},{2,3},{3,2},{4,7},{5,6},{6,5},{7,4},{8,9},{9,8},{10,11... | collective-permute-start | bytes 1769480 | tf_op jit(solution)/shard_map/ppermute | solution.py:74
  76.7 15.6 %collective-permute-start.8 = (bf16[4,8,24,384]{3,2,1,0:T(8,128)(2,1)S(1)}, bf16[4,8,24,384]{3,2,1,0:T(8,128)(2,1)S(1)}, u32[]{:S(2)}, u32[]{:S(2)}) collective-permute-start(bf16[4,8,24,384]{3,2,1,0:T(8,128)(2,1)S(1)} %get-tuple-element.49), channel_id=1, source_target_pairs={{0,8},{1,9},{2,10},{3,11},{4,28},{5,29},{6,30},{7,31},{8,0},{9,1},... | collective-permute-start | bytes 1769480 | tf_op jit(solution)/shard_map/ppermute | solution.py:74
  77.2 18.6 %collective-permute-start.10 = (bf16[4,8,24,384]{3,2,1,0:T(8,128)(2,1)S(1)}, bf16[4,8,24,384]{3,2,1,0:T(8,128)(2,1)S(1)}, u32[]{:S(2)}, u32[]{:S(2)}) collective-permute-start(bf16[4,8,24,384]{3,2,1,0:T(8,128)(2,1)S(1)} %get-tuple-element.53), channel_id=1, source_target_pairs={{0,8},{1,9},{2,10},{3,11},{4,28},{5,29},{6,30},{7,31},{8,0},{9,1},... | collective-permute-start | bytes 1769480 | tf_op jit(solution)/shard_map/ppermute | solution.py:74
  82.7 13.3 %collective-permute-start.2 = (bf16[2,8,24,384]{3,2,1,0:T(8,128)(2,1)S(1)}, bf16[2,8,24,384]{3,2,1,0:T(8,128)(2,1)S(1)}, u32[]{:S(2)}, u32[]{:S(2)}) collective-permute-start(bf16[2,8,24,384]{3,2,1,0:T(8,128)(2,1)S(1)} %get-tuple-element.38), channel_id=1, source_target_pairs={{0,3},{1,2},{2,1},{3,0},{4,5},{5,4},{6,7},{7,6},{8,11},{9,10},{10,... | collective-permute-start | bytes 884744 | tf_op jit(solution)/shard_map/ppermute | solution.py:74
  85.6 20.2 %collective-permute-start.5 = (bf16[2,8,24,384]{3,2,1,0:T(8,128)(2,1)S(1)}, bf16[2,8,24,384]{3,2,1,0:T(8,128)(2,1)S(1)}, u32[]{:S(2)}, u32[]{:S(2)}) collective-permute-start(bf16[2,8,24,384]{3,2,1,0:T(8,128)(2,1)S(1)} %get-tuple-element.43), channel_id=1, source_target_pairs={{0,3},{1,2},{2,1},{3,0},{4,5},{5,4},{6,7},{7,6},{8,11},{9,10},{10,... | collective-permute-start | bytes 884744 | tf_op jit(solution)/shard_map/ppermute | solution.py:74
  92.5 10.8 %collective-permute-start.9 = (bf16[2,8,24,384]{3,2,1,0:T(8,128)(2,1)S(1)}, bf16[2,8,24,384]{3,2,1,0:T(8,128)(2,1)S(1)}, u32[]{:S(2)}, u32[]{:S(2)}) collective-permute-start(bf16[2,8,24,384]{3,2,1,0:T(8,128)(2,1)S(1)} %get-tuple-element.51), channel_id=1, source_target_pairs={{0,24},{1,25},{2,26},{3,27},{4,12},{5,13},{6,14},{7,15},{8,16},{9,... | collective-permute-start | bytes 884744 | tf_op jit(solution)/shard_map/ppermute | solution.py:74
  94.1 13.3 %collective-permute-start.12 = (bf16[2,8,24,384]{3,2,1,0:T(8,128)(2,1)S(1)}, bf16[2,8,24,384]{3,2,1,0:T(8,128)(2,1)S(1)}, u32[]{:S(2)}, u32[]{:S(2)}) collective-permute-start(bf16[2,8,24,384]{3,2,1,0:T(8,128)(2,1)S(1)} %get-tuple-element.56), channel_id=1, source_target_pairs={{0,24},{1,25},{2,26},{3,27},{4,12},{5,13},{6,14},{7,15},{8,16},{9,... | collective-permute-start | bytes 884744 | tf_op jit(solution)/shard_map/ppermute | solution.py:74
  96.0 9.7 %collective-permute-start.4 = (bf16[2,8,24,384]{3,2,1,0:T(8,128)(2,1)S(1)}, bf16[2,8,24,384]{3,2,1,0:T(8,128)(2,1)S(1)}, u32[]{:S(2)}, u32[]{:S(2)}) collective-permute-start(bf16[2,8,24,384]{3,2,1,0:T(8,128)(2,1)S(1)} %add_convert_fusion.5), channel_id=1, source_target_pairs={{0,8},{1,9},{2,10},{3,11},{4,28},{5,29},{6,30},{7,31},{8,0},{9,1},... | collective-permute-start | bytes 884744 | tf_op jit(solution)/shard_map/ppermute | solution.py:74
  103.4 8.5 %collective-permute-start.11 = (bf16[2,8,24,384]{3,2,1,0:T(8,128)(2,1)S(1)}, bf16[2,8,24,384]{3,2,1,0:T(8,128)(2,1)S(1)}, u32[]{:S(2)}, u32[]{:S(2)}) collective-permute-start(bf16[2,8,24,384]{3,2,1,0:T(8,128)(2,1)S(1)} %add_convert_fusion.4), channel_id=1, source_target_pairs={{0,1},{1,0},{2,3},{3,2},{4,7},{5,6},{6,5},{7,4},{8,9},{9,8},{10,11... | collective-permute-start | bytes 884744 | tf_op jit(solution)/shard_map/ppermute | solution.py:74
  105.8 9.1 %collective-permute-start.6 = (bf16[1,8,24,384]{3,2,1,0:T(8,128)(2,1)S(1)}, bf16[1,8,24,384]{3,2,1,0:T(8,128)(2,1)S(1)}, u32[]{:S(2)}, u32[]{:S(2)}) collective-permute-start(bf16[1,8,24,384]{3,2,1,0:T(8,128)(2,1)S(1)} %slice.236), channel_id=1, source_target_pairs={{0,24},{1,25},{2,26},{3,27},{4,12},{5,13},{6,14},{7,15},{8,16},{9,... | collective-permute-start | bytes 442376 | tf_op jit(solution)/shard_map/ppermute | solution.py:74
  112.0 6.4 %collective-permute-start.13 = (bf16[1,8,24,384]{3,2,1,0:T(8,128)(2,1)S(1)}, bf16[1,8,24,384]{3,2,1,0:T(8,128)(2,1)S(1)}, u32[]{:S(2)}, u32[]{:S(2)}) collective-permute-start(bf16[1,8,24,384]{3,2,1,0:T(8,128)(2,1)S(1)} %slice.235), channel_id=1, source_target_pairs={{0,3},{1,2},{2,1},{3,0},{4,5},{5,4},{6,7},{7,6},{8,11},{9,10},{10,... | collective-permute-start | bytes 442376 | tf_op jit(solution)/shard_map/ppermute | solution.py:74
  118.6 5.2 %collective-permute-start.14 = (bf16[4,2,24,384]{3,2,0,1:T(8,128)(2,1)S(1)}, bf16[4,2,24,384]{3,2,0,1:T(8,128)(2,1)S(1)}, u32[]{:S(2)}, u32[]{:S(2)}) collective-permute-start(bf16[4,2,24,384]{3,2,0,1:T(8,128)(2,1)S(1)} %slice.234), channel_id=1, source_target_pairs={{0,32},{1,33},{2,34},{3,35},{4,228},{5,229},{6,230},{7,231},{8,40}... | collective-permute-start | bytes 442376 | tf_op jit(solution)/shard_map/ppermute | solution.py:74
  123.8 5.4 %collective-permute-start.15 = (bf16[2,2,24,384]{3,2,0,1:T(8,128)(2,1)S(1)}, bf16[2,2,24,384]{3,2,0,1:T(8,128)(2,1)S(1)}, u32[]{:S(2)}, u32[]{:S(2)}) collective-permute-start(bf16[2,2,24,384]{3,2,0,1:T(8,128)(2,1)S(1)} %get-tuple-element.73), channel_id=1, source_target_pairs={{0,64},{1,65},{2,66},{3,67},{4,196},{5,197},{6,198},{7,199},{8,72}... | collective-permute-start | bytes 221192 | tf_op jit(solution)/shard_map/ppermute | solution.py:74
  129.3 7.1 %collective-permute-start.16 = (bf16[1,2,24,384]{3,2,0,1:T(8,128)(2,1)S(1)}, bf16[1,2,24,384]{3,2,0,1:T(8,128)(2,1)S(1)}, u32[]{:S(2)}, u32[]{:S(2)}) collective-permute-start(bf16[1,2,24,384]{3,2,0,1:T(8,128)(2,1)S(1)} %fusion.4), channel_id=1, source_target_pairs={{0,224},{1,225},{2,226},{3,227},{4,36},{5,37},{6,38},{7,39},{8,232... | collective-permute-start | bytes 110600 | tf_op jit(solution)/shard_map/ppermute | solution.py:74
  136.4 5.7 %collective-permute-start.17 = (f32[2,24,384]{2,1,0:T(8,128)S(1)}, f32[2,24,384]{2,1,0:T(8,128)S(1)}, u32[]{:S(2)}, u32[]{:S(2)}) collective-permute-start(f32[2,24,384]{2,1,0:T(8,128)S(1)} %fusion.6), channel_id=1, source_target_pairs={{0,3},{1,2},{2,1},{3,0},{4,5},{5,4},{6,7},{7,6},{8,11},{9,10},{10,... | collective-permute-start | bytes 221192 | tf_op jit(solution)/shard_map/ppermute | solution.py:74
  142.1 5.2 %collective-permute-start.18 = (f32[2,48,384]{2,1,0:T(8,128)S(1)}, f32[2,48,384]{2,1,0:T(8,128)S(1)}, u32[]{:S(2)}, u32[]{:S(2)}) collective-permute-start(f32[2,48,384]{2,1,0:T(8,128)S(1)} %pad_maximum_fusion.1), channel_id=1, source_target_pairs={{0,1},{1,0},{2,3},{3,2},{4,7},{5,6},{6,5},{7,4},{8,9},{9,8},{10,11... | collective-permute-start | bytes 442376 | tf_op jit(solution)/shard_map/ppermute | solution.py:74

commit v5 on v4

--- a/solution.py
+++ b/solution.py
@@ -1,3 +1,4 @@
+import functools
 import itertools
 
 import jax
@@ -14,7 +15,7 @@
 OWN = 48
 CHUNK = NY * NC * OWN
 HALF_R, HALF_C = 24, 384
-WIDE = 512
+WIDE = 2 * CHUNK
 
 normalizer_heat = 0.1
 loss_scale = 64.0
@@ -41,6 +42,12 @@
 def label4(v, core):
     low, high = low_bit(v), high_bit(v)
     return (low * (1 - core) + high * core) * 2 + (high * (1 - core) + low * core)
+
+
+def place4(label, core):
+    first, second = label >> 1, label & 1
+    low, high = first * (1 - core) + second * core, second * (1 - core) + first * core
+    return high * 2 + (low ^ high)
 
 
 def label8(v, core):
@@ -128,37 +135,40 @@
     out_ref[...] = got.reshape(shards, cap, width).astype(bf16)
 
 
-def place_gradient(place_ref, value_ref, outs, z, x_first):
-    y, c, x = place_ref[1], place_ref[2], place_ref[3]
-    for other, out_ref in enumerate(outs):
-        core = c ^ other
-        mine_x, mine_y = label4(x, core), label4(y, core)
-        at_z = label8(z, core) ^ label8(place_ref[0], core)
-        for j in range(NY):
-            at_y = label4(j, core) ^ mine_y
-            for piece in range(4):
-                at_x = piece ^ mine_x
-                at = at_x * NY + at_y if x_first else at_y * NX + at_x
-                start = pl.multiple_of(j * NC * OWN + core * OWN + (piece & 1) * HALF_R, 8)
-                columns = (piece >> 1) * HALF_C
-                out_ref[at, at_z] = value_ref[pl.ds(start, HALF_R), columns : columns + HALF_C].astype(bf16)
+def turn_kernel(up_hbm, up_t_ref, up_ref, sems):
+    parts = sems.shape[0]
+    copies = []
+    for t in range(parts):
+        cut = pl.ds(t * WIDE, WIDE)
+        copies.append(pltpu.make_async_copy(up_hbm.at[:, cut], up_ref.at[:, cut], sems.at[t]))
+        copies[t].start()
+    for t in range(parts):
+        cut = slice(t * WIDE, (t + 1) * WIDE)
+        copies[t].wait()
+        up_t_ref[cut, :] = up_ref[:, cut].T
+
+
+def share_units(units_ref, core, mine_ref, other_ref, t):
+    for block in range(2 * t * NY, 2 * (t + 1) * NY):
+        for own, out_ref in ((core, mine_ref), (1 - core, other_ref)):
+            start = pl.multiple_of(block * NC * OWN + own * OWN, 16)
+            out_ref[block * OWN : (block + 1) * OWN, :] = units_ref[pl.ds(start, OWN), :]
 
 
 def forward_kernel(
-    place_ref, got_ref, slot_ref, question_ref, reader_ref, up_hbm, down_hbm,
-    derivative_ref, states_ref, grad_emb_ref, slope_ref, keep_ref, send_ref,
-    up_ref, down_ref, hidden_ref, value_ref, sems,
+    place_ref, got_ref, slot_ref, question_ref, reader_ref, up_t_hbm, down_hbm,
+    derivative_ref, states_ref, grad_emb_ref, slope_ref, mine_ref, pack_ref, down_ref,
+    hidden_ref, up_t_ref, sems,
 ):
     width = question_ref.shape[1]
-    parts = up_ref.shape[1] // WIDE
+    parts = hidden_ref.shape[0] // WIDE
     ups, downs = [], []
     for t in range(parts):
         cut = pl.ds(t * WIDE, WIDE)
-        ups.append(pltpu.make_async_copy(up_hbm.at[:, cut], up_ref.at[:, cut], sems.at[0, t]))
+        ups.append(pltpu.make_async_copy(up_t_hbm.at[cut, :], up_t_ref.at[cut, :], sems.at[0, t]))
         downs.append(pltpu.make_async_copy(down_hbm.at[cut, :], down_ref.at[cut, :], sems.at[1, t]))
-        ups[t].start()
-        downs[t].start()
-
+    ups[0].start()
+    ups[1].start()
     lanes = lax.broadcasted_iota(i32, (Q * K, got_ref.shape[0]), 1)
     onehot = (lanes == slot_ref[:, :1]).astype(f32).astype(bf16)
     states = dot(onehot, got_ref[...], ((1,), (0,))).astype(bf16)
@@ -166,18 +176,21 @@
     for t in range(parts):
         cut = slice(t * WIDE, (t + 1) * WIDE)
         ups[t].wait()
-        pre = dot(states, up_ref[:, cut], ((1,), (0,)))
+        for copy in (ups + downs)[2 * t + 2 : 2 * t + 4]:
+            copy.start()
+        pre = dot(up_t_ref[cut, :], states, ((1,), (1,)))
         square = pre * pre
         tangent = jnp.tanh(pre * (gelu_coeff + (gelu_coeff * cubic) * square))
         gate = 0.5 + 0.5 * tangent
-        hidden = (pre * gate).astype(bf16)
-        slope_ref[:, cut] = gate + pre * (1.0 - tangent * tangent) * (
+        hidden_ref[cut, :] = (pre * gate).astype(bf16)
+        slope_ref[cut, :] = gate + pre * (1.0 - tangent * tangent) * (
             0.5 * gelu_coeff + (1.5 * gelu_coeff * cubic) * square
         )
-        hidden_ref[:, cut] = hidden
+        share_units(hidden_ref, place_ref[2], mine_ref, pack_ref, t)
     for copy in downs:
         copy.wait()
-    embedded = states.astype(f32) + dot(hidden_ref[...], down_ref[...], ((1,), (0,)))
+    embedded = states.astype(f32) + dot(hidden_ref[...], down_ref[...], ((0,), (0,)))
+
     norms = jnp.sqrt(jnp.sum(embedded * embedded, -1, keepdims=True) + epsilon)
     unit = embedded / norms
     wide = question_ref[...].astype(f32)
@@ -193,31 +206,53 @@
     derivative_ref[...] = uncolumn(derivative, K)
     grad_emb = ((derivative / normalizer_heat) * (query - cosine * unit) / norms).astype(bf16)
     grad_emb_ref[...] = grad_emb
-    for z in range(NZ):
-        value_ref[z % 2] = dot(hidden_ref[:, z * CHUNK : (z + 1) * CHUNK], grad_emb, ((0,), (0,)))
-        place_gradient(place_ref, value_ref.at[z % 2], (keep_ref, send_ref), z, True)
-
-
-def backward_kernel(
-    place_ref, grad_emb_ref, states_ref, slope_ref, down_hbm,
-    keep_ref, send_ref,
-    down_ref, grad_pre_ref, value_ref, sems,
+    units = mine_ref.shape[0]
+    for block, array in enumerate((grad_emb, states)):
+        for part in range(width // (Q * K)):
+            start = units + block * width + part * Q * K
+            pack_ref[start : start + Q * K, :] = array[:, part * Q * K : (part + 1) * Q * K]
+
+
+def backward_kernel(place_ref, grad_emb_ref, slope_ref, down_ref, mine_ref, other_ref, grad_pre_ref):
+    grad_emb = grad_emb_ref[...]
+    for t in range(down_ref.shape[0] // WIDE):
+        cut = slice(t * WIDE, (t + 1) * WIDE)
+        grad_hidden = dot(down_ref[cut, :], grad_emb, ((1,), (1,)))
+        grad_pre_ref[cut, :] = (grad_hidden * slope_ref[cut, :]).astype(bf16)
+        share_units(grad_pre_ref, place_ref[2], mine_ref, other_ref, t)
+
+
+def gradient_kernel(
+    x_first, right_at, place_ref, mine_ref, came_ref, right_ref, pack_ref,
+    next_keep_ref, keep_ref, next_send_ref, send_ref, value_ref,
 ):
-    parts = down_ref.shape[0] // WIDE
-    downs = []
-    for t in range(parts):
-        cut = pl.ds(t * WIDE, WIDE)
-        downs.append(pltpu.make_async_copy(down_hbm.at[cut, :], down_ref.at[cut, :], sems.at[t]))
-        downs[t].start()
-    grad_emb, states = grad_emb_ref[...], states_ref[...]
-    for t in range(parts):
-        cut = slice(t * WIDE, (t + 1) * WIDE)
-        downs[t].wait()
-        grad_hidden = dot(grad_emb, down_ref[cut, :], ((1,), (1,)))
-        grad_pre_ref[:, cut] = (grad_hidden * slope_ref[:, cut]).astype(bf16)
-    for z in range(NZ):
-        value_ref[z % 2] = dot(grad_pre_ref[:, z * CHUNK : (z + 1) * CHUNK], states, ((0,), (0,)))
-        place_gradient(place_ref, value_ref.at[z % 2], (keep_ref, send_ref), z, False)
+    z, y, core, x = place_ref[0], place_ref[1], place_ref[2], place_ref[3]
+    mine_x, mine_y, mine_z = label4(x, core), label4(y, core), label8(z, core)
+    right = right_ref[...]
+    rows, width = right.shape
+    right_came = jnp.concatenate(
+        [pack_ref[right_at + part * rows : right_at + (part + 1) * rows, :] for part in range(width // rows)], 1
+    )
+    outs = (keep_ref, next_keep_ref, send_ref, next_send_ref)
+    per = 2 * NY * OWN
+    spots = []
+    for at in range(NX * NY):
+        at_x, at_y = (at >> 2, at & 3) if x_first else (at & 3, at >> 2)
+        piece, j = at_x ^ mine_x, place4(at_y ^ mine_y, core)
+        spots.append((j * OWN + (piece & 1) * HALF_R, pl.multiple_of((piece >> 1) * HALF_C, 128)))
+    for t in range(NZ // 2):
+        cut = slice(t * per, (t + 1) * per)
+        value_ref[t % 2] = dot(mine_ref[cut, :], right, ((1,), (0,))) + dot(
+            came_ref[cut, :], right_came, ((1,), (0,))
+        )
+        for half in range(2):
+            at_z = label8(2 * t + half, core) ^ mine_z
+            for at, (row, column) in enumerate(spots):
+                row = pl.multiple_of(half * NY * OWN + row, 8)
+                out_ref = outs[at >> 2]
+                out_ref[at & 3, at_z] = value_ref[
+                    t % 2, pl.ds(row, HALF_R), pl.ds(column, HALF_C)
+                ].astype(out_ref.dtype)
 
 
 def far(array):
@@ -256,58 +291,85 @@
     )(rows_in, pltpu.with_memory_space_constraint(index_states, pltpu.VMEM))
 
 
-def forward(place, got, slot, questions, reader, w_up, w_down):
+def near(array):
+    return pltpu.with_memory_space_constraint(array, pltpu.VMEM)
+
+
+def turn(w_up):
     width, hidden = w_up.shape
+    return pl.pallas_call(
+        turn_kernel,
+        in_specs=[HBM],
+        out_specs=VMEM,
+        scratch_shapes=[pltpu.VMEM((width, hidden), bf16), pltpu.SemaphoreType.DMA((hidden // WIDE,))],
+        out_shape=jax.ShapeDtypeStruct((hidden, width), bf16),
+        compiler_params=pltpu.CompilerParams(vmem_limit_bytes=24 << 20),
+        cost_estimate=pl.CostEstimate(flops=0, bytes_accessed=16 << 20, transcendentals=0),
+        name="turn",
+    )(far(w_up))
+
+
+def forward(place, got, slot, questions, reader, up_t, w_down):
+    hidden, width = up_t.shape
     rows = Q * K
-    piece = (NX * NY, NZ, HALF_R, HALF_C)
     return pl.pallas_call(
         forward_kernel,
         in_specs=[SMEM, VMEM, VMEM, VMEM, VMEM, HBM, HBM],
-        out_specs=[VMEM] * 6,
+        out_specs=[VMEM] * 7,
         scratch_shapes=[
-            pltpu.VMEM((width, hidden), bf16),
+            pltpu.VMEM((hidden, rows), bf16),
             pltpu.VMEM((hidden, width), bf16),
-            pltpu.VMEM((rows, hidden), bf16),
-            pltpu.VMEM((2, CHUNK, width), f32),
             pltpu.SemaphoreType.DMA((2, hidden // WIDE)),
         ],
         out_shape=(
             jax.ShapeDtypeStruct((Q, K), f32),
             jax.ShapeDtypeStruct((rows, width), bf16),
             jax.ShapeDtypeStruct((rows, width), bf16),
-            jax.ShapeDtypeStruct((rows, hidden), f32),
-            jax.ShapeDtypeStruct(piece, bf16),
-            jax.ShapeDtypeStruct(piece, bf16),
+            jax.ShapeDtypeStruct((hidden, rows), f32),
+            jax.ShapeDtypeStruct((hidden // NC, rows), bf16),
+            jax.ShapeDtypeStruct((hidden // NC + 2 * width, rows), bf16),
+            pltpu.VMEM((hidden, width), bf16),
         ),
-        compiler_params=pltpu.CompilerParams(vmem_limit_bytes=32 << 20),
+        compiler_params=pltpu.CompilerParams(vmem_limit_bytes=24 << 20),
         cost_estimate=pl.CostEstimate(
-            flops=6 * rows * width * hidden, bytes_accessed=24 << 20, transcendentals=rows * hidden
+            flops=4 * rows * width * hidden, bytes_accessed=16 << 20, transcendentals=rows * hidden
         ),
         name="forward",
-    )(place, got, slot, questions, reader, far(w_up), far(w_down))
-
-
-def backward(place, grad_emb, states, slope, w_down):
+    )(place, got, slot, questions, reader, far(up_t), far(w_down))
+
+
+def backward(place, grad_emb, slope, w_down):
     hidden, width = w_down.shape
     rows = Q * K
-    piece = (NX * NY, NZ, HALF_R, HALF_C)
     return pl.pallas_call(
         backward_kernel,
-        in_specs=[SMEM, VMEM, VMEM, VMEM, HBM],
+        in_specs=[SMEM] + [VMEM] * 3,
         out_specs=[VMEM] * 2,
-        scratch_shapes=[
-            pltpu.VMEM((hidden, width), bf16),
-            pltpu.VMEM((rows, hidden), bf16),
-            pltpu.VMEM((2, CHUNK, width), f32),
-            pltpu.SemaphoreType.DMA((hidden // WIDE,)),
-        ],
-        out_shape=(jax.ShapeDtypeStruct(piece, bf16), jax.ShapeDtypeStruct(piece, bf16)),
+        scratch_shapes=[pltpu.VMEM((hidden, rows), bf16)],
+        out_shape=(jax.ShapeDtypeStruct((hidden // NC, rows), bf16),) * 2,
         compiler_params=pltpu.CompilerParams(vmem_limit_bytes=24 << 20),
         cost_estimate=pl.CostEstimate(
-            flops=4 * rows * width * hidden, bytes_accessed=16 << 20, transcendentals=0
+            flops=2 * rows * width * hidden, bytes_accessed=8 << 20, transcendentals=0
         ),
         name="backward",
-    )(place, grad_emb, states, slope, far(w_down))
+    )(place, grad_emb, slope, near(w_down))
+
+
+def gradient(place, mine, came, right, pack, right_at, x_first, name):
+    rows, width = right.shape
+    piece = (4, NZ, HALF_R, HALF_C)
+    return pl.pallas_call(
+        functools.partial(gradient_kernel, x_first, right_at),
+        in_specs=[SMEM] + [VMEM] * 4,
+        out_specs=[VMEM] * 4,
+        scratch_shapes=[pltpu.VMEM((2, 2 * NY * OWN, width), f32)],
+        out_shape=(jax.ShapeDtypeStruct(piece, f32),) * 2 + (jax.ShapeDtypeStruct(piece, bf16),) * 2,
+        compiler_params=pltpu.CompilerParams(vmem_limit_bytes=24 << 20),
+        cost_estimate=pl.CostEstimate(
+            flops=4 * rows * width * mine.shape[0], bytes_accessed=8 << 20, transcendentals=0
+        ),
+        name=name,
+    )(place, mine, came, right, pack)
 
 
 def halves(array):
@@ -334,8 +396,7 @@
     return array[half:], array[:half]
 
 
-def sum_plane(keep, send, steps):
-    next_keep, keep, next_send, send = lax.optimization_barrier((*apart(keep), *apart(send)))
+def sum_plane(next_keep, keep, next_send, send, steps):
     ahead, rest = swap(next_send, steps[0]), swap(send, steps[0])
     next_send, send = apart((ahead.astype(f32) + next_keep).astype(bf16))
     next_send, send = lax.optimization_barrier((next_send, send))
@@ -354,23 +415,29 @@
     place = jnp.stack([z, y, c, x]).astype(i32)
 
     send_rows, slot, index_near = route(owners.reshape(Q, K), passage_rows, index_states, shards)
+    send_rows, place = lax.optimization_barrier((send_rows, place))
     rows_in = lax.all_to_all(send_rows, "shard", split_axis=0, concat_axis=0, tiled=True)
     states_out = fetch(rows_in, index_near)
     got = lax.all_to_all(states_out, "shard", split_axis=0, concat_axis=0, tiled=True)
-    derivative, states, grad_emb, slope, keep_down, send_down = forward(
-        place, got.reshape(shards * CAP, width), slot, questions, reader, w_up, w_down
+    derivative, states, grad_emb, slope, hidden, pack, down = forward(
+        place, got.reshape(shards * CAP, width), slot, questions, reader, turn(w_up), w_down
     )
-    keep_up, send_up = backward(place, grad_emb, states, slope, w_down)
-
-    down = sum_plane(*meet(keep_down, send_down, "c"), ("x1", "x2", "y1", "y2"))
-    up = sum_plane(*meet(keep_up, send_up, "c"), ("y1", "y2", "x1", "x2"))
+    pack = swap(pack, "c")
+    grad_pre, other = backward(place, grad_emb, slope, down)
+    other = swap(other, "c")
+    units = hidden.shape[0]
+    down = gradient(place, hidden, pack, grad_emb, pack, units, True, "gradient_down")
+    down, other = lax.optimization_barrier((down, other))
+    up = gradient(place, grad_pre, other, states, pack, units + width, False, "gradient_up")
+    down = sum_plane(*down, ("x1", "x2", "y1", "y2"))
+    up = sum_plane(*up, ("y1", "y2", "x1", "x2"))
     both = jnp.concatenate([down, up])
     both = both.reshape(2, NZ, HALF_R, HALF_C).swapaxes(0, 1)
     keep, send = halves(both)
     send = send.astype(bf16)
     for step in ("z1", "z2"):
         keep, send = meet(keep, send, step)
-    mine = total(keep, send, "z3")[0]
+    mine = total(keep, send, "z3")[0].astype(bf16)
 
     label = label4(x, c)
     came = swap(mine, "x2")
@@ -379,7 +446,7 @@
     came = swap(mine, "x1")
     first = (label >> 1) == 0
     mine = jnp.concatenate([jnp.where(first, mine, came), jnp.where(first, came, mine)], 2)
-    return derivative, mine[1], mine[0]
+    return derivative, mine[1].astype(f32), mine[0].astype(f32)
 
 
 def solution(mesh):

time: 148 us -> 142 us (0.959)
  waiting for transfers between devices: 71.7 us -> 64.8 us
  local copies, waits for them, and re-layouts: 0.91 us -> 2.49 us
  Pallas kernels: 21.1 us -> 22.6 us
    all_to_all x1, waiting for transfers between devices: 23.2 us -> 18.3 us  [on_device(): lax.all_to_all(states_out, 'shard', split_axis=0, concat_axis=0, tiled=True)]
    pallas_call x1 -> x4, Pallas kernels: 6.1 us -> 9.28 us  [the longest x2 4.34 us: gradient(): pl.pallas_call(functools.partial(gradient_kernel, x_first, right_at), in_...]
    unnamed x6 -> x8, local copies, waits for them, and re-layouts: 0.01 us -> 2.15 us
    ppermute x19, waiting for transfers between devices: 48.5 us -> 46.5 us  [swap(): return lax.ppermute(array, AXES, partner(step))]
    pallas_call x1, Pallas kernels: 10.3 us -> 8.59 us  [forward(): pl.pallas_call(forward_kernel, in_specs=[SMEM, VMEM, VMEM, VMEM, VMEM, HB...]
  transfers between devices with their start and end apart: 20 -> 20, of which waited for: 12 -> 13; matrix products, arithmetic and copies ran while one was open for 2% -> 1% of each run, Pallas kernels for 4% -> 7%
where the time goes in v5:
time: 142 us
  waiting for transfers between devices  64.8 us (46%)
  starting transfers between devices  30.3 us (21%)
  Pallas kernels  22.6 us (16%)
  blocking collectives  19 us (13%)
  local copies, waits for them, and re-layouts  2.49 us (2%)
  other arithmetic  1.91 us (1%)
    ppermute x19, waiting for transfers between devices, swap(): return lax.ppermute(array, AXES, partner(step))  46.5 us
    ppermute x19, starting transfers between devices, swap(): return lax.ppermute(array, AXES, partner(step))  23.9 us
    all_to_all x1, blocking collectives, on_device(): lax.all_to_all(send_rows, 'shard', split_axis=0, concat_axis=0, tiled=True)  19 us
    all_to_all x1, waiting for transfers between devices, on_device(): lax.all_to_all(states_out, 'shard', split_axis=0, concat_axis=0, tiled=True)  18.3 us
    pallas_call x1, Pallas kernels, forward(): pl.pallas_call(forward_kernel, in_specs=[SMEM, VMEM, VMEM, VMEM, VMEM, HB...  8.59 us
    all_to_all x1, starting transfers between devices, on_device(): lax.all_to_all(states_out, 'shard', split_axis=0, concat_axis=0, tiled=True)  6.44 us
    pallas_call x2, Pallas kernels, gradient(): pl.pallas_call(functools.partial(gradient_kernel, x_first, right_at), in_...  4.34 us
  transfers between devices with their start and end apart: 20, of which 13 were waited for; matrix products, arithmetic and copies ran while one was open for 1% of the time, Pallas kernels for 7%

profile of v5, /device:TPU:64, one launch (start us, length us, event | category | flops | bytes accessed | tf_op | source)
XLA Modules:
  0.0 142.1 jit_solution(11646582280325449968)
XLA Ops:
  0.6 2.8 %route.1 = (s32[64,1,128]{2,1,0:T(1,128)}, s32[256,128]{1,0:T(8,128)}, bf16[1024,768]{1,0:T(8,128)(2,1)S(1)}) custom-call(s32[8,32]{1,0:T(8,128)} %bitcast.21, s32[8,32]{1,0:T(8,128)} %row_ref.1, bf16[1024,768]{1,0:T(8,128)(2,1)} %index_hbm.1), custom_call_target="tpu_custom_call" | custom-call | tf_op jit(solution)/shard_map/route/pallas_call | solution.py:270
  3.5 19.0 %all_to_all.10.rows_ref = s32[64,1,128]{2,1,0:T(1,128)S(1)} all-to-all(s32[64,1,128]{2,1,0:T(1,128)} %get-tuple-element.40), channel_id=1, replica_groups=mesh['shard'=64,'rep'=4] {'shard'}, dimensions={0} | all-to-all | bytes 65536 | tf_op jit(solution)/shard_map/all_to_all | solution.py:419
  22.5 2.0 %fetch.1 = bf16[64,8,768]{2,1,0:T(8,128)(2,1)} custom-call(s32[64,1,128]{2,1,0:T(1,128)S(1)} %all_to_all.10.rows_ref, bf16[1024,768]{1,0:T(8,128)(2,1)S(1)} %get-tuple-element.41.index_ref), custom_call_target="tpu_custom_call" | custom-call | tf_op jit(solution)/shard_map/fetch/pallas_call | solution.py:286
  24.5 6.4 %all-to-all-start.1 = ((bf16[64,8,768]{2,1,0:T(8,128)(2,1)}), bf16[64,8,768]{2,1,0:T(8,128)(2,1)S(1)}, u32[]{:S(2)}, u32[]{:S(2)}) async-start(bf16[64,8,768]{2,1,0:T(8,128)(2,1)} %fetch.1), calls=%async_computation.1 | async-start | bytes 1572864 | tf_op jit(solution)/shard_map/all_to_all | solution.py:421
  31.0 2.8 %turn.1.up_t_hbm = bf16[3072,768]{1,0:T(8,128)(2,1)S(1)} custom-call(bf16[768,3072]{1,0:T(8,128)(2,1)} %up_hbm.1), custom_call_target="tpu_custom_call" | custom-call | bytes 16777216 | tf_op jit(solution)/shard_map/turn/pallas_call | solution.py:300
  33.8 2.1 %copy-done = bf16[3072,768]{1,0:T(8,128)(2,1)} copy-done((bf16[3072,768]{1,0:T(8,128)(2,1)}, bf16[3072,768]{1,0:T(8,128)(2,1)S(1)}, u32[]{:S(2)}) %copy-start) | copy-done | bytes 4718616
  35.9 18.3 %all-to-all-done.1 = bf16[64,8,768]{2,1,0:T(8,128)(2,1)S(1)} async-done(((bf16[64,8,768]{2,1,0:T(8,128)(2,1)}), bf16[64,8,768]{2,1,0:T(8,128)(2,1)S(1)}, u32[]{:S(2)}, u32[]{:S(2)}) %all-to-all-start.1) | async-done | bytes 786464 | tf_op jit(solution)/shard_map/all_to_all | solution.py:421
  54.3 8.6 %forward.1 = (f32[8,32]{1,0:T(8,128)}, bf16[256,768]{1,0:T(8,128)(2,1)S(1)}, bf16[256,768]{1,0:T(8,128)(2,1)S(1)}, f32[3072,256]{1,0:T(8,128)S(1)}, bf16[1536,25...) custom-call(s32[4]{0:T(128)S(1)} %pad_add_fusion.place_ref, ...), custom_call_target="tpu_custom_call" | custom-call | flops 2415919104 | bytes 16777216 | tf_op jit(solution)/shard_map/forward/pallas_call | solution.py:315
  63.0 2.1 %backward.1 = (bf16[1536,256]{1,0:T(8,128)(2,1)S(1)}, bf16[1536,256]{1,0:T(8,128)(2,1)S(1)}) custom-call(s32[4]{0:T(128)S(1)} %pad_add_fusion.place_ref, bf16[256,768]{1,0:T(8,128)(2,1)S(1)} %get-tuple-element.46.right_ref.grad_emb_ref, f32[3072,256]{1,0:T(8,128)S(1)} %get-tuple-element.51.slope_ref, bf16[3072,768]{1,0:T(8,128)(2,1)S(1)} %get-tuple-element.52.down_ref), custom_call_target="tpu_custom_call" | custom-call | flops 1207959552 | bytes 8388608 | tf_op jit(solution)/shard_map/backward/pallas_call | solution.py:344
  66.4 2.2 %gradient_down.1 = (f32[4,8,24,384]{3,2,1,0:T(8,128)S(1)}, f32[4,8,24,384]{3,2,1,0:T(8,128)S(1)}, bf16[4,8,24,384]{3,2,1,0:T(8,128)(2,1)S(1)}, bf16[4,8,24,384]{3,2,1,0:T(8,128)(2,1)S(1)}) custom-call(s32[4]{0:T(128)S(1)} %pad_add_fusion.place_ref, bf16[1536,256]{1,0:T(8,128)(2,1)S(1)} %get-tuple-element.44.mine_ref, ...), custom_call_target="tpu_custom_call" | custom-call | flops 1207959552 | bytes 8388608 | tf_op jit(solution)/shard_map/gradient_down/pallas_call | solution.py:361
  68.6 1.6 %collective-permute-start.2 = (bf16[4,8,24,384]{3,2,1,0:T(8,128)(2,1)S(1)}, bf16[4,8,24,384]{3,2,1,0:T(8,128)(2,1)S(1)}, u32[]{:S(2)}, u32[]{:S(2)}) collective-permute-start(bf16[4,8,24,384]{3,2,1,0:T(8,128)(2,1)S(1)} %get-tuple-element.54), channel_id=1, source_target_pairs={{0,1},{1,0},{2,3},{3,2},{4,7},{5,6},{6,5},{7,4},{8,9},{9,8},{10,11... | collective-permute-start | bytes 1769480 | tf_op jit(solution)/shard_map/ppermute | solution.py:81
  70.7 2.2 %gradient_up.1 = (f32[4,8,24,384]{3,2,1,0:T(8,128)S(1)}, f32[4,8,24,384]{3,2,1,0:T(8,128)S(1)}, bf16[4,8,24,384]{3,2,1,0:T(8,128)(2,1)S(1)}, bf16[4,8,24,384]{3,2,1,0:T(8,128)(2,1)S(1)}) custom-call(s32[4]{0:T(128)S(1)} %pad_add_fusion.place_ref, bf16[1536,256]{1,0:T(8,128)(2,1)S(1)} %get-tuple-element.62.mine_ref, ...), custom_call_target="tpu_custom_call" | custom-call | flops 1207959552 | bytes 8388608 | tf_op jit(solution)/shard_map/gradient_up/pallas_call | solution.py:361
  73.4 1.6 %collective-permute-start.10 = (bf16[4,8,24,384]{3,2,1,0:T(8,128)(2,1)S(1)}, bf16[4,8,24,384]{3,2,1,0:T(8,128)(2,1)S(1)}, u32[]{:S(2)}, u32[]{:S(2)}) collective-permute-start(bf16[4,8,24,384]{3,2,1,0:T(8,128)(2,1)S(1)} %get-tuple-element.69), channel_id=1, source_target_pairs={{0,8},{1,9},{2,10},{3,11},{4,28},{5,29},{6,30},{7,31},{8,0},{9,1},... | collective-permute-start | bytes 1769480 | tf_op jit(solution)/shard_map/ppermute | solution.py:81
  75.0 3.6 %collective-permute-done.2 = bf16[4,8,24,384]{3,2,1,0:T(8,128)(2,1)S(1)} collective-permute-done((bf16[4,8,24,384]{3,2,1,0:T(8,128)(2,1)S(1)}, bf16[4,8,24,384]{3,2,1,0:T(8,128)(2,1)S(1)}, u32[]{:S(2)}, u32[]{:S(2)}) %collective-permute-start.2) | collective-permute-done | bytes 589856 | tf_op jit(solution)/shard_map/ppermute | solution.py:81
  78.8 2.8 %collective-permute-start.3 = (bf16[2,8,24,384]{3,2,1,0:T(8,128)(2,1)S(1)}, bf16[2,8,24,384]{3,2,1,0:T(8,128)(2,1)S(1)}, u32[]{:S(2)}, u32[]{:S(2)}) collective-permute-start(bf16[2,8,24,384]{3,2,1,0:T(8,128)(2,1)S(1)} %get-tuple-element.56), channel_id=1, source_target_pairs={{0,3},{1,2},{2,1},{3,0},{4,5},{5,4},{6,7},{7,6},{8,11},{9,10},{10,... | collective-permute-start | bytes 884744 | tf_op jit(solution)/shard_map/ppermute | solution.py:81
  82.1 5.9 %collective-permute-done.4 = bf16[4,8,24,384]{3,2,1,0:T(8,128)(2,1)S(1)} collective-permute-done((bf16[4,8,24,384]{3,2,1,0:T(8,128)(2,1)S(1)}, bf16[4,8,24,384]{3,2,1,0:T(8,128)(2,1)S(1)}, u32[]{:S(2)}, u32[]{:S(2)}) %collective-permute-start.4) | collective-permute-done | bytes 589856 | tf_op jit(solution)/shard_map/ppermute | solution.py:81
  88.5 1.6 %collective-permute-start.9 = (bf16[2,8,24,384]{3,2,1,0:T(8,128)(2,1)S(1)}, bf16[2,8,24,384]{3,2,1,0:T(8,128)(2,1)S(1)}, u32[]{:S(2)}, u32[]{:S(2)}) collective-permute-start(bf16[2,8,24,384]{3,2,1,0:T(8,128)(2,1)S(1)} %get-tuple-element.67), channel_id=1, source_target_pairs={{0,24},{1,25},{2,26},{3,27},{4,12},{5,13},{6,14},{7,15},{8,16},{9,... | collective-permute-start | bytes 884744 | tf_op jit(solution)/shard_map/ppermute | solution.py:81
  90.0 1.8 %collective-permute-start.12 = (bf16[2,8,24,384]{3,2,1,0:T(8,128)(2,1)S(1)}, bf16[2,8,24,384]{3,2,1,0:T(8,128)(2,1)S(1)}, u32[]{:S(2)}, u32[]{:S(2)}) collective-permute-start(bf16[2,8,24,384]{3,2,1,0:T(8,128)(2,1)S(1)} %get-tuple-element.72), channel_id=1, source_target_pairs={{0,24},{1,25},{2,26},{3,27},{4,12},{5,13},{6,14},{7,15},{8,16},{9,... | collective-permute-start | bytes 884744 | tf_op jit(solution)/shard_map/ppermute | solution.py:81
  92.2 6.4 %collective-permute-done.9 = bf16[2,8,24,384]{3,2,1,0:T(8,128)(2,1)S(1)} collective-permute-done((bf16[2,8,24,384]{3,2,1,0:T(8,128)(2,1)S(1)}, bf16[2,8,24,384]{3,2,1,0:T(8,128)(2,1)S(1)}, u32[]{:S(2)}, u32[]{:S(2)}) %collective-permute-start.9) | collective-permute-done | bytes 294944 | tf_op jit(solution)/shard_map/ppermute | solution.py:81
  98.6 2.2 %collective-permute-start.11 = (bf16[2,8,24,384]{3,2,1,0:T(8,128)(2,1)S(1)}, bf16[2,8,24,384]{3,2,1,0:T(8,128)(2,1)S(1)}, u32[]{:S(2)}, u32[]{:S(2)}) collective-permute-start(bf16[2,8,24,384]{3,2,1,0:T(8,128)(2,1)S(1)} %add_convert_fusion.2), channel_id=1, source_target_pairs={{0,1},{1,0},{2,3},{3,2},{4,7},{5,6},{6,5},{7,4},{8,9},{9,8},{10,11... | collective-permute-start | bytes 884744 | tf_op jit(solution)/shard_map/ppermute | solution.py:81
  101.0 1.6 %collective-permute-start.7 = (bf16[1,8,24,384]{3,2,1,0:T(8,128)(2,1)S(1)}, bf16[1,8,24,384]{3,2,1,0:T(8,128)(2,1)S(1)}, u32[]{:S(2)}, u32[]{:S(2)}) collective-permute-start(bf16[1,8,24,384]{3,2,1,0:T(8,128)(2,1)S(1)} %slice.156), channel_id=1, source_target_pairs={{0,24},{1,25},{2,26},{3,27},{4,12},{5,13},{6,14},{7,15},{8,16},{9,... | collective-permute-start | bytes 442376 | tf_op jit(solution)/shard_map/ppermute | solution.py:81
  102.8 4.3 %collective-permute-done.11 = bf16[2,8,24,384]{3,2,1,0:T(8,128)(2,1)S(1)} collective-permute-done((bf16[2,8,24,384]{3,2,1,0:T(8,128)(2,1)S(1)}, bf16[2,8,24,384]{3,2,1,0:T(8,128)(2,1)S(1)}, u32[]{:S(2)}, u32[]{:S(2)}) %collective-permute-start.11) | collective-permute-done | bytes 294944 | tf_op jit(solution)/shard_map/ppermute | solution.py:81
  107.3 2.7 %collective-permute-start.13 = (bf16[1,8,24,384]{3,2,1,0:T(8,128)(2,1)S(1)}, bf16[1,8,24,384]{3,2,1,0:T(8,128)(2,1)S(1)}, u32[]{:S(2)}, u32[]{:S(2)}) collective-permute-start(bf16[1,8,24,384]{3,2,1,0:T(8,128)(2,1)S(1)} %slice.155), channel_id=1, source_target_pairs={{0,3},{1,2},{2,1},{3,0},{4,5},{5,4},{6,7},{7,6},{8,11},{9,10},{10,... | collective-permute-start | bytes 442376 | tf_op jit(solution)/shard_map/ppermute | solution.py:81
  110.0 3.7 %collective-permute-done.13 = bf16[1,8,24,384]{3,2,1,0:T(8,128)(2,1)S(1)} collective-permute-done((bf16[1,8,24,384]{3,2,1,0:T(8,128)(2,1)S(1)}, bf16[1,8,24,384]{3,2,1,0:T(8,128)(2,1)S(1)}, u32[]{:S(2)}, u32[]{:S(2)}) %collective-permute-start.13) | collective-permute-done | bytes 147488 | tf_op jit(solution)/shard_map/ppermute | solution.py:81
  113.8 0.9 collective-permute-start.14
  114.7 4.3 %collective-permute-done.14 = bf16[4,2,24,384]{3,2,0,1:T(8,128)(2,1)S(1)} collective-permute-done((bf16[4,2,24,384]{3,2,0,1:T(8,128)(2,1)S(1)}, bf16[4,2,24,384]{3,2,0,1:T(8,128)(2,1)S(1)}, u32[]{:S(2)}, u32[]{:S(2)}) %collective-permute-start.14) | collective-permute-done | bytes 147488 | tf_op jit(solution)/shard_map/ppermute | solution.py:81
  119.6 5.0 %collective-permute-done.15 = bf16[2,2,24,384]{3,2,0,1:T(8,128)(2,1)S(1)} collective-permute-done((bf16[2,2,24,384]{3,2,0,1:T(8,128)(2,1)S(1)}, bf16[2,2,24,384]{3,2,0,1:T(8,128)(2,1)S(1)}, u32[]{:S(2)}, u32[]{:S(2)}) %collective-permute-start.15) | collective-permute-done | bytes 73760 | tf_op jit(solution)/shard_map/ppermute | solution.py:81
  124.5 1.4 %collective-permute-start.16 = (bf16[1,2,24,384]{3,2,0,1:T(8,128)(2,1)S(1)}, bf16[1,2,24,384]{3,2,0,1:T(8,128)(2,1)S(1)}, u32[]{:S(2)}, u32[]{:S(2)}) collective-permute-start(bf16[1,2,24,384]{3,2,0,1:T(8,128)(2,1)S(1)} %fusion.6), channel_id=1, source_target_pairs={{0,224},{1,225},{2,226},{3,227},{4,36},{5,37},{6,38},{7,39},{8,232... | collective-permute-start | bytes 110600 | tf_op jit(solution)/shard_map/ppermute | solution.py:81
  126.0 5.6 %collective-permute-done.16 = bf16[1,2,24,384]{3,2,0,1:T(8,128)(2,1)S(1)} collective-permute-done((bf16[1,2,24,384]{3,2,0,1:T(8,128)(2,1)S(1)}, bf16[1,2,24,384]{3,2,0,1:T(8,128)(2,1)S(1)}, u32[]{:S(2)}, u32[]{:S(2)}) %collective-permute-start.16) | collective-permute-done | bytes 36896 | tf_op jit(solution)/shard_map/ppermute | solution.py:81
  131.6 2.7 %collective-permute-start.17 = (bf16[2,24,384]{2,1,0:T(8,128)(2,1)S(1)}, bf16[2,24,384]{2,1,0:T(8,128)(2,1)S(1)}, u32[]{:S(2)}, u32[]{:S(2)}) collective-permute-start(bf16[2,24,384]{2,1,0:T(8,128)(2,1)S(1)} %fusion.9), channel_id=1, source_target_pairs={{0,3},{1,2},{2,1},{3,0},{4,5},{5,4},{6,7},{7,6},{8,11},{9,10},{10,... | collective-permute-start | bytes 110600 | tf_op jit(solution)/shard_map/ppermute | solution.py:81
  134.3 2.6 %collective-permute-done.17 = bf16[2,24,384]{2,1,0:T(8,128)(2,1)S(1)} collective-permute-done((bf16[2,24,384]{2,1,0:T(8,128)(2,1)S(1)}, bf16[2,24,384]{2,1,0:T(8,128)(2,1)S(1)}, u32[]{:S(2)}, u32[]{:S(2)}) %collective-permute-start.17) | collective-permute-done | bytes 36896 | tf_op jit(solution)/shard_map/ppermute | solution.py:81
  137.0 4.3 %collective-permute-done.18 = bf16[2,48,384]{2,1,0:T(8,128)(2,1)S(1)} collective-permute-done((bf16[2,48,384]{2,1,0:T(8,128)(2,1)S(1)}, bf16[2,48,384]{2,1,0:T(8,128)(2,1)S(1)}, u32[]{:S(2)}, u32[]{:S(2)}) %collective-permute-start.18) | collective-permute-done | bytes 73760 | tf_op jit(solution)/shard_map/ppermute | solution.py:81
  (50 shorter events, 6.2 us)
Async XLA Ops:
  24.5 29.8 %all-to-all-start.1 = ((bf16[64,8,768]{2,1,0:T(8,128)(2,1)}), bf16[64,8,768]{2,1,0:T(8,128)(2,1)S(1)}, u32[]{:S(2)}, u32[]{:S(2)}) async-start(bf16[64,8,768]{2,1,0:T(8,128)(2,1)} %fetch.1), calls=%async_computation.1 | async-start | bytes 1572864 | tf_op jit(solution)/shard_map/all_to_all | solution.py:421
  31.0 23.3 %copy-start.1 = (s32[256,128]{1,0:T(8,128)S(1)}, s32[256,128]{1,0:T(8,128)}, u32[]{:S(2)}) copy-start(s32[256,128]{1,0:T(8,128)} %get-tuple-element.42.slot_ref) | copy-start | bytes 393220
  31.0 23.3 %copy-start.2 = (bf16[8,768]{1,0:T(8,128)(2,1)S(1)}, bf16[8,768]{1,0:T(8,128)(2,1)}, u32[]{:S(2)}) copy-start(bf16[8,768]{1,0:T(8,128)(2,1)} %question_ref.1) | copy-start | bytes 36868
  31.0 23.3 %copy-start.3 = (f32[8,32]{1,0:T(8,128)S(1)}, f32[8,32]{1,0:T(8,128)}, u32[]{:S(2)}) copy-start(f32[8,32]{1,0:T(8,128)} %reader_ref.1) | copy-start | bytes 3076
  33.8 2.1 %copy-start = (bf16[3072,768]{1,0:T(8,128)(2,1)}, bf16[3072,768]{1,0:T(8,128)(2,1)S(1)}, u32[]{:S(2)}) copy-start(bf16[3072,768]{1,0:T(8,128)(2,1)S(1)} %turn.1.up_t_hbm) | copy-start | bytes 14155780
  62.9 3.5 %collective-permute-start = (bf16[3072,256]{1,0:T(8,128)(2,1)S(1)}, bf16[3072,256]{1,0:T(8,128)(2,1)S(1)}, u32[]{:S(2)}, u32[]{:S(2)}) collective-permute-start(bf16[3072,256]{1,0:T(8,128)(2,1)S(1)} %get-tuple-element.45), channel_id=1, source_target_pairs={{0,4},{1,5},{2,6},{3,7},{4,0},{5,1},{6,2},{7,3},{8,12},{9,13},{10,... | collective-permute-start | bytes 4718600 | tf_op jit(solution)/shard_map/ppermute | solution.py:81
  65.1 3.4 %collective-permute-start.1 = (bf16[1536,256]{1,0:T(8,128)(2,1)S(1)}, bf16[1536,256]{1,0:T(8,128)(2,1)S(1)}, u32[]{:S(2)}, u32[]{:S(2)}) collective-permute-start(bf16[1536,256]{1,0:T(8,128)(2,1)S(1)} %get-tuple-element.53), channel_id=1, source_target_pairs={{0,4},{1,5},{2,6},{3,7},{4,0},{5,1},{6,2},{7,3},{8,12},{9,13},{10,... | collective-permute-start | bytes 2359304 | tf_op jit(solution)/shard_map/ppermute | solution.py:81
  68.6 10.0 %collective-permute-start.2 = (bf16[4,8,24,384]{3,2,1,0:T(8,128)(2,1)S(1)}, bf16[4,8,24,384]{3,2,1,0:T(8,128)(2,1)S(1)}, u32[]{:S(2)}, u32[]{:S(2)}) collective-permute-start(bf16[4,8,24,384]{3,2,1,0:T(8,128)(2,1)S(1)} %get-tuple-element.54), channel_id=1, source_target_pairs={{0,1},{1,0},{2,3},{3,2},{4,7},{5,6},{6,5},{7,4},{8,9},{9,8},{10,11... | collective-permute-start | bytes 1769480 | tf_op jit(solution)/shard_map/ppermute | solution.py:81
  70.2 17.9 %collective-permute-start.4 = (bf16[4,8,24,384]{3,2,1,0:T(8,128)(2,1)S(1)}, bf16[4,8,24,384]{3,2,1,0:T(8,128)(2,1)S(1)}, u32[]{:S(2)}, u32[]{:S(2)}) collective-permute-start(bf16[4,8,24,384]{3,2,1,0:T(8,128)(2,1)S(1)} %get-tuple-element.58), channel_id=1, source_target_pairs={{0,1},{1,0},{2,3},{3,2},{4,7},{5,6},{6,5},{7,4},{8,9},{9,8},{10,11... | collective-permute-start | bytes 1769480 | tf_op jit(solution)/shard_map/ppermute | solution.py:81
  72.9 15.4 %collective-permute-start.8 = (bf16[4,8,24,384]{3,2,1,0:T(8,128)(2,1)S(1)}, bf16[4,8,24,384]{3,2,1,0:T(8,128)(2,1)S(1)}, u32[]{:S(2)}, u32[]{:S(2)}) collective-permute-start(bf16[4,8,24,384]{3,2,1,0:T(8,128)(2,1)S(1)} %get-tuple-element.65), channel_id=1, source_target_pairs={{0,8},{1,9},{2,10},{3,11},{4,28},{5,29},{6,30},{7,31},{8,0},{9,1},... | collective-permute-start | bytes 1769480 | tf_op jit(solution)/shard_map/ppermute | solution.py:81
  73.4 18.4 %collective-permute-start.10 = (bf16[4,8,24,384]{3,2,1,0:T(8,128)(2,1)S(1)}, bf16[4,8,24,384]{3,2,1,0:T(8,128)(2,1)S(1)}, u32[]{:S(2)}, u32[]{:S(2)}) collective-permute-start(bf16[4,8,24,384]{3,2,1,0:T(8,128)(2,1)S(1)} %get-tuple-element.69), channel_id=1, source_target_pairs={{0,8},{1,9},{2,10},{3,11},{4,28},{5,29},{6,30},{7,31},{8,0},{9,1},... | collective-permute-start | bytes 1769480 | tf_op jit(solution)/shard_map/ppermute | solution.py:81
  78.8 13.2 %collective-permute-start.3 = (bf16[2,8,24,384]{3,2,1,0:T(8,128)(2,1)S(1)}, bf16[2,8,24,384]{3,2,1,0:T(8,128)(2,1)S(1)}, u32[]{:S(2)}, u32[]{:S(2)}) collective-permute-start(bf16[2,8,24,384]{3,2,1,0:T(8,128)(2,1)S(1)} %get-tuple-element.56), channel_id=1, source_target_pairs={{0,3},{1,2},{2,1},{3,0},{4,5},{5,4},{6,7},{7,6},{8,11},{9,10},{10,... | collective-permute-start | bytes 884744 | tf_op jit(solution)/shard_map/ppermute | solution.py:81
  81.6 19.2 %collective-permute-start.6 = (bf16[2,8,24,384]{3,2,1,0:T(8,128)(2,1)S(1)}, bf16[2,8,24,384]{3,2,1,0:T(8,128)(2,1)S(1)}, u32[]{:S(2)}, u32[]{:S(2)}) collective-permute-start(bf16[2,8,24,384]{3,2,1,0:T(8,128)(2,1)S(1)} %get-tuple-element.61), channel_id=1, source_target_pairs={{0,3},{1,2},{2,1},{3,0},{4,5},{5,4},{6,7},{7,6},{8,11},{9,10},{10,... | collective-permute-start | bytes 884744 | tf_op jit(solution)/shard_map/ppermute | solution.py:81
  88.5 10.1 %collective-permute-start.9 = (bf16[2,8,24,384]{3,2,1,0:T(8,128)(2,1)S(1)}, bf16[2,8,24,384]{3,2,1,0:T(8,128)(2,1)S(1)}, u32[]{:S(2)}, u32[]{:S(2)}) collective-permute-start(bf16[2,8,24,384]{3,2,1,0:T(8,128)(2,1)S(1)} %get-tuple-element.67), channel_id=1, source_target_pairs={{0,24},{1,25},{2,26},{3,27},{4,12},{5,13},{6,14},{7,15},{8,16},{9,... | collective-permute-start | bytes 884744 | tf_op jit(solution)/shard_map/ppermute | solution.py:81
  90.0 12.8 %collective-permute-start.12 = (bf16[2,8,24,384]{3,2,1,0:T(8,128)(2,1)S(1)}, bf16[2,8,24,384]{3,2,1,0:T(8,128)(2,1)S(1)}, u32[]{:S(2)}, u32[]{:S(2)}) collective-permute-start(bf16[2,8,24,384]{3,2,1,0:T(8,128)(2,1)S(1)} %get-tuple-element.72), channel_id=1, source_target_pairs={{0,24},{1,25},{2,26},{3,27},{4,12},{5,13},{6,14},{7,15},{8,16},{9,... | collective-permute-start | bytes 884744 | tf_op jit(solution)/shard_map/ppermute | solution.py:81
  92.0 8.8 %collective-permute-start.5 = (bf16[2,8,24,384]{3,2,1,0:T(8,128)(2,1)S(1)}, bf16[2,8,24,384]{3,2,1,0:T(8,128)(2,1)S(1)}, u32[]{:S(2)}, u32[]{:S(2)}) collective-permute-start(bf16[2,8,24,384]{3,2,1,0:T(8,128)(2,1)S(1)} %add_convert_fusion.3), channel_id=1, source_target_pairs={{0,8},{1,9},{2,10},{3,11},{4,28},{5,29},{6,30},{7,31},{8,0},{9,1},... | collective-permute-start | bytes 884744 | tf_op jit(solution)/shard_map/ppermute | solution.py:81
  98.6 8.5 %collective-permute-start.11 = (bf16[2,8,24,384]{3,2,1,0:T(8,128)(2,1)S(1)}, bf16[2,8,24,384]{3,2,1,0:T(8,128)(2,1)S(1)}, u32[]{:S(2)}, u32[]{:S(2)}) collective-permute-start(bf16[2,8,24,384]{3,2,1,0:T(8,128)(2,1)S(1)} %add_convert_fusion.2), channel_id=1, source_target_pairs={{0,1},{1,0},{2,3},{3,2},{4,7},{5,6},{6,5},{7,4},{8,9},{9,8},{10,11... | collective-permute-start | bytes 884744 | tf_op jit(solution)/shard_map/ppermute | solution.py:81
  101.0 9.0 %collective-permute-start.7 = (bf16[1,8,24,384]{3,2,1,0:T(8,128)(2,1)S(1)}, bf16[1,8,24,384]{3,2,1,0:T(8,128)(2,1)S(1)}, u32[]{:S(2)}, u32[]{:S(2)}) collective-permute-start(bf16[1,8,24,384]{3,2,1,0:T(8,128)(2,1)S(1)} %slice.156), channel_id=1, source_target_pairs={{0,24},{1,25},{2,26},{3,27},{4,12},{5,13},{6,14},{7,15},{8,16},{9,... | collective-permute-start | bytes 442376 | tf_op jit(solution)/shard_map/ppermute | solution.py:81
  107.3 6.4 %collective-permute-start.13 = (bf16[1,8,24,384]{3,2,1,0:T(8,128)(2,1)S(1)}, bf16[1,8,24,384]{3,2,1,0:T(8,128)(2,1)S(1)}, u32[]{:S(2)}, u32[]{:S(2)}) collective-permute-start(bf16[1,8,24,384]{3,2,1,0:T(8,128)(2,1)S(1)} %slice.155), channel_id=1, source_target_pairs={{0,3},{1,2},{2,1},{3,0},{4,5},{5,4},{6,7},{7,6},{8,11},{9,10},{10,... | collective-permute-start | bytes 442376 | tf_op jit(solution)/shard_map/ppermute | solution.py:81
  113.8 5.2 %collective-permute-start.14 = (bf16[4,2,24,384]{3,2,0,1:T(8,128)(2,1)S(1)}, bf16[4,2,24,384]{3,2,0,1:T(8,128)(2,1)S(1)}, u32[]{:S(2)}, u32[]{:S(2)}) collective-permute-start(bf16[4,2,24,384]{3,2,0,1:T(8,128)(2,1)S(1)} %slice.154), channel_id=1, source_target_pairs={{0,32},{1,33},{2,34},{3,35},{4,228},{5,229},{6,230},{7,231},{8,40}... | collective-permute-start | bytes 442376 | tf_op jit(solution)/shard_map/ppermute | solution.py:81
  119.1 5.4 %collective-permute-start.15 = (bf16[2,2,24,384]{3,2,0,1:T(8,128)(2,1)S(1)}, bf16[2,2,24,384]{3,2,0,1:T(8,128)(2,1)S(1)}, u32[]{:S(2)}, u32[]{:S(2)}) collective-permute-start(bf16[2,2,24,384]{3,2,0,1:T(8,128)(2,1)S(1)} %get-tuple-element.77), channel_id=1, source_target_pairs={{0,64},{1,65},{2,66},{3,67},{4,196},{5,197},{6,198},{7,199},{8,72}... | collective-permute-start | bytes 221192 | tf_op jit(solution)/shard_map/ppermute | solution.py:81
  124.5 7.1 %collective-permute-start.16 = (bf16[1,2,24,384]{3,2,0,1:T(8,128)(2,1)S(1)}, bf16[1,2,24,384]{3,2,0,1:T(8,128)(2,1)S(1)}, u32[]{:S(2)}, u32[]{:S(2)}) collective-permute-start(bf16[1,2,24,384]{3,2,0,1:T(8,128)(2,1)S(1)} %fusion.6), channel_id=1, source_target_pairs={{0,224},{1,225},{2,226},{3,227},{4,36},{5,37},{6,38},{7,39},{8,232... | collective-permute-start | bytes 110600 | tf_op jit(solution)/shard_map/ppermute | solution.py:81
  131.6 5.3 %collective-permute-start.17 = (bf16[2,24,384]{2,1,0:T(8,128)(2,1)S(1)}, bf16[2,24,384]{2,1,0:T(8,128)(2,1)S(1)}, u32[]{:S(2)}, u32[]{:S(2)}) collective-permute-start(bf16[2,24,384]{2,1,0:T(8,128)(2,1)S(1)} %fusion.9), channel_id=1, source_target_pairs={{0,3},{1,2},{2,1},{3,0},{4,5},{5,4},{6,7},{7,6},{8,11},{9,10},{10,... | collective-permute-start | bytes 110600 | tf_op jit(solution)/shard_map/ppermute | solution.py:81
  136.9 4.4 %collective-permute-start.18 = (bf16[2,48,384]{2,1,0:T(8,128)(2,1)S(1)}, bf16[2,48,384]{2,1,0:T(8,128)(2,1)S(1)}, u32[]{:S(2)}, u32[]{:S(2)}) collective-permute-start(bf16[2,48,384]{2,1,0:T(8,128)(2,1)S(1)} %pad_maximum_fusion.1), channel_id=1, source_target_pairs={{0,1},{1,0},{2,3},{3,2},{4,7},{5,6},{6,5},{7,4},{8,9},{9,8},{10,11... | collective-permute-start | bytes 221192 | tf_op jit(solution)/shard_map/ppermute | solution.py:81

commit v6 on v5

--- a/solution.py
+++ b/solution.py
@@ -396,15 +396,33 @@
     return array[half:], array[:half]
 
 
-def sum_plane(next_keep, keep, next_send, send, steps):
-    ahead, rest = swap(next_send, steps[0]), swap(send, steps[0])
-    next_send, send = apart((ahead.astype(f32) + next_keep).astype(bf16))
-    next_send, send = lax.optimization_barrier((next_send, send))
-    ahead, rest_two = swap(next_send, steps[1]), swap(send, steps[1])
-    next_keep, keep = lax.optimization_barrier(apart(keep + rest.astype(f32)))
-    came = swap((ahead.astype(f32) + next_keep).astype(bf16), steps[2])
-    keep = came.astype(f32) + (keep + rest_two.astype(f32))
-    return swap(keep[1:].astype(bf16), steps[3]).astype(f32) + keep[:1]
+def after(array, other):
+    return lax.optimization_barrier((array, other))[0]
+
+
+def sum_planes(down, up):
+    plans = (("x1", "x2", "y1", "y2"), ("y1", "y2", "x1", "x2"))
+    both = list(zip((down, up), plans))
+    first = [(swap(chain[2], plan[0]), swap(chain[3], plan[0])) for chain, plan in both]
+    ahead, sends = [], []
+    for ((next_keep, *_), plan), (came, _) in zip(both, first):
+        next_send, send = lax.optimization_barrier(apart((came.astype(f32) + next_keep).astype(bf16)))
+        ahead.append(swap(next_send, plan[1]))
+        sends.append((next_send, send))
+    keeps, rest = [], []
+    for at, (((_, keep, *_), plan), (_, came)) in enumerate(zip(both, first)):
+        came = after(came, sends[1][0])
+        next_keep, keep = apart(keep + came.astype(f32))
+        next_keep, keep, send = lax.optimization_barrier((next_keep, keep, sends[at][1]))
+        rest.append(swap(send, plan[1]))
+        keeps.append((next_keep, keep))
+    sends = [(ahead[at].astype(f32) + keeps[at][0]).astype(bf16) for at in range(2)]
+    third = [swap(sends[at], plan[2]) for at, (_, plan) in enumerate(both)]
+    sums = []
+    for at, (_, plan) in enumerate(both):
+        keep = after(third[at], sends[1]).astype(f32) + (keeps[at][1] + rest[at].astype(f32))
+        sums.append(swap(keep[1:].astype(bf16), plan[3]).astype(f32) + keep[:1])
+    return sums
 
 
 def on_device(index_states, questions, reader, owners, passage_rows, w_up, w_down):
@@ -429,9 +447,7 @@
     down = gradient(place, hidden, pack, grad_emb, pack, units, True, "gradient_down")
     down, other = lax.optimization_barrier((down, other))
     up = gradient(place, grad_pre, other, states, pack, units + width, False, "gradient_up")
-    down = sum_plane(*down, ("x1", "x2", "y1", "y2"))
-    up = sum_plane(*up, ("y1", "y2", "x1", "x2"))
-    both = jnp.concatenate([down, up])
+    both = jnp.concatenate(sum_planes(down, up))
     both = both.reshape(2, NZ, HALF_R, HALF_C).swapaxes(0, 1)
     keep, send = halves(both)
     send = send.astype(bf16)

time: 142 us -> 140 us (0.986)
  starting transfers between devices: 30.3 us -> 24.7 us
  waiting for transfers between devices: 64.8 us -> 68.2 us
    ppermute x19, starting transfers between devices: 23.9 us -> 18.3 us  [swap(): return lax.ppermute(array, AXES, partner(step))]
    ppermute x19, waiting for transfers between devices: 46.5 us -> 49.9 us  [swap(): return lax.ppermute(array, AXES, partner(step))]
  transfers between devices with their start and end apart: 20 -> 20, of which waited for: 13 -> 15; matrix products, arithmetic and copies ran while one was open for 1% -> 1% of each run, Pallas kernels for 7% -> 7%
where the time goes in v6:
time: 140 us
  waiting for transfers between devices  68.2 us (49%)
  starting transfers between devices  24.7 us (18%)
  Pallas kernels  22.6 us (16%)
  blocking collectives  19 us (14%)
  local copies, waits for them, and re-layouts  2.49 us (2%)
  other arithmetic  1.9 us (1%)
    ppermute x19, waiting for transfers between devices, swap(): return lax.ppermute(array, AXES, partner(step))  49.9 us
    all_to_all x1, blocking collectives, on_device(): lax.all_to_all(send_rows, 'shard', split_axis=0, concat_axis=0, tiled=True)  19 us
    all_to_all x1, waiting for transfers between devices, on_device(): lax.all_to_all(states_out, 'shard', split_axis=0, concat_axis=0, tiled=True)  18.3 us
    ppermute x19, starting transfers between devices, swap(): return lax.ppermute(array, AXES, partner(step))  18.3 us
    pallas_call x1, Pallas kernels, forward(): pl.pallas_call(forward_kernel, in_specs=[SMEM, VMEM, VMEM, VMEM, VMEM, HB...  8.59 us
    all_to_all x1, starting transfers between devices, on_device(): lax.all_to_all(states_out, 'shard', split_axis=0, concat_axis=0, tiled=True)  6.44 us
    pallas_call x2, Pallas kernels, gradient(): pl.pallas_call(functools.partial(gradient_kernel, x_first, right_at), in_...  4.34 us
    pallas_call x1, Pallas kernels, turn(): pl.pallas_call(turn_kernel, in_specs=[HBM], out_specs=VMEM, scratch_shape...  2.81 us
  transfers between devices with their start and end apart: 20, of which 15 were waited for; matrix products, arithmetic and copies ran while one was open for 1% of the time, Pallas kernels for 7%

profile of v6, /device:TPU:64, one launch (start us, length us, event | category | flops | bytes accessed | tf_op | source)
XLA Modules:
  0.0 139.9 jit_solution(15784550831536407672)
XLA Ops:
  0.6 2.8 %route.1 = (s32[64,1,128]{2,1,0:T(1,128)}, s32[256,128]{1,0:T(8,128)}, bf16[1024,768]{1,0:T(8,128)(2,1)S(1)}) custom-call(s32[8,32]{1,0:T(8,128)} %bitcast.21, s32[8,32]{1,0:T(8,128)} %row_ref.1, bf16[1024,768]{1,0:T(8,128)(2,1)} %index_hbm.1), custom_call_target="tpu_custom_call" | custom-call | tf_op jit(solution)/shard_map/route/pallas_call | solution.py:270
  3.5 19.0 %all_to_all.10.rows_ref = s32[64,1,128]{2,1,0:T(1,128)S(1)} all-to-all(s32[64,1,128]{2,1,0:T(1,128)} %get-tuple-element.46), channel_id=1, replica_groups=mesh['shard'=64,'rep'=4] {'shard'}, dimensions={0} | all-to-all | bytes 65536 | tf_op jit(solution)/shard_map/all_to_all | solution.py:437
  22.5 2.0 %fetch.1 = bf16[64,8,768]{2,1,0:T(8,128)(2,1)} custom-call(s32[64,1,128]{2,1,0:T(1,128)S(1)} %all_to_all.10.rows_ref, bf16[1024,768]{1,0:T(8,128)(2,1)S(1)} %get-tuple-element.47.index_ref), custom_call_target="tpu_custom_call" | custom-call | tf_op jit(solution)/shard_map/fetch/pallas_call | solution.py:286
  24.5 6.4 %all-to-all-start.1 = ((bf16[64,8,768]{2,1,0:T(8,128)(2,1)}), bf16[64,8,768]{2,1,0:T(8,128)(2,1)S(1)}, u32[]{:S(2)}, u32[]{:S(2)}) async-start(bf16[64,8,768]{2,1,0:T(8,128)(2,1)} %fetch.1), calls=%async_computation.1 | async-start | bytes 1572864 | tf_op jit(solution)/shard_map/all_to_all | solution.py:439
  31.0 2.8 %turn.1.up_t_hbm = bf16[3072,768]{1,0:T(8,128)(2,1)S(1)} custom-call(bf16[768,3072]{1,0:T(8,128)(2,1)} %up_hbm.1), custom_call_target="tpu_custom_call" | custom-call | bytes 16777216 | tf_op jit(solution)/shard_map/turn/pallas_call | solution.py:300
  33.8 2.1 %copy-done = bf16[3072,768]{1,0:T(8,128)(2,1)} copy-done((bf16[3072,768]{1,0:T(8,128)(2,1)}, bf16[3072,768]{1,0:T(8,128)(2,1)S(1)}, u32[]{:S(2)}) %copy-start) | copy-done | bytes 4718616
  35.9 18.3 %all-to-all-done.1 = bf16[64,8,768]{2,1,0:T(8,128)(2,1)S(1)} async-done(((bf16[64,8,768]{2,1,0:T(8,128)(2,1)}), bf16[64,8,768]{2,1,0:T(8,128)(2,1)S(1)}, u32[]{:S(2)}, u32[]{:S(2)}) %all-to-all-start.1) | async-done | bytes 786464 | tf_op jit(solution)/shard_map/all_to_all | solution.py:439
  54.3 8.6 %forward.1 = (f32[8,32]{1,0:T(8,128)}, bf16[256,768]{1,0:T(8,128)(2,1)S(1)}, bf16[256,768]{1,0:T(8,128)(2,1)S(1)}, f32[3072,256]{1,0:T(8,128)S(1)}, bf16[1536,25...) custom-call(s32[4]{0:T(128)S(1)} %pad_add_fusion.place_ref, ...), custom_call_target="tpu_custom_call" | custom-call | flops 2415919104 | bytes 16777216 | tf_op jit(solution)/shard_map/forward/pallas_call | solution.py:315
  63.0 2.1 %backward.1 = (bf16[1536,256]{1,0:T(8,128)(2,1)S(1)}, bf16[1536,256]{1,0:T(8,128)(2,1)S(1)}) custom-call(s32[4]{0:T(128)S(1)} %pad_add_fusion.place_ref, bf16[256,768]{1,0:T(8,128)(2,1)S(1)} %get-tuple-element.52.right_ref.grad_emb_ref, f32[3072,256]{1,0:T(8,128)S(1)} %get-tuple-element.57.slope_ref, bf16[3072,768]{1,0:T(8,128)(2,1)S(1)} %get-tuple-element.58.down_ref), custom_call_target="tpu_custom_call" | custom-call | flops 1207959552 | bytes 8388608 | tf_op jit(solution)/shard_map/backward/pallas_call | solution.py:344
  66.4 2.2 %gradient_down.1 = (f32[4,8,24,384]{3,2,1,0:T(8,128)S(1)}, f32[4,8,24,384]{3,2,1,0:T(8,128)S(1)}, bf16[4,8,24,384]{3,2,1,0:T(8,128)(2,1)S(1)}, bf16[4,8,24,384]{3,2,1,0:T(8,128)(2,1)S(1)}) custom-call(s32[4]{0:T(128)S(1)} %pad_add_fusion.place_ref, bf16[1536,256]{1,0:T(8,128)(2,1)S(1)} %get-tuple-element.50.mine_ref, ...), custom_call_target="tpu_custom_call" | custom-call | flops 1207959552 | bytes 8388608 | tf_op jit(solution)/shard_map/gradient_down/pallas_call | solution.py:361
  68.6 1.6 %collective-permute-start.2 = (bf16[4,8,24,384]{3,2,1,0:T(8,128)(2,1)S(1)}, bf16[4,8,24,384]{3,2,1,0:T(8,128)(2,1)S(1)}, u32[]{:S(2)}, u32[]{:S(2)}) collective-permute-start(bf16[4,8,24,384]{3,2,1,0:T(8,128)(2,1)S(1)} %get-tuple-element.60), channel_id=1, source_target_pairs={{0,1},{1,0},{2,3},{3,2},{4,7},{5,6},{6,5},{7,4},{8,9},{9,8},{10,11... | collective-permute-start | bytes 1769480 | tf_op jit(solution)/shard_map/ppermute | solution.py:81
  70.2 2.2 %gradient_up.1 = (f32[4,8,24,384]{3,2,1,0:T(8,128)S(1)}, f32[4,8,24,384]{3,2,1,0:T(8,128)S(1)}, bf16[4,8,24,384]{3,2,1,0:T(8,128)(2,1)S(1)}, bf16[4,8,24,384]{3,2,1,0:T(8,128)(2,1)S(1)}) custom-call(s32[4]{0:T(128)S(1)} %pad_add_fusion.place_ref, bf16[1536,256]{1,0:T(8,128)(2,1)S(1)} %get-tuple-element.65.mine_ref, ...), custom_call_target="tpu_custom_call" | custom-call | flops 1207959552 | bytes 8388608 | tf_op jit(solution)/shard_map/gradient_up/pallas_call | solution.py:361
  73.4 1.6 %collective-permute-start.8 = (bf16[4,8,24,384]{3,2,1,0:T(8,128)(2,1)S(1)}, bf16[4,8,24,384]{3,2,1,0:T(8,128)(2,1)S(1)}, u32[]{:S(2)}, u32[]{:S(2)}) collective-permute-start(bf16[4,8,24,384]{3,2,1,0:T(8,128)(2,1)S(1)} %get-tuple-element.75), channel_id=1, source_target_pairs={{0,8},{1,9},{2,10},{3,11},{4,28},{5,29},{6,30},{7,31},{8,0},{9,1},... | collective-permute-start | bytes 1769480 | tf_op jit(solution)/shard_map/ppermute | solution.py:81
  75.0 3.6 %collective-permute-done.2 = bf16[4,8,24,384]{3,2,1,0:T(8,128)(2,1)S(1)} collective-permute-done((bf16[4,8,24,384]{3,2,1,0:T(8,128)(2,1)S(1)}, bf16[4,8,24,384]{3,2,1,0:T(8,128)(2,1)S(1)}, u32[]{:S(2)}, u32[]{:S(2)}) %collective-permute-start.2) | collective-permute-done | bytes 589856 | tf_op jit(solution)/shard_map/ppermute | solution.py:81
  78.8 2.8 %collective-permute-start.3 = (bf16[2,8,24,384]{3,2,1,0:T(8,128)(2,1)S(1)}, bf16[2,8,24,384]{3,2,1,0:T(8,128)(2,1)S(1)}, u32[]{:S(2)}, u32[]{:S(2)}) collective-permute-start(bf16[2,8,24,384]{3,2,1,0:T(8,128)(2,1)S(1)} %get-tuple-element.62), channel_id=1, source_target_pairs={{0,3},{1,2},{2,1},{3,0},{4,5},{5,4},{6,7},{7,6},{8,11},{9,10},{10,... | collective-permute-start | bytes 884744 | tf_op jit(solution)/shard_map/ppermute | solution.py:81
  82.5 1.6 %collective-permute-start.7 = (bf16[2,8,24,384]{3,2,1,0:T(8,128)(2,1)S(1)}, bf16[2,8,24,384]{3,2,1,0:T(8,128)(2,1)S(1)}, u32[]{:S(2)}, u32[]{:S(2)}) collective-permute-start(bf16[2,8,24,384]{3,2,1,0:T(8,128)(2,1)S(1)} %get-tuple-element.70), channel_id=1, source_target_pairs={{0,24},{1,25},{2,26},{3,27},{4,12},{5,13},{6,14},{7,15},{8,16},{9,... | collective-permute-start | bytes 884744 | tf_op jit(solution)/shard_map/ppermute | solution.py:81
  84.1 3.9 %collective-permute-done.4 = bf16[4,8,24,384]{3,2,1,0:T(8,128)(2,1)S(1)} collective-permute-done((bf16[4,8,24,384]{3,2,1,0:T(8,128)(2,1)S(1)}, bf16[4,8,24,384]{3,2,1,0:T(8,128)(2,1)S(1)}, u32[]{:S(2)}, u32[]{:S(2)}) %collective-permute-start.4) | collective-permute-done | bytes 589856 | tf_op jit(solution)/shard_map/ppermute | solution.py:81
  88.2 2.8 %collective-permute-start.9 = (bf16[2,8,24,384]{3,2,1,0:T(8,128)(2,1)S(1)}, bf16[2,8,24,384]{3,2,1,0:T(8,128)(2,1)S(1)}, u32[]{:S(2)}, u32[]{:S(2)}) collective-permute-start(bf16[2,8,24,384]{3,2,1,0:T(8,128)(2,1)S(1)} %get-tuple-element.81), channel_id=1, source_target_pairs={{0,3},{1,2},{2,1},{3,0},{4,5},{5,4},{6,7},{7,6},{8,11},{9,10},{10,... | collective-permute-start | bytes 884744 | tf_op jit(solution)/shard_map/ppermute | solution.py:81
  91.9 1.2 collective-permute-done.7
  93.5 1.5 %collective-permute-start.12 = (bf16[2,8,24,384]{3,2,1,0:T(8,128)(2,1)S(1)}, bf16[2,8,24,384]{3,2,1,0:T(8,128)(2,1)S(1)}, u32[]{:S(2)}, u32[]{:S(2)}) collective-permute-start(bf16[2,8,24,384]{3,2,1,0:T(8,128)(2,1)S(1)} %get-tuple-element.84), channel_id=1, source_target_pairs={{0,24},{1,25},{2,26},{3,27},{4,12},{5,13},{6,14},{7,15},{8,16},{9,... | collective-permute-start | bytes 884744 | tf_op jit(solution)/shard_map/ppermute | solution.py:81
  95.0 4.1 %collective-permute-done.6 = bf16[2,8,24,384]{3,2,1,0:T(8,128)(2,1)S(1)} collective-permute-done((bf16[2,8,24,384]{3,2,1,0:T(8,128)(2,1)S(1)}, bf16[2,8,24,384]{3,2,1,0:T(8,128)(2,1)S(1)}, u32[]{:S(2)}, u32[]{:S(2)}) %collective-permute-start.6) | collective-permute-done | bytes 294944 | tf_op jit(solution)/shard_map/ppermute | solution.py:81
  99.2 1.3 collective-permute-start.10
  100.5 2.5 %collective-permute-done.12 = bf16[2,8,24,384]{3,2,1,0:T(8,128)(2,1)S(1)} collective-permute-done((bf16[2,8,24,384]{3,2,1,0:T(8,128)(2,1)S(1)}, bf16[2,8,24,384]{3,2,1,0:T(8,128)(2,1)S(1)}, u32[]{:S(2)}, u32[]{:S(2)}) %collective-permute-start.12) | collective-permute-done | bytes 294944 | tf_op jit(solution)/shard_map/ppermute | solution.py:81
  103.1 1.1 collective-permute-start.13
  104.2 1.4 %collective-permute-done.10 = bf16[1,8,24,384]{3,2,1,0:T(8,128)(2,1)S(1)} collective-permute-done((bf16[1,8,24,384]{3,2,1,0:T(8,128)(2,1)S(1)}, bf16[1,8,24,384]{3,2,1,0:T(8,128)(2,1)S(1)}, u32[]{:S(2)}, u32[]{:S(2)}) %collective-permute-start.10) | collective-permute-done | bytes 147488 | tf_op jit(solution)/shard_map/ppermute | solution.py:81
  105.7 3.9 %collective-permute-done.13 = bf16[1,8,24,384]{3,2,1,0:T(8,128)(2,1)S(1)} collective-permute-done((bf16[1,8,24,384]{3,2,1,0:T(8,128)(2,1)S(1)}, bf16[1,8,24,384]{3,2,1,0:T(8,128)(2,1)S(1)}, u32[]{:S(2)}, u32[]{:S(2)}) %collective-permute-start.13) | collective-permute-done | bytes 147488 | tf_op jit(solution)/shard_map/ppermute | solution.py:81
  109.7 0.9 collective-permute-start.14
  110.6 5.9 %collective-permute-done.14 = bf16[4,2,24,384]{3,2,0,1:T(8,128)(2,1)S(1)} collective-permute-done((bf16[4,2,24,384]{3,2,0,1:T(8,128)(2,1)S(1)}, bf16[4,2,24,384]{3,2,0,1:T(8,128)(2,1)S(1)}, u32[]{:S(2)}, u32[]{:S(2)}) %collective-permute-start.14) | collective-permute-done | bytes 147488 | tf_op jit(solution)/shard_map/ppermute | solution.py:81
  116.6 5.7 %collective-permute-done.15 = bf16[2,2,24,384]{3,2,0,1:T(8,128)(2,1)S(1)} collective-permute-done((bf16[2,2,24,384]{3,2,0,1:T(8,128)(2,1)S(1)}, bf16[2,2,24,384]{3,2,0,1:T(8,128)(2,1)S(1)}, u32[]{:S(2)}, u32[]{:S(2)}) %collective-permute-start.15) | collective-permute-done | bytes 73760 | tf_op jit(solution)/shard_map/ppermute | solution.py:81
  122.5 7.0 %collective-permute-done.16 = bf16[1,2,24,384]{3,2,0,1:T(8,128)(2,1)S(1)} collective-permute-done((bf16[1,2,24,384]{3,2,0,1:T(8,128)(2,1)S(1)}, bf16[1,2,24,384]{3,2,0,1:T(8,128)(2,1)S(1)}, u32[]{:S(2)}, u32[]{:S(2)}) %collective-permute-start.16) | collective-permute-done | bytes 36896 | tf_op jit(solution)/shard_map/ppermute | solution.py:81
  129.6 5.1 %collective-permute-done.17 = bf16[2,24,384]{2,1,0:T(8,128)(2,1)S(1)} collective-permute-done((bf16[2,24,384]{2,1,0:T(8,128)(2,1)S(1)}, bf16[2,24,384]{2,1,0:T(8,128)(2,1)S(1)}, u32[]{:S(2)}, u32[]{:S(2)}) %collective-permute-start.17) | collective-permute-done | bytes 36896 | tf_op jit(solution)/shard_map/ppermute | solution.py:81
  134.8 4.3 %collective-permute-done.18 = bf16[2,48,384]{2,1,0:T(8,128)(2,1)S(1)} collective-permute-done((bf16[2,48,384]{2,1,0:T(8,128)(2,1)S(1)}, bf16[2,48,384]{2,1,0:T(8,128)(2,1)S(1)}, u32[]{:S(2)}, u32[]{:S(2)}) %collective-permute-start.18) | collective-permute-done | bytes 73760 | tf_op jit(solution)/shard_map/ppermute | solution.py:81
  (50 shorter events, 6.6 us)
Async XLA Ops:
  24.5 29.8 %all-to-all-start.1 = ((bf16[64,8,768]{2,1,0:T(8,128)(2,1)}), bf16[64,8,768]{2,1,0:T(8,128)(2,1)S(1)}, u32[]{:S(2)}, u32[]{:S(2)}) async-start(bf16[64,8,768]{2,1,0:T(8,128)(2,1)} %fetch.1), calls=%async_computation.1 | async-start | bytes 1572864 | tf_op jit(solution)/shard_map/all_to_all | solution.py:439
  31.0 23.3 %copy-start.1 = (s32[256,128]{1,0:T(8,128)S(1)}, s32[256,128]{1,0:T(8,128)}, u32[]{:S(2)}) copy-start(s32[256,128]{1,0:T(8,128)} %get-tuple-element.48.slot_ref) | copy-start | bytes 393220
  31.0 23.3 %copy-start.2 = (bf16[8,768]{1,0:T(8,128)(2,1)S(1)}, bf16[8,768]{1,0:T(8,128)(2,1)}, u32[]{:S(2)}) copy-start(bf16[8,768]{1,0:T(8,128)(2,1)} %question_ref.1) | copy-start | bytes 36868
  31.0 23.3 %copy-start.3 = (f32[8,32]{1,0:T(8,128)S(1)}, f32[8,32]{1,0:T(8,128)}, u32[]{:S(2)}) copy-start(f32[8,32]{1,0:T(8,128)} %reader_ref.1) | copy-start | bytes 3076
  33.8 2.1 %copy-start = (bf16[3072,768]{1,0:T(8,128)(2,1)}, bf16[3072,768]{1,0:T(8,128)(2,1)S(1)}, u32[]{:S(2)}) copy-start(bf16[3072,768]{1,0:T(8,128)(2,1)S(1)} %turn.1.up_t_hbm) | copy-start | bytes 14155780
  62.9 3.5 %collective-permute-start = (bf16[3072,256]{1,0:T(8,128)(2,1)S(1)}, bf16[3072,256]{1,0:T(8,128)(2,1)S(1)}, u32[]{:S(2)}, u32[]{:S(2)}) collective-permute-start(bf16[3072,256]{1,0:T(8,128)(2,1)S(1)} %get-tuple-element.51), channel_id=1, source_target_pairs={{0,4},{1,5},{2,6},{3,7},{4,0},{5,1},{6,2},{7,3},{8,12},{9,13},{10,... | collective-permute-start | bytes 4718600 | tf_op jit(solution)/shard_map/ppermute | solution.py:81
  65.1 3.4 %collective-permute-start.1 = (bf16[1536,256]{1,0:T(8,128)(2,1)S(1)}, bf16[1536,256]{1,0:T(8,128)(2,1)S(1)}, u32[]{:S(2)}, u32[]{:S(2)}) collective-permute-start(bf16[1536,256]{1,0:T(8,128)(2,1)S(1)} %get-tuple-element.59), channel_id=1, source_target_pairs={{0,4},{1,5},{2,6},{3,7},{4,0},{5,1},{6,2},{7,3},{8,12},{9,13},{10,... | collective-permute-start | bytes 2359304 | tf_op jit(solution)/shard_map/ppermute | solution.py:81
  68.6 10.0 %collective-permute-start.2 = (bf16[4,8,24,384]{3,2,1,0:T(8,128)(2,1)S(1)}, bf16[4,8,24,384]{3,2,1,0:T(8,128)(2,1)S(1)}, u32[]{:S(2)}, u32[]{:S(2)}) collective-permute-start(bf16[4,8,24,384]{3,2,1,0:T(8,128)(2,1)S(1)} %get-tuple-element.60), channel_id=1, source_target_pairs={{0,1},{1,0},{2,3},{3,2},{4,7},{5,6},{6,5},{7,4},{8,9},{9,8},{10,11... | collective-permute-start | bytes 1769480 | tf_op jit(solution)/shard_map/ppermute | solution.py:81
  72.3 10.0 %collective-permute-start.5 = (bf16[4,8,24,384]{3,2,1,0:T(8,128)(2,1)S(1)}, bf16[4,8,24,384]{3,2,1,0:T(8,128)(2,1)S(1)}, u32[]{:S(2)}, u32[]{:S(2)}) collective-permute-start(bf16[4,8,24,384]{3,2,1,0:T(8,128)(2,1)S(1)} %get-tuple-element.68), channel_id=1, source_target_pairs={{0,8},{1,9},{2,10},{3,11},{4,28},{5,29},{6,30},{7,31},{8,0},{9,1},... | collective-permute-start | bytes 1769480 | tf_op jit(solution)/shard_map/ppermute | solution.py:81
  72.9 15.1 %collective-permute-start.4 = (bf16[4,8,24,384]{3,2,1,0:T(8,128)(2,1)S(1)}, bf16[4,8,24,384]{3,2,1,0:T(8,128)(2,1)S(1)}, u32[]{:S(2)}, u32[]{:S(2)}) collective-permute-start(bf16[4,8,24,384]{3,2,1,0:T(8,128)(2,1)S(1)} %get-tuple-element.64), channel_id=1, source_target_pairs={{0,1},{1,0},{2,3},{3,2},{4,7},{5,6},{6,5},{7,4},{8,9},{9,8},{10,11... | collective-permute-start | bytes 1769480 | tf_op jit(solution)/shard_map/ppermute | solution.py:81
  73.4 17.7 %collective-permute-start.8 = (bf16[4,8,24,384]{3,2,1,0:T(8,128)(2,1)S(1)}, bf16[4,8,24,384]{3,2,1,0:T(8,128)(2,1)S(1)}, u32[]{:S(2)}, u32[]{:S(2)}) collective-permute-start(bf16[4,8,24,384]{3,2,1,0:T(8,128)(2,1)S(1)} %get-tuple-element.75), channel_id=1, source_target_pairs={{0,8},{1,9},{2,10},{3,11},{4,28},{5,29},{6,30},{7,31},{8,0},{9,1},... | collective-permute-start | bytes 1769480 | tf_op jit(solution)/shard_map/ppermute | solution.py:81
  78.8 12.4 %collective-permute-start.3 = (bf16[2,8,24,384]{3,2,1,0:T(8,128)(2,1)S(1)}, bf16[2,8,24,384]{3,2,1,0:T(8,128)(2,1)S(1)}, u32[]{:S(2)}, u32[]{:S(2)}) collective-permute-start(bf16[2,8,24,384]{3,2,1,0:T(8,128)(2,1)S(1)} %get-tuple-element.62), channel_id=1, source_target_pairs={{0,3},{1,2},{2,1},{3,0},{4,5},{5,4},{6,7},{7,6},{8,11},{9,10},{10,... | collective-permute-start | bytes 884744 | tf_op jit(solution)/shard_map/ppermute | solution.py:81
  82.5 10.6 %collective-permute-start.7 = (bf16[2,8,24,384]{3,2,1,0:T(8,128)(2,1)S(1)}, bf16[2,8,24,384]{3,2,1,0:T(8,128)(2,1)S(1)}, u32[]{:S(2)}, u32[]{:S(2)}) collective-permute-start(bf16[2,8,24,384]{3,2,1,0:T(8,128)(2,1)S(1)} %get-tuple-element.70), channel_id=1, source_target_pairs={{0,24},{1,25},{2,26},{3,27},{4,12},{5,13},{6,14},{7,15},{8,16},{9,... | collective-permute-start | bytes 884744 | tf_op jit(solution)/shard_map/ppermute | solution.py:81
  88.2 10.8 %collective-permute-start.9 = (bf16[2,8,24,384]{3,2,1,0:T(8,128)(2,1)S(1)}, bf16[2,8,24,384]{3,2,1,0:T(8,128)(2,1)S(1)}, u32[]{:S(2)}, u32[]{:S(2)}) collective-permute-start(bf16[2,8,24,384]{3,2,1,0:T(8,128)(2,1)S(1)} %get-tuple-element.81), channel_id=1, source_target_pairs={{0,3},{1,2},{2,1},{3,0},{4,5},{5,4},{6,7},{7,6},{8,11},{9,10},{10,... | collective-permute-start | bytes 884744 | tf_op jit(solution)/shard_map/ppermute | solution.py:81
  91.3 7.8 %collective-permute-start.6 = (bf16[2,8,24,384]{3,2,1,0:T(8,128)(2,1)S(1)}, bf16[2,8,24,384]{3,2,1,0:T(8,128)(2,1)S(1)}, u32[]{:S(2)}, u32[]{:S(2)}) collective-permute-start(bf16[2,8,24,384]{3,2,1,0:T(8,128)(2,1)S(1)} %add_convert_fusion.3), channel_id=1, source_target_pairs={{0,8},{1,9},{2,10},{3,11},{4,28},{5,29},{6,30},{7,31},{8,0},{9,1},... | collective-permute-start | bytes 884744 | tf_op jit(solution)/shard_map/ppermute | solution.py:81
  93.2 7.3 %collective-permute-start.11 = (bf16[2,8,24,384]{3,2,1,0:T(8,128)(2,1)S(1)}, bf16[2,8,24,384]{3,2,1,0:T(8,128)(2,1)S(1)}, u32[]{:S(2)}, u32[]{:S(2)}) collective-permute-start(bf16[2,8,24,384]{3,2,1,0:T(8,128)(2,1)S(1)} %add_convert_fusion.2), channel_id=1, source_target_pairs={{0,1},{1,0},{2,3},{3,2},{4,7},{5,6},{6,5},{7,4},{8,9},{9,8},{10,11... | collective-permute-start | bytes 884744 | tf_op jit(solution)/shard_map/ppermute | solution.py:81
  93.5 9.5 %collective-permute-start.12 = (bf16[2,8,24,384]{3,2,1,0:T(8,128)(2,1)S(1)}, bf16[2,8,24,384]{3,2,1,0:T(8,128)(2,1)S(1)}, u32[]{:S(2)}, u32[]{:S(2)}) collective-permute-start(bf16[2,8,24,384]{3,2,1,0:T(8,128)(2,1)S(1)} %get-tuple-element.84), channel_id=1, source_target_pairs={{0,24},{1,25},{2,26},{3,27},{4,12},{5,13},{6,14},{7,15},{8,16},{9,... | collective-permute-start | bytes 884744 | tf_op jit(solution)/shard_map/ppermute | solution.py:81
  99.2 6.4 %collective-permute-start.10 = (bf16[1,8,24,384]{3,2,1,0:T(8,128)(2,1)S(1)}, bf16[1,8,24,384]{3,2,1,0:T(8,128)(2,1)S(1)}, u32[]{:S(2)}, u32[]{:S(2)}) collective-permute-start(bf16[1,8,24,384]{3,2,1,0:T(8,128)(2,1)S(1)} %slice.156), channel_id=1, source_target_pairs={{0,24},{1,25},{2,26},{3,27},{4,12},{5,13},{6,14},{7,15},{8,16},{9,... | collective-permute-start | bytes 442376 | tf_op jit(solution)/shard_map/ppermute | solution.py:81
  103.1 6.4 %collective-permute-start.13 = (bf16[1,8,24,384]{3,2,1,0:T(8,128)(2,1)S(1)}, bf16[1,8,24,384]{3,2,1,0:T(8,128)(2,1)S(1)}, u32[]{:S(2)}, u32[]{:S(2)}) collective-permute-start(bf16[1,8,24,384]{3,2,1,0:T(8,128)(2,1)S(1)} %slice.155), channel_id=1, source_target_pairs={{0,3},{1,2},{2,1},{3,0},{4,5},{5,4},{6,7},{7,6},{8,11},{9,10},{10,... | collective-permute-start | bytes 442376 | tf_op jit(solution)/shard_map/ppermute | solution.py:81
  109.7 6.8 %collective-permute-start.14 = (bf16[4,2,24,384]{3,2,0,1:T(8,128)(2,1)S(1)}, bf16[4,2,24,384]{3,2,0,1:T(8,128)(2,1)S(1)}, u32[]{:S(2)}, u32[]{:S(2)}) collective-permute-start(bf16[4,2,24,384]{3,2,0,1:T(8,128)(2,1)S(1)} %slice.154), channel_id=1, source_target_pairs={{0,32},{1,33},{2,34},{3,35},{4,228},{5,229},{6,230},{7,231},{8,40}... | collective-permute-start | bytes 442376 | tf_op jit(solution)/shard_map/ppermute | solution.py:81
  116.5 5.8 %collective-permute-start.15 = (bf16[2,2,24,384]{3,2,0,1:T(8,128)(2,1)S(1)}, bf16[2,2,24,384]{3,2,0,1:T(8,128)(2,1)S(1)}, u32[]{:S(2)}, u32[]{:S(2)}) collective-permute-start(bf16[2,2,24,384]{3,2,0,1:T(8,128)(2,1)S(1)} %get-tuple-element.89), channel_id=1, source_target_pairs={{0,64},{1,65},{2,66},{3,67},{4,196},{5,197},{6,198},{7,199},{8,72}... | collective-permute-start | bytes 221192 | tf_op jit(solution)/shard_map/ppermute | solution.py:81
  122.4 7.1 %collective-permute-start.16 = (bf16[1,2,24,384]{3,2,0,1:T(8,128)(2,1)S(1)}, bf16[1,2,24,384]{3,2,0,1:T(8,128)(2,1)S(1)}, u32[]{:S(2)}, u32[]{:S(2)}) collective-permute-start(bf16[1,2,24,384]{3,2,0,1:T(8,128)(2,1)S(1)} %fusion.6), channel_id=1, source_target_pairs={{0,224},{1,225},{2,226},{3,227},{4,36},{5,37},{6,38},{7,39},{8,232... | collective-permute-start | bytes 110600 | tf_op jit(solution)/shard_map/ppermute | solution.py:81
  129.4 5.3 %collective-permute-start.17 = (bf16[2,24,384]{2,1,0:T(8,128)(2,1)S(1)}, bf16[2,24,384]{2,1,0:T(8,128)(2,1)S(1)}, u32[]{:S(2)}, u32[]{:S(2)}) collective-permute-start(bf16[2,24,384]{2,1,0:T(8,128)(2,1)S(1)} %fusion.9), channel_id=1, source_target_pairs={{0,3},{1,2},{2,1},{3,0},{4,5},{5,4},{6,7},{7,6},{8,11},{9,10},{10,... | collective-permute-start | bytes 110600 | tf_op jit(solution)/shard_map/ppermute | solution.py:81
  134.7 4.4 %collective-permute-start.18 = (bf16[2,48,384]{2,1,0:T(8,128)(2,1)S(1)}, bf16[2,48,384]{2,1,0:T(8,128)(2,1)S(1)}, u32[]{:S(2)}, u32[]{:S(2)}) collective-permute-start(bf16[2,48,384]{2,1,0:T(8,128)(2,1)S(1)} %pad_maximum_fusion.1), channel_id=1, source_target_pairs={{0,1},{1,0},{2,3},{3,2},{4,7},{5,6},{6,5},{7,4},{8,9},{9,8},{10,11... | collective-permute-start | bytes 221192 | tf_op jit(solution)/shard_map/ppermute | solution.py:81

commit v7 on v6

--- a/solution.py
+++ b/solution.py
@@ -404,23 +404,18 @@
     plans = (("x1", "x2", "y1", "y2"), ("y1", "y2", "x1", "x2"))
     both = list(zip((down, up), plans))
     first = [(swap(chain[2], plan[0]), swap(chain[3], plan[0])) for chain, plan in both]
-    ahead, sends = [], []
-    for ((next_keep, *_), plan), (came, _) in zip(both, first):
-        next_send, send = lax.optimization_barrier(apart((came.astype(f32) + next_keep).astype(bf16)))
-        ahead.append(swap(next_send, plan[1]))
-        sends.append((next_send, send))
-    keeps, rest = [], []
-    for at, (((_, keep, *_), plan), (_, came)) in enumerate(zip(both, first)):
-        came = after(came, sends[1][0])
-        next_keep, keep = apart(keep + came.astype(f32))
-        next_keep, keep, send = lax.optimization_barrier((next_keep, keep, sends[at][1]))
-        rest.append(swap(send, plan[1]))
-        keeps.append((next_keep, keep))
-    sends = [(ahead[at].astype(f32) + keeps[at][0]).astype(bf16) for at in range(2)]
-    third = [swap(sends[at], plan[2]) for at, (_, plan) in enumerate(both)]
+    sends = [(came.astype(f32) + chain[0]).astype(bf16) for (chain, _), (came, _) in zip(both, first)]
+    second = [swap(send, plan[1]) for send, (_, plan) in zip(sends, both)]
+    keeps = [
+        apart(chain[1] + after(came, sends[1]).astype(f32)) for (chain, _), (_, came) in zip(both, first)
+    ]
+    keeps = [lax.optimization_barrier(keep) for keep in keeps]
+    parts = [apart(came) for came in second]
+    sends = [(part[0].astype(f32) + keep[0]).astype(bf16) for part, keep in zip(parts, keeps)]
+    third = [swap(send, plan[2]) for send, (_, plan) in zip(sends, both)]
     sums = []
     for at, (_, plan) in enumerate(both):
-        keep = after(third[at], sends[1]).astype(f32) + (keeps[at][1] + rest[at].astype(f32))
+        keep = after(third[at], sends[1]).astype(f32) + (keeps[at][1] + parts[at][1].astype(f32))
         sums.append(swap(keep[1:].astype(bf16), plan[3]).astype(f32) + keep[:1])
     return sums
 

time: 140 us -> 140 us (level)
  waiting for transfers between devices: 68.2 us -> 73 us
  starting transfers between devices: 24.7 us -> 20.2 us
    ppermute x19 -> x17, waiting for transfers between devices: 49.9 us -> 54.6 us  [swap(): return lax.ppermute(array, AXES, partner(step))]
    ppermute x19 -> x17, starting transfers between devices: 18.3 us -> 13.8 us  [swap(): return lax.ppermute(array, AXES, partner(step))]
  transfers between devices with their start and end apart: 20 -> 18, of which waited for: 15 -> 17; matrix products, arithmetic and copies ran while one was open for 1% -> 1% of each run, Pallas kernels for 7% -> 7%
where the time goes in v7:
time: 140 us
  waiting for transfers between devices  73 us (52%)
  Pallas kernels  22.6 us (16%)
  starting transfers between devices  20.2 us (14%)
  blocking collectives  19 us (14%)
  local copies, waits for them, and re-layouts  2.37 us (2%)
  other arithmetic  1.93 us (1%)
    ppermute x17, waiting for transfers between devices, swap(): return lax.ppermute(array, AXES, partner(step))  54.6 us
    all_to_all x1, blocking collectives, on_device(): lax.all_to_all(send_rows, 'shard', split_axis=0, concat_axis=0, tiled=True)  19 us
    all_to_all x1, waiting for transfers between devices, on_device(): lax.all_to_all(states_out, 'shard', split_axis=0, concat_axis=0, tiled=True)  18.3 us
    ppermute x17, starting transfers between devices, swap(): return lax.ppermute(array, AXES, partner(step))  13.8 us
    pallas_call x1, Pallas kernels, forward(): pl.pallas_call(forward_kernel, in_specs=[SMEM, VMEM, VMEM, VMEM, VMEM, HB...  8.59 us
    all_to_all x1, starting transfers between devices, on_device(): lax.all_to_all(states_out, 'shard', split_axis=0, concat_axis=0, tiled=True)  6.44 us
    pallas_call x2, Pallas kernels, gradient(): pl.pallas_call(functools.partial(gradient_kernel, x_first, right_at), in_...  4.34 us
    pallas_call x1, Pallas kernels, turn(): pl.pallas_call(turn_kernel, in_specs=[HBM], out_specs=VMEM, scratch_shape...  2.81 us
  transfers between devices with their start and end apart: 18, of which 17 were waited for; matrix products, arithmetic and copies ran while one was open for 1% of the time, Pallas kernels for 7%

profile of v7, /device:TPU:64, one launch (start us, length us, event | category | flops | bytes accessed | tf_op | source)
XLA Modules:
  0.0 140.1 jit_solution(15757131088201499390)
XLA Ops:
  0.6 2.8 %route.1 = (s32[64,1,128]{2,1,0:T(1,128)}, s32[256,128]{1,0:T(8,128)}, bf16[1024,768]{1,0:T(8,128)(2,1)S(1)}) custom-call(s32[8,32]{1,0:T(8,128)} %bitcast.21, s32[8,32]{1,0:T(8,128)} %row_ref.1, bf16[1024,768]{1,0:T(8,128)(2,1)} %index_hbm.1), custom_call_target="tpu_custom_call" | custom-call | tf_op jit(solution)/shard_map/route/pallas_call | solution.py:270
  3.5 19.0 %all_to_all.10.rows_ref = s32[64,1,128]{2,1,0:T(1,128)S(1)} all-to-all(s32[64,1,128]{2,1,0:T(1,128)} %get-tuple-element.40), channel_id=1, replica_groups=mesh['shard'=64,'rep'=4] {'shard'}, dimensions={0} | all-to-all | bytes 65536 | tf_op jit(solution)/shard_map/all_to_all | solution.py:432
  22.5 2.0 %fetch.1 = bf16[64,8,768]{2,1,0:T(8,128)(2,1)} custom-call(s32[64,1,128]{2,1,0:T(1,128)S(1)} %all_to_all.10.rows_ref, bf16[1024,768]{1,0:T(8,128)(2,1)S(1)} %get-tuple-element.41.index_ref), custom_call_target="tpu_custom_call" | custom-call | tf_op jit(solution)/shard_map/fetch/pallas_call | solution.py:286
  24.5 6.4 %all-to-all-start.1 = ((bf16[64,8,768]{2,1,0:T(8,128)(2,1)}), bf16[64,8,768]{2,1,0:T(8,128)(2,1)S(1)}, u32[]{:S(2)}, u32[]{:S(2)}) async-start(bf16[64,8,768]{2,1,0:T(8,128)(2,1)} %fetch.1), calls=%async_computation.1 | async-start | bytes 1572864 | tf_op jit(solution)/shard_map/all_to_all | solution.py:434
  31.0 2.8 %turn.1.up_t_hbm = bf16[3072,768]{1,0:T(8,128)(2,1)S(1)} custom-call(bf16[768,3072]{1,0:T(8,128)(2,1)} %up_hbm.1), custom_call_target="tpu_custom_call" | custom-call | bytes 16777216 | tf_op jit(solution)/shard_map/turn/pallas_call | solution.py:300
  33.8 2.1 %copy-done = bf16[3072,768]{1,0:T(8,128)(2,1)} copy-done((bf16[3072,768]{1,0:T(8,128)(2,1)}, bf16[3072,768]{1,0:T(8,128)(2,1)S(1)}, u32[]{:S(2)}) %copy-start) | copy-done | bytes 4718616
  36.0 18.3 %all-to-all-done.1 = bf16[64,8,768]{2,1,0:T(8,128)(2,1)S(1)} async-done(((bf16[64,8,768]{2,1,0:T(8,128)(2,1)}), bf16[64,8,768]{2,1,0:T(8,128)(2,1)S(1)}, u32[]{:S(2)}, u32[]{:S(2)}) %all-to-all-start.1) | async-done | bytes 786464 | tf_op jit(solution)/shard_map/all_to_all | solution.py:434
  54.3 8.6 %forward.1 = (f32[8,32]{1,0:T(8,128)}, bf16[256,768]{1,0:T(8,128)(2,1)S(1)}, bf16[256,768]{1,0:T(8,128)(2,1)S(1)}, f32[3072,256]{1,0:T(8,128)S(1)}, bf16[1536,25...) custom-call(s32[4]{0:T(128)S(1)} %pad_add_fusion.place_ref, ...), custom_call_target="tpu_custom_call" | custom-call | flops 2415919104 | bytes 16777216 | tf_op jit(solution)/shard_map/forward/pallas_call | solution.py:315
  63.0 2.1 %backward.1 = (bf16[1536,256]{1,0:T(8,128)(2,1)S(1)}, bf16[1536,256]{1,0:T(8,128)(2,1)S(1)}) custom-call(s32[4]{0:T(128)S(1)} %pad_add_fusion.place_ref, bf16[256,768]{1,0:T(8,128)(2,1)S(1)} %get-tuple-element.46.right_ref.grad_emb_ref, f32[3072,256]{1,0:T(8,128)S(1)} %get-tuple-element.51.slope_ref, bf16[3072,768]{1,0:T(8,128)(2,1)S(1)} %get-tuple-element.52.down_ref), custom_call_target="tpu_custom_call" | custom-call | flops 1207959552 | bytes 8388608 | tf_op jit(solution)/shard_map/backward/pallas_call | solution.py:344
  65.1 0.8 collective-permute-start.1
  66.4 2.2 %gradient_down.1 = (f32[4,8,24,384]{3,2,1,0:T(8,128)S(1)}, f32[4,8,24,384]{3,2,1,0:T(8,128)S(1)}, bf16[4,8,24,384]{3,2,1,0:T(8,128)(2,1)S(1)}, bf16[4,8,24,384]{3,2,1,0:T(8,128)(2,1)S(1)}) custom-call(s32[4]{0:T(128)S(1)} %pad_add_fusion.place_ref, bf16[1536,256]{1,0:T(8,128)(2,1)S(1)} %get-tuple-element.44.mine_ref, ...), custom_call_target="tpu_custom_call" | custom-call | flops 1207959552 | bytes 8388608 | tf_op jit(solution)/shard_map/gradient_down/pallas_call | solution.py:361
  68.6 1.6 %collective-permute-start.2 = (bf16[4,8,24,384]{3,2,1,0:T(8,128)(2,1)S(1)}, bf16[4,8,24,384]{3,2,1,0:T(8,128)(2,1)S(1)}, u32[]{:S(2)}, u32[]{:S(2)}) collective-permute-start(bf16[4,8,24,384]{3,2,1,0:T(8,128)(2,1)S(1)} %get-tuple-element.54), channel_id=1, source_target_pairs={{0,1},{1,0},{2,3},{3,2},{4,7},{5,6},{6,5},{7,4},{8,9},{9,8},{10,11... | collective-permute-start | bytes 1769480 | tf_op jit(solution)/shard_map/ppermute | solution.py:81
  70.2 2.2 %gradient_up.1 = (f32[4,8,24,384]{3,2,1,0:T(8,128)S(1)}, f32[4,8,24,384]{3,2,1,0:T(8,128)S(1)}, bf16[4,8,24,384]{3,2,1,0:T(8,128)(2,1)S(1)}, bf16[4,8,24,384]{3,2,1,0:T(8,128)(2,1)S(1)}) custom-call(s32[4]{0:T(128)S(1)} %pad_add_fusion.place_ref, bf16[1536,256]{1,0:T(8,128)(2,1)S(1)} %get-tuple-element.58.mine_ref, ...), custom_call_target="tpu_custom_call" | custom-call | flops 1207959552 | bytes 8388608 | tf_op jit(solution)/shard_map/gradient_up/pallas_call | solution.py:361
  73.4 1.6 %collective-permute-start.8 = (bf16[4,8,24,384]{3,2,1,0:T(8,128)(2,1)S(1)}, bf16[4,8,24,384]{3,2,1,0:T(8,128)(2,1)S(1)}, u32[]{:S(2)}, u32[]{:S(2)}) collective-permute-start(bf16[4,8,24,384]{3,2,1,0:T(8,128)(2,1)S(1)} %get-tuple-element.66), channel_id=1, source_target_pairs={{0,8},{1,9},{2,10},{3,11},{4,28},{5,29},{6,30},{7,31},{8,0},{9,1},... | collective-permute-start | bytes 1769480 | tf_op jit(solution)/shard_map/ppermute | solution.py:81
  75.0 3.6 %collective-permute-done.2 = bf16[4,8,24,384]{3,2,1,0:T(8,128)(2,1)S(1)} collective-permute-done((bf16[4,8,24,384]{3,2,1,0:T(8,128)(2,1)S(1)}, bf16[4,8,24,384]{3,2,1,0:T(8,128)(2,1)S(1)}, u32[]{:S(2)}, u32[]{:S(2)}) %collective-permute-start.2) | collective-permute-done | bytes 589856 | tf_op jit(solution)/shard_map/ppermute | solution.py:81
  78.7 2.8 %collective-permute-start.3 = (bf16[4,8,24,384]{3,2,1,0:T(8,128)(2,1)S(1)}, bf16[4,8,24,384]{3,2,1,0:T(8,128)(2,1)S(1)}, u32[]{:S(2)}, u32[]{:S(2)}) collective-permute-start(bf16[4,8,24,384]{3,2,1,0:T(8,128)(2,1)S(1)} %add_convert_fusion.1), channel_id=1, source_target_pairs={{0,3},{1,2},{2,1},{3,0},{4,5},{5,4},{6,7},{7,6},{8,11},{9,10},{10,... | collective-permute-start | bytes 1769480 | tf_op jit(solution)/shard_map/ppermute | solution.py:81
  82.5 1.6 %collective-permute-start.7 = (bf16[4,8,24,384]{3,2,1,0:T(8,128)(2,1)S(1)}, bf16[4,8,24,384]{3,2,1,0:T(8,128)(2,1)S(1)}, u32[]{:S(2)}, u32[]{:S(2)}) collective-permute-start(bf16[4,8,24,384]{3,2,1,0:T(8,128)(2,1)S(1)} %add_convert_fusion), channel_id=1, source_target_pairs={{0,24},{1,25},{2,26},{3,27},{4,12},{5,13},{6,14},{7,15},{8,16},{9,... | collective-permute-start | bytes 1769480 | tf_op jit(solution)/shard_map/ppermute | solution.py:81
  84.0 4.0 %collective-permute-done.4 = bf16[4,8,24,384]{3,2,1,0:T(8,128)(2,1)S(1)} collective-permute-done((bf16[4,8,24,384]{3,2,1,0:T(8,128)(2,1)S(1)}, bf16[4,8,24,384]{3,2,1,0:T(8,128)(2,1)S(1)}, u32[]{:S(2)}, u32[]{:S(2)}) %collective-permute-start.4) | collective-permute-done | bytes 589856 | tf_op jit(solution)/shard_map/ppermute | solution.py:81
  88.2 2.4 %collective-permute-done.8 = bf16[4,8,24,384]{3,2,1,0:T(8,128)(2,1)S(1)} collective-permute-done((bf16[4,8,24,384]{3,2,1,0:T(8,128)(2,1)S(1)}, bf16[4,8,24,384]{3,2,1,0:T(8,128)(2,1)S(1)}, u32[]{:S(2)}, u32[]{:S(2)}) %collective-permute-start.8) | collective-permute-done | bytes 589856 | tf_op jit(solution)/shard_map/ppermute | solution.py:81
  90.8 0.8 collective-permute-done.3
  92.3 4.0 %collective-permute-done.7 = bf16[4,8,24,384]{3,2,1,0:T(8,128)(2,1)S(1)} collective-permute-done((bf16[4,8,24,384]{3,2,1,0:T(8,128)(2,1)S(1)}, bf16[4,8,24,384]{3,2,1,0:T(8,128)(2,1)S(1)}, u32[]{:S(2)}, u32[]{:S(2)}) %collective-permute-start.7) | collective-permute-done | bytes 589856 | tf_op jit(solution)/shard_map/ppermute | solution.py:81
  96.7 1.7 %collective-permute-done.6 = bf16[2,8,24,384]{3,2,1,0:T(8,128)(2,1)S(1)} collective-permute-done((bf16[2,8,24,384]{3,2,1,0:T(8,128)(2,1)S(1)}, bf16[2,8,24,384]{3,2,1,0:T(8,128)(2,1)S(1)}, u32[]{:S(2)}, u32[]{:S(2)}) %collective-permute-start.6) | collective-permute-done | bytes 294944 | tf_op jit(solution)/shard_map/ppermute | solution.py:81
  98.6 1.6 %collective-permute-start.9 = (bf16[1,8,24,384]{3,2,1,0:T(8,128)(2,1)S(1)}, bf16[1,8,24,384]{3,2,1,0:T(8,128)(2,1)S(1)}, u32[]{:S(2)}, u32[]{:S(2)}) collective-permute-start(bf16[1,8,24,384]{3,2,1,0:T(8,128)(2,1)S(1)} %slice.160), channel_id=1, source_target_pairs={{0,24},{1,25},{2,26},{3,27},{4,12},{5,13},{6,14},{7,15},{8,16},{9,... | collective-permute-start | bytes 442376 | tf_op jit(solution)/shard_map/ppermute | solution.py:81
  100.1 3.1 %collective-permute-done.10 = bf16[2,8,24,384]{3,2,1,0:T(8,128)(2,1)S(1)} collective-permute-done((bf16[2,8,24,384]{3,2,1,0:T(8,128)(2,1)S(1)}, bf16[2,8,24,384]{3,2,1,0:T(8,128)(2,1)S(1)}, u32[]{:S(2)}, u32[]{:S(2)}) %collective-permute-start.10) | collective-permute-done | bytes 294944 | tf_op jit(solution)/shard_map/ppermute | solution.py:81
  103.9 1.1 collective-permute-done.9
  105.0 4.7 %collective-permute-done.11 = bf16[1,8,24,384]{3,2,1,0:T(8,128)(2,1)S(1)} collective-permute-done((bf16[1,8,24,384]{3,2,1,0:T(8,128)(2,1)S(1)}, bf16[1,8,24,384]{3,2,1,0:T(8,128)(2,1)S(1)}, u32[]{:S(2)}, u32[]{:S(2)}) %collective-permute-start.11) | collective-permute-done | bytes 147488 | tf_op jit(solution)/shard_map/ppermute | solution.py:81
  109.9 0.9 collective-permute-start.12
  110.8 5.8 %collective-permute-done.12 = bf16[4,2,24,384]{3,2,0,1:T(8,128)(2,1)S(1)} collective-permute-done((bf16[4,2,24,384]{3,2,0,1:T(8,128)(2,1)S(1)}, bf16[4,2,24,384]{3,2,0,1:T(8,128)(2,1)S(1)}, u32[]{:S(2)}, u32[]{:S(2)}) %collective-permute-start.12) | collective-permute-done | bytes 147488 | tf_op jit(solution)/shard_map/ppermute | solution.py:81
  116.7 5.7 %collective-permute-done.13 = bf16[2,2,24,384]{3,2,0,1:T(8,128)(2,1)S(1)} collective-permute-done((bf16[2,2,24,384]{3,2,0,1:T(8,128)(2,1)S(1)}, bf16[2,2,24,384]{3,2,0,1:T(8,128)(2,1)S(1)}, u32[]{:S(2)}, u32[]{:S(2)}) %collective-permute-start.13) | collective-permute-done | bytes 73760 | tf_op jit(solution)/shard_map/ppermute | solution.py:81
  122.6 7.0 %collective-permute-done.14 = bf16[1,2,24,384]{3,2,0,1:T(8,128)(2,1)S(1)} collective-permute-done((bf16[1,2,24,384]{3,2,0,1:T(8,128)(2,1)S(1)}, bf16[1,2,24,384]{3,2,0,1:T(8,128)(2,1)S(1)}, u32[]{:S(2)}, u32[]{:S(2)}) %collective-permute-start.14) | collective-permute-done | bytes 36896 | tf_op jit(solution)/shard_map/ppermute | solution.py:81
  129.7 5.1 %collective-permute-done.15 = bf16[2,24,384]{2,1,0:T(8,128)(2,1)S(1)} collective-permute-done((bf16[2,24,384]{2,1,0:T(8,128)(2,1)S(1)}, bf16[2,24,384]{2,1,0:T(8,128)(2,1)S(1)}, u32[]{:S(2)}, u32[]{:S(2)}) %collective-permute-start.15) | collective-permute-done | bytes 36896 | tf_op jit(solution)/shard_map/ppermute | solution.py:81
  135.0 4.3 %collective-permute-done.16 = bf16[2,48,384]{2,1,0:T(8,128)(2,1)S(1)} collective-permute-done((bf16[2,48,384]{2,1,0:T(8,128)(2,1)S(1)}, bf16[2,48,384]{2,1,0:T(8,128)(2,1)S(1)}, u32[]{:S(2)}, u32[]{:S(2)}) %collective-permute-start.16) | collective-permute-done | bytes 73760 | tf_op jit(solution)/shard_map/ppermute | solution.py:81
  (44 shorter events, 6.4 us)
Async XLA Ops:
  24.5 29.8 %all-to-all-start.1 = ((bf16[64,8,768]{2,1,0:T(8,128)(2,1)}), bf16[64,8,768]{2,1,0:T(8,128)(2,1)S(1)}, u32[]{:S(2)}, u32[]{:S(2)}) async-start(bf16[64,8,768]{2,1,0:T(8,128)(2,1)} %fetch.1), calls=%async_computation.1 | async-start | bytes 1572864 | tf_op jit(solution)/shard_map/all_to_all | solution.py:434
  31.0 23.3 %copy-start.1 = (s32[256,128]{1,0:T(8,128)S(1)}, s32[256,128]{1,0:T(8,128)}, u32[]{:S(2)}) copy-start(s32[256,128]{1,0:T(8,128)} %get-tuple-element.42.slot_ref) | copy-start | bytes 393220
  31.0 23.3 %copy-start.2 = (bf16[8,768]{1,0:T(8,128)(2,1)S(1)}, bf16[8,768]{1,0:T(8,128)(2,1)}, u32[]{:S(2)}) copy-start(bf16[8,768]{1,0:T(8,128)(2,1)} %question_ref.1) | copy-start | bytes 36868
  31.0 23.3 %copy-start.3 = (f32[8,32]{1,0:T(8,128)S(1)}, f32[8,32]{1,0:T(8,128)}, u32[]{:S(2)}) copy-start(f32[8,32]{1,0:T(8,128)} %reader_ref.1) | copy-start | bytes 3076
  33.8 2.1 %copy-start = (bf16[3072,768]{1,0:T(8,128)(2,1)}, bf16[3072,768]{1,0:T(8,128)(2,1)S(1)}, u32[]{:S(2)}) copy-start(bf16[3072,768]{1,0:T(8,128)(2,1)S(1)} %turn.1.up_t_hbm) | copy-start | bytes 14155780
  62.9 3.5 %collective-permute-start = (bf16[3072,256]{1,0:T(8,128)(2,1)S(1)}, bf16[3072,256]{1,0:T(8,128)(2,1)S(1)}, u32[]{:S(2)}, u32[]{:S(2)}) collective-permute-start(bf16[3072,256]{1,0:T(8,128)(2,1)S(1)} %get-tuple-element.45), channel_id=1, source_target_pairs={{0,4},{1,5},{2,6},{3,7},{4,0},{5,1},{6,2},{7,3},{8,12},{9,13},{10,... | collective-permute-start | bytes 4718600 | tf_op jit(solution)/shard_map/ppermute | solution.py:81
  65.1 3.4 %collective-permute-start.1 = (bf16[1536,256]{1,0:T(8,128)(2,1)S(1)}, bf16[1536,256]{1,0:T(8,128)(2,1)S(1)}, u32[]{:S(2)}, u32[]{:S(2)}) collective-permute-start(bf16[1536,256]{1,0:T(8,128)(2,1)S(1)} %get-tuple-element.53), channel_id=1, source_target_pairs={{0,4},{1,5},{2,6},{3,7},{4,0},{5,1},{6,2},{7,3},{8,12},{9,13},{10,... | collective-permute-start | bytes 2359304 | tf_op jit(solution)/shard_map/ppermute | solution.py:81
  68.6 10.0 %collective-permute-start.2 = (bf16[4,8,24,384]{3,2,1,0:T(8,128)(2,1)S(1)}, bf16[4,8,24,384]{3,2,1,0:T(8,128)(2,1)S(1)}, u32[]{:S(2)}, u32[]{:S(2)}) collective-permute-start(bf16[4,8,24,384]{3,2,1,0:T(8,128)(2,1)S(1)} %get-tuple-element.54), channel_id=1, source_target_pairs={{0,1},{1,0},{2,3},{3,2},{4,7},{5,6},{6,5},{7,4},{8,9},{9,8},{10,11... | collective-permute-start | bytes 1769480 | tf_op jit(solution)/shard_map/ppermute | solution.py:81
  72.3 10.0 %collective-permute-start.5 = (bf16[4,8,24,384]{3,2,1,0:T(8,128)(2,1)S(1)}, bf16[4,8,24,384]{3,2,1,0:T(8,128)(2,1)S(1)}, u32[]{:S(2)}, u32[]{:S(2)}) collective-permute-start(bf16[4,8,24,384]{3,2,1,0:T(8,128)(2,1)S(1)} %get-tuple-element.61), channel_id=1, source_target_pairs={{0,8},{1,9},{2,10},{3,11},{4,28},{5,29},{6,30},{7,31},{8,0},{9,1},... | collective-permute-start | bytes 1769480 | tf_op jit(solution)/shard_map/ppermute | solution.py:81
  72.9 15.2 %collective-permute-start.4 = (bf16[4,8,24,384]{3,2,1,0:T(8,128)(2,1)S(1)}, bf16[4,8,24,384]{3,2,1,0:T(8,128)(2,1)S(1)}, u32[]{:S(2)}, u32[]{:S(2)}) collective-permute-start(bf16[4,8,24,384]{3,2,1,0:T(8,128)(2,1)S(1)} %get-tuple-element.57), channel_id=1, source_target_pairs={{0,1},{1,0},{2,3},{3,2},{4,7},{5,6},{6,5},{7,4},{8,9},{9,8},{10,11... | collective-permute-start | bytes 1769480 | tf_op jit(solution)/shard_map/ppermute | solution.py:81
  73.4 17.2 %collective-permute-start.8 = (bf16[4,8,24,384]{3,2,1,0:T(8,128)(2,1)S(1)}, bf16[4,8,24,384]{3,2,1,0:T(8,128)(2,1)S(1)}, u32[]{:S(2)}, u32[]{:S(2)}) collective-permute-start(bf16[4,8,24,384]{3,2,1,0:T(8,128)(2,1)S(1)} %get-tuple-element.66), channel_id=1, source_target_pairs={{0,8},{1,9},{2,10},{3,11},{4,28},{5,29},{6,30},{7,31},{8,0},{9,1},... | collective-permute-start | bytes 1769480 | tf_op jit(solution)/shard_map/ppermute | solution.py:81
  78.7 12.9 %collective-permute-start.3 = (bf16[4,8,24,384]{3,2,1,0:T(8,128)(2,1)S(1)}, bf16[4,8,24,384]{3,2,1,0:T(8,128)(2,1)S(1)}, u32[]{:S(2)}, u32[]{:S(2)}) collective-permute-start(bf16[4,8,24,384]{3,2,1,0:T(8,128)(2,1)S(1)} %add_convert_fusion.1), channel_id=1, source_target_pairs={{0,3},{1,2},{2,1},{3,0},{4,5},{5,4},{6,7},{7,6},{8,11},{9,10},{10,... | collective-permute-start | bytes 1769480 | tf_op jit(solution)/shard_map/ppermute | solution.py:81
  82.5 13.8 %collective-permute-start.7 = (bf16[4,8,24,384]{3,2,1,0:T(8,128)(2,1)S(1)}, bf16[4,8,24,384]{3,2,1,0:T(8,128)(2,1)S(1)}, u32[]{:S(2)}, u32[]{:S(2)}) collective-permute-start(bf16[4,8,24,384]{3,2,1,0:T(8,128)(2,1)S(1)} %add_convert_fusion), channel_id=1, source_target_pairs={{0,24},{1,25},{2,26},{3,27},{4,12},{5,13},{6,14},{7,15},{8,16},{9,... | collective-permute-start | bytes 1769480 | tf_op jit(solution)/shard_map/ppermute | solution.py:81
  91.6 6.8 %collective-permute-start.6 = (bf16[2,8,24,384]{3,2,1,0:T(8,128)(2,1)S(1)}, bf16[2,8,24,384]{3,2,1,0:T(8,128)(2,1)S(1)}, u32[]{:S(2)}, u32[]{:S(2)}) collective-permute-start(bf16[2,8,24,384]{3,2,1,0:T(8,128)(2,1)S(1)} %add_convert_fusion.3), channel_id=1, source_target_pairs={{0,8},{1,9},{2,10},{3,11},{4,28},{5,29},{6,30},{7,31},{8,0},{9,1},... | collective-permute-start | bytes 884744 | tf_op jit(solution)/shard_map/ppermute | solution.py:81
  96.4 6.8 %collective-permute-start.10 = (bf16[2,8,24,384]{3,2,1,0:T(8,128)(2,1)S(1)}, bf16[2,8,24,384]{3,2,1,0:T(8,128)(2,1)S(1)}, u32[]{:S(2)}, u32[]{:S(2)}) collective-permute-start(bf16[2,8,24,384]{3,2,1,0:T(8,128)(2,1)S(1)} %add_convert_fusion.2), channel_id=1, source_target_pairs={{0,1},{1,0},{2,3},{3,2},{4,7},{5,6},{6,5},{7,4},{8,9},{9,8},{10,11... | collective-permute-start | bytes 884744 | tf_op jit(solution)/shard_map/ppermute | solution.py:81
  98.6 6.4 %collective-permute-start.9 = (bf16[1,8,24,384]{3,2,1,0:T(8,128)(2,1)S(1)}, bf16[1,8,24,384]{3,2,1,0:T(8,128)(2,1)S(1)}, u32[]{:S(2)}, u32[]{:S(2)}) collective-permute-start(bf16[1,8,24,384]{3,2,1,0:T(8,128)(2,1)S(1)} %slice.160), channel_id=1, source_target_pairs={{0,24},{1,25},{2,26},{3,27},{4,12},{5,13},{6,14},{7,15},{8,16},{9,... | collective-permute-start | bytes 442376 | tf_op jit(solution)/shard_map/ppermute | solution.py:81
  103.3 6.4 %collective-permute-start.11 = (bf16[1,8,24,384]{3,2,1,0:T(8,128)(2,1)S(1)}, bf16[1,8,24,384]{3,2,1,0:T(8,128)(2,1)S(1)}, u32[]{:S(2)}, u32[]{:S(2)}) collective-permute-start(bf16[1,8,24,384]{3,2,1,0:T(8,128)(2,1)S(1)} %slice.159), channel_id=1, source_target_pairs={{0,3},{1,2},{2,1},{3,0},{4,5},{5,4},{6,7},{7,6},{8,11},{9,10},{10,... | collective-permute-start | bytes 442376 | tf_op jit(solution)/shard_map/ppermute | solution.py:81
  109.9 6.7 %collective-permute-start.12 = (bf16[4,2,24,384]{3,2,0,1:T(8,128)(2,1)S(1)}, bf16[4,2,24,384]{3,2,0,1:T(8,128)(2,1)S(1)}, u32[]{:S(2)}, u32[]{:S(2)}) collective-permute-start(bf16[4,2,24,384]{3,2,0,1:T(8,128)(2,1)S(1)} %slice.158), channel_id=1, source_target_pairs={{0,32},{1,33},{2,34},{3,35},{4,228},{5,229},{6,230},{7,231},{8,40}... | collective-permute-start | bytes 442376 | tf_op jit(solution)/shard_map/ppermute | solution.py:81
  116.6 5.8 %collective-permute-start.13 = (bf16[2,2,24,384]{3,2,0,1:T(8,128)(2,1)S(1)}, bf16[2,2,24,384]{3,2,0,1:T(8,128)(2,1)S(1)}, u32[]{:S(2)}, u32[]{:S(2)}) collective-permute-start(bf16[2,2,24,384]{3,2,0,1:T(8,128)(2,1)S(1)} %get-tuple-element.77), channel_id=1, source_target_pairs={{0,64},{1,65},{2,66},{3,67},{4,196},{5,197},{6,198},{7,199},{8,72}... | collective-permute-start | bytes 221192 | tf_op jit(solution)/shard_map/ppermute | solution.py:81
  122.5 7.1 %collective-permute-start.14 = (bf16[1,2,24,384]{3,2,0,1:T(8,128)(2,1)S(1)}, bf16[1,2,24,384]{3,2,0,1:T(8,128)(2,1)S(1)}, u32[]{:S(2)}, u32[]{:S(2)}) collective-permute-start(bf16[1,2,24,384]{3,2,0,1:T(8,128)(2,1)S(1)} %fusion.6), channel_id=1, source_target_pairs={{0,224},{1,225},{2,226},{3,227},{4,36},{5,37},{6,38},{7,39},{8,232... | collective-permute-start | bytes 110600 | tf_op jit(solution)/shard_map/ppermute | solution.py:81
  129.6 5.3 %collective-permute-start.15 = (bf16[2,24,384]{2,1,0:T(8,128)(2,1)S(1)}, bf16[2,24,384]{2,1,0:T(8,128)(2,1)S(1)}, u32[]{:S(2)}, u32[]{:S(2)}) collective-permute-start(bf16[2,24,384]{2,1,0:T(8,128)(2,1)S(1)} %fusion.9), channel_id=1, source_target_pairs={{0,3},{1,2},{2,1},{3,0},{4,5},{5,4},{6,7},{7,6},{8,11},{9,10},{10,... | collective-permute-start | bytes 110600 | tf_op jit(solution)/shard_map/ppermute | solution.py:81
  134.8 4.4 %collective-permute-start.16 = (bf16[2,48,384]{2,1,0:T(8,128)(2,1)S(1)}, bf16[2,48,384]{2,1,0:T(8,128)(2,1)S(1)}, u32[]{:S(2)}, u32[]{:S(2)}) collective-permute-start(bf16[2,48,384]{2,1,0:T(8,128)(2,1)S(1)} %pad_maximum_fusion.1), channel_id=1, source_target_pairs={{0,1},{1,0},{2,3},{3,2},{4,7},{5,6},{6,5},{7,4},{8,9},{9,8},{10,11... | collective-permute-start | bytes 221192 | tf_op jit(solution)/shard_map/ppermute | solution.py:81

commit v8 on v7

--- a/solution.py
+++ b/solution.py
@@ -277,6 +277,7 @@
             pltpu.VMEM(index_states.shape, index_states.dtype),
         ),
         scratch_shapes=[pltpu.SemaphoreType.DMA],
+        compiler_params=pltpu.CompilerParams(vmem_limit_bytes=16 << 20),
         name="route",
     )(owners, passage_rows, far(index_states))
 

time: 140 us -> 140 us (level)
  Pallas kernels: 22.6 us -> 21.2 us
    unnamed x8 -> x10, local copies, waits for them, and re-layouts: 2.16 us -> 3.51 us
where the time goes in v8:
time: 140 us
  waiting for transfers between devices  73.1 us (52%)
  Pallas kernels  21.2 us (15%)
  starting transfers between devices  20.2 us (14%)
  blocking collectives  18.9 us (13%)
  local copies, waits for them, and re-layouts  3.73 us (3%)
  other arithmetic  1.93 us (1%)
    ppermute x17, waiting for transfers between devices, swap(): return lax.ppermute(array, AXES, partner(step))  54.7 us
    all_to_all x1, blocking collectives, on_device(): lax.all_to_all(send_rows, 'shard', split_axis=0, concat_axis=0, tiled=True)  18.9 us
    all_to_all x1, waiting for transfers between devices, on_device(): lax.all_to_all(states_out, 'shard', split_axis=0, concat_axis=0, tiled=True)  18.4 us
    ppermute x17, starting transfers between devices, swap(): return lax.ppermute(array, AXES, partner(step))  13.8 us
    pallas_call x1, Pallas kernels, forward(): pl.pallas_call(forward_kernel, in_specs=[SMEM, VMEM, VMEM, VMEM, VMEM, HB...  8.59 us
    all_to_all x1, starting transfers between devices, on_device(): lax.all_to_all(states_out, 'shard', split_axis=0, concat_axis=0, tiled=True)  6.44 us
    pallas_call x2, Pallas kernels, gradient(): pl.pallas_call(functools.partial(gradient_kernel, x_first, right_at), in_...  4.34 us
    unnamed x10, local copies, waits for them, and re-layouts  3.51 us
  transfers between devices with their start and end apart: 18, of which 17 were waited for; matrix products, arithmetic and copies ran while one was open for 1% of the time, Pallas kernels for 7%

profile of v8, /device:TPU:64, one launch (start us, length us, event | category | flops | bytes accessed | tf_op | source)
XLA Modules:
  0.0 139.9 jit_solution(10980675019834519940)
XLA Ops:
  2.0 1.4 %route.1 = (s32[64,1,128]{2,1,0:T(1,128)S(1)}, s32[256,128]{1,0:T(8,128)S(1)}, bf16[1024,768]{1,0:T(8,128)(2,1)S(1)}) custom-call(s32[8,32]{1,0:T(8,128)S(1)} %bitcast.21, s32[8,32]{1,0:T(8,128)S(1)} %copy-done.3, bf16[1024,768]{1,0:T(8,128)(2,1)} %index_hbm.1), custom_call_target="tpu_custom_call" | custom-call | tf_op jit(solution)/shard_map/route/pallas_call | solution.py:270
  3.5 18.9 %all_to_all.10.rows_ref = s32[64,1,128]{2,1,0:T(1,128)S(1)} all-to-all(s32[64,1,128]{2,1,0:T(1,128)S(1)} %get-tuple-element.40), channel_id=1, replica_groups=mesh['shard'=64,'rep'=4] {'shard'}, dimensions={0} | all-to-all | bytes 65536 | tf_op jit(solution)/shard_map/all_to_all | solution.py:433
  22.4 2.0 %fetch.1 = bf16[64,8,768]{2,1,0:T(8,128)(2,1)} custom-call(s32[64,1,128]{2,1,0:T(1,128)S(1)} %all_to_all.10.rows_ref, bf16[1024,768]{1,0:T(8,128)(2,1)S(1)} %get-tuple-element.41.index_ref), custom_call_target="tpu_custom_call" | custom-call | tf_op jit(solution)/shard_map/fetch/pallas_call | solution.py:287
  24.4 6.4 %all-to-all-start.1 = ((bf16[64,8,768]{2,1,0:T(8,128)(2,1)}), bf16[64,8,768]{2,1,0:T(8,128)(2,1)S(1)}, u32[]{:S(2)}, u32[]{:S(2)}) async-start(bf16[64,8,768]{2,1,0:T(8,128)(2,1)} %fetch.1), calls=%async_computation.1 | async-start | bytes 1572864 | tf_op jit(solution)/shard_map/all_to_all | solution.py:435
  30.8 2.8 %turn.1.up_t_hbm = bf16[3072,768]{1,0:T(8,128)(2,1)S(1)} custom-call(bf16[768,3072]{1,0:T(8,128)(2,1)} %up_hbm.1), custom_call_target="tpu_custom_call" | custom-call | bytes 16777216 | tf_op jit(solution)/shard_map/turn/pallas_call | solution.py:301
  33.6 2.1 %copy-done = bf16[3072,768]{1,0:T(8,128)(2,1)} copy-done((bf16[3072,768]{1,0:T(8,128)(2,1)}, bf16[3072,768]{1,0:T(8,128)(2,1)S(1)}, u32[]{:S(2)}) %copy-start) | copy-done | bytes 4718616
  35.8 18.4 %all-to-all-done.1 = bf16[64,8,768]{2,1,0:T(8,128)(2,1)S(1)} async-done(((bf16[64,8,768]{2,1,0:T(8,128)(2,1)}), bf16[64,8,768]{2,1,0:T(8,128)(2,1)S(1)}, u32[]{:S(2)}, u32[]{:S(2)}) %all-to-all-start.1) | async-done | bytes 786464 | tf_op jit(solution)/shard_map/all_to_all | solution.py:435
  54.2 8.6 %forward.1 = (f32[8,32]{1,0:T(8,128)}, bf16[256,768]{1,0:T(8,128)(2,1)S(1)}, bf16[256,768]{1,0:T(8,128)(2,1)S(1)}, f32[3072,256]{1,0:T(8,128)S(1)}, bf16[1536,25...) custom-call(s32[4]{0:T(128)S(1)} %pad_add_fusion.place_ref, ...), custom_call_target="tpu_custom_call" | custom-call | flops 2415919104 | bytes 16777216 | tf_op jit(solution)/shard_map/forward/pallas_call | solution.py:316
  62.9 2.1 %backward.1 = (bf16[1536,256]{1,0:T(8,128)(2,1)S(1)}, bf16[1536,256]{1,0:T(8,128)(2,1)S(1)}) custom-call(s32[4]{0:T(128)S(1)} %pad_add_fusion.place_ref, bf16[256,768]{1,0:T(8,128)(2,1)S(1)} %get-tuple-element.46.right_ref.grad_emb_ref, f32[3072,256]{1,0:T(8,128)S(1)} %get-tuple-element.51.slope_ref, bf16[3072,768]{1,0:T(8,128)(2,1)S(1)} %get-tuple-element.52.down_ref), custom_call_target="tpu_custom_call" | custom-call | flops 1207959552 | bytes 8388608 | tf_op jit(solution)/shard_map/backward/pallas_call | solution.py:345
  66.3 2.2 %gradient_down.1 = (f32[4,8,24,384]{3,2,1,0:T(8,128)S(1)}, f32[4,8,24,384]{3,2,1,0:T(8,128)S(1)}, bf16[4,8,24,384]{3,2,1,0:T(8,128)(2,1)S(1)}, bf16[4,8,24,384]{3,2,1,0:T(8,128)(2,1)S(1)}) custom-call(s32[4]{0:T(128)S(1)} %pad_add_fusion.place_ref, bf16[1536,256]{1,0:T(8,128)(2,1)S(1)} %get-tuple-element.44.mine_ref, ...), custom_call_target="tpu_custom_call" | custom-call | flops 1207959552 | bytes 8388608 | tf_op jit(solution)/shard_map/gradient_down/pallas_call | solution.py:362
  68.4 1.6 %collective-permute-start.2 = (bf16[4,8,24,384]{3,2,1,0:T(8,128)(2,1)S(1)}, bf16[4,8,24,384]{3,2,1,0:T(8,128)(2,1)S(1)}, u32[]{:S(2)}, u32[]{:S(2)}) collective-permute-start(bf16[4,8,24,384]{3,2,1,0:T(8,128)(2,1)S(1)} %get-tuple-element.54), channel_id=1, source_target_pairs={{0,1},{1,0},{2,3},{3,2},{4,7},{5,6},{6,5},{7,4},{8,9},{9,8},{10,11... | collective-permute-start | bytes 1769480 | tf_op jit(solution)/shard_map/ppermute | solution.py:81
  70.0 2.2 %gradient_up.1 = (f32[4,8,24,384]{3,2,1,0:T(8,128)S(1)}, f32[4,8,24,384]{3,2,1,0:T(8,128)S(1)}, bf16[4,8,24,384]{3,2,1,0:T(8,128)(2,1)S(1)}, bf16[4,8,24,384]{3,2,1,0:T(8,128)(2,1)S(1)}) custom-call(s32[4]{0:T(128)S(1)} %pad_add_fusion.place_ref, bf16[1536,256]{1,0:T(8,128)(2,1)S(1)} %get-tuple-element.58.mine_ref, ...), custom_call_target="tpu_custom_call" | custom-call | flops 1207959552 | bytes 8388608 | tf_op jit(solution)/shard_map/gradient_up/pallas_call | solution.py:362
  73.3 1.6 %collective-permute-start.8 = (bf16[4,8,24,384]{3,2,1,0:T(8,128)(2,1)S(1)}, bf16[4,8,24,384]{3,2,1,0:T(8,128)(2,1)S(1)}, u32[]{:S(2)}, u32[]{:S(2)}) collective-permute-start(bf16[4,8,24,384]{3,2,1,0:T(8,128)(2,1)S(1)} %get-tuple-element.66), channel_id=1, source_target_pairs={{0,8},{1,9},{2,10},{3,11},{4,28},{5,29},{6,30},{7,31},{8,0},{9,1},... | collective-permute-start | bytes 1769480 | tf_op jit(solution)/shard_map/ppermute | solution.py:81
  74.9 3.6 %collective-permute-done.2 = bf16[4,8,24,384]{3,2,1,0:T(8,128)(2,1)S(1)} collective-permute-done((bf16[4,8,24,384]{3,2,1,0:T(8,128)(2,1)S(1)}, bf16[4,8,24,384]{3,2,1,0:T(8,128)(2,1)S(1)}, u32[]{:S(2)}, u32[]{:S(2)}) %collective-permute-start.2) | collective-permute-done | bytes 589856 | tf_op jit(solution)/shard_map/ppermute | solution.py:81
  78.6 2.8 %collective-permute-start.3 = (bf16[4,8,24,384]{3,2,1,0:T(8,128)(2,1)S(1)}, bf16[4,8,24,384]{3,2,1,0:T(8,128)(2,1)S(1)}, u32[]{:S(2)}, u32[]{:S(2)}) collective-permute-start(bf16[4,8,24,384]{3,2,1,0:T(8,128)(2,1)S(1)} %add_convert_fusion.1), channel_id=1, source_target_pairs={{0,3},{1,2},{2,1},{3,0},{4,5},{5,4},{6,7},{7,6},{8,11},{9,10},{10,... | collective-permute-start | bytes 1769480 | tf_op jit(solution)/shard_map/ppermute | solution.py:81
  81.4 0.8 collective-permute-done.5
  82.3 1.6 %collective-permute-start.7 = (bf16[4,8,24,384]{3,2,1,0:T(8,128)(2,1)S(1)}, bf16[4,8,24,384]{3,2,1,0:T(8,128)(2,1)S(1)}, u32[]{:S(2)}, u32[]{:S(2)}) collective-permute-start(bf16[4,8,24,384]{3,2,1,0:T(8,128)(2,1)S(1)} %add_convert_fusion), channel_id=1, source_target_pairs={{0,24},{1,25},{2,26},{3,27},{4,12},{5,13},{6,14},{7,15},{8,16},{9,... | collective-permute-start | bytes 1769480 | tf_op jit(solution)/shard_map/ppermute | solution.py:81
  83.9 4.1 %collective-permute-done.4 = bf16[4,8,24,384]{3,2,1,0:T(8,128)(2,1)S(1)} collective-permute-done((bf16[4,8,24,384]{3,2,1,0:T(8,128)(2,1)S(1)}, bf16[4,8,24,384]{3,2,1,0:T(8,128)(2,1)S(1)}, u32[]{:S(2)}, u32[]{:S(2)}) %collective-permute-start.4) | collective-permute-done | bytes 589856 | tf_op jit(solution)/shard_map/ppermute | solution.py:81
  88.1 2.4 %collective-permute-done.8 = bf16[4,8,24,384]{3,2,1,0:T(8,128)(2,1)S(1)} collective-permute-done((bf16[4,8,24,384]{3,2,1,0:T(8,128)(2,1)S(1)}, bf16[4,8,24,384]{3,2,1,0:T(8,128)(2,1)S(1)}, u32[]{:S(2)}, u32[]{:S(2)}) %collective-permute-start.8) | collective-permute-done | bytes 589856 | tf_op jit(solution)/shard_map/ppermute | solution.py:81
  90.7 0.8 collective-permute-done.3
  92.1 4.0 %collective-permute-done.7 = bf16[4,8,24,384]{3,2,1,0:T(8,128)(2,1)S(1)} collective-permute-done((bf16[4,8,24,384]{3,2,1,0:T(8,128)(2,1)S(1)}, bf16[4,8,24,384]{3,2,1,0:T(8,128)(2,1)S(1)}, u32[]{:S(2)}, u32[]{:S(2)}) %collective-permute-start.7) | collective-permute-done | bytes 589856 | tf_op jit(solution)/shard_map/ppermute | solution.py:81
  96.6 1.8 %collective-permute-done.6 = bf16[2,8,24,384]{3,2,1,0:T(8,128)(2,1)S(1)} collective-permute-done((bf16[2,8,24,384]{3,2,1,0:T(8,128)(2,1)S(1)}, bf16[2,8,24,384]{3,2,1,0:T(8,128)(2,1)S(1)}, u32[]{:S(2)}, u32[]{:S(2)}) %collective-permute-start.6) | collective-permute-done | bytes 294944 | tf_op jit(solution)/shard_map/ppermute | solution.py:81
  98.4 1.6 %collective-permute-start.9 = (bf16[1,8,24,384]{3,2,1,0:T(8,128)(2,1)S(1)}, bf16[1,8,24,384]{3,2,1,0:T(8,128)(2,1)S(1)}, u32[]{:S(2)}, u32[]{:S(2)}) collective-permute-start(bf16[1,8,24,384]{3,2,1,0:T(8,128)(2,1)S(1)} %slice.160), channel_id=1, source_target_pairs={{0,24},{1,25},{2,26},{3,27},{4,12},{5,13},{6,14},{7,15},{8,16},{9,... | collective-permute-start | bytes 442376 | tf_op jit(solution)/shard_map/ppermute | solution.py:81
  100.0 3.1 %collective-permute-done.10 = bf16[2,8,24,384]{3,2,1,0:T(8,128)(2,1)S(1)} collective-permute-done((bf16[2,8,24,384]{3,2,1,0:T(8,128)(2,1)S(1)}, bf16[2,8,24,384]{3,2,1,0:T(8,128)(2,1)S(1)}, u32[]{:S(2)}, u32[]{:S(2)}) %collective-permute-start.10) | collective-permute-done | bytes 294944 | tf_op jit(solution)/shard_map/ppermute | solution.py:81
  103.8 1.1 collective-permute-done.9
  104.9 4.7 %collective-permute-done.11 = bf16[1,8,24,384]{3,2,1,0:T(8,128)(2,1)S(1)} collective-permute-done((bf16[1,8,24,384]{3,2,1,0:T(8,128)(2,1)S(1)}, bf16[1,8,24,384]{3,2,1,0:T(8,128)(2,1)S(1)}, u32[]{:S(2)}, u32[]{:S(2)}) %collective-permute-start.11) | collective-permute-done | bytes 147488 | tf_op jit(solution)/shard_map/ppermute | solution.py:81
  109.7 0.9 collective-permute-start.12
  110.7 5.8 %collective-permute-done.12 = bf16[4,2,24,384]{3,2,0,1:T(8,128)(2,1)S(1)} collective-permute-done((bf16[4,2,24,384]{3,2,0,1:T(8,128)(2,1)S(1)}, bf16[4,2,24,384]{3,2,0,1:T(8,128)(2,1)S(1)}, u32[]{:S(2)}, u32[]{:S(2)}) %collective-permute-start.12) | collective-permute-done | bytes 147488 | tf_op jit(solution)/shard_map/ppermute | solution.py:81
  116.6 5.7 %collective-permute-done.13 = bf16[2,2,24,384]{3,2,0,1:T(8,128)(2,1)S(1)} collective-permute-done((bf16[2,2,24,384]{3,2,0,1:T(8,128)(2,1)S(1)}, bf16[2,2,24,384]{3,2,0,1:T(8,128)(2,1)S(1)}, u32[]{:S(2)}, u32[]{:S(2)}) %collective-permute-start.13) | collective-permute-done | bytes 73760 | tf_op jit(solution)/shard_map/ppermute | solution.py:81
  122.4 7.0 %collective-permute-done.14 = bf16[1,2,24,384]{3,2,0,1:T(8,128)(2,1)S(1)} collective-permute-done((bf16[1,2,24,384]{3,2,0,1:T(8,128)(2,1)S(1)}, bf16[1,2,24,384]{3,2,0,1:T(8,128)(2,1)S(1)}, u32[]{:S(2)}, u32[]{:S(2)}) %collective-permute-start.14) | collective-permute-done | bytes 36896 | tf_op jit(solution)/shard_map/ppermute | solution.py:81
  129.5 5.1 %collective-permute-done.15 = bf16[2,24,384]{2,1,0:T(8,128)(2,1)S(1)} collective-permute-done((bf16[2,24,384]{2,1,0:T(8,128)(2,1)S(1)}, bf16[2,24,384]{2,1,0:T(8,128)(2,1)S(1)}, u32[]{:S(2)}, u32[]{:S(2)}) %collective-permute-start.15) | collective-permute-done | bytes 36896 | tf_op jit(solution)/shard_map/ppermute | solution.py:81
  134.8 4.3 %collective-permute-done.16 = bf16[2,48,384]{2,1,0:T(8,128)(2,1)S(1)} collective-permute-done((bf16[2,48,384]{2,1,0:T(8,128)(2,1)S(1)}, bf16[2,48,384]{2,1,0:T(8,128)(2,1)S(1)}, u32[]{:S(2)}, u32[]{:S(2)}) %collective-permute-start.16) | collective-permute-done | bytes 73760 | tf_op jit(solution)/shard_map/ppermute | solution.py:81
  (46 shorter events, 7.8 us)
Async XLA Ops:
  0.6 0.7 copy-start.2
  1.3 0.7 copy-start.3
  24.4 29.8 %all-to-all-start.1 = ((bf16[64,8,768]{2,1,0:T(8,128)(2,1)}), bf16[64,8,768]{2,1,0:T(8,128)(2,1)S(1)}, u32[]{:S(2)}, u32[]{:S(2)}) async-start(bf16[64,8,768]{2,1,0:T(8,128)(2,1)} %fetch.1), calls=%async_computation.1 | async-start | bytes 1572864 | tf_op jit(solution)/shard_map/all_to_all | solution.py:435
  30.8 23.3 %copy-start.1 = (bf16[8,768]{1,0:T(8,128)(2,1)S(1)}, bf16[8,768]{1,0:T(8,128)(2,1)}, u32[]{:S(2)}) copy-start(bf16[8,768]{1,0:T(8,128)(2,1)} %question_ref.1) | copy-start | bytes 36868
  30.8 23.3 %copy-start.4 = (f32[8,32]{1,0:T(8,128)S(1)}, f32[8,32]{1,0:T(8,128)}, u32[]{:S(2)}) copy-start(f32[8,32]{1,0:T(8,128)} %reader_ref.1) | copy-start | bytes 3076
  33.6 2.1 %copy-start = (bf16[3072,768]{1,0:T(8,128)(2,1)}, bf16[3072,768]{1,0:T(8,128)(2,1)S(1)}, u32[]{:S(2)}) copy-start(bf16[3072,768]{1,0:T(8,128)(2,1)S(1)} %turn.1.up_t_hbm) | copy-start | bytes 14155780
  62.8 3.5 %collective-permute-start = (bf16[3072,256]{1,0:T(8,128)(2,1)S(1)}, bf16[3072,256]{1,0:T(8,128)(2,1)S(1)}, u32[]{:S(2)}, u32[]{:S(2)}) collective-permute-start(bf16[3072,256]{1,0:T(8,128)(2,1)S(1)} %get-tuple-element.45), channel_id=1, source_target_pairs={{0,4},{1,5},{2,6},{3,7},{4,0},{5,1},{6,2},{7,3},{8,12},{9,13},{10,... | collective-permute-start | bytes 4718600 | tf_op jit(solution)/shard_map/ppermute | solution.py:81
  65.0 3.4 %collective-permute-start.1 = (bf16[1536,256]{1,0:T(8,128)(2,1)S(1)}, bf16[1536,256]{1,0:T(8,128)(2,1)S(1)}, u32[]{:S(2)}, u32[]{:S(2)}) collective-permute-start(bf16[1536,256]{1,0:T(8,128)(2,1)S(1)} %get-tuple-element.53), channel_id=1, source_target_pairs={{0,4},{1,5},{2,6},{3,7},{4,0},{5,1},{6,2},{7,3},{8,12},{9,13},{10,... | collective-permute-start | bytes 2359304 | tf_op jit(solution)/shard_map/ppermute | solution.py:81
  68.4 10.0 %collective-permute-start.2 = (bf16[4,8,24,384]{3,2,1,0:T(8,128)(2,1)S(1)}, bf16[4,8,24,384]{3,2,1,0:T(8,128)(2,1)S(1)}, u32[]{:S(2)}, u32[]{:S(2)}) collective-permute-start(bf16[4,8,24,384]{3,2,1,0:T(8,128)(2,1)S(1)} %get-tuple-element.54), channel_id=1, source_target_pairs={{0,1},{1,0},{2,3},{3,2},{4,7},{5,6},{6,5},{7,4},{8,9},{9,8},{10,11... | collective-permute-start | bytes 1769480 | tf_op jit(solution)/shard_map/ppermute | solution.py:81
  72.2 10.0 %collective-permute-start.5 = (bf16[4,8,24,384]{3,2,1,0:T(8,128)(2,1)S(1)}, bf16[4,8,24,384]{3,2,1,0:T(8,128)(2,1)S(1)}, u32[]{:S(2)}, u32[]{:S(2)}) collective-permute-start(bf16[4,8,24,384]{3,2,1,0:T(8,128)(2,1)S(1)} %get-tuple-element.61), channel_id=1, source_target_pairs={{0,8},{1,9},{2,10},{3,11},{4,28},{5,29},{6,30},{7,31},{8,0},{9,1},... | collective-permute-start | bytes 1769480 | tf_op jit(solution)/shard_map/ppermute | solution.py:81
  72.7 15.2 %collective-permute-start.4 = (bf16[4,8,24,384]{3,2,1,0:T(8,128)(2,1)S(1)}, bf16[4,8,24,384]{3,2,1,0:T(8,128)(2,1)S(1)}, u32[]{:S(2)}, u32[]{:S(2)}) collective-permute-start(bf16[4,8,24,384]{3,2,1,0:T(8,128)(2,1)S(1)} %get-tuple-element.57), channel_id=1, source_target_pairs={{0,1},{1,0},{2,3},{3,2},{4,7},{5,6},{6,5},{7,4},{8,9},{9,8},{10,11... | collective-permute-start | bytes 1769480 | tf_op jit(solution)/shard_map/ppermute | solution.py:81
  73.3 17.2 %collective-permute-start.8 = (bf16[4,8,24,384]{3,2,1,0:T(8,128)(2,1)S(1)}, bf16[4,8,24,384]{3,2,1,0:T(8,128)(2,1)S(1)}, u32[]{:S(2)}, u32[]{:S(2)}) collective-permute-start(bf16[4,8,24,384]{3,2,1,0:T(8,128)(2,1)S(1)} %get-tuple-element.66), channel_id=1, source_target_pairs={{0,8},{1,9},{2,10},{3,11},{4,28},{5,29},{6,30},{7,31},{8,0},{9,1},... | collective-permute-start | bytes 1769480 | tf_op jit(solution)/shard_map/ppermute | solution.py:81
  78.6 12.9 %collective-permute-start.3 = (bf16[4,8,24,384]{3,2,1,0:T(8,128)(2,1)S(1)}, bf16[4,8,24,384]{3,2,1,0:T(8,128)(2,1)S(1)}, u32[]{:S(2)}, u32[]{:S(2)}) collective-permute-start(bf16[4,8,24,384]{3,2,1,0:T(8,128)(2,1)S(1)} %add_convert_fusion.1), channel_id=1, source_target_pairs={{0,3},{1,2},{2,1},{3,0},{4,5},{5,4},{6,7},{7,6},{8,11},{9,10},{10,... | collective-permute-start | bytes 1769480 | tf_op jit(solution)/shard_map/ppermute | solution.py:81
  82.3 13.8 %collective-permute-start.7 = (bf16[4,8,24,384]{3,2,1,0:T(8,128)(2,1)S(1)}, bf16[4,8,24,384]{3,2,1,0:T(8,128)(2,1)S(1)}, u32[]{:S(2)}, u32[]{:S(2)}) collective-permute-start(bf16[4,8,24,384]{3,2,1,0:T(8,128)(2,1)S(1)} %add_convert_fusion), channel_id=1, source_target_pairs={{0,24},{1,25},{2,26},{3,27},{4,12},{5,13},{6,14},{7,15},{8,16},{9,... | collective-permute-start | bytes 1769480 | tf_op jit(solution)/shard_map/ppermute | solution.py:81
  91.5 6.8 %collective-permute-start.6 = (bf16[2,8,24,384]{3,2,1,0:T(8,128)(2,1)S(1)}, bf16[2,8,24,384]{3,2,1,0:T(8,128)(2,1)S(1)}, u32[]{:S(2)}, u32[]{:S(2)}) collective-permute-start(bf16[2,8,24,384]{3,2,1,0:T(8,128)(2,1)S(1)} %add_convert_fusion.3), channel_id=1, source_target_pairs={{0,8},{1,9},{2,10},{3,11},{4,28},{5,29},{6,30},{7,31},{8,0},{9,1},... | collective-permute-start | bytes 884744 | tf_op jit(solution)/shard_map/ppermute | solution.py:81
  96.2 6.8 %collective-permute-start.10 = (bf16[2,8,24,384]{3,2,1,0:T(8,128)(2,1)S(1)}, bf16[2,8,24,384]{3,2,1,0:T(8,128)(2,1)S(1)}, u32[]{:S(2)}, u32[]{:S(2)}) collective-permute-start(bf16[2,8,24,384]{3,2,1,0:T(8,128)(2,1)S(1)} %add_convert_fusion.2), channel_id=1, source_target_pairs={{0,1},{1,0},{2,3},{3,2},{4,7},{5,6},{6,5},{7,4},{8,9},{9,8},{10,11... | collective-permute-start | bytes 884744 | tf_op jit(solution)/shard_map/ppermute | solution.py:81
  98.4 6.4 %collective-permute-start.9 = (bf16[1,8,24,384]{3,2,1,0:T(8,128)(2,1)S(1)}, bf16[1,8,24,384]{3,2,1,0:T(8,128)(2,1)S(1)}, u32[]{:S(2)}, u32[]{:S(2)}) collective-permute-start(bf16[1,8,24,384]{3,2,1,0:T(8,128)(2,1)S(1)} %slice.160), channel_id=1, source_target_pairs={{0,24},{1,25},{2,26},{3,27},{4,12},{5,13},{6,14},{7,15},{8,16},{9,... | collective-permute-start | bytes 442376 | tf_op jit(solution)/shard_map/ppermute | solution.py:81
  103.2 6.4 %collective-permute-start.11 = (bf16[1,8,24,384]{3,2,1,0:T(8,128)(2,1)S(1)}, bf16[1,8,24,384]{3,2,1,0:T(8,128)(2,1)S(1)}, u32[]{:S(2)}, u32[]{:S(2)}) collective-permute-start(bf16[1,8,24,384]{3,2,1,0:T(8,128)(2,1)S(1)} %slice.159), channel_id=1, source_target_pairs={{0,3},{1,2},{2,1},{3,0},{4,5},{5,4},{6,7},{7,6},{8,11},{9,10},{10,... | collective-permute-start | bytes 442376 | tf_op jit(solution)/shard_map/ppermute | solution.py:81
  109.7 6.7 %collective-permute-start.12 = (bf16[4,2,24,384]{3,2,0,1:T(8,128)(2,1)S(1)}, bf16[4,2,24,384]{3,2,0,1:T(8,128)(2,1)S(1)}, u32[]{:S(2)}, u32[]{:S(2)}) collective-permute-start(bf16[4,2,24,384]{3,2,0,1:T(8,128)(2,1)S(1)} %slice.158), channel_id=1, source_target_pairs={{0,32},{1,33},{2,34},{3,35},{4,228},{5,229},{6,230},{7,231},{8,40}... | collective-permute-start | bytes 442376 | tf_op jit(solution)/shard_map/ppermute | solution.py:81
  116.5 5.8 %collective-permute-start.13 = (bf16[2,2,24,384]{3,2,0,1:T(8,128)(2,1)S(1)}, bf16[2,2,24,384]{3,2,0,1:T(8,128)(2,1)S(1)}, u32[]{:S(2)}, u32[]{:S(2)}) collective-permute-start(bf16[2,2,24,384]{3,2,0,1:T(8,128)(2,1)S(1)} %get-tuple-element.77), channel_id=1, source_target_pairs={{0,64},{1,65},{2,66},{3,67},{4,196},{5,197},{6,198},{7,199},{8,72}... | collective-permute-start | bytes 221192 | tf_op jit(solution)/shard_map/ppermute | solution.py:81
  122.3 7.1 %collective-permute-start.14 = (bf16[1,2,24,384]{3,2,0,1:T(8,128)(2,1)S(1)}, bf16[1,2,24,384]{3,2,0,1:T(8,128)(2,1)S(1)}, u32[]{:S(2)}, u32[]{:S(2)}) collective-permute-start(bf16[1,2,24,384]{3,2,0,1:T(8,128)(2,1)S(1)} %fusion.6), channel_id=1, source_target_pairs={{0,224},{1,225},{2,226},{3,227},{4,36},{5,37},{6,38},{7,39},{8,232... | collective-permute-start | bytes 110600 | tf_op jit(solution)/shard_map/ppermute | solution.py:81
  129.4 5.3 %collective-permute-start.15 = (bf16[2,24,384]{2,1,0:T(8,128)(2,1)S(1)}, bf16[2,24,384]{2,1,0:T(8,128)(2,1)S(1)}, u32[]{:S(2)}, u32[]{:S(2)}) collective-permute-start(bf16[2,24,384]{2,1,0:T(8,128)(2,1)S(1)} %fusion.9), channel_id=1, source_target_pairs={{0,3},{1,2},{2,1},{3,0},{4,5},{5,4},{6,7},{7,6},{8,11},{9,10},{10,... | collective-permute-start | bytes 110600 | tf_op jit(solution)/shard_map/ppermute | solution.py:81
  134.7 4.4 %collective-permute-start.16 = (bf16[2,48,384]{2,1,0:T(8,128)(2,1)S(1)}, bf16[2,48,384]{2,1,0:T(8,128)(2,1)S(1)}, u32[]{:S(2)}, u32[]{:S(2)}) collective-permute-start(bf16[2,48,384]{2,1,0:T(8,128)(2,1)S(1)} %pad_maximum_fusion.1), channel_id=1, source_target_pairs={{0,1},{1,0},{2,3},{3,2},{4,7},{5,6},{6,5},{7,4},{8,9},{9,8},{10,11... | collective-permute-start | bytes 221192 | tf_op jit(solution)/shard_map/ppermute | solution.py:81

commit v9 on v8

--- a/solution.py
+++ b/solution.py
@@ -135,7 +135,7 @@
     out_ref[...] = got.reshape(shards, cap, width).astype(bf16)
 
 
-def turn_kernel(up_hbm, up_t_ref, up_ref, sems):
+def turn_kernel(up_hbm, first_ref, rest_ref, up_ref, sems):
     parts = sems.shape[0]
     copies = []
     for t in range(parts):
@@ -145,7 +145,10 @@
     for t in range(parts):
         cut = slice(t * WIDE, (t + 1) * WIDE)
         copies[t].wait()
-        up_t_ref[cut, :] = up_ref[:, cut].T
+        if t:
+            rest_ref[(t - 1) * WIDE : t * WIDE, :] = up_ref[:, cut].T
+        else:
+            first_ref[...] = up_ref[:, cut].T
 
 
 def share_units(units_ref, core, mine_ref, other_ref, t):
@@ -156,29 +159,33 @@
 
 
 def forward_kernel(
-    place_ref, got_ref, slot_ref, question_ref, reader_ref, up_t_hbm, down_hbm,
+    place_ref, got_ref, slot_ref, question_ref, reader_ref, first_ref, rest_hbm, down_hbm,
     derivative_ref, states_ref, grad_emb_ref, slope_ref, mine_ref, pack_ref, down_ref,
-    hidden_ref, up_t_ref, sems,
+    hidden_ref, rest_ref, sems,
 ):
     width = question_ref.shape[1]
     parts = hidden_ref.shape[0] // WIDE
     ups, downs = [], []
     for t in range(parts):
         cut = pl.ds(t * WIDE, WIDE)
-        ups.append(pltpu.make_async_copy(up_t_hbm.at[cut, :], up_t_ref.at[cut, :], sems.at[0, t]))
+        if t < parts - 1:
+            ups.append(pltpu.make_async_copy(rest_hbm.at[cut, :], rest_ref.at[cut, :], sems.at[0, t]))
         downs.append(pltpu.make_async_copy(down_hbm.at[cut, :], down_ref.at[cut, :], sems.at[1, t]))
-    ups[0].start()
-    ups[1].start()
+    copies = ups + downs
+    copies[0].start()
+    copies[1].start()
     lanes = lax.broadcasted_iota(i32, (Q * K, got_ref.shape[0]), 1)
     onehot = (lanes == slot_ref[:, :1]).astype(f32).astype(bf16)
     states = dot(onehot, got_ref[...], ((1,), (0,))).astype(bf16)
     states_ref[...] = states
     for t in range(parts):
         cut = slice(t * WIDE, (t + 1) * WIDE)
-        ups[t].wait()
-        for copy in (ups + downs)[2 * t + 2 : 2 * t + 4]:
+        for copy in copies[2 * t + 2 : 2 * t + 4]:
             copy.start()
-        pre = dot(up_t_ref[cut, :], states, ((1,), (1,)))
+        if t:
+            ups[t - 1].wait()
+        wide_up = rest_ref[(t - 1) * WIDE : t * WIDE, :] if t else first_ref[...]
+        pre = dot(wide_up, states, ((1,), (1,)))
         square = pre * pre
         tangent = jnp.tanh(pre * (gelu_coeff + (gelu_coeff * cubic) * square))
         gate = 0.5 + 0.5 * tangent
@@ -279,7 +286,7 @@
         scratch_shapes=[pltpu.SemaphoreType.DMA],
         compiler_params=pltpu.CompilerParams(vmem_limit_bytes=16 << 20),
         name="route",
-    )(owners, passage_rows, far(index_states))
+    )(far(owners), far(passage_rows), far(index_states))
 
 
 def fetch(rows_in, index_states):
@@ -301,25 +308,28 @@
     return pl.pallas_call(
         turn_kernel,
         in_specs=[HBM],
-        out_specs=VMEM,
+        out_specs=[VMEM] * 2,
         scratch_shapes=[pltpu.VMEM((width, hidden), bf16), pltpu.SemaphoreType.DMA((hidden // WIDE,))],
-        out_shape=jax.ShapeDtypeStruct((hidden, width), bf16),
+        out_shape=(
+            pltpu.VMEM((WIDE, width), bf16),
+            jax.ShapeDtypeStruct((hidden - WIDE, width), bf16),
+        ),
         compiler_params=pltpu.CompilerParams(vmem_limit_bytes=24 << 20),
         cost_estimate=pl.CostEstimate(flops=0, bytes_accessed=16 << 20, transcendentals=0),
         name="turn",
     )(far(w_up))
 
 
-def forward(place, got, slot, questions, reader, up_t, w_down):
-    hidden, width = up_t.shape
+def forward(place, got, slot, questions, reader, first, rest, w_down):
+    hidden, width = w_down.shape
     rows = Q * K
     return pl.pallas_call(
         forward_kernel,
-        in_specs=[SMEM, VMEM, VMEM, VMEM, VMEM, HBM, HBM],
+        in_specs=[SMEM] + [VMEM] * 5 + [HBM] * 2,
         out_specs=[VMEM] * 7,
         scratch_shapes=[
             pltpu.VMEM((hidden, rows), bf16),
-            pltpu.VMEM((hidden, width), bf16),
+            pltpu.VMEM((hidden - WIDE, width), bf16),
             pltpu.SemaphoreType.DMA((2, hidden // WIDE)),
         ],
         out_shape=(
@@ -336,7 +346,7 @@
             flops=4 * rows * width * hidden, bytes_accessed=16 << 20, transcendentals=rows * hidden
         ),
         name="forward",
-    )(place, got, slot, questions, reader, far(up_t), far(w_down))
+    )(place, got, slot, questions, reader, near(first), far(rest), far(w_down))
 
 
 def backward(place, grad_emb, slope, w_down):
@@ -434,7 +444,7 @@
     states_out = fetch(rows_in, index_near)
     got = lax.all_to_all(states_out, "shard", split_axis=0, concat_axis=0, tiled=True)
     derivative, states, grad_emb, slope, hidden, pack, down = forward(
-        place, got.reshape(shards * CAP, width), slot, questions, reader, turn(w_up), w_down
+        place, got.reshape(shards * CAP, width), slot, questions, reader, *turn(w_up), w_down
     )
     pack = swap(pack, "c")
     grad_pre, other = backward(place, grad_emb, slope, down)

time: 140 us -> 139 us (level)
  local copies, waits for them, and re-layouts: 3.73 us -> 1.96 us
    unnamed x10 -> x6, local copies, waits for them, and re-layouts: 3.51 us -> 1.75 us
where the time goes in v9:
time: 139 us; the launch traced here: 138 us
  waiting for transfers between devices  73.5 us (53%)
  Pallas kernels  21 us (15%)
  starting transfers between devices  20.2 us (15%)
  blocking collectives  18.9 us (14%)
  local copies, waits for them, and re-layouts  1.96 us (1%)
  other arithmetic  1.91 us (1%)
    ppermute x17, waiting for transfers between devices, swap(): return lax.ppermute(array, AXES, partner(step))  54.7 us
    all_to_all x1, blocking collectives, on_device(): lax.all_to_all(send_rows, 'shard', split_axis=0, concat_axis=0, tiled=True)  18.9 us
    all_to_all x1, waiting for transfers between devices, on_device(): lax.all_to_all(states_out, 'shard', split_axis=0, concat_axis=0, tiled=True)  18.8 us
    ppermute x17, starting transfers between devices, swap(): return lax.ppermute(array, AXES, partner(step))  13.8 us
    pallas_call x1, Pallas kernels, forward(): pl.pallas_call(forward_kernel, in_specs=[SMEM] + [VMEM] * 5 + [HBM] * 2,...  7.71 us
    all_to_all x1, starting transfers between devices, on_device(): lax.all_to_all(states_out, 'shard', split_axis=0, concat_axis=0, tiled=True)  6.44 us
    pallas_call x2, Pallas kernels, gradient(): pl.pallas_call(functools.partial(gradient_kernel, x_first, right_at), in_...  4.31 us
  transfers between devices with their start and end apart: 18, of which 17 were waited for; matrix products, arithmetic and copies ran while one was open for 1% of the time, Pallas kernels for 7%

profile of v9, /device:TPU:64, one launch (start us, length us, event | category | flops | bytes accessed | tf_op | source)
XLA Modules:
  0.0 138.3 jit_solution(1103719075123321999)
XLA Ops:
  0.6 2.1 %route.1 = (s32[64,1,128]{2,1,0:T(1,128)S(1)}, s32[256,128]{1,0:T(8,128)S(1)}, bf16[1024,768]{1,0:T(8,128)(2,1)S(1)}) custom-call(s32[8,32]{1,0:T(8,128)} %bitcast.21, s32[8,32]{1,0:T(8,128)} %row_ref.1, bf16[1024,768]{1,0:T(8,128)(2,1)} %index_hbm.1), custom_call_target="tpu_custom_call" | custom-call | tf_op jit(solution)/shard_map/route/pallas_call | solution.py:277
  2.8 18.9 %all_to_all.10.rows_ref = s32[64,1,128]{2,1,0:T(1,128)S(1)} all-to-all(s32[64,1,128]{2,1,0:T(1,128)S(1)} %get-tuple-element.42), channel_id=1, replica_groups=mesh['shard'=64,'rep'=4] {'shard'}, dimensions={0} | all-to-all | bytes 65536 | tf_op jit(solution)/shard_map/all_to_all | solution.py:443
  21.7 1.9 %fetch.1 = bf16[64,8,768]{2,1,0:T(8,128)(2,1)} custom-call(s32[64,1,128]{2,1,0:T(1,128)S(1)} %all_to_all.10.rows_ref, bf16[1024,768]{1,0:T(8,128)(2,1)S(1)} %get-tuple-element.43.index_ref), custom_call_target="tpu_custom_call" | custom-call | tf_op jit(solution)/shard_map/fetch/pallas_call | solution.py:294
  23.7 6.4 %all-to-all-start.1 = ((bf16[64,8,768]{2,1,0:T(8,128)(2,1)}), bf16[64,8,768]{2,1,0:T(8,128)(2,1)S(1)}, u32[]{:S(2)}, u32[]{:S(2)}) async-start(bf16[64,8,768]{2,1,0:T(8,128)(2,1)} %fetch.1), calls=%async_computation.1 | async-start | bytes 1572864 | tf_op jit(solution)/shard_map/all_to_all | solution.py:445
  30.2 2.8 %turn.1 = (bf16[768,768]{1,0:T(8,128)(2,1)S(1)}, bf16[2304,768]{1,0:T(8,128)(2,1)S(1)}) custom-call(bf16[768,3072]{1,0:T(8,128)(2,1)} %up_hbm.1), custom_call_target="tpu_custom_call" | custom-call | bytes 16777216 | tf_op jit(solution)/shard_map/turn/pallas_call | solution.py:308
  32.9 1.7 %copy-done = bf16[2304,768]{1,0:T(8,128)(2,1)} copy-done((bf16[2304,768]{1,0:T(8,128)(2,1)}, bf16[2304,768]{1,0:T(8,128)(2,1)S(1)}, u32[]{:S(2)}) %copy-start) | copy-done | bytes 3538968
  34.7 18.8 %all-to-all-done.1 = bf16[64,8,768]{2,1,0:T(8,128)(2,1)S(1)} async-done(((bf16[64,8,768]{2,1,0:T(8,128)(2,1)}), bf16[64,8,768]{2,1,0:T(8,128)(2,1)S(1)}, u32[]{:S(2)}, u32[]{:S(2)}) %all-to-all-start.1) | async-done | bytes 786464 | tf_op jit(solution)/shard_map/all_to_all | solution.py:445
  53.5 7.7 %forward.1 = (f32[8,32]{1,0:T(8,128)}, bf16[256,768]{1,0:T(8,128)(2,1)S(1)}, bf16[256,768]{1,0:T(8,128)(2,1)S(1)}, f32[3072,256]{1,0:T(8,128)S(1)}, bf16[1536,25...) custom-call(s32[4]{0:T(128)S(1)} %pad_add_fusion.place_ref, ...), custom_call_target="tpu_custom_call" | custom-call | flops 2415919104 | bytes 16777216 | tf_op jit(solution)/shard_map/forward/pallas_call | solution.py:326
  61.3 2.1 %backward.1 = (bf16[1536,256]{1,0:T(8,128)(2,1)S(1)}, bf16[1536,256]{1,0:T(8,128)(2,1)S(1)}) custom-call(s32[4]{0:T(128)S(1)} %pad_add_fusion.place_ref, bf16[256,768]{1,0:T(8,128)(2,1)S(1)} %get-tuple-element.50.right_ref.grad_emb_ref, f32[3072,256]{1,0:T(8,128)S(1)} %get-tuple-element.55.slope_ref, bf16[3072,768]{1,0:T(8,128)(2,1)S(1)} %get-tuple-element.56.down_ref), custom_call_target="tpu_custom_call" | custom-call | flops 1207959552 | bytes 8388608 | tf_op jit(solution)/shard_map/backward/pallas_call | solution.py:355
  64.7 2.1 %gradient_down.1 = (f32[4,8,24,384]{3,2,1,0:T(8,128)S(1)}, f32[4,8,24,384]{3,2,1,0:T(8,128)S(1)}, bf16[4,8,24,384]{3,2,1,0:T(8,128)(2,1)S(1)}, bf16[4,8,24,384]{3,2,1,0:T(8,128)(2,1)S(1)}) custom-call(s32[4]{0:T(128)S(1)} %pad_add_fusion.place_ref, bf16[1536,256]{1,0:T(8,128)(2,1)S(1)} %get-tuple-element.48.mine_ref, ...), custom_call_target="tpu_custom_call" | custom-call | flops 1207959552 | bytes 8388608 | tf_op jit(solution)/shard_map/gradient_down/pallas_call | solution.py:372
  66.9 1.6 %collective-permute-start.2 = (bf16[4,8,24,384]{3,2,1,0:T(8,128)(2,1)S(1)}, bf16[4,8,24,384]{3,2,1,0:T(8,128)(2,1)S(1)}, u32[]{:S(2)}, u32[]{:S(2)}) collective-permute-start(bf16[4,8,24,384]{3,2,1,0:T(8,128)(2,1)S(1)} %get-tuple-element.58), channel_id=1, source_target_pairs={{0,1},{1,0},{2,3},{3,2},{4,7},{5,6},{6,5},{7,4},{8,9},{9,8},{10,11... | collective-permute-start | bytes 1769480 | tf_op jit(solution)/shard_map/ppermute | solution.py:81
  68.4 2.2 %gradient_up.1 = (f32[4,8,24,384]{3,2,1,0:T(8,128)S(1)}, f32[4,8,24,384]{3,2,1,0:T(8,128)S(1)}, bf16[4,8,24,384]{3,2,1,0:T(8,128)(2,1)S(1)}, bf16[4,8,24,384]{3,2,1,0:T(8,128)(2,1)S(1)}) custom-call(s32[4]{0:T(128)S(1)} %pad_add_fusion.place_ref, bf16[1536,256]{1,0:T(8,128)(2,1)S(1)} %get-tuple-element.62.mine_ref, ...), custom_call_target="tpu_custom_call" | custom-call | flops 1207959552 | bytes 8388608 | tf_op jit(solution)/shard_map/gradient_up/pallas_call | solution.py:372
  71.7 1.6 %collective-permute-start.8 = (bf16[4,8,24,384]{3,2,1,0:T(8,128)(2,1)S(1)}, bf16[4,8,24,384]{3,2,1,0:T(8,128)(2,1)S(1)}, u32[]{:S(2)}, u32[]{:S(2)}) collective-permute-start(bf16[4,8,24,384]{3,2,1,0:T(8,128)(2,1)S(1)} %get-tuple-element.70), channel_id=1, source_target_pairs={{0,8},{1,9},{2,10},{3,11},{4,28},{5,29},{6,30},{7,31},{8,0},{9,1},... | collective-permute-start | bytes 1769480 | tf_op jit(solution)/shard_map/ppermute | solution.py:81
  73.3 3.6 %collective-permute-done.2 = bf16[4,8,24,384]{3,2,1,0:T(8,128)(2,1)S(1)} collective-permute-done((bf16[4,8,24,384]{3,2,1,0:T(8,128)(2,1)S(1)}, bf16[4,8,24,384]{3,2,1,0:T(8,128)(2,1)S(1)}, u32[]{:S(2)}, u32[]{:S(2)}) %collective-permute-start.2) | collective-permute-done | bytes 589856 | tf_op jit(solution)/shard_map/ppermute | solution.py:81
  77.0 2.8 %collective-permute-start.3 = (bf16[4,8,24,384]{3,2,1,0:T(8,128)(2,1)S(1)}, bf16[4,8,24,384]{3,2,1,0:T(8,128)(2,1)S(1)}, u32[]{:S(2)}, u32[]{:S(2)}) collective-permute-start(bf16[4,8,24,384]{3,2,1,0:T(8,128)(2,1)S(1)} %add_convert_fusion.1), channel_id=1, source_target_pairs={{0,3},{1,2},{2,1},{3,0},{4,5},{5,4},{6,7},{7,6},{8,11},{9,10},{10,... | collective-permute-start | bytes 1769480 | tf_op jit(solution)/shard_map/ppermute | solution.py:81
  79.8 0.8 collective-permute-done.5
  80.7 1.6 %collective-permute-start.7 = (bf16[4,8,24,384]{3,2,1,0:T(8,128)(2,1)S(1)}, bf16[4,8,24,384]{3,2,1,0:T(8,128)(2,1)S(1)}, u32[]{:S(2)}, u32[]{:S(2)}) collective-permute-start(bf16[4,8,24,384]{3,2,1,0:T(8,128)(2,1)S(1)} %add_convert_fusion), channel_id=1, source_target_pairs={{0,24},{1,25},{2,26},{3,27},{4,12},{5,13},{6,14},{7,15},{8,16},{9,... | collective-permute-start | bytes 1769480 | tf_op jit(solution)/shard_map/ppermute | solution.py:81
  82.3 4.1 %collective-permute-done.4 = bf16[4,8,24,384]{3,2,1,0:T(8,128)(2,1)S(1)} collective-permute-done((bf16[4,8,24,384]{3,2,1,0:T(8,128)(2,1)S(1)}, bf16[4,8,24,384]{3,2,1,0:T(8,128)(2,1)S(1)}, u32[]{:S(2)}, u32[]{:S(2)}) %collective-permute-start.4) | collective-permute-done | bytes 589856 | tf_op jit(solution)/shard_map/ppermute | solution.py:81
  86.5 2.3 %collective-permute-done.8 = bf16[4,8,24,384]{3,2,1,0:T(8,128)(2,1)S(1)} collective-permute-done((bf16[4,8,24,384]{3,2,1,0:T(8,128)(2,1)S(1)}, bf16[4,8,24,384]{3,2,1,0:T(8,128)(2,1)S(1)}, u32[]{:S(2)}, u32[]{:S(2)}) %collective-permute-start.8) | collective-permute-done | bytes 589856 | tf_op jit(solution)/shard_map/ppermute | solution.py:81
  89.0 0.8 collective-permute-done.3
  90.6 4.0 %collective-permute-done.7 = bf16[4,8,24,384]{3,2,1,0:T(8,128)(2,1)S(1)} collective-permute-done((bf16[4,8,24,384]{3,2,1,0:T(8,128)(2,1)S(1)}, bf16[4,8,24,384]{3,2,1,0:T(8,128)(2,1)S(1)}, u32[]{:S(2)}, u32[]{:S(2)}) %collective-permute-start.7) | collective-permute-done | bytes 589856 | tf_op jit(solution)/shard_map/ppermute | solution.py:81
  95.0 1.8 %collective-permute-done.6 = bf16[2,8,24,384]{3,2,1,0:T(8,128)(2,1)S(1)} collective-permute-done((bf16[2,8,24,384]{3,2,1,0:T(8,128)(2,1)S(1)}, bf16[2,8,24,384]{3,2,1,0:T(8,128)(2,1)S(1)}, u32[]{:S(2)}, u32[]{:S(2)}) %collective-permute-start.6) | collective-permute-done | bytes 294944 | tf_op jit(solution)/shard_map/ppermute | solution.py:81
  96.9 1.6 %collective-permute-start.9 = (bf16[1,8,24,384]{3,2,1,0:T(8,128)(2,1)S(1)}, bf16[1,8,24,384]{3,2,1,0:T(8,128)(2,1)S(1)}, u32[]{:S(2)}, u32[]{:S(2)}) collective-permute-start(bf16[1,8,24,384]{3,2,1,0:T(8,128)(2,1)S(1)} %slice.160), channel_id=1, source_target_pairs={{0,24},{1,25},{2,26},{3,27},{4,12},{5,13},{6,14},{7,15},{8,16},{9,... | collective-permute-start | bytes 442376 | tf_op jit(solution)/shard_map/ppermute | solution.py:81
  98.4 3.0 %collective-permute-done.10 = bf16[2,8,24,384]{3,2,1,0:T(8,128)(2,1)S(1)} collective-permute-done((bf16[2,8,24,384]{3,2,1,0:T(8,128)(2,1)S(1)}, bf16[2,8,24,384]{3,2,1,0:T(8,128)(2,1)S(1)}, u32[]{:S(2)}, u32[]{:S(2)}) %collective-permute-start.10) | collective-permute-done | bytes 294944 | tf_op jit(solution)/shard_map/ppermute | solution.py:81
  102.2 1.1 collective-permute-done.9
  103.3 4.7 %collective-permute-done.11 = bf16[1,8,24,384]{3,2,1,0:T(8,128)(2,1)S(1)} collective-permute-done((bf16[1,8,24,384]{3,2,1,0:T(8,128)(2,1)S(1)}, bf16[1,8,24,384]{3,2,1,0:T(8,128)(2,1)S(1)}, u32[]{:S(2)}, u32[]{:S(2)}) %collective-permute-start.11) | collective-permute-done | bytes 147488 | tf_op jit(solution)/shard_map/ppermute | solution.py:81
  108.2 0.9 collective-permute-start.12
  109.1 5.8 %collective-permute-done.12 = bf16[4,2,24,384]{3,2,0,1:T(8,128)(2,1)S(1)} collective-permute-done((bf16[4,2,24,384]{3,2,0,1:T(8,128)(2,1)S(1)}, bf16[4,2,24,384]{3,2,0,1:T(8,128)(2,1)S(1)}, u32[]{:S(2)}, u32[]{:S(2)}) %collective-permute-start.12) | collective-permute-done | bytes 147488 | tf_op jit(solution)/shard_map/ppermute | solution.py:81
  115.0 5.7 %collective-permute-done.13 = bf16[2,2,24,384]{3,2,0,1:T(8,128)(2,1)S(1)} collective-permute-done((bf16[2,2,24,384]{3,2,0,1:T(8,128)(2,1)S(1)}, bf16[2,2,24,384]{3,2,0,1:T(8,128)(2,1)S(1)}, u32[]{:S(2)}, u32[]{:S(2)}) %collective-permute-start.13) | collective-permute-done | bytes 73760 | tf_op jit(solution)/shard_map/ppermute | solution.py:81
  120.9 7.0 %collective-permute-done.14 = bf16[1,2,24,384]{3,2,0,1:T(8,128)(2,1)S(1)} collective-permute-done((bf16[1,2,24,384]{3,2,0,1:T(8,128)(2,1)S(1)}, bf16[1,2,24,384]{3,2,0,1:T(8,128)(2,1)S(1)}, u32[]{:S(2)}, u32[]{:S(2)}) %collective-permute-start.14) | collective-permute-done | bytes 36896 | tf_op jit(solution)/shard_map/ppermute | solution.py:81
  128.0 5.1 %collective-permute-done.15 = bf16[2,24,384]{2,1,0:T(8,128)(2,1)S(1)} collective-permute-done((bf16[2,24,384]{2,1,0:T(8,128)(2,1)S(1)}, bf16[2,24,384]{2,1,0:T(8,128)(2,1)S(1)}, u32[]{:S(2)}, u32[]{:S(2)}) %collective-permute-start.15) | collective-permute-done | bytes 36896 | tf_op jit(solution)/shard_map/ppermute | solution.py:81
  133.2 4.3 %collective-permute-done.16 = bf16[2,48,384]{2,1,0:T(8,128)(2,1)S(1)} collective-permute-done((bf16[2,48,384]{2,1,0:T(8,128)(2,1)S(1)}, bf16[2,48,384]{2,1,0:T(8,128)(2,1)S(1)}, u32[]{:S(2)}, u32[]{:S(2)}) %collective-permute-start.16) | collective-permute-done | bytes 73760 | tf_op jit(solution)/shard_map/ppermute | solution.py:81
  (42 shorter events, 6.3 us)
Async XLA Ops:
  23.7 29.8 %all-to-all-start.1 = ((bf16[64,8,768]{2,1,0:T(8,128)(2,1)}), bf16[64,8,768]{2,1,0:T(8,128)(2,1)S(1)}, u32[]{:S(2)}, u32[]{:S(2)}) async-start(bf16[64,8,768]{2,1,0:T(8,128)(2,1)} %fetch.1), calls=%async_computation.1 | async-start | bytes 1572864 | tf_op jit(solution)/shard_map/all_to_all | solution.py:445
  30.1 23.3 %copy-start.1 = (bf16[8,768]{1,0:T(8,128)(2,1)S(1)}, bf16[8,768]{1,0:T(8,128)(2,1)}, u32[]{:S(2)}) copy-start(bf16[8,768]{1,0:T(8,128)(2,1)} %question_ref.1) | copy-start | bytes 36868
  30.1 23.3 %copy-start.2 = (f32[8,32]{1,0:T(8,128)S(1)}, f32[8,32]{1,0:T(8,128)}, u32[]{:S(2)}) copy-start(f32[8,32]{1,0:T(8,128)} %reader_ref.1) | copy-start | bytes 3076
  32.9 1.7 %copy-start = (bf16[2304,768]{1,0:T(8,128)(2,1)}, bf16[2304,768]{1,0:T(8,128)(2,1)S(1)}, u32[]{:S(2)}) copy-start(bf16[2304,768]{1,0:T(8,128)(2,1)S(1)} %get-tuple-element.46.rest_hbm) | copy-start | bytes 10616836
  61.2 3.5 %collective-permute-start = (bf16[3072,256]{1,0:T(8,128)(2,1)S(1)}, bf16[3072,256]{1,0:T(8,128)(2,1)S(1)}, u32[]{:S(2)}, u32[]{:S(2)}) collective-permute-start(bf16[3072,256]{1,0:T(8,128)(2,1)S(1)} %get-tuple-element.49), channel_id=1, source_target_pairs={{0,4},{1,5},{2,6},{3,7},{4,0},{5,1},{6,2},{7,3},{8,12},{9,13},{10,... | collective-permute-start | bytes 4718600 | tf_op jit(solution)/shard_map/ppermute | solution.py:81
  63.4 3.4 %collective-permute-start.1 = (bf16[1536,256]{1,0:T(8,128)(2,1)S(1)}, bf16[1536,256]{1,0:T(8,128)(2,1)S(1)}, u32[]{:S(2)}, u32[]{:S(2)}) collective-permute-start(bf16[1536,256]{1,0:T(8,128)(2,1)S(1)} %get-tuple-element.57), channel_id=1, source_target_pairs={{0,4},{1,5},{2,6},{3,7},{4,0},{5,1},{6,2},{7,3},{8,12},{9,13},{10,... | collective-permute-start | bytes 2359304 | tf_op jit(solution)/shard_map/ppermute | solution.py:81
  66.9 10.0 %collective-permute-start.2 = (bf16[4,8,24,384]{3,2,1,0:T(8,128)(2,1)S(1)}, bf16[4,8,24,384]{3,2,1,0:T(8,128)(2,1)S(1)}, u32[]{:S(2)}, u32[]{:S(2)}) collective-permute-start(bf16[4,8,24,384]{3,2,1,0:T(8,128)(2,1)S(1)} %get-tuple-element.58), channel_id=1, source_target_pairs={{0,1},{1,0},{2,3},{3,2},{4,7},{5,6},{6,5},{7,4},{8,9},{9,8},{10,11... | collective-permute-start | bytes 1769480 | tf_op jit(solution)/shard_map/ppermute | solution.py:81
  70.6 10.0 %collective-permute-start.5 = (bf16[4,8,24,384]{3,2,1,0:T(8,128)(2,1)S(1)}, bf16[4,8,24,384]{3,2,1,0:T(8,128)(2,1)S(1)}, u32[]{:S(2)}, u32[]{:S(2)}) collective-permute-start(bf16[4,8,24,384]{3,2,1,0:T(8,128)(2,1)S(1)} %get-tuple-element.65), channel_id=1, source_target_pairs={{0,8},{1,9},{2,10},{3,11},{4,28},{5,29},{6,30},{7,31},{8,0},{9,1},... | collective-permute-start | bytes 1769480 | tf_op jit(solution)/shard_map/ppermute | solution.py:81
  71.2 15.2 %collective-permute-start.4 = (bf16[4,8,24,384]{3,2,1,0:T(8,128)(2,1)S(1)}, bf16[4,8,24,384]{3,2,1,0:T(8,128)(2,1)S(1)}, u32[]{:S(2)}, u32[]{:S(2)}) collective-permute-start(bf16[4,8,24,384]{3,2,1,0:T(8,128)(2,1)S(1)} %get-tuple-element.61), channel_id=1, source_target_pairs={{0,1},{1,0},{2,3},{3,2},{4,7},{5,6},{6,5},{7,4},{8,9},{9,8},{10,11... | collective-permute-start | bytes 1769480 | tf_op jit(solution)/shard_map/ppermute | solution.py:81
  71.7 17.1 %collective-permute-start.8 = (bf16[4,8,24,384]{3,2,1,0:T(8,128)(2,1)S(1)}, bf16[4,8,24,384]{3,2,1,0:T(8,128)(2,1)S(1)}, u32[]{:S(2)}, u32[]{:S(2)}) collective-permute-start(bf16[4,8,24,384]{3,2,1,0:T(8,128)(2,1)S(1)} %get-tuple-element.70), channel_id=1, source_target_pairs={{0,8},{1,9},{2,10},{3,11},{4,28},{5,29},{6,30},{7,31},{8,0},{9,1},... | collective-permute-start | bytes 1769480 | tf_op jit(solution)/shard_map/ppermute | solution.py:81
  77.0 12.9 %collective-permute-start.3 = (bf16[4,8,24,384]{3,2,1,0:T(8,128)(2,1)S(1)}, bf16[4,8,24,384]{3,2,1,0:T(8,128)(2,1)S(1)}, u32[]{:S(2)}, u32[]{:S(2)}) collective-permute-start(bf16[4,8,24,384]{3,2,1,0:T(8,128)(2,1)S(1)} %add_convert_fusion.1), channel_id=1, source_target_pairs={{0,3},{1,2},{2,1},{3,0},{4,5},{5,4},{6,7},{7,6},{8,11},{9,10},{10,... | collective-permute-start | bytes 1769480 | tf_op jit(solution)/shard_map/ppermute | solution.py:81
  80.7 13.8 %collective-permute-start.7 = (bf16[4,8,24,384]{3,2,1,0:T(8,128)(2,1)S(1)}, bf16[4,8,24,384]{3,2,1,0:T(8,128)(2,1)S(1)}, u32[]{:S(2)}, u32[]{:S(2)}) collective-permute-start(bf16[4,8,24,384]{3,2,1,0:T(8,128)(2,1)S(1)} %add_convert_fusion), channel_id=1, source_target_pairs={{0,24},{1,25},{2,26},{3,27},{4,12},{5,13},{6,14},{7,15},{8,16},{9,... | collective-permute-start | bytes 1769480 | tf_op jit(solution)/shard_map/ppermute | solution.py:81
  89.9 6.8 %collective-permute-start.6 = (bf16[2,8,24,384]{3,2,1,0:T(8,128)(2,1)S(1)}, bf16[2,8,24,384]{3,2,1,0:T(8,128)(2,1)S(1)}, u32[]{:S(2)}, u32[]{:S(2)}) collective-permute-start(bf16[2,8,24,384]{3,2,1,0:T(8,128)(2,1)S(1)} %add_convert_fusion.3), channel_id=1, source_target_pairs={{0,8},{1,9},{2,10},{3,11},{4,28},{5,29},{6,30},{7,31},{8,0},{9,1},... | collective-permute-start | bytes 884744 | tf_op jit(solution)/shard_map/ppermute | solution.py:81
  94.7 6.8 %collective-permute-start.10 = (bf16[2,8,24,384]{3,2,1,0:T(8,128)(2,1)S(1)}, bf16[2,8,24,384]{3,2,1,0:T(8,128)(2,1)S(1)}, u32[]{:S(2)}, u32[]{:S(2)}) collective-permute-start(bf16[2,8,24,384]{3,2,1,0:T(8,128)(2,1)S(1)} %add_convert_fusion.2), channel_id=1, source_target_pairs={{0,1},{1,0},{2,3},{3,2},{4,7},{5,6},{6,5},{7,4},{8,9},{9,8},{10,11... | collective-permute-start | bytes 884744 | tf_op jit(solution)/shard_map/ppermute | solution.py:81
  96.9 6.4 %collective-permute-start.9 = (bf16[1,8,24,384]{3,2,1,0:T(8,128)(2,1)S(1)}, bf16[1,8,24,384]{3,2,1,0:T(8,128)(2,1)S(1)}, u32[]{:S(2)}, u32[]{:S(2)}) collective-permute-start(bf16[1,8,24,384]{3,2,1,0:T(8,128)(2,1)S(1)} %slice.160), channel_id=1, source_target_pairs={{0,24},{1,25},{2,26},{3,27},{4,12},{5,13},{6,14},{7,15},{8,16},{9,... | collective-permute-start | bytes 442376 | tf_op jit(solution)/shard_map/ppermute | solution.py:81
  101.6 6.4 %collective-permute-start.11 = (bf16[1,8,24,384]{3,2,1,0:T(8,128)(2,1)S(1)}, bf16[1,8,24,384]{3,2,1,0:T(8,128)(2,1)S(1)}, u32[]{:S(2)}, u32[]{:S(2)}) collective-permute-start(bf16[1,8,24,384]{3,2,1,0:T(8,128)(2,1)S(1)} %slice.159), channel_id=1, source_target_pairs={{0,3},{1,2},{2,1},{3,0},{4,5},{5,4},{6,7},{7,6},{8,11},{9,10},{10,... | collective-permute-start | bytes 442376 | tf_op jit(solution)/shard_map/ppermute | solution.py:81
  108.2 6.7 %collective-permute-start.12 = (bf16[4,2,24,384]{3,2,0,1:T(8,128)(2,1)S(1)}, bf16[4,2,24,384]{3,2,0,1:T(8,128)(2,1)S(1)}, u32[]{:S(2)}, u32[]{:S(2)}) collective-permute-start(bf16[4,2,24,384]{3,2,0,1:T(8,128)(2,1)S(1)} %slice.158), channel_id=1, source_target_pairs={{0,32},{1,33},{2,34},{3,35},{4,228},{5,229},{6,230},{7,231},{8,40}... | collective-permute-start | bytes 442376 | tf_op jit(solution)/shard_map/ppermute | solution.py:81
  114.9 5.8 %collective-permute-start.13 = (bf16[2,2,24,384]{3,2,0,1:T(8,128)(2,1)S(1)}, bf16[2,2,24,384]{3,2,0,1:T(8,128)(2,1)S(1)}, u32[]{:S(2)}, u32[]{:S(2)}) collective-permute-start(bf16[2,2,24,384]{3,2,0,1:T(8,128)(2,1)S(1)} %get-tuple-element.81), channel_id=1, source_target_pairs={{0,64},{1,65},{2,66},{3,67},{4,196},{5,197},{6,198},{7,199},{8,72}... | collective-permute-start | bytes 221192 | tf_op jit(solution)/shard_map/ppermute | solution.py:81
  120.8 7.1 %collective-permute-start.14 = (bf16[1,2,24,384]{3,2,0,1:T(8,128)(2,1)S(1)}, bf16[1,2,24,384]{3,2,0,1:T(8,128)(2,1)S(1)}, u32[]{:S(2)}, u32[]{:S(2)}) collective-permute-start(bf16[1,2,24,384]{3,2,0,1:T(8,128)(2,1)S(1)} %fusion.6), channel_id=1, source_target_pairs={{0,224},{1,225},{2,226},{3,227},{4,36},{5,37},{6,38},{7,39},{8,232... | collective-permute-start | bytes 110600 | tf_op jit(solution)/shard_map/ppermute | solution.py:81
  127.8 5.3 %collective-permute-start.15 = (bf16[2,24,384]{2,1,0:T(8,128)(2,1)S(1)}, bf16[2,24,384]{2,1,0:T(8,128)(2,1)S(1)}, u32[]{:S(2)}, u32[]{:S(2)}) collective-permute-start(bf16[2,24,384]{2,1,0:T(8,128)(2,1)S(1)} %fusion.9), channel_id=1, source_target_pairs={{0,3},{1,2},{2,1},{3,0},{4,5},{5,4},{6,7},{7,6},{8,11},{9,10},{10,... | collective-permute-start | bytes 110600 | tf_op jit(solution)/shard_map/ppermute | solution.py:81
  133.1 4.4 %collective-permute-start.16 = (bf16[2,48,384]{2,1,0:T(8,128)(2,1)S(1)}, bf16[2,48,384]{2,1,0:T(8,128)(2,1)S(1)}, u32[]{:S(2)}, u32[]{:S(2)}) collective-permute-start(bf16[2,48,384]{2,1,0:T(8,128)(2,1)S(1)} %pad_maximum_fusion.1), channel_id=1, source_target_pairs={{0,1},{1,0},{2,3},{3,2},{4,7},{5,6},{6,5},{7,4},{8,9},{9,8},{10,11... | collective-permute-start | bytes 221192 | tf_op jit(solution)/shard_map/ppermute | solution.py:81

commit v10 on v9

--- a/solution.py
+++ b/solution.py
@@ -99,7 +99,7 @@
 
 
 def route_kernel(owner_ref, row_ref, index_hbm, send_ref, slot_ref, index_ref, sem):
-    load = pltpu.make_async_copy(index_hbm, index_ref, sem)
+    load = pltpu.make_async_copy(index_hbm.at[pl.ds(0, index_ref.shape[0]), :], index_ref, sem)
     load.start()
     rows = Q * K
     shards = send_ref.shape[0]
@@ -123,15 +123,21 @@
     load.wait()
 
 
-def fetch_kernel(rows_ref, index_ref, out_ref):
+def fetch_kernel(rows_ref, index_ref, index_hbm, out_ref, rest_ref, sem):
+    half = index_ref.shape[0]
+    load = pltpu.make_async_copy(index_hbm.at[pl.ds(half, half), :], rest_ref, sem)
+    load.start()
     shards, cap, width = out_ref.shape
     want = rows_ref[...].astype(f32)
     spread = jnp.broadcast_to(want, (shards, cap, want.shape[2]))
     mask = lax.broadcasted_iota(i32, spread.shape, 1) == lax.broadcasted_iota(i32, spread.shape, 2)
     at = jnp.sum(jnp.where(mask, spread, 0.0).reshape(shards * cap, -1), -1, keepdims=True)
-    lanes = lax.broadcasted_iota(i32, (shards * cap, index_ref.shape[0]), 1).astype(f32)
+    lanes = lax.broadcasted_iota(i32, (shards * cap, half), 1).astype(f32)
     here = (lanes == at).astype(f32).astype(bf16)
+    there = (lanes + half == at).astype(f32).astype(bf16)
     got = dot(here, index_ref[...], ((1,), (0,)))
+    load.wait()
+    got = got + dot(there, rest_ref[...], ((1,), (0,)))
     out_ref[...] = got.reshape(shards, cap, width).astype(bf16)
 
 
@@ -199,7 +205,8 @@
     embedded = states.astype(f32) + dot(hidden_ref[...], down_ref[...], ((0,), (0,)))
 
     norms = jnp.sqrt(jnp.sum(embedded * embedded, -1, keepdims=True) + epsilon)
-    unit = embedded / norms
+    scale = 1.0 / norms
+    unit = embedded * scale
     wide = question_ref[...].astype(f32)
     q_hat = (wide / jnp.sqrt(jnp.sum(wide * wide, -1, keepdims=True) + epsilon)).astype(bf16)
     query = jnp.broadcast_to(q_hat.astype(f32)[:, None, :], (Q, K, width)).reshape(Q * K, width)
@@ -211,7 +218,7 @@
 
     derivative = loss_scale * (share(cosine / normalizer_heat) - share(column(reader_ref[...])))
     derivative_ref[...] = uncolumn(derivative, K)
-    grad_emb = ((derivative / normalizer_heat) * (query - cosine * unit) / norms).astype(bf16)
+    grad_emb = ((derivative / normalizer_heat) * scale * (query - cosine * unit)).astype(bf16)
     grad_emb_ref[...] = grad_emb
     units = mine_ref.shape[0]
     for block, array in enumerate((grad_emb, states)):
@@ -281,7 +288,7 @@
         out_shape=(
             jax.ShapeDtypeStruct((shards, 1, 128), i32),
             jax.ShapeDtypeStruct((Q * K, 128), i32),
-            pltpu.VMEM(index_states.shape, index_states.dtype),
+            pltpu.VMEM((index_states.shape[0] // 2, index_states.shape[1]), index_states.dtype),
         ),
         scratch_shapes=[pltpu.SemaphoreType.DMA],
         compiler_params=pltpu.CompilerParams(vmem_limit_bytes=16 << 20),
@@ -289,14 +296,17 @@
     )(far(owners), far(passage_rows), far(index_states))
 
 
-def fetch(rows_in, index_states):
-    shards, width = rows_in.shape[0], index_states.shape[1]
+def fetch(rows_in, first_half, index_states):
+    shards, (half, width) = rows_in.shape[0], first_half.shape
     return pl.pallas_call(
         fetch_kernel,
+        in_specs=[VMEM, VMEM, HBM],
+        out_specs=VMEM,
+        scratch_shapes=[pltpu.VMEM((half, width), bf16), pltpu.SemaphoreType.DMA],
         out_shape=jax.ShapeDtypeStruct((shards, CAP, width), bf16),
         compiler_params=pltpu.CompilerParams(vmem_limit_bytes=32 << 20),
         name="fetch",
-    )(rows_in, pltpu.with_memory_space_constraint(index_states, pltpu.VMEM))
+    )(rows_in, near(first_half), far(index_states))
 
 
 def near(array):
@@ -441,7 +451,7 @@
     send_rows, slot, index_near = route(owners.reshape(Q, K), passage_rows, index_states, shards)
     send_rows, place = lax.optimization_barrier((send_rows, place))
     rows_in = lax.all_to_all(send_rows, "shard", split_axis=0, concat_axis=0, tiled=True)
-    states_out = fetch(rows_in, index_near)
+    states_out = fetch(rows_in, index_near, index_states)
     got = lax.all_to_all(states_out, "shard", split_axis=0, concat_axis=0, tiled=True)
     derivative, states, grad_emb, slope, hidden, pack, down = forward(
         place, got.reshape(shards * CAP, width), slot, questions, reader, *turn(w_up), w_down

time: 139 us -> 140 us (level)
  no operation moved by 1% of the time
where the time goes in v10:
time: 140 us; the launch traced here: 139 us
  waiting for transfers between devices  73.6 us (53%)
  Pallas kernels  21.8 us (16%)
  starting transfers between devices  20.1 us (14%)
  blocking collectives  18.9 us (13%)
  local copies, waits for them, and re-layouts  1.96 us (1%)
  other arithmetic  1.91 us (1%)
    ppermute x17, waiting for transfers between devices, swap(): return lax.ppermute(array, AXES, partner(step))  54.8 us
    all_to_all x1, blocking collectives, on_device(): lax.all_to_all(send_rows, 'shard', split_axis=0, concat_axis=0, tiled=True)  18.9 us
    all_to_all x1, waiting for transfers between devices, on_device(): lax.all_to_all(states_out, 'shard', split_axis=0, concat_axis=0, tiled=True)  18.8 us
    ppermute x17, starting transfers between devices, swap(): return lax.ppermute(array, AXES, partner(step))  13.7 us
    pallas_call x1, Pallas kernels, forward(): pl.pallas_call(forward_kernel, in_specs=[SMEM] + [VMEM] * 5 + [HBM] * 2,...  7.71 us
    all_to_all x1, starting transfers between devices, on_device(): lax.all_to_all(states_out, 'shard', split_axis=0, concat_axis=0, tiled=True)  6.45 us
    pallas_call x2, Pallas kernels, gradient(): pl.pallas_call(functools.partial(gradient_kernel, x_first, right_at), in_...  4.31 us
    pallas_call x1, Pallas kernels, fetch(): pl.pallas_call(fetch_kernel, in_specs=[VMEM, VMEM, HBM], out_specs=VMEM,...  3.06 us
  transfers between devices with their start and end apart: 18, of which 17 were waited for; matrix products, arithmetic and copies ran while one was open for 1% of the time, Pallas kernels for 7%

profile of v10, /device:TPU:64, one launch (start us, length us, event | category | flops | bytes accessed | tf_op | source)
XLA Modules:
  0.0 139.2 jit_solution(1122143020289098485)
XLA Ops:
  0.6 1.8 %route.1 = (s32[64,1,128]{2,1,0:T(1,128)S(1)}, s32[256,128]{1,0:T(8,128)S(1)}, bf16[512,768]{1,0:T(8,128)(2,1)S(1)}) custom-call(s32[8,32]{1,0:T(8,128)} %bitcast.21, s32[8,32]{1,0:T(8,128)} %row_ref.1, bf16[1024,768]{1,0:T(8,128)(2,1)} %index_hbm.3), custom_call_target="tpu_custom_call" | custom-call | tf_op jit(solution)/shard_map/route/pallas_call | solution.py:284
  2.6 18.9 %all_to_all.10.rows_ref = s32[64,1,128]{2,1,0:T(1,128)S(1)} all-to-all(s32[64,1,128]{2,1,0:T(1,128)S(1)} %get-tuple-element.42), channel_id=1, replica_groups=mesh['shard'=64,'rep'=4] {'shard'}, dimensions={0} | all-to-all | bytes 65536 | tf_op jit(solution)/shard_map/all_to_all | solution.py:453
  21.5 3.1 %fetch.1 = bf16[64,8,768]{2,1,0:T(8,128)(2,1)} custom-call(s32[64,1,128]{2,1,0:T(1,128)S(1)} %all_to_all.10.rows_ref, bf16[512,768]{1,0:T(8,128)(2,1)S(1)} %get-tuple-element.43.index_ref, bf16[1024,768]{1,0:T(8,128)(2,1)} %index_hbm.3), custom_call_target="tpu_custom_call" | custom-call | tf_op jit(solution)/shard_map/fetch/pallas_call | solution.py:301
  24.5 6.5 %all-to-all-start.1 = ((bf16[64,8,768]{2,1,0:T(8,128)(2,1)}), bf16[64,8,768]{2,1,0:T(8,128)(2,1)S(1)}, u32[]{:S(2)}, u32[]{:S(2)}) async-start(bf16[64,8,768]{2,1,0:T(8,128)(2,1)} %fetch.1), calls=%async_computation.1 | async-start | bytes 1572864 | tf_op jit(solution)/shard_map/all_to_all | solution.py:455
  31.0 2.8 %turn.1 = (bf16[768,768]{1,0:T(8,128)(2,1)S(1)}, bf16[2304,768]{1,0:T(8,128)(2,1)S(1)}) custom-call(bf16[768,3072]{1,0:T(8,128)(2,1)} %up_hbm.1), custom_call_target="tpu_custom_call" | custom-call | bytes 16777216 | tf_op jit(solution)/shard_map/turn/pallas_call | solution.py:318
  33.8 1.7 %copy-done = bf16[2304,768]{1,0:T(8,128)(2,1)} copy-done((bf16[2304,768]{1,0:T(8,128)(2,1)}, bf16[2304,768]{1,0:T(8,128)(2,1)S(1)}, u32[]{:S(2)}) %copy-start) | copy-done | bytes 3538968
  35.5 18.8 %all-to-all-done.1 = bf16[64,8,768]{2,1,0:T(8,128)(2,1)S(1)} async-done(((bf16[64,8,768]{2,1,0:T(8,128)(2,1)}), bf16[64,8,768]{2,1,0:T(8,128)(2,1)S(1)}, u32[]{:S(2)}, u32[]{:S(2)}) %all-to-all-start.1) | async-done | bytes 786464 | tf_op jit(solution)/shard_map/all_to_all | solution.py:455
  54.3 7.7 %forward.1 = (f32[8,32]{1,0:T(8,128)}, bf16[256,768]{1,0:T(8,128)(2,1)S(1)}, bf16[256,768]{1,0:T(8,128)(2,1)S(1)}, f32[3072,256]{1,0:T(8,128)S(1)}, bf16[1536,25...) custom-call(s32[4]{0:T(128)S(1)} %pad_add_fusion.place_ref, ...), custom_call_target="tpu_custom_call" | custom-call | flops 2415919104 | bytes 16777216 | tf_op jit(solution)/shard_map/forward/pallas_call | solution.py:336
  62.1 2.1 %backward.1 = (bf16[1536,256]{1,0:T(8,128)(2,1)S(1)}, bf16[1536,256]{1,0:T(8,128)(2,1)S(1)}) custom-call(s32[4]{0:T(128)S(1)} %pad_add_fusion.place_ref, bf16[256,768]{1,0:T(8,128)(2,1)S(1)} %get-tuple-element.50.right_ref.grad_emb_ref, f32[3072,256]{1,0:T(8,128)S(1)} %get-tuple-element.55.slope_ref, bf16[3072,768]{1,0:T(8,128)(2,1)S(1)} %get-tuple-element.56.down_ref), custom_call_target="tpu_custom_call" | custom-call | flops 1207959552 | bytes 8388608 | tf_op jit(solution)/shard_map/backward/pallas_call | solution.py:365
  65.5 2.1 %gradient_down.1 = (f32[4,8,24,384]{3,2,1,0:T(8,128)S(1)}, f32[4,8,24,384]{3,2,1,0:T(8,128)S(1)}, bf16[4,8,24,384]{3,2,1,0:T(8,128)(2,1)S(1)}, bf16[4,8,24,384]{3,2,1,0:T(8,128)(2,1)S(1)}) custom-call(s32[4]{0:T(128)S(1)} %pad_add_fusion.place_ref, bf16[1536,256]{1,0:T(8,128)(2,1)S(1)} %get-tuple-element.48.mine_ref, ...), custom_call_target="tpu_custom_call" | custom-call | flops 1207959552 | bytes 8388608 | tf_op jit(solution)/shard_map/gradient_down/pallas_call | solution.py:382
  67.7 1.6 %collective-permute-start.2 = (bf16[4,8,24,384]{3,2,1,0:T(8,128)(2,1)S(1)}, bf16[4,8,24,384]{3,2,1,0:T(8,128)(2,1)S(1)}, u32[]{:S(2)}, u32[]{:S(2)}) collective-permute-start(bf16[4,8,24,384]{3,2,1,0:T(8,128)(2,1)S(1)} %get-tuple-element.58), channel_id=1, source_target_pairs={{0,1},{1,0},{2,3},{3,2},{4,7},{5,6},{6,5},{7,4},{8,9},{9,8},{10,11... | collective-permute-start | bytes 1769480 | tf_op jit(solution)/shard_map/ppermute | solution.py:81
  69.3 2.2 %gradient_up.1 = (f32[4,8,24,384]{3,2,1,0:T(8,128)S(1)}, f32[4,8,24,384]{3,2,1,0:T(8,128)S(1)}, bf16[4,8,24,384]{3,2,1,0:T(8,128)(2,1)S(1)}, bf16[4,8,24,384]{3,2,1,0:T(8,128)(2,1)S(1)}) custom-call(s32[4]{0:T(128)S(1)} %pad_add_fusion.place_ref, bf16[1536,256]{1,0:T(8,128)(2,1)S(1)} %get-tuple-element.62.mine_ref, ...), custom_call_target="tpu_custom_call" | custom-call | flops 1207959552 | bytes 8388608 | tf_op jit(solution)/shard_map/gradient_up/pallas_call | solution.py:382
  72.5 1.6 %collective-permute-start.8 = (bf16[4,8,24,384]{3,2,1,0:T(8,128)(2,1)S(1)}, bf16[4,8,24,384]{3,2,1,0:T(8,128)(2,1)S(1)}, u32[]{:S(2)}, u32[]{:S(2)}) collective-permute-start(bf16[4,8,24,384]{3,2,1,0:T(8,128)(2,1)S(1)} %get-tuple-element.70), channel_id=1, source_target_pairs={{0,8},{1,9},{2,10},{3,11},{4,28},{5,29},{6,30},{7,31},{8,0},{9,1},... | collective-permute-start | bytes 1769480 | tf_op jit(solution)/shard_map/ppermute | solution.py:81
  74.1 3.6 %collective-permute-done.2 = bf16[4,8,24,384]{3,2,1,0:T(8,128)(2,1)S(1)} collective-permute-done((bf16[4,8,24,384]{3,2,1,0:T(8,128)(2,1)S(1)}, bf16[4,8,24,384]{3,2,1,0:T(8,128)(2,1)S(1)}, u32[]{:S(2)}, u32[]{:S(2)}) %collective-permute-start.2) | collective-permute-done | bytes 589856 | tf_op jit(solution)/shard_map/ppermute | solution.py:81
  77.8 2.8 %collective-permute-start.3 = (bf16[4,8,24,384]{3,2,1,0:T(8,128)(2,1)S(1)}, bf16[4,8,24,384]{3,2,1,0:T(8,128)(2,1)S(1)}, u32[]{:S(2)}, u32[]{:S(2)}) collective-permute-start(bf16[4,8,24,384]{3,2,1,0:T(8,128)(2,1)S(1)} %add_convert_fusion.1), channel_id=1, source_target_pairs={{0,3},{1,2},{2,1},{3,0},{4,5},{5,4},{6,7},{7,6},{8,11},{9,10},{10,... | collective-permute-start | bytes 1769480 | tf_op jit(solution)/shard_map/ppermute | solution.py:81
  80.7 0.8 collective-permute-done.5
  81.6 1.6 %collective-permute-start.7 = (bf16[4,8,24,384]{3,2,1,0:T(8,128)(2,1)S(1)}, bf16[4,8,24,384]{3,2,1,0:T(8,128)(2,1)S(1)}, u32[]{:S(2)}, u32[]{:S(2)}) collective-permute-start(bf16[4,8,24,384]{3,2,1,0:T(8,128)(2,1)S(1)} %add_convert_fusion), channel_id=1, source_target_pairs={{0,24},{1,25},{2,26},{3,27},{4,12},{5,13},{6,14},{7,15},{8,16},{9,... | collective-permute-start | bytes 1769480 | tf_op jit(solution)/shard_map/ppermute | solution.py:81
  83.2 4.1 %collective-permute-done.4 = bf16[4,8,24,384]{3,2,1,0:T(8,128)(2,1)S(1)} collective-permute-done((bf16[4,8,24,384]{3,2,1,0:T(8,128)(2,1)S(1)}, bf16[4,8,24,384]{3,2,1,0:T(8,128)(2,1)S(1)}, u32[]{:S(2)}, u32[]{:S(2)}) %collective-permute-start.4) | collective-permute-done | bytes 589856 | tf_op jit(solution)/shard_map/ppermute | solution.py:81
  87.4 2.3 %collective-permute-done.8 = bf16[4,8,24,384]{3,2,1,0:T(8,128)(2,1)S(1)} collective-permute-done((bf16[4,8,24,384]{3,2,1,0:T(8,128)(2,1)S(1)}, bf16[4,8,24,384]{3,2,1,0:T(8,128)(2,1)S(1)}, u32[]{:S(2)}, u32[]{:S(2)}) %collective-permute-start.8) | collective-permute-done | bytes 589856 | tf_op jit(solution)/shard_map/ppermute | solution.py:81
  89.9 0.9 collective-permute-done.3
  91.4 4.1 %collective-permute-done.7 = bf16[4,8,24,384]{3,2,1,0:T(8,128)(2,1)S(1)} collective-permute-done((bf16[4,8,24,384]{3,2,1,0:T(8,128)(2,1)S(1)}, bf16[4,8,24,384]{3,2,1,0:T(8,128)(2,1)S(1)}, u32[]{:S(2)}, u32[]{:S(2)}) %collective-permute-start.7) | collective-permute-done | bytes 589856 | tf_op jit(solution)/shard_map/ppermute | solution.py:81
  95.8 1.8 %collective-permute-done.6 = bf16[2,8,24,384]{3,2,1,0:T(8,128)(2,1)S(1)} collective-permute-done((bf16[2,8,24,384]{3,2,1,0:T(8,128)(2,1)S(1)}, bf16[2,8,24,384]{3,2,1,0:T(8,128)(2,1)S(1)}, u32[]{:S(2)}, u32[]{:S(2)}) %collective-permute-start.6) | collective-permute-done | bytes 294944 | tf_op jit(solution)/shard_map/ppermute | solution.py:81
  97.7 1.5 %collective-permute-start.9 = (bf16[1,8,24,384]{3,2,1,0:T(8,128)(2,1)S(1)}, bf16[1,8,24,384]{3,2,1,0:T(8,128)(2,1)S(1)}, u32[]{:S(2)}, u32[]{:S(2)}) collective-permute-start(bf16[1,8,24,384]{3,2,1,0:T(8,128)(2,1)S(1)} %slice.160), channel_id=1, source_target_pairs={{0,24},{1,25},{2,26},{3,27},{4,12},{5,13},{6,14},{7,15},{8,16},{9,... | collective-permute-start | bytes 442376 | tf_op jit(solution)/shard_map/ppermute | solution.py:81
  99.3 3.1 %collective-permute-done.10 = bf16[2,8,24,384]{3,2,1,0:T(8,128)(2,1)S(1)} collective-permute-done((bf16[2,8,24,384]{3,2,1,0:T(8,128)(2,1)S(1)}, bf16[2,8,24,384]{3,2,1,0:T(8,128)(2,1)S(1)}, u32[]{:S(2)}, u32[]{:S(2)}) %collective-permute-start.10) | collective-permute-done | bytes 294944 | tf_op jit(solution)/shard_map/ppermute | solution.py:81
  103.0 1.1 collective-permute-done.9
  104.2 4.7 %collective-permute-done.11 = bf16[1,8,24,384]{3,2,1,0:T(8,128)(2,1)S(1)} collective-permute-done((bf16[1,8,24,384]{3,2,1,0:T(8,128)(2,1)S(1)}, bf16[1,8,24,384]{3,2,1,0:T(8,128)(2,1)S(1)}, u32[]{:S(2)}, u32[]{:S(2)}) %collective-permute-start.11) | collective-permute-done | bytes 147488 | tf_op jit(solution)/shard_map/ppermute | solution.py:81
  109.0 0.9 collective-permute-start.12
  109.9 5.8 %collective-permute-done.12 = bf16[4,2,24,384]{3,2,0,1:T(8,128)(2,1)S(1)} collective-permute-done((bf16[4,2,24,384]{3,2,0,1:T(8,128)(2,1)S(1)}, bf16[4,2,24,384]{3,2,0,1:T(8,128)(2,1)S(1)}, u32[]{:S(2)}, u32[]{:S(2)}) %collective-permute-start.12) | collective-permute-done | bytes 147488 | tf_op jit(solution)/shard_map/ppermute | solution.py:81
  115.9 5.7 %collective-permute-done.13 = bf16[2,2,24,384]{3,2,0,1:T(8,128)(2,1)S(1)} collective-permute-done((bf16[2,2,24,384]{3,2,0,1:T(8,128)(2,1)S(1)}, bf16[2,2,24,384]{3,2,0,1:T(8,128)(2,1)S(1)}, u32[]{:S(2)}, u32[]{:S(2)}) %collective-permute-start.13) | collective-permute-done | bytes 73760 | tf_op jit(solution)/shard_map/ppermute | solution.py:81
  121.7 7.0 %collective-permute-done.14 = bf16[1,2,24,384]{3,2,0,1:T(8,128)(2,1)S(1)} collective-permute-done((bf16[1,2,24,384]{3,2,0,1:T(8,128)(2,1)S(1)}, bf16[1,2,24,384]{3,2,0,1:T(8,128)(2,1)S(1)}, u32[]{:S(2)}, u32[]{:S(2)}) %collective-permute-start.14) | collective-permute-done | bytes 36896 | tf_op jit(solution)/shard_map/ppermute | solution.py:81
  128.8 5.1 %collective-permute-done.15 = bf16[2,24,384]{2,1,0:T(8,128)(2,1)S(1)} collective-permute-done((bf16[2,24,384]{2,1,0:T(8,128)(2,1)S(1)}, bf16[2,24,384]{2,1,0:T(8,128)(2,1)S(1)}, u32[]{:S(2)}, u32[]{:S(2)}) %collective-permute-start.15) | collective-permute-done | bytes 36896 | tf_op jit(solution)/shard_map/ppermute | solution.py:81
  134.1 4.3 %collective-permute-done.16 = bf16[2,48,384]{2,1,0:T(8,128)(2,1)S(1)} collective-permute-done((bf16[2,48,384]{2,1,0:T(8,128)(2,1)S(1)}, bf16[2,48,384]{2,1,0:T(8,128)(2,1)S(1)}, u32[]{:S(2)}, u32[]{:S(2)}) %collective-permute-start.16) | collective-permute-done | bytes 73760 | tf_op jit(solution)/shard_map/ppermute | solution.py:81
  (42 shorter events, 6.3 us)
Async XLA Ops:
  24.5 29.8 %all-to-all-start.1 = ((bf16[64,8,768]{2,1,0:T(8,128)(2,1)}), bf16[64,8,768]{2,1,0:T(8,128)(2,1)S(1)}, u32[]{:S(2)}, u32[]{:S(2)}) async-start(bf16[64,8,768]{2,1,0:T(8,128)(2,1)} %fetch.1), calls=%async_computation.1 | async-start | bytes 1572864 | tf_op jit(solution)/shard_map/all_to_all | solution.py:455
  31.0 23.3 %copy-start.1 = (bf16[8,768]{1,0:T(8,128)(2,1)S(1)}, bf16[8,768]{1,0:T(8,128)(2,1)}, u32[]{:S(2)}) copy-start(bf16[8,768]{1,0:T(8,128)(2,1)} %question_ref.1) | copy-start | bytes 36868
  31.0 23.3 %copy-start.2 = (f32[8,32]{1,0:T(8,128)S(1)}, f32[8,32]{1,0:T(8,128)}, u32[]{:S(2)}) copy-start(f32[8,32]{1,0:T(8,128)} %reader_ref.1) | copy-start | bytes 3076
  33.8 1.7 %copy-start = (bf16[2304,768]{1,0:T(8,128)(2,1)}, bf16[2304,768]{1,0:T(8,128)(2,1)S(1)}, u32[]{:S(2)}) copy-start(bf16[2304,768]{1,0:T(8,128)(2,1)S(1)} %get-tuple-element.46.rest_hbm) | copy-start | bytes 10616836
  62.0 3.5 %collective-permute-start = (bf16[3072,256]{1,0:T(8,128)(2,1)S(1)}, bf16[3072,256]{1,0:T(8,128)(2,1)S(1)}, u32[]{:S(2)}, u32[]{:S(2)}) collective-permute-start(bf16[3072,256]{1,0:T(8,128)(2,1)S(1)} %get-tuple-element.49), channel_id=1, source_target_pairs={{0,4},{1,5},{2,6},{3,7},{4,0},{5,1},{6,2},{7,3},{8,12},{9,13},{10,... | collective-permute-start | bytes 4718600 | tf_op jit(solution)/shard_map/ppermute | solution.py:81
  64.3 3.4 %collective-permute-start.1 = (bf16[1536,256]{1,0:T(8,128)(2,1)S(1)}, bf16[1536,256]{1,0:T(8,128)(2,1)S(1)}, u32[]{:S(2)}, u32[]{:S(2)}) collective-permute-start(bf16[1536,256]{1,0:T(8,128)(2,1)S(1)} %get-tuple-element.57), channel_id=1, source_target_pairs={{0,4},{1,5},{2,6},{3,7},{4,0},{5,1},{6,2},{7,3},{8,12},{9,13},{10,... | collective-permute-start | bytes 2359304 | tf_op jit(solution)/shard_map/ppermute | solution.py:81
  67.7 10.0 %collective-permute-start.2 = (bf16[4,8,24,384]{3,2,1,0:T(8,128)(2,1)S(1)}, bf16[4,8,24,384]{3,2,1,0:T(8,128)(2,1)S(1)}, u32[]{:S(2)}, u32[]{:S(2)}) collective-permute-start(bf16[4,8,24,384]{3,2,1,0:T(8,128)(2,1)S(1)} %get-tuple-element.58), channel_id=1, source_target_pairs={{0,1},{1,0},{2,3},{3,2},{4,7},{5,6},{6,5},{7,4},{8,9},{9,8},{10,11... | collective-permute-start | bytes 1769480 | tf_op jit(solution)/shard_map/ppermute | solution.py:81
  71.5 10.0 %collective-permute-start.5 = (bf16[4,8,24,384]{3,2,1,0:T(8,128)(2,1)S(1)}, bf16[4,8,24,384]{3,2,1,0:T(8,128)(2,1)S(1)}, u32[]{:S(2)}, u32[]{:S(2)}) collective-permute-start(bf16[4,8,24,384]{3,2,1,0:T(8,128)(2,1)S(1)} %get-tuple-element.65), channel_id=1, source_target_pairs={{0,8},{1,9},{2,10},{3,11},{4,28},{5,29},{6,30},{7,31},{8,0},{9,1},... | collective-permute-start | bytes 1769480 | tf_op jit(solution)/shard_map/ppermute | solution.py:81
  72.0 15.2 %collective-permute-start.4 = (bf16[4,8,24,384]{3,2,1,0:T(8,128)(2,1)S(1)}, bf16[4,8,24,384]{3,2,1,0:T(8,128)(2,1)S(1)}, u32[]{:S(2)}, u32[]{:S(2)}) collective-permute-start(bf16[4,8,24,384]{3,2,1,0:T(8,128)(2,1)S(1)} %get-tuple-element.61), channel_id=1, source_target_pairs={{0,1},{1,0},{2,3},{3,2},{4,7},{5,6},{6,5},{7,4},{8,9},{9,8},{10,11... | collective-permute-start | bytes 1769480 | tf_op jit(solution)/shard_map/ppermute | solution.py:81
  72.5 17.1 %collective-permute-start.8 = (bf16[4,8,24,384]{3,2,1,0:T(8,128)(2,1)S(1)}, bf16[4,8,24,384]{3,2,1,0:T(8,128)(2,1)S(1)}, u32[]{:S(2)}, u32[]{:S(2)}) collective-permute-start(bf16[4,8,24,384]{3,2,1,0:T(8,128)(2,1)S(1)} %get-tuple-element.70), channel_id=1, source_target_pairs={{0,8},{1,9},{2,10},{3,11},{4,28},{5,29},{6,30},{7,31},{8,0},{9,1},... | collective-permute-start | bytes 1769480 | tf_op jit(solution)/shard_map/ppermute | solution.py:81
  77.8 12.9 %collective-permute-start.3 = (bf16[4,8,24,384]{3,2,1,0:T(8,128)(2,1)S(1)}, bf16[4,8,24,384]{3,2,1,0:T(8,128)(2,1)S(1)}, u32[]{:S(2)}, u32[]{:S(2)}) collective-permute-start(bf16[4,8,24,384]{3,2,1,0:T(8,128)(2,1)S(1)} %add_convert_fusion.1), channel_id=1, source_target_pairs={{0,3},{1,2},{2,1},{3,0},{4,5},{5,4},{6,7},{7,6},{8,11},{9,10},{10,... | collective-permute-start | bytes 1769480 | tf_op jit(solution)/shard_map/ppermute | solution.py:81
  81.6 13.9 %collective-permute-start.7 = (bf16[4,8,24,384]{3,2,1,0:T(8,128)(2,1)S(1)}, bf16[4,8,24,384]{3,2,1,0:T(8,128)(2,1)S(1)}, u32[]{:S(2)}, u32[]{:S(2)}) collective-permute-start(bf16[4,8,24,384]{3,2,1,0:T(8,128)(2,1)S(1)} %add_convert_fusion), channel_id=1, source_target_pairs={{0,24},{1,25},{2,26},{3,27},{4,12},{5,13},{6,14},{7,15},{8,16},{9,... | collective-permute-start | bytes 1769480 | tf_op jit(solution)/shard_map/ppermute | solution.py:81
  90.8 6.8 %collective-permute-start.6 = (bf16[2,8,24,384]{3,2,1,0:T(8,128)(2,1)S(1)}, bf16[2,8,24,384]{3,2,1,0:T(8,128)(2,1)S(1)}, u32[]{:S(2)}, u32[]{:S(2)}) collective-permute-start(bf16[2,8,24,384]{3,2,1,0:T(8,128)(2,1)S(1)} %add_convert_fusion.3), channel_id=1, source_target_pairs={{0,8},{1,9},{2,10},{3,11},{4,28},{5,29},{6,30},{7,31},{8,0},{9,1},... | collective-permute-start | bytes 884744 | tf_op jit(solution)/shard_map/ppermute | solution.py:81
  95.5 6.8 %collective-permute-start.10 = (bf16[2,8,24,384]{3,2,1,0:T(8,128)(2,1)S(1)}, bf16[2,8,24,384]{3,2,1,0:T(8,128)(2,1)S(1)}, u32[]{:S(2)}, u32[]{:S(2)}) collective-permute-start(bf16[2,8,24,384]{3,2,1,0:T(8,128)(2,1)S(1)} %add_convert_fusion.2), channel_id=1, source_target_pairs={{0,1},{1,0},{2,3},{3,2},{4,7},{5,6},{6,5},{7,4},{8,9},{9,8},{10,11... | collective-permute-start | bytes 884744 | tf_op jit(solution)/shard_map/ppermute | solution.py:81
  97.7 6.4 %collective-permute-start.9 = (bf16[1,8,24,384]{3,2,1,0:T(8,128)(2,1)S(1)}, bf16[1,8,24,384]{3,2,1,0:T(8,128)(2,1)S(1)}, u32[]{:S(2)}, u32[]{:S(2)}) collective-permute-start(bf16[1,8,24,384]{3,2,1,0:T(8,128)(2,1)S(1)} %slice.160), channel_id=1, source_target_pairs={{0,24},{1,25},{2,26},{3,27},{4,12},{5,13},{6,14},{7,15},{8,16},{9,... | collective-permute-start | bytes 442376 | tf_op jit(solution)/shard_map/ppermute | solution.py:81
  102.5 6.4 %collective-permute-start.11 = (bf16[1,8,24,384]{3,2,1,0:T(8,128)(2,1)S(1)}, bf16[1,8,24,384]{3,2,1,0:T(8,128)(2,1)S(1)}, u32[]{:S(2)}, u32[]{:S(2)}) collective-permute-start(bf16[1,8,24,384]{3,2,1,0:T(8,128)(2,1)S(1)} %slice.159), channel_id=1, source_target_pairs={{0,3},{1,2},{2,1},{3,0},{4,5},{5,4},{6,7},{7,6},{8,11},{9,10},{10,... | collective-permute-start | bytes 442376 | tf_op jit(solution)/shard_map/ppermute | solution.py:81
  109.0 6.7 %collective-permute-start.12 = (bf16[4,2,24,384]{3,2,0,1:T(8,128)(2,1)S(1)}, bf16[4,2,24,384]{3,2,0,1:T(8,128)(2,1)S(1)}, u32[]{:S(2)}, u32[]{:S(2)}) collective-permute-start(bf16[4,2,24,384]{3,2,0,1:T(8,128)(2,1)S(1)} %slice.158), channel_id=1, source_target_pairs={{0,32},{1,33},{2,34},{3,35},{4,228},{5,229},{6,230},{7,231},{8,40}... | collective-permute-start | bytes 442376 | tf_op jit(solution)/shard_map/ppermute | solution.py:81
  115.8 5.8 %collective-permute-start.13 = (bf16[2,2,24,384]{3,2,0,1:T(8,128)(2,1)S(1)}, bf16[2,2,24,384]{3,2,0,1:T(8,128)(2,1)S(1)}, u32[]{:S(2)}, u32[]{:S(2)}) collective-permute-start(bf16[2,2,24,384]{3,2,0,1:T(8,128)(2,1)S(1)} %get-tuple-element.81), channel_id=1, source_target_pairs={{0,64},{1,65},{2,66},{3,67},{4,196},{5,197},{6,198},{7,199},{8,72}... | collective-permute-start | bytes 221192 | tf_op jit(solution)/shard_map/ppermute | solution.py:81
  121.6 7.1 %collective-permute-start.14 = (bf16[1,2,24,384]{3,2,0,1:T(8,128)(2,1)S(1)}, bf16[1,2,24,384]{3,2,0,1:T(8,128)(2,1)S(1)}, u32[]{:S(2)}, u32[]{:S(2)}) collective-permute-start(bf16[1,2,24,384]{3,2,0,1:T(8,128)(2,1)S(1)} %fusion.6), channel_id=1, source_target_pairs={{0,224},{1,225},{2,226},{3,227},{4,36},{5,37},{6,38},{7,39},{8,232... | collective-permute-start | bytes 110600 | tf_op jit(solution)/shard_map/ppermute | solution.py:81
  128.7 5.3 %collective-permute-start.15 = (bf16[2,24,384]{2,1,0:T(8,128)(2,1)S(1)}, bf16[2,24,384]{2,1,0:T(8,128)(2,1)S(1)}, u32[]{:S(2)}, u32[]{:S(2)}) collective-permute-start(bf16[2,24,384]{2,1,0:T(8,128)(2,1)S(1)} %fusion.9), channel_id=1, source_target_pairs={{0,3},{1,2},{2,1},{3,0},{4,5},{5,4},{6,7},{7,6},{8,11},{9,10},{10,... | collective-permute-start | bytes 110600 | tf_op jit(solution)/shard_map/ppermute | solution.py:81
  134.0 4.4 %collective-permute-start.16 = (bf16[2,48,384]{2,1,0:T(8,128)(2,1)S(1)}, bf16[2,48,384]{2,1,0:T(8,128)(2,1)S(1)}, u32[]{:S(2)}, u32[]{:S(2)}) collective-permute-start(bf16[2,48,384]{2,1,0:T(8,128)(2,1)S(1)} %pad_maximum_fusion.1), channel_id=1, source_target_pairs={{0,1},{1,0},{2,3},{3,2},{4,7},{5,6},{6,5},{7,4},{8,9},{9,8},{10,11... | collective-permute-start | bytes 221192 | tf_op jit(solution)/shard_map/ppermute | solution.py:81
